TPU v7x, 32 devices: a whole 2x2x4 slice. The times are simulated.
32 devices in a mesh: head: 4 (over y, core), blk: 8 (over z, x).
Axes of the slice: x: 2, y: 2, z: 4, core: 2. Of those that a mesh axis runs over, the one named last changes fastest.
Arguments:
- tokens: bfloat16 [4, 2048, 1024], P(None, ('head', 'blk')), may hold values from -6 to 6
- chosen: int32 [4, 256], replicated, may hold values from 0 to 2047, as said below
- w_qkv: bfloat16 [1024, 3072], P(('head', 'blk')), may hold values from -0.1875 to 0.1875
- w_out: bfloat16 [1024, 1024], P(('head', 'blk')), may hold values from -1.5 to 1.5
- w_up: bfloat16 [1024, 4096], P(('head', 'blk')), may hold values from -0.1875 to 0.1875
- w_down: bfloat16 [4096, 1024], P(('head', 'blk')), may hold values from -0.09375 to 0.09375
- gain_attn: bfloat16 [1024], P(('head', 'blk')), may hold values from 0.099609375 to 1.8984375
- gain_mlp: bfloat16 [1024], P(('head', 'blk')), may hold values from 0.099609375 to 1.8984375
- router: bfloat16 [1024], P(('head', 'blk')), may hold values from -0.1875 to 0.1875
- cotangent: bfloat16 [4, 2048, 1024], P(None, ('head', 'blk')), may hold values from -6 to 6
Outputs:
- output: bfloat16 [4, 2048, 1024], P(None, ('head', 'blk'))
- grad_tokens: bfloat16 [4, 2048, 1024], P(None, ('head', 'blk'))
- grad_qkv: float32 [1024, 3072], P(('head', 'blk'))
- grad_out: float32 [1024, 1024], P(('head', 'blk'))
- grad_up: float32 [1024, 4096], P(('head', 'blk'))
- grad_down: float32 [4096, 1024], P(('head', 'blk'))
- grad_gain_attn: float32 [1024], P(('head', 'blk'))
- grad_gain_mlp: float32 [1024], P(('head', 'blk'))
- grad_router: float32 [1024], P(('head', 'blk'))
Inputs may be any that keep to these rules, and one draw needn't show every extreme that they name: `chosen`: each row lists 256 distinct positions of one sequence in ascending order. Of the 64 positions that one device holds, at most 16 are listed; in every sequence some device holds exactly 16 and some device none.
All inputs are finite; a program needn't handle non-finite values.
Results may differ from a plain program's by a relative error of at most 0.024.
Values may be sent and summed in bfloat16 or wider, within the bound.
No kernel may reach another device: no remote copies, remote signals or barrier semaphores. Data moves between devices by JAX's collectives and lax.ppermute only.
A program may use at most 192 MiB of HBM per device.

v0:
```python
import jax
import jax.numpy as jnp
from jax import lax
from jax.sharding import PartitionSpec as P

HEADS = 16
HDIM = 64


epsilon = 1e-06
neg_large = -1e30


def rms_norm(values, gain_vec):
    inverse_rms = lax.rsqrt(jnp.mean(values * values, axis=-1, keepdims=True) + epsilon)
    return values * inverse_rms * gain_vec


def exact_gelu(values):
    return jax.nn.gelu(values, approximate=False)


def take_rows(seq_rows, row_index):
    return seq_rows[row_index]


def add_rows(seq_rows, row_index, additions):
    return seq_rows.at[row_index].add(additions)


def shards(tokens, chosen, w_qkv, w_out, w_up, w_down, gain_attn, gain_mlp, router, cotangent):
    head_count = lax.axis_size("head")
    block_count = lax.axis_size("blk")
    shard_count = head_count * block_count
    seq_count, seg_len, model_width = tokens.shape
    cap_len = seg_len // 4
    routed_count = chosen.shape[1]
    seq_len = seg_len * shard_count
    local_heads = HEADS // head_count
    slot_rows = head_count * cap_len
    scale_factor = HDIM ** (-0.5)
    head_index = lax.axis_index("head")
    block_index = lax.axis_index("blk")
    my_shard = head_index * block_count + block_index
    bounds = jnp.arange(shard_count + 1, dtype=jnp.int32) * seg_len
    before = jax.vmap(lambda chosen_row: jnp.searchsorted(chosen_row, bounds, side="left"))(chosen)
    first_index = before[:, :-1]
    shard_load = before[:, 1:] - first_index
    slot_iota = jnp.arange(cap_len, dtype=jnp.int32)
    live_table = slot_iota[None, None, :] < shard_load[:, :, None]
    lookup = jnp.minimum(first_index[:, :, None] + slot_iota[None, None, :], routed_count - 1)
    place_table = jnp.take_along_axis(
        chosen, lookup.reshape(seq_count, shard_count * cap_len), axis=1
    )
    place_table = jnp.where(
        live_table, place_table.reshape(seq_count, shard_count, cap_len), seq_len
    )
    my_positions = lax.dynamic_index_in_dim(place_table, my_shard, 1, False)
    my_live = lax.dynamic_index_in_dim(live_table, my_shard, 1, False)
    local_rows = jnp.clip(my_positions - my_shard * seg_len, 0, seg_len - 1)
    cycle_positions = place_table.reshape(seq_count, head_count, block_count, cap_len).transpose(
        0, 2, 1, 3
    )
    cycle_positions = cycle_positions.reshape(seq_count, block_count * slot_rows)
    query_positions = lax.dynamic_slice_in_dim(
        cycle_positions, block_index * slot_rows, slot_rows, 1
    )
    live_weight = my_live.astype(jnp.float32)[:, :, None]
    gathered = (
        lax.all_gather(w_qkv, ("head", "blk"), axis=0, tiled=True),
        lax.all_gather(w_out, ("head", "blk"), axis=0, tiled=True),
        lax.all_gather(w_up, ("head", "blk"), axis=0, tiled=True),
        lax.all_gather(w_down, ("head", "blk"), axis=0, tiled=True),
        lax.all_gather(gain_attn, ("head", "blk"), axis=0, tiled=True),
        lax.all_gather(gain_mlp, ("head", "blk"), axis=0, tiled=True),
        lax.all_gather(router, ("head", "blk"), axis=0, tiled=True),
    )
    full_qkv, full_out, full_up, full_down, full_gain_attn, full_gain_mlp, full_router = gathered
    picked = jax.vmap(take_rows)(tokens, local_rows)
    picked = jnp.where(my_live[:, :, None], picked, jnp.zeros_like(picked))
    picked_exact = picked.astype(jnp.float32)
    router_gate = jax.nn.sigmoid(
        jnp.einsum("scd,d->sc", picked, full_router, preferred_element_type=jnp.float32)
    )
    normed_exact, norm_attn_back = jax.vjp(
        rms_norm, picked_exact, full_gain_attn.astype(jnp.float32)
    )
    normed = normed_exact.astype(jnp.bfloat16)
    joined = jnp.einsum("scd,de->sce", normed, full_qkv, preferred_element_type=jnp.float32).astype(
        jnp.bfloat16
    )
    to_heads = lax.all_to_all(
        joined.reshape(seq_count, cap_len, 3, model_width),
        "head",
        split_axis=3,
        concat_axis=1,
        tiled=True,
    )
    queries_tok = to_heads[:, :, 0]
    queries_heads = queries_tok.reshape(seq_count, slot_rows, local_heads, HDIM)
    key_values = to_heads[:, :, 1:3]
    my_keys = key_values[:, :, 0].reshape(seq_count, slot_rows, local_heads, HDIM)
    my_values = key_values[:, :, 1].reshape(seq_count, slot_rows, local_heads, HDIM)
    stat_shape = (seq_count, local_heads, slot_rows)
    piece = lax.all_gather(key_values, "blk", axis=1, tiled=True)
    run_max = jnp.full(stat_shape, neg_large, jnp.float32)
    piece_rows = piece.shape[1]
    key_pos = cycle_positions
    keys_piece = piece[:, :, 0].reshape(seq_count, piece_rows, local_heads, HDIM)
    values_piece = piece[:, :, 1].reshape(seq_count, piece_rows, local_heads, HDIM)
    scores = (
        jnp.einsum("sqhd,skhd->shqk", queries_heads, keys_piece, preferred_element_type=jnp.float32)
        * scale_factor
    )
    allowed = key_pos[:, None, None, :] <= query_positions[:, None, :, None]
    scores = jnp.where(allowed, scores, neg_large)
    new_max = jnp.maximum(run_max, jnp.max(scores, axis=3))
    prob_block = jnp.where(allowed, jnp.exp(scores - new_max[..., None]), 0.0)
    new_total = jnp.sum(prob_block, axis=3)
    added = jnp.einsum(
        "shqk,skhd->sqhd",
        prob_block.astype(jnp.bfloat16),
        values_piece,
        preferred_element_type=jnp.float32,
    )
    attended_exact = added / new_total.transpose(0, 2, 1)[..., None]
    log_sum = new_max + jnp.log(new_total)
    attended_tok = attended_exact.astype(jnp.bfloat16).reshape(
        seq_count, slot_rows, local_heads * HDIM
    )
    attended = lax.all_to_all(attended_tok, "head", split_axis=1, concat_axis=2, tiled=True)
    branch = jnp.einsum("sce,ed->scd", attended, full_out, preferred_element_type=jnp.float32)
    hidden_state = picked_exact + branch
    normed_mlp_exact, norm_mlp_back = jax.vjp(
        rms_norm, hidden_state, full_gain_mlp.astype(jnp.float32)
    )
    normed_mlp = normed_mlp_exact.astype(jnp.bfloat16)
    upper = jnp.einsum("scd,di->sci", normed_mlp, full_up, preferred_element_type=jnp.float32)
    active_exact, gelu_back = jax.vjp(exact_gelu, upper)
    active = active_exact.astype(jnp.bfloat16)
    result = jnp.einsum("sci,id->scd", active, full_down, preferred_element_type=jnp.float32)
    combined = branch + result
    update = router_gate[:, :, None] * combined * live_weight
    output = jax.vmap(add_rows)(tokens.astype(jnp.float32), local_rows, update).astype(jnp.bfloat16)
    regathered = (
        lax.all_gather(w_qkv, ("head", "blk"), axis=0, tiled=True),
        lax.all_gather(w_out, ("head", "blk"), axis=0, tiled=True),
        lax.all_gather(w_up, ("head", "blk"), axis=0, tiled=True),
        lax.all_gather(w_down, ("head", "blk"), axis=0, tiled=True),
        lax.all_gather(gain_attn, ("head", "blk"), axis=0, tiled=True),
        lax.all_gather(gain_mlp, ("head", "blk"), axis=0, tiled=True),
        lax.all_gather(router, ("head", "blk"), axis=0, tiled=True),
    )
    back_qkv, back_out, back_up, back_down, back_gain_attn, back_gain_mlp, back_router = regathered
    picked_cot = jax.vmap(take_rows)(cotangent, local_rows).astype(jnp.float32) * live_weight
    d_update = router_gate[:, :, None] * picked_cot
    d_logit = jnp.sum(picked_cot * combined, axis=2) * router_gate * (1.0 - router_gate)
    grad_router = jnp.einsum("sc,scd->d", d_logit, picked_exact, precision=lax.Precision.HIGHEST)
    d_result = d_update.astype(jnp.bfloat16)
    d_active = jnp.einsum("scd,id->sci", d_result, back_down, preferred_element_type=jnp.float32)
    d_upper = gelu_back(d_active)[0].astype(jnp.bfloat16)
    d_normed_mlp = jnp.einsum("sci,di->scd", d_upper, back_up, preferred_element_type=jnp.float32)
    d_hidden, grad_gain_mlp = norm_mlp_back(d_normed_mlp)
    d_branch = (d_update + d_hidden).astype(jnp.bfloat16)
    d_attended = jnp.einsum(
        "scd,ed->sce", d_branch, back_out, preferred_element_type=jnp.float32
    ).astype(jnp.bfloat16)
    d_att_tok = lax.all_to_all(d_attended, "head", split_axis=2, concat_axis=1, tiled=True)
    d_att_heads = d_att_tok.reshape(seq_count, slot_rows, local_heads, HDIM)
    delta_tok = jnp.sum(d_att_heads.astype(jnp.float32) * attended_exact, axis=3)
    delta_sq = delta_tok.transpose(0, 2, 1)
    piece = lax.all_gather(key_values, "blk", axis=1, tiled=True)
    piece_rows = piece.shape[1]
    key_pos = cycle_positions
    keys_piece = piece[:, :, 0].reshape(seq_count, piece_rows, local_heads, HDIM)
    values_piece = piece[:, :, 1].reshape(seq_count, piece_rows, local_heads, HDIM)
    scores = (
        jnp.einsum("sqhd,skhd->shqk", queries_heads, keys_piece, preferred_element_type=jnp.float32)
        * scale_factor
    )
    allowed = key_pos[:, None, None, :] <= query_positions[:, None, :, None]
    prob_block = jnp.where(allowed, jnp.exp(scores - log_sum[..., None]), 0.0)
    d_prob = jnp.einsum(
        "sqhd,skhd->shqk", d_att_heads, values_piece, preferred_element_type=jnp.float32
    )
    d_scores = (prob_block * (d_prob - delta_sq[..., None])).astype(jnp.bfloat16)
    d_queries = (
        jnp.einsum("shqk,skhd->sqhd", d_scores, keys_piece, preferred_element_type=jnp.float32)
        * scale_factor
    )
    lse_tok = log_sum.transpose(0, 2, 1)
    lse_high = lse_tok.astype(jnp.bfloat16)
    lse_low = (lse_tok - lse_high.astype(jnp.float32)).astype(jnp.bfloat16)
    delta_high = delta_tok.astype(jnp.bfloat16)
    delta_low = (delta_tok - delta_high.astype(jnp.float32)).astype(jnp.bfloat16)
    query_piece = lax.all_gather(queries_tok, "blk", axis=1, tiled=True)
    dout_piece = lax.all_gather(d_att_tok, "blk", axis=1, tiled=True)
    piece_lse_high = lax.all_gather(lse_high, "blk", axis=1, tiled=True)
    piece_lse_low = lax.all_gather(lse_low, "blk", axis=1, tiled=True)
    piece_delta_high = lax.all_gather(delta_high, "blk", axis=1, tiled=True)
    piece_delta_low = lax.all_gather(delta_low, "blk", axis=1, tiled=True)
    piece_rows = query_piece.shape[1]
    query_heads = query_piece.reshape(seq_count, piece_rows, local_heads, HDIM)
    dout_heads = dout_piece.reshape(seq_count, piece_rows, local_heads, HDIM)
    piece_lse = (piece_lse_high.astype(jnp.float32) + piece_lse_low.astype(jnp.float32)).transpose(
        0, 2, 1
    )
    piece_delta = (
        piece_delta_high.astype(jnp.float32) + piece_delta_low.astype(jnp.float32)
    ).transpose(0, 2, 1)
    scores = (
        jnp.einsum("sqhd,skhd->shqk", query_heads, my_keys, preferred_element_type=jnp.float32)
        * scale_factor
    )
    allowed = query_positions[:, None, None, :] <= cycle_positions[:, None, :, None]
    prob_block = jnp.where(allowed, jnp.exp(scores - piece_lse[..., None]), 0.0)
    grad_values = jnp.einsum(
        "shqk,sqhd->skhd",
        prob_block.astype(jnp.bfloat16),
        dout_heads,
        preferred_element_type=jnp.float32,
    )
    d_prob = jnp.einsum(
        "sqhd,skhd->shqk", dout_heads, my_values, preferred_element_type=jnp.float32
    )
    d_scores = (prob_block * (d_prob - piece_delta[..., None])).astype(jnp.bfloat16)
    grad_keys = (
        jnp.einsum("shqk,sqhd->skhd", d_scores, query_heads, preferred_element_type=jnp.float32)
        * scale_factor
    )
    d_heads = jnp.stack(
        [
            d_queries.astype(jnp.bfloat16),
            grad_keys.astype(jnp.bfloat16),
            grad_values.astype(jnp.bfloat16),
        ],
        axis=2,
    )
    d_heads = d_heads.reshape(seq_count, slot_rows, 3, local_heads * HDIM)
    d_joined = lax.all_to_all(d_heads, "head", split_axis=1, concat_axis=3, tiled=True).reshape(
        seq_count, cap_len, 3 * model_width
    )
    d_normed = jnp.einsum("sce,de->scd", d_joined, back_qkv, preferred_element_type=jnp.float32)
    d_picked_norm, grad_gain_attn = norm_attn_back(d_normed)
    d_picked = (
        d_hidden
        + d_picked_norm
        + d_logit[:, :, None] * back_router.astype(jnp.float32)[None, None, :]
    )
    grad_tokens = jax.vmap(add_rows)(
        cotangent.astype(jnp.float32), local_rows, d_picked * live_weight
    ).astype(jnp.bfloat16)
    grad_qkv = jnp.einsum("scd,sce->de", normed, d_joined, preferred_element_type=jnp.float32)
    grad_out = jnp.einsum("sce,scd->ed", attended, d_branch, preferred_element_type=jnp.float32)
    grad_up = jnp.einsum("scd,sci->di", normed_mlp, d_upper, preferred_element_type=jnp.float32)
    grad_down = jnp.einsum("sci,scd->id", active, d_result, preferred_element_type=jnp.float32)
    owned = (
        lax.psum_scatter(grad_qkv, ("head", "blk"), scatter_dimension=0, tiled=True),
        lax.psum_scatter(grad_out, ("head", "blk"), scatter_dimension=0, tiled=True),
        lax.psum_scatter(grad_up, ("head", "blk"), scatter_dimension=0, tiled=True),
        lax.psum_scatter(grad_down, ("head", "blk"), scatter_dimension=0, tiled=True),
        lax.psum_scatter(grad_gain_attn, ("head", "blk"), scatter_dimension=0, tiled=True),
        lax.psum_scatter(grad_gain_mlp, ("head", "blk"), scatter_dimension=0, tiled=True),
        lax.psum_scatter(grad_router, ("head", "blk"), scatter_dimension=0, tiled=True),
    )
    return (
        output,
        grad_tokens,
        owned[0],
        owned[1],
        owned[2],
        owned[3],
        owned[4],
        owned[5],
        owned[6],
    )


def solution(mesh):
    in_specs = (
        P(None, ("head", "blk"), None),
        P(),
        P(("head", "blk"), None),
        P(("head", "blk"), None),
        P(("head", "blk"), None),
        P(("head", "blk"), None),
        P(("head", "blk")),
        P(("head", "blk")),
        P(("head", "blk")),
        P(None, ("head", "blk"), None),
    )
    out_specs = (
        P(None, ("head", "blk"), None),
        P(None, ("head", "blk"), None),
        P(("head", "blk"), None),
        P(("head", "blk"), None),
        P(("head", "blk"), None),
        P(("head", "blk"), None),
        P(("head", "blk")),
        P(("head", "blk")),
        P(("head", "blk")),
    )
    return jax.shard_map(shards, mesh=mesh, in_specs=in_specs, out_specs=out_specs, check_vma=False)
```

profile of v0, /device:TPU:0, one launch (start us, length us, event | category | flops | bytes accessed | tf_op | source)
XLA Modules:
  0.0 1519.8 jit_solution(8068638697563409654)
XLA Ops:
  8.0 26.2 %while.24 = (s32[]{:T(128)}, u32[4,33]{1,0:T(4,128)S(1)}, u32[4,33]{1,0:T(4,128)S(1)}, s32[4,256]{1,0:T(4,128)}, s32[]{:T(128)}, /*index=5*/s32[]{:T(128)}) while((s32[]{:T(128)}, u32[4,33]{1,0:T(4,128)S(1)}, u32[4,33]{1,0:T(4,128)S(1)}, s32[4,256]{1,0:T(4,128)}, s32[]{:T(128)}, /*index=5*/s32[]{:T(128)}) %tuple.56), condition=%wide.region_1.2_spmd.clone, body=%wide.region_0.1_spmd.clone.sunk | while | flops 3072 | bytes 11169 | solution.py:46
  8.1 2.7 gather_fusion
  11.0 2.7 gather_fusion
  13.9 2.7 gather_fusion
  16.8 2.7 gather_fusion
  19.8 2.7 gather_fusion
  22.7 2.7 gather_fusion
  25.6 2.7 gather_fusion
  28.5 2.7 gather_fusion
  31.4 2.7 gather_fusion
  34.9 17.7 %gather_fusion.1 = s32[2048]{0:T(1024)S(1)} fusion(s32[4,256]{1,0:T(4,128)S(1)} %copy-done, s32[2048]{0:T(1024)S(1)} %bitcast.171), kind=kCustom, calls=%fused_computation.1 | custom fusion | bytes 32768 | tf_op jit(solution)/shard_map/jit(take_along_axis)/gather | solution.py:52
  54.3 43.0 %all-reduce.7 = (bf16[1024]{0:T(1024)(128)(2,1)S(1)}, bf16[1024]{0:T(1024)(128)(2,1)}, bf16[1024]{0:T(1024)(128)(2,1)S(1)}) all-reduce(bf16[1024]{0:T(1024)(128)(2,1)S(1)} %dynamic-update-slice.1, bf16[1024]{0:T(1024)(128)(2,1)S(1)} %dynamic-update-slice.2, ...), channel_id=1, replica_groups=mesh['head'=4,'blk'=8] {'head','blk'}, use_global_device_ids=true, to_apply=%add.1 | all-reduce | flops 3072 | bytes 12288
  99.3 4.0 fusion.14
  104.6 5.1 copy.139
  109.7 4.0 reshape.309
  113.7 11.6 all_to_all.69
  125.3 3.5 reshape.310
  128.8 3.6 copy.141
  139.7 43.6 %all-gather.11.cloned.1.call-done = bf16[4,512,2,256]{3,1,2,0:T(8,128)(2,1)} async-done(((bf16[4,64,2,256]{3,1,2,0:T(8,128)(2,1)}), bf16[4,512,2,256]{3,1,2,0:T(8,128)(2,1)}) %all-gather.11.cloned.1.call-update) | async-done | bytes 2097168 | tf_op jit(solution)/shard_map/all_gather | solution.py:105
  191.7 3.3 all-to-all-start.1
  199.7 41.7 %all-gather.13.cloned.1.call-done = bf16[1024,1024]{1,0:T(8,128)(2,1)} async-done(((bf16[32,1024]{1,0:T(8,128)(2,1)}), bf16[1024,1024]{1,0:T(8,128)(2,1)}) %all-gather.13.cloned.1.call-update) | async-done | bytes 2097168 | tf_op jit(solution)/shard_map/all_gather | solution.py:71
  241.4 2.8 convert_add_fusion
  244.8 75.7 %all-gather.15.cloned.1.call-done = bf16[1024,4096]{1,0:T(8,128)(2,1)} async-done(((bf16[32,4096]{1,0:T(8,128)(2,1)}), bf16[1024,4096]{1,0:T(8,128)(2,1)}) %all-gather.15.cloned.1.call-update) | async-done | bytes 8388624 | tf_op jit(solution)/shard_map/all_gather | solution.py:72
  320.5 5.9 fusion.78
  326.4 72.9 %all-gather.17.cloned.1.call-done = bf16[4096,1024]{1,0:T(8,128)(2,1)} async-done(((bf16[128,1024]{1,0:T(8,128)(2,1)}), bf16[4096,1024]{1,0:T(8,128)(2,1)}) %all-gather.17.cloned.1.call-update) | async-done | bytes 8388624 | tf_op jit(solution)/shard_map/all_gather | solution.py:73
  399.4 8.1 add_convert_fusion
  407.6 3.3 multiply_reduce_fusion.1
  411.3 5.0 fusion.71
  422.1 8.6 all_to_all.70
  433.7 3.7 convolution_bitcast_fusion.3
  443.2 32.3 %all_gather.57 = bf16[4,512,4]{2,0,1:T(4,128)(2,1)S(1)} all-gather(bf16[4,64,4]{2,0,1:T(4,128)(2,1)S(1)} %copy.156), channel_id=1, replica_groups=mesh['head'=4,'blk'=8] {'blk'}, dimensions={1}, use_global_device_ids=true | all-gather | bytes 18432 | tf_op jit(solution)/shard_map/all_gather | solution.py:198
  475.5 31.8 %all_gather.58 = bf16[4,512,4]{2,0,1:T(4,128)(2,1)S(1)} all-gather(bf16[4,64,4]{2,0,1:T(4,128)(2,1)S(1)} %copy.157), channel_id=1, replica_groups=mesh['head'=4,'blk'=8] {'blk'}, dimensions={1}, use_global_device_ids=true | all-gather | bytes 18432 | tf_op jit(solution)/shard_map/all_gather | solution.py:199
  509.9 3.4 exponential_select_fusion
  518.1 3.3 fusion.28
  523.4 32.0 %all_gather.60 = bf16[4,512,4]{2,0,1:T(4,128)(2,1)S(1)} all-gather(bf16[4,64,4]{2,0,1:T(4,128)(2,1)S(1)} %copy.162), channel_id=1, replica_groups=mesh['head'=4,'blk'=8] {'blk'}, dimensions={1}, use_global_device_ids=true | all-gather | bytes 18432 | tf_op jit(solution)/shard_map/all_gather | solution.py:200
  555.4 32.5 %all_gather.61 = bf16[4,512,4]{2,0,1:T(4,128)(2,1)S(1)} all-gather(bf16[4,64,4]{2,0,1:T(4,128)(2,1)S(1)} %copy.163), channel_id=1, replica_groups=mesh['head'=4,'blk'=8] {'blk'}, dimensions={1}, use_global_device_ids=true | all-gather | bytes 18432 | tf_op jit(solution)/shard_map/all_gather | solution.py:201
  590.6 2.7 fusion.29
  598.6 10.7 all_to_all.71
  609.8 6.5 convolution_bitcast_fusion.2
  617.5 8.1 convolution_bitcast_fusion
  626.6 8.2 convolution_bitcast_fusion.1
  636.3 6.9 scatter_fusion
  644.4 5.3 fusion.60
  649.7 37.6 %all-reduce.6 = (f32[1024]{0:T(1024)S(1)}, f32[1024]{0:T(1024)S(1)}, f32[1024]{0:T(1024)S(1)}) all-reduce(f32[1024]{0:T(1024)S(1)} %get-tuple-element.96, f32[1024]{0:T(1024)S(1)} %copy-done.48, f32[1024]{0:T(1024)S(1)} %bitcast.212), channel_id=7, replica_groups=mesh['head'=4,'blk'=8] {'head','blk'}, use_global_device_ids=true, to_apply=%region_17.18.clone | all-reduce | flops 3072 | bytes 24576
  689.3 4.5 scatter_fusion.1
  694.7 98.0 %reduce-scatter.5.cloned.1.call-done = f32[32,3072]{1,0:T(8,128)} async-done(((f32[1024,3072]{1,0:T(8,128)}), f32[32,3072]{1,0:T(8,128)}) %reduce-scatter.5.cloned.1.call-update) | async-done | bytes 393232 | tf_op jit(solution)/shard_map/reduce_scatter | solution.py:258
  792.8 359.9 %reduce-scatter.11.cloned.1.call-done = f32[128,1024]{1,0:T(8,128)} async-done(((f32[4096,1024]{1,0:T(8,128)}), f32[128,1024]{1,0:T(8,128)}) %reduce-scatter.11.cloned.1.call-update) | async-done | bytes 524304 | tf_op jit(solution)/shard_map/reduce_scatter | solution.py:261
  1152.7 360.4 %reduce-scatter.9.cloned.1.call-done = f32[32,4096]{1,0:T(8,128)} async-done(((f32[1024,4096]{1,0:T(8,128)}), f32[32,4096]{1,0:T(8,128)}) %reduce-scatter.9.cloned.1.call-update) | async-done | bytes 524304 | tf_op jit(solution)/shard_map/reduce_scatter | solution.py:260
  (327 shorter events, 69.3 us)
Async XLA Ops:
  7.2 92.1 %all-gather.9.cloned.1.call-start = ((), (), s32[]{:S(2)}) async-start(), calls=%async_computation.8 | async-start | bytes 6488064 | tf_op jit(solution)/shard_map/all_gather | solution.py:70
  7.9 175.3 %all-gather.11.cloned.1.call-start = ((), (), s32[]{:S(2)}) async-start(), calls=%async_computation.9 | async-start | bytes 2359296 | tf_op jit(solution)/shard_map/all_gather | solution.py:105
  34.9 18.7 %copy-start.64 = (bf16[32]{0:T(256)(128)(2,1)S(1)}, bf16[32]{0:T(256)(128)(2,1)}, u32[]{:S(2)}) copy-start(bf16[32]{0:T(256)(128)(2,1)} %param.20) | copy-start | bytes 196
  34.9 19.0 %copy-start.65 = (bf16[32]{0:T(256)(128)(2,1)S(1)}, bf16[32]{0:T(256)(128)(2,1)}, u32[]{:S(2)}) copy-start(bf16[32]{0:T(256)(128)(2,1)} %param.18) | copy-start | bytes 196
  34.9 19.2 %copy-start.66 = (bf16[32]{0:T(256)(128)(2,1)S(1)}, bf16[32]{0:T(256)(128)(2,1)}, u32[]{:S(2)}) copy-start(bf16[32]{0:T(256)(128)(2,1)} %param.19) | copy-start | bytes 196
  34.9 62.5 %copy-start.6 = (bf16[4,64,1024]{2,1,0:T(8,128)(2,1)S(1)}, bf16[4,64,1024]{2,1,0:T(8,128)(2,1)}, u32[]{:S(2)}) copy-start(bf16[4,64,1024]{2,1,0:T(8,128)(2,1)} %param.12) | copy-start | bytes 1572868
  97.4 39.3 %copy-start.55 = (bf16[1024]{0:T(1024)(128)(2,1)}, bf16[1024]{0:T(1024)(128)(2,1)S(1)}, u32[]{:S(2)}) copy-start(bf16[1024]{0:T(1024)(128)(2,1)S(1)} %get-tuple-element.111) | copy-start | bytes 6148
  99.1 37.6 %copy-start.39 = (pred[4,16]{1,0:T(4,128)(4,1)}, pred[4,16]{1,0:T(4,128)(4,1)S(1)}, u32[]{:S(2)}) copy-start(pred[4,16]{1,0:T(4,128)(4,1)S(1)} %get-tuple-element.117) | copy-start | bytes 196
  99.3 4.1 copy-start.44
  99.3 4.1 copy-start.37
  132.4 5.7 copy-start.10
  134.2 107.1 %all-gather.13.cloned.1.call-start = ((), (), s32[]{:S(2)}) async-start(), calls=%async_computation.10 | async-start | bytes 2162688 | tf_op jit(solution)/shard_map/all_gather | solution.py:71
  134.9 185.5 %all-gather.15.cloned.1.call-start = ((), (), s32[]{:S(2)}) async-start(), calls=%async_computation.11 | async-start | bytes 8650752 | tf_op jit(solution)/shard_map/all_gather | solution.py:72
  135.5 263.8 %all-gather.17.cloned.1.call-start = ((), (), s32[]{:S(2)}) async-start(), calls=%async_computation.12 | async-start | bytes 8650752 | tf_op jit(solution)/shard_map/all_gather | solution.py:73
  137.3 57.8 %copy-start.57 = (f32[1,4,16]{2,0,1:T(1,128)}, f32[1,4,16]{2,0,1:T(1,128)S(1)}, u32[]{:S(2)}) copy-start(f32[1,4,16]{2,0,1:T(1,128)S(1)} %fusion.91) | copy-start | bytes 772
  189.2 6.5 copy-start.60
  189.2 6.5 copy-start.4
  190.9 50.5 %copy-start.40 = (pred[4,16]{1,0:T(4,128)(4,1)S(1)}, pred[4,16]{1,0:T(4,128)(4,1)}, u32[]{:S(2)}) copy-start(pred[4,16]{1,0:T(4,128)(4,1)} %copy-done.39) | copy-start | bytes 196
  191.7 7.9 all-to-all-start.1
  195.0 245.6 %all-gather.21.cloned.1.call-start = ((), (), s32[]{:S(2)}) async-start(), calls=%async_computation.18 | async-start | bytes 1179648 | tf_op jit(solution)/shard_map/all_gather | solution.py:196
  197.5 391.6 %all-gather.19.cloned.1.call-start = ((), (), s32[]{:S(2)}) async-start(), calls=%async_computation.13 | async-start | bytes 1179648 | tf_op jit(solution)/shard_map/all_gather | solution.py:197
  199.7 45.2 %copy-start.20 = (bf16[4,4,2,8,256]{4,3,1,2,0:T(8,128)(2,1)}, bf16[4,4,2,8,256]{4,3,1,2,0:T(8,128)(2,1)S(1)}, u32[]{:S(2)}) copy-start(bf16[4,4,2,8,256]{4,3,1,2,0:T(8,128)(2,1)S(1)} %copy.178) | copy-start | bytes 393220
  326.4 84.5 %copy-start.15 = (f32[4,16,4096]{2,1,0:T(8,128)}, f32[4,16,4096]{2,1,0:T(8,128)S(1)}, u32[]{:S(2)}) copy-start(f32[4,16,4096]{2,1,0:T(8,128)S(1)} %get-tuple-element.138) | copy-start | bytes 3145732
  399.4 8.1 copy-start.1
  399.4 8.1 copy-start.31
  407.5 3.4 copy-start.23
  407.5 3.4 copy-start.24
  407.5 3.4 copy-start.33
  407.5 3.4 copy-start.35
  407.6 3.8 copy-start.63
  410.8 5.6 copy-start.18
  410.9 5.5 copy-start.49
  411.3 5.7 copy-start.2
  433.7 261.1 %reduce-scatter.7.cloned.1.call-start = ((), (), s32[]{:S(2)}) async-start(), calls=%async_computation.15 | async-start | bytes 4325376 | tf_op jit(solution)/shard_map/reduce_scatter | solution.py:259
  437.4 5.5 copy-start.30
  437.4 355.3 %reduce-scatter.5.cloned.1.call-start = ((), (), s32[]{:S(2)}) async-start(), calls=%async_computation.14 | async-start | bytes 12976128 | tf_op jit(solution)/shard_map/reduce_scatter | solution.py:258
  509.9 8.2 copy-start.9
  596.2 13.6 copy-start.38
  596.2 13.6 copy-start.41
  616.3 536.4 %reduce-scatter.11.cloned.1.call-start = ((), (), s32[]{:S(2)}) async-start(), calls=%async_computation.17 | async-start | bytes 17301504 | tf_op jit(solution)/shard_map/reduce_scatter | solution.py:261
  625.6 887.5 %reduce-scatter.9.cloned.1.call-start = ((), (), s32[]{:S(2)}) async-start(), calls=%async_computation.16 | async-start | bytes 17301504 | tf_op jit(solution)/shard_map/reduce_scatter | solution.py:260
  636.3 7.8 copy-start.58
  636.3 7.8 copy-start.59
  644.3 5.4 copy-start.48
  644.3 44.8 %copy-start.45 = (f32[4,16]{1,0:T(4,128)S(1)}, f32[4,16]{1,0:T(4,128)}, u32[]{:S(2)}) copy-start(f32[4,16]{1,0:T(4,128)} %copy-done.44) | copy-start | bytes 772
  644.3 44.8 %copy-start.19 = (f32[4,16,1024]{2,1,0:T(8,128)S(1)}, f32[4,16,1024]{2,1,0:T(8,128)}, u32[]{:S(2)}) copy-start(f32[4,16,1024]{2,1,0:T(8,128)} %copy-done.18) | copy-start | bytes 786436
  644.3 44.8 %copy-start.50 = (f32[4,16]{1,0:T(4,128)S(1)}, f32[4,16]{1,0:T(4,128)}, u32[]{:S(2)}) copy-start(f32[4,16]{1,0:T(4,128)} %copy-done.49) | copy-start | bytes 772
  644.4 44.8 %copy-start.53 = (f32[4,16]{1,0:T(4,128)S(1)}, f32[4,16]{1,0:T(4,128)}, u32[]{:S(2)}) copy-start(f32[4,16]{1,0:T(4,128)} %get-tuple-element.116) | copy-start | bytes 772
  (31 other events, 47.6 us)
Sparse Core Ops, SparseCore 0:
  11.0 73.3 all-gather.8
  134.3 48.8 all-gather.10
  186.2 55.0 all-gather.12
  244.2 76.2 all-gather.14
  323.3 75.9 all-gather.16
  401.4 38.7 all-gather.20
  442.3 41.4 all-gather.18
  486.7 145.4 reduce-scatter.6
  638.8 153.8 reduce-scatter.4
  795.6 357.0 reduce-scatter.10
  1155.7 357.3 reduce-scatter.8
where the time goes:
time: 1530 us; the launch traced here: 1520 us
  waiting for transfers between devices  1060 us (69%)
  blocking collectives  240 us (16%)
  local copies, waits for them, and re-layouts  103 us (7%)
  matrix products  77 us (5%)
  other arithmetic  23.7 us (2%)
    reduce_scatter x1, waiting for transfers between devices, shards(): lax.psum_scatter(grad_up, ('head', 'blk'), scatter_dimension=0, tiled=True)  360 us
    reduce_scatter x1, waiting for transfers between devices, shards(): lax.psum_scatter(grad_down, ('head', 'blk'), scatter_dimension=0, tiled=T...  360 us
    reduce_scatter x1, waiting for transfers between devices, shards(): lax.psum_scatter(grad_qkv, ('head', 'blk'), scatter_dimension=0, tiled=True)  98 us
    unnamed x2, blocking collectives  80.6 us
    all_gather x1, waiting for transfers between devices, shards(): lax.all_gather(w_up, ('head', 'blk'), axis=0, tiled=True)  75.7 us
    all_gather x1, waiting for transfers between devices, shards(): lax.all_gather(w_down, ('head', 'blk'), axis=0, tiled=True)  72.9 us
    all_gather x1, waiting for transfers between devices, shards(): piece = lax.all_gather(key_values, 'blk', axis=1, tiled=True)  43.6 us
    all_gather x1, waiting for transfers between devices, shards(): lax.all_gather(w_out, ('head', 'blk'), axis=0, tiled=True)  41.7 us
  transfers between devices with their start and end apart: 12, of which 8 were waited for; matrix products, arithmetic and copies ran while one was open for 12% of the time, Pallas kernels for 0%

commit v1 on v0

--- a/solution.py
+++ b/solution.py
@@ -1,3 +1,5 @@
+from functools import partial
+
 import jax
 import jax.numpy as jnp
 from jax import lax
@@ -276,28 +278,268 @@
     )
 
 
+def flips(count):
+    return [[(i, i ^ k) for i in range(count)] for k in range(count)]
+
+
+def gather_group(own):
+    blocks = [own] + [lax.ppermute(own, "z", f) for f in flips(lax.axis_size("z"))[1:]]
+    blocks = jnp.stack(blocks)
+    rest = [lax.ppermute(blocks, "c", f) for f in flips(lax.axis_size("c"))[1:]]
+    return jnp.concatenate([blocks] + rest)
+
+
+def scatter_group(parts):
+    depth = lax.axis_size("z")
+    total = parts[:depth].astype(jnp.float32)
+    for k, f in enumerate(flips(lax.axis_size("c"))[1:], 1):
+        piece = parts[k * depth : (k + 1) * depth].astype(jnp.bfloat16)
+        total = total + lax.ppermute(piece, "c", f).astype(jnp.float32)
+    mine = total[0]
+    low = total.astype(jnp.bfloat16)
+    for k, f in enumerate(flips(depth)[1:], 1):
+        mine = mine + lax.ppermute(low[k], "z", f).astype(jnp.float32)
+    return mine
+
+
+def xor_blocks(rows, bits):
+    shape = rows.shape
+    rows = rows.reshape((2,) * len(bits) + (-1,))
+    for axis, bit in enumerate(bits):
+        rows = jnp.where(bit == 1, jnp.flip(rows, axis), rows)
+    return rows.reshape(shape)
+
+
+def index_bits(index, count):
+    return [(index >> k) & 1 for k in reversed(range(count.bit_length() - 1))]
+
+
+def split_two(values):
+    high = values.astype(jnp.bfloat16)
+    return high, (values - high.astype(jnp.float32)).astype(jnp.bfloat16)
+
+
+def grouped(
+    tokens, chosen, w_qkv, w_out, w_up, w_down, gain_attn, gain_mlp, router, cotangent
+):
+    f32, bf16 = jnp.float32, jnp.bfloat16
+    dot = partial(jnp.einsum, preferred_element_type=f32)
+    ny, nc, nz, nx = (lax.axis_size(a) for a in ("y", "c", "z", "x"))
+    y, c, z, x = (lax.axis_index(a) for a in ("y", "c", "z", "x"))
+    seq_count, seg_len, width = tokens.shape
+    cap = seg_len // 4
+    routed = chosen.shape[1]
+    members, lines = nc * nz, ny * nx
+    member = c * nz + z
+    line = y * nx + x
+    shard = ((y * nc + c) * nz + z) * nx + x
+    rows, ff_rows = w_qkv.shape[0], w_down.shape[0]
+    heads = HEADS // members
+    own = routed // members
+    scale_factor = HDIM ** (-0.5)
+    line_axes, group_axes = ("y", "x"), ("c", "z")
+    bits = index_bits(c, nc) + index_bits(z, nz)
+
+    send_qkv = w_qkv.reshape(rows, 3, heads, members, HDIM).transpose(3, 0, 1, 2, 4)
+    send_qkv = send_qkv.reshape(members, rows, 3 * heads * HDIM)
+    vectors = jnp.stack([gain_attn, gain_mlp, router])
+    vec_rows = jnp.pad(vectors, ((0, 5), (0, 3 * heads * HDIM - rows)))
+    send_qkv = jnp.concatenate(
+        [send_qkv, jnp.broadcast_to(vec_rows, (members,) + vec_rows.shape)], 1
+    )
+    send_up = w_up.reshape(rows, ny, members, nx, ff_rows).transpose(2, 0, 1, 3, 4)
+    send_up = send_up.reshape(members, rows, lines * ff_rows)
+
+    def along_lines(block):
+        return lax.all_to_all(
+            jnp.broadcast_to(block, (lines,) + block.shape), line_axes, 0, 0, tiled=True
+        )
+
+    got_qkv = along_lines(lax.all_to_all(send_qkv, group_axes, 0, 0, tiled=True))
+    got_up = along_lines(lax.all_to_all(send_up, group_axes, 0, 0, tiled=True))
+    full_down = along_lines(w_down).reshape(lines * ff_rows, width)
+    full_out = along_lines(w_out).reshape(lines * rows, width)
+
+    def natural(got):
+        got = got.reshape((ny, nx, members) + got.shape[2:])
+        got = got.transpose((0, 2, 1) + tuple(range(3, got.ndim)))
+        return got.reshape((width,) + got.shape[4:])
+
+    full_qkv = natural(got_qkv[:, :, :rows])
+    full_up = natural(got_up)
+    vecs = got_qkv[:, :, rows : rows + 3, :rows].reshape(ny, nx, members, 3, rows)
+    vecs = vecs.transpose(3, 0, 2, 1, 4).reshape(3, width).astype(f32)
+    full_gain_attn, full_gain_mlp, full_router = vecs[0], vecs[1], vecs[2]
+
+    base = shard * seg_len
+    places = base + jnp.arange(seg_len, dtype=jnp.int32)
+    at = chosen[:, :, None]
+    present = jnp.any(at == places, 1)
+    rank = jnp.sum((at >= base) & (at < places), 1, dtype=jnp.int32)
+    slots = jnp.arange(cap, dtype=jnp.int32)
+    pick = (present[:, None, :] & (rank[:, None, :] == slots[:, None])).astype(bf16)
+    mine = lax.dynamic_index_in_dim(chosen, line, 0, False)
+    owner = mine // seg_len
+    order = jnp.arange(routed, dtype=jnp.int32)
+    slot = jnp.sum(
+        (owner[:, None] == owner[None, :]) & (order[None, :] < order[:, None]), 1, dtype=jnp.int32
+    )
+    ox, oz = owner % nx, (owner // nx) % nz
+    oc, oy = (owner // (nx * nz)) % nc, owner // (nx * nz * nc)
+    cell = ((((oc ^ c) * nz + (oz ^ z)) * ny + oy) * nx + ox) * cap + slot
+    cell = xor_blocks(cell, bits)
+    stand = xor_blocks(mine, bits)
+    spots = members * lines * cap
+    spread = (cell[:, None] == jnp.arange(spots, dtype=jnp.int32)).astype(bf16)
+
+    picked_slots = dot("scp,spd->scd", pick, tokens).astype(bf16)
+    cot_slots = dot("scp,spd->scd", pick, cotangent).astype(bf16)
+    both = jnp.stack([picked_slots, cot_slots], 1)
+    both = lax.all_to_all(both, line_axes, 0, 0, tiled=True)
+    picked_pad = gather_group(both[:, 0].reshape(lines * cap, width)).reshape(spots, width)
+    cot_pad = gather_group(both[:, 1].reshape(lines * cap, width)).reshape(spots, width)
+    picked_low = dot("rj,jd->rd", spread, picked_pad).astype(bf16)
+    picked = picked_low.astype(f32)
+    cot_low = dot("rj,jd->rd", spread, cot_pad).astype(bf16)
+    cot = cot_low.astype(f32)
+    gate = jax.nn.sigmoid(jnp.sum(picked * full_router, 1, keepdims=True))
+
+    inv = lax.rsqrt(jnp.mean(picked * picked, 1, keepdims=True) + epsilon)
+    normed = (picked * inv * full_gain_attn).astype(bf16)
+    joined = dot("rd,de->re", normed, full_qkv).astype(bf16).reshape(routed, 3, heads, HDIM)
+    queries, keys, values = joined[:, 0], joined[:, 1], joined[:, 2]
+    allowed = stand[None, :] <= stand[:, None]
+    scores = dot("qhd,khd->hqk", queries, keys) * scale_factor
+    scores = jnp.where(allowed, scores, neg_large)
+    top = jnp.max(scores, 2, keepdims=True)
+    probs = jnp.where(allowed, jnp.exp(scores - top), 0.0)
+    total = jnp.sum(probs, 2, keepdims=True)
+    probs_low = probs.astype(bf16)
+    attended_exact = dot("hqk,khd->hqd", probs_low, values) / total
+    attended = attended_exact.astype(bf16).transpose(1, 0, 2).reshape(routed, heads * HDIM)
+    branch_part = dot("re,ed->rd", attended, full_out)
+    branch = scatter_group(branch_part.reshape(members, own, width))
+    picked_own = picked[:own]
+    hidden = picked_own + branch
+    inv_mlp = lax.rsqrt(jnp.mean(hidden * hidden, 1, keepdims=True) + epsilon)
+    normed_mlp = gather_group((hidden * inv_mlp * full_gain_mlp).astype(bf16))
+    normed_mlp = normed_mlp.reshape(routed, width)
+
+    upper = dot("rd,di->ri", normed_mlp, full_up)
+    active_exact, gelu_back = jax.vjp(exact_gelu, upper)
+    active = active_exact.astype(bf16)
+    combined_part = branch_part + dot("ri,id->rd", active, full_down)
+    d_update = gate * cot
+    d_result = d_update.astype(bf16)
+    d_active = dot("rd,id->ri", d_result, full_down)
+    d_upper = gelu_back(d_active)[0].astype(bf16)
+    d_normed_mlp_part = dot("ri,di->rd", d_upper, full_up)
+    logit_part = jnp.sum(cot * combined_part, 1, keepdims=True)
+    logit_high, logit_low = split_two(logit_part)
+    logit_cols = jnp.concatenate([logit_high, logit_low], 1).astype(f32)
+    d_parts = jnp.concatenate(
+        [d_normed_mlp_part, jnp.pad(logit_cols, ((0, 0), (0, 126)))], 1
+    )
+    d_own = scatter_group(d_parts.reshape(members, own, width + 128))
+    d_normed_mlp = d_own[:, :width]
+    gate_own = gate[:own]
+    d_logit = jnp.sum(d_own[:, width:], 1, keepdims=True) * gate_own * (1.0 - gate_own)
+    u = d_normed_mlp * full_gain_mlp
+    d_hidden = inv_mlp * u - hidden * inv_mlp**3 * jnp.mean(u * hidden, 1, keepdims=True)
+    d_branch = gather_group((d_update[:own] + d_hidden).astype(bf16)).reshape(routed, width)
+    vec_mlp = jnp.sum(d_normed_mlp * hidden * inv_mlp, 0)
+    vec_router = jnp.sum(d_logit * picked_own, 0)
+
+    d_attended = dot("rd,ed->re", d_branch, full_out).astype(bf16)
+    d_att = d_attended.reshape(routed, heads, HDIM).transpose(1, 0, 2)
+    delta = jnp.sum(d_att.astype(f32) * attended_exact, 2, keepdims=True)
+    d_prob = dot("hqd,khd->hqk", d_att, values)
+    d_scores = (probs / total * (d_prob - delta)).astype(bf16)
+    d_queries = dot("hqk,khd->qhd", d_scores, keys) * scale_factor
+    d_keys = dot("hqk,qhd->khd", d_scores, queries) * scale_factor
+    d_values = dot("hqk,hqd->khd", probs_low, (d_att.astype(f32) / total).astype(bf16))
+    d_joined = jnp.stack([d_queries, d_keys, d_values], 1).astype(bf16)
+    d_joined = d_joined.reshape(routed, 3 * heads * HDIM)
+    d_normed_part = dot("re,de->rd", d_joined, full_qkv)
+    v = d_normed_part * full_gain_attn
+    d_picked_part = inv * v - picked * inv**3 * jnp.mean(v * picked, 1, keepdims=True)
+    d_picked_part = d_picked_part.at[:own].add(d_hidden + d_logit * full_router)
+    vec_attn = jnp.sum(d_normed_part * picked * inv, 0)
+
+    def to_slots(part):
+        pad = dot("rj,rd->jd", spread, part.astype(bf16)).astype(bf16)
+        mine = scatter_group(pad.reshape(members, lines * cap, width)).astype(bf16)
+        return lax.all_to_all(mine.reshape(lines, cap, width), line_axes, 0, 0, tiled=True)
+
+    update = to_slots(gate * combined_part)
+    d_picked = to_slots(d_picked_part)
+    output = (tokens.astype(f32) + dot("scp,scd->spd", pick, update)).astype(bf16)
+    grad_tokens = (cotangent.astype(f32) + dot("scp,scd->spd", pick, d_picked)).astype(bf16)
+
+    def sum_lines(part):
+        got = lax.all_to_all(part.astype(bf16), line_axes, 0, 0, tiled=True)
+        return jnp.sum(got.astype(f32), 0)
+
+    def by_line(part):
+        part = part.reshape((ny, members, nx, rows) + part.shape[1:])
+        part = part.transpose((0, 2, 1, 3) + tuple(range(4, part.ndim)))
+        return part.reshape((lines, members) + part.shape[3:])
+
+    grad_down = sum_lines(
+        dot("ri,rd->id", active, d_result).reshape(lines, ff_rows, width)
+    )
+    grad_out = sum_lines(dot("re,rd->ed", attended, d_branch).reshape(lines, rows, width))
+    grad_up = sum_lines(by_line(dot("rd,ri->di", normed_mlp, d_upper))).astype(bf16)
+    grad_up = lax.all_to_all(grad_up, group_axes, 0, 0, tiled=True).astype(f32)
+    grad_up = grad_up.reshape(members, rows, ny, nx, ff_rows).transpose(1, 2, 0, 3, 4)
+    grad_up = grad_up.reshape(rows, ny * members * nx * ff_rows)
+    cols = 3 * heads * HDIM
+    grad_qkv = by_line(dot("rd,re->de", normed, d_joined)).astype(bf16)
+    vec_parts = by_line(jnp.stack([vec_attn, vec_mlp, vec_router], 1))
+    vec_parts = vec_parts.transpose(0, 1, 3, 2).reshape(lines, members, 3 * rows)
+
+    def pack(vec):
+        vec = jnp.concatenate(split_two(vec), -1)[..., None, :]
+        pads = [(0, 0)] * (vec.ndim - 2) + [(0, 7), (0, cols - 6 * rows)]
+        return jnp.pad(vec, pads)
+
+    qkv_sum = sum_lines(jnp.concatenate([grad_qkv, pack(vec_parts)], 2))
+    vec_sum = qkv_sum[:, rows, : 3 * rows] + qkv_sum[:, rows, 3 * rows : 6 * rows]
+    send = jnp.concatenate([qkv_sum[:, :rows].astype(bf16), pack(vec_sum)], 1)
+    got = lax.all_to_all(send, group_axes, 0, 0, tiled=True).astype(f32)
+    grad_qkv = got[:, :rows].reshape(members, rows, 3, heads, HDIM).transpose(1, 2, 3, 0, 4)
+    grad_qkv = grad_qkv.reshape(rows, 3 * HEADS * HDIM)
+    vec_own = jnp.sum(got[:, rows, : 6 * rows], 0)
+    vec_own = (vec_own[: 3 * rows] + vec_own[3 * rows :]).reshape(3, rows)
+    return (
+        output,
+        grad_tokens,
+        grad_qkv,
+        grad_out,
+        grad_up,
+        grad_down,
+        vec_own[0],
+        vec_own[1],
+        vec_own[2],
+    )
+
+
+def fits(mesh):
+    head_count, block_count = mesh.devices.shape
+    members = (head_count // 2) * (block_count // 2)
+    power = members & (members - 1) == 0
+    return power and HEADS == 2 * members
+
+
 def solution(mesh):
-    in_specs = (
-        P(None, ("head", "blk"), None),
-        P(),
-        P(("head", "blk"), None),
-        P(("head", "blk"), None),
-        P(("head", "blk"), None),
-        P(("head", "blk"), None),
-        P(("head", "blk")),
-        P(("head", "blk")),
-        P(("head", "blk")),
-        P(None, ("head", "blk"), None),
-    )
-    out_specs = (
-        P(None, ("head", "blk"), None),
-        P(None, ("head", "blk"), None),
-        P(("head", "blk"), None),
-        P(("head", "blk"), None),
-        P(("head", "blk"), None),
-        P(("head", "blk"), None),
-        P(("head", "blk")),
-        P(("head", "blk")),
-        P(("head", "blk")),
-    )
-    return jax.shard_map(shards, mesh=mesh, in_specs=in_specs, out_specs=out_specs, check_vma=False)
+    if fits(mesh):
+        head_count, block_count = mesh.devices.shape
+        devices = mesh.devices.reshape(2, head_count // 2, block_count // 2, 2)
+        mesh = jax.sharding.Mesh(devices, ("y", "c", "z", "x"))
+        body, all_axes = grouped, ("y", "c", "z", "x")
+    else:
+        body, all_axes = shards, ("head", "blk")
+    seqs, mats, vecs = P(None, all_axes, None), P(all_axes, None), P(all_axes)
+    in_specs = (seqs, P(), mats, mats, mats, mats, vecs, vecs, vecs, seqs)
+    out_specs = (seqs, seqs, mats, mats, mats, mats, vecs, vecs, vecs)
+    return jax.shard_map(body, mesh=mesh, in_specs=in_specs, out_specs=out_specs, check_vma=False)

time: 1530 us -> 298 us (0.19)
  waiting for transfers between devices: 1060 us -> 99.7 us
  blocking collectives: 240 us -> 0 us
  starting transfers between devices: 3.98 us -> 102 us
  local copies, waits for them, and re-layouts: 103 us -> 34.2 us
  matrix products: 77 us -> 27.4 us
    reduce_scatter x4 -> x0, waiting for transfers between devices: 818 us -> none  [the longest x1 360 us: shards(): lax.psum_scatter(grad_up, ('head', 'blk'), scatter_dimension=0, tiled=True)]
    all_gather x7 -> x0, waiting for transfers between devices: 234 us -> none  [the longest x1 75.7 us: shards(): lax.all_gather(w_up, ('head', 'blk'), axis=0, tiled=True)]
    all_gather x4 -> x0, blocking collectives: 129 us -> none  [the longest x1 32.5 us: shards(): piece_delta_low = lax.all_gather(delta_low, 'blk', axis=1, tiled=True)]
    unnamed x2 -> x0, blocking collectives: 80.6 us -> none
    all_to_all x1 -> x15, waiting for transfers between devices: 1.88 us -> 63.5 us  [the longest x4 23.3 us: sum_lines(): got = lax.all_to_all(part.astype(bf16), line_axes, 0, 0, tiled=True)]
    all_to_all x1 -> x15, starting transfers between devices: 3.33 us -> 58.1 us  [the longest x4 15.5 us: along_lines(): lax.all_to_all(jnp.broadcast_to(block, (lines,) + block.shape), line_axes...]
    dot_general x20 -> x25, matrix products: 77 us -> 26.2 us  [the longest x1 2.49 us: grouped(): picked_low = dot('rj,jd->rd', spread, picked_pad).astype(bf16)]
    gather x23 -> x0, local copies, waits for them, and re-layouts: 45.5 us -> none  [the longest x18 24.8 us: shards(): jnp.searchsorted(chosen_row, bounds, side='left')]
  transfers between devices with their start and end apart: 12 -> 47, of which waited for: 8 -> 25; matrix products, arithmetic and copies ran while one was open for 12% -> 24% of each run, Pallas kernels for 0% -> 0%
where the time goes in v1:
time: 298 us; the launch traced here: 296 us
  starting transfers between devices  102 us (34%)
  waiting for transfers between devices  99.7 us (33%)
  local copies, waits for them, and re-layouts  34.2 us (11%)
  other arithmetic  30.1 us (10%)
  matrix products  27.4 us (9%)
    ppermute x12, starting transfers between devices, gather_group(): lax.ppermute(own, 'z', f)  29.2 us
    all_to_all x4, waiting for transfers between devices, sum_lines(): got = lax.all_to_all(part.astype(bf16), line_axes, 0, 0, tiled=True)  23.3 us
    ppermute x12, waiting for transfers between devices, scatter_group(): mine = mine + lax.ppermute(low[k], 'z', f).astype(jnp.float32)  22.8 us
    all_to_all x4, starting transfers between devices, along_lines(): lax.all_to_all(jnp.broadcast_to(block, (lines,) + block.shape), line_axes...  15.5 us
    all_to_all x4, waiting for transfers between devices, along_lines(): lax.all_to_all(jnp.broadcast_to(block, (lines,) + block.shape), line_axes...  15.5 us
    all_to_all x4, starting transfers between devices, sum_lines(): got = lax.all_to_all(part.astype(bf16), line_axes, 0, 0, tiled=True)  14.9 us
    ppermute x12, starting transfers between devices, scatter_group(): mine = mine + lax.ppermute(low[k], 'z', f).astype(jnp.float32)  14.1 us
    ppermute x12, waiting for transfers between devices, gather_group(): lax.ppermute(own, 'z', f)  12.4 us
  transfers between devices with their start and end apart: 47, of which 25 were waited for; matrix products, arithmetic and copies ran while one was open for 24% of the time, Pallas kernels for 0%

profile of v1, /device:TPU:0, one launch (start us, length us, event | category | flops | bytes accessed | tf_op | source)
XLA Modules:
  0.0 295.5 jit_solution(10778638363721621828)
XLA Ops:
  6.5 5.2 %all-to-all-start = ((bf16[4,2,16,1024]{3,2,1,0:T(8,128)(2,1)}), bf16[4,2,16,1024]{3,2,1,0:T(8,128)(2,1)S(1)}, u32[]{:S(2)}, u32[]{:S(2)}) async-start(bf16[4,2,16,1024]{3,2,1,0:T(8,128)(2,1)} %copy.104), calls=%async_computation | async-start | bytes 524288 | tf_op jit(solution)/shard_map/all_to_all | solution.py:398
  17.0 4.9 %all-to-all-start.1 = ((bf16[8,40,384]{2,1,0:T(8,128)(2,1)}), bf16[8,40,384]{2,1,0:T(8,128)(2,1)S(1)}, u32[]{:S(2)}, u32[]{:S(2)}) async-start(bf16[8,40,384]{2,1,0:T(8,128)(2,1)} %pad_maximum_fusion.6), calls=%async_computation.1 | async-start | bytes 491520 | tf_op jit(solution)/shard_map/all_to_all | solution.py:358
  21.9 3.9 %collective-permute-start.2 = (bf16[64,1024]{1,0:T(8,128)(2,1)S(1)}, bf16[64,1024]{1,0:T(8,128)(2,1)S(1)}, u32[]{:S(2)}, u32[]{:S(2)}) collective-permute-start(bf16[64,1024]{1,0:T(8,128)(2,1)S(1)} %bitcast.306), channel_id=1, source_target_pairs={{0,6},{2,4},{4,2},{6,0},{1,7},{3,5},{5,3},{7,1},{8,14},{10,12},{12... | collective-permute-start | bytes 393224 | tf_op jit(solution)/shard_map/ppermute | solution.py:286
  28.3 3.8 %collective-permute-start.18 = (bf16[64,1024]{1,0:T(8,128)(2,1)S(1)}, bf16[64,1024]{1,0:T(8,128)(2,1)S(1)}, u32[]{:S(2)}, u32[]{:S(2)}) collective-permute-start(bf16[64,1024]{1,0:T(8,128)(2,1)S(1)} %bitcast.301), channel_id=1, source_target_pairs={{0,6},{2,4},{4,2},{6,0},{1,7},{3,5},{5,3},{7,1},{8,14},{10,12},{12... | collective-permute-start | bytes 393224 | tf_op jit(solution)/shard_map/ppermute | solution.py:286
  34.3 12.1 %collective-permute-start.16 = (bf16[64,1024]{1,0:T(8,128)(2,1)S(1)}, bf16[64,1024]{1,0:T(8,128)(2,1)S(1)}, u32[]{:S(2)}, u32[]{:S(2)}) collective-permute-start(bf16[64,1024]{1,0:T(8,128)(2,1)S(1)} %bitcast.303), channel_id=1, source_target_pairs={{0,2},{2,0},{4,6},{6,4},{1,3},{3,1},{5,7},{7,5},{8,10},{10,8},{12,... | collective-permute-start | bytes 393224 | tf_op jit(solution)/shard_map/ppermute | solution.py:286
  46.4 2.3 collective-permute-done.1
  48.9 5.0 %collective-permute-done.17 = bf16[64,1024]{1,0:T(8,128)(2,1)S(1)} collective-permute-done((bf16[64,1024]{1,0:T(8,128)(2,1)S(1)}, bf16[64,1024]{1,0:T(8,128)(2,1)S(1)}, u32[]{:S(2)}, u32[]{:S(2)}) %collective-permute-start.17) | collective-permute-done | bytes 131104 | tf_op jit(solution)/shard_map/ppermute | solution.py:286
  56.5 3.9 %all-to-all-start.2 = ((bf16[4,8,40,384]{3,1,2,0:T(8,128)(2,1)}), bf16[4,8,40,384]{3,1,2,0:T(8,128)(2,1)S(1)}, u32[]{:S(2)}, u32[]{:S(2)}) async-start(bf16[4,8,40,384]{3,1,2,0:T(8,128)(2,1)} %broadcast_in_dim.29), calls=%async_computation.2 | async-start | bytes 1966080 | tf_op jit(solution)/shard_map/all_to_all | solution.py:354
  63.4 10.6 %all-to-all-done.2 = bf16[4,8,40,384]{3,1,2,0:T(8,128)(2,1)S(1)} async-done(((bf16[4,8,40,384]{3,1,2,0:T(8,128)(2,1)}), bf16[4,8,40,384]{3,1,2,0:T(8,128)(2,1)S(1)}, u32[]{:S(2)}, u32[]{:S(2)}) %all-to-all-start.2) | async-done | bytes 983072 | tf_op jit(solution)/shard_map/all_to_all | solution.py:354
  74.8 3.4 %all-to-all-start.3 = ((bf16[4,32,1024]{2,1,0:T(8,128)(2,1)}), bf16[4,32,1024]{2,1,0:T(8,128)(2,1)S(1)}, u32[]{:S(2)}, u32[]{:S(2)}) async-start(bf16[4,32,1024]{2,1,0:T(8,128)(2,1)} %broadcast_in_dim.60), calls=%async_computation.3 | async-start | bytes 524288 | tf_op jit(solution)/shard_map/all_to_all | solution.py:354
  79.5 2.5 fusion.20
  86.5 3.4 %all-to-all-start.4 = ((bf16[8,32,512]{2,1,0:T(8,128)(2,1)}), bf16[8,32,512]{2,1,0:T(8,128)(2,1)S(1)}, u32[]{:S(2)}, u32[]{:S(2)}) async-start(bf16[8,32,512]{2,1,0:T(8,128)(2,1)} %reshape.337), calls=%async_computation.4 | async-start | bytes 524288 | tf_op jit(solution)/shard_map/all_to_all | solution.py:359
  91.4 7.8 %all-to-all-done.4 = bf16[8,32,512]{2,1,0:T(8,128)(2,1)S(1)} async-done(((bf16[8,32,512]{2,1,0:T(8,128)(2,1)}), bf16[8,32,512]{2,1,0:T(8,128)(2,1)S(1)}, u32[]{:S(2)}, u32[]{:S(2)}) %all-to-all-start.4) | async-done | bytes 262176 | tf_op jit(solution)/shard_map/all_to_all | solution.py:359
  100.3 4.2 %all-to-all-start.5 = ((bf16[4,8,32,512]{3,2,1,0:T(8,128)(2,1)}), bf16[4,8,32,512]{3,2,1,0:T(8,128)(2,1)S(1)}, u32[]{:S(2)}, u32[]{:S(2)}) async-start(bf16[4,8,32,512]{3,2,1,0:T(8,128)(2,1)} %broadcast_in_dim.61), calls=%async_computation.5 | async-start | bytes 2097152 | tf_op jit(solution)/shard_map/all_to_all | solution.py:354
  104.5 1.9 fusion.129
  106.5 2.2 collective-permute-start.7
  113.1 2.8 collective-permute-done.6
  120.3 2.5 collective-permute-start.8
  124.7 4.1 %all-to-all-start.6 = ((bf16[4,128,1024]{2,1,0:T(8,128)(2,1)}), bf16[4,128,1024]{2,1,0:T(8,128)(2,1)S(1)}, u32[]{:S(2)}, u32[]{:S(2)}) async-start(bf16[4,128,1024]{2,1,0:T(8,128)(2,1)} %broadcast_in_dim.62), calls=%async_computation.6 | async-start | bytes 2097152 | tf_op jit(solution)/shard_map/all_to_all | solution.py:354
  133.7 2.3 multiply_convert_fusion.2
  135.9 4.9 %all-to-all-done.6 = bf16[4,128,1024]{2,1,0:T(8,128)(2,1)S(1)} async-done(((bf16[4,128,1024]{2,1,0:T(8,128)(2,1)}), bf16[4,128,1024]{2,1,0:T(8,128)(2,1)S(1)}, u32[]{:S(2)}, u32[]{:S(2)}) %all-to-all-start.6) | async-done | bytes 1048608 | tf_op jit(solution)/shard_map/all_to_all | solution.py:354
  153.1 2.2 collective-permute-start.23
  157.5 2.5 collective-permute-done.23
  159.9 3.2 %collective-permute-done.22 = bf16[32,1152]{1,0:T(8,128)(2,1)S(1)} collective-permute-done((bf16[32,1152]{1,0:T(8,128)(2,1)S(1)}, bf16[32,1152]{1,0:T(8,128)(2,1)S(1)}, u32[]{:S(2)}, u32[]{:S(2)}) %collective-permute-start.22) | collective-permute-done | bytes 73760 | tf_op jit(solution)/shard_map/ppermute | solution.py:301
  164.5 2.2 collective-permute-start.26
  166.6 2.3 collective-permute-start.24
  169.0 2.2 collective-permute-done.26
  175.5 2.1 collective-permute-start.15
  178.4 2.4 collective-permute-done.13
  180.8 4.1 %collective-permute-done.15 = bf16[64,1024]{1,0:T(8,128)(2,1)S(1)} collective-permute-done((bf16[64,1024]{1,0:T(8,128)(2,1)S(1)}, bf16[64,1024]{1,0:T(8,128)(2,1)S(1)}, u32[]{:S(2)}, u32[]{:S(2)}) %collective-permute-start.15) | collective-permute-done | bytes 131104 | tf_op jit(solution)/shard_map/ppermute | solution.py:301
  184.8 5.5 %collective-permute-done.14 = bf16[64,1024]{1,0:T(8,128)(2,1)S(1)} collective-permute-done((bf16[64,1024]{1,0:T(8,128)(2,1)S(1)}, bf16[64,1024]{1,0:T(8,128)(2,1)S(1)}, u32[]{:S(2)}, u32[]{:S(2)}) %collective-permute-start.14) | collective-permute-done | bytes 131104 | tf_op jit(solution)/shard_map/ppermute | solution.py:301
  191.1 4.1 %all-to-all-start.7 = ((bf16[4,16,1024]{2,1,0:T(8,128)(2,1)}), bf16[4,16,1024]{2,1,0:T(8,128)(2,1)}, u32[]{:S(2)}, u32[]{:S(2)}) async-start(bf16[4,16,1024]{2,1,0:T(8,128)(2,1)} %bitcast.51), calls=%async_computation.7 | async-start | bytes 262144 | tf_op jit(solution)/shard_map/all_to_all | solution.py:472
  201.3 4.3 %all-to-all-start.12 = ((bf16[4,8,32,512]{3,2,1,0:T(8,128)(2,1)}), bf16[4,8,32,512]{3,2,1,0:T(8,128)(2,1)S(1)}, u32[]{:S(2)}, u32[]{:S(2)}) async-start(bf16[4,8,32,512]{3,2,1,0:T(8,128)(2,1)} %bitcast.107), calls=%async_computation.12 | async-start | bytes 2097152 | tf_op jit(solution)/shard_map/all_to_all | solution.py:480
  208.6 9.8 %all-to-all-done.12 = bf16[4,8,32,512]{3,2,1,0:T(8,128)(2,1)S(1)} async-done(((bf16[4,8,32,512]{3,2,1,0:T(8,128)(2,1)}), bf16[4,8,32,512]{3,2,1,0:T(8,128)(2,1)S(1)}, u32[]{:S(2)}, u32[]{:S(2)}) %all-to-all-start.12) | async-done | bytes 1048608 | tf_op jit(solution)/shard_map/all_to_all | solution.py:480
  218.5 3.7 %all-to-all-start.14 = ((bf16[4,128,1024]{2,1,0:T(8,128)(2,1)}), bf16[4,128,1024]{2,1,0:T(8,128)(2,1)S(1)}, u32[]{:S(2)}, u32[]{:S(2)}) async-start(bf16[4,128,1024]{2,1,0:T(8,128)(2,1)} %bitcast.109), calls=%async_computation.14 | async-start | bytes 2097152 | tf_op jit(solution)/shard_map/all_to_all | solution.py:480
  226.0 9.0 %all-to-all-done.14 = bf16[4,128,1024]{2,1,0:T(8,128)(2,1)S(1)} async-done(((bf16[4,128,1024]{2,1,0:T(8,128)(2,1)}), bf16[4,128,1024]{2,1,0:T(8,128)(2,1)S(1)}, u32[]{:S(2)}, u32[]{:S(2)}) %all-to-all-start.14) | async-done | bytes 1048608 | tf_op jit(solution)/shard_map/all_to_all | solution.py:480
  235.0 3.5 %all-to-all-start.9 = ((bf16[4,8,40,384]{3,2,1,0:T(8,128)(2,1)}), bf16[4,8,40,384]{3,2,1,0:T(8,128)(2,1)S(1)}, u32[]{:S(2)}, u32[]{:S(2)}) async-start(bf16[4,8,40,384]{3,2,1,0:T(8,128)(2,1)} %fusion.29), calls=%async_computation.9 | async-start | bytes 1966080 | tf_op jit(solution)/shard_map/all_to_all | solution.py:480
  238.6 2.4 fusion.125
  241.7 1.9 collective-permute-start.31
  245.2 2.0 fusion.3
  248.2 2.7 all-to-all-done.9
  250.9 3.4 %all-to-all-start.11 = ((bf16[4,32,1024]{2,1,0:T(8,128)(2,1)}), bf16[4,32,1024]{2,1,0:T(8,128)(2,1)S(1)}, u32[]{:S(2)}, u32[]{:S(2)}) async-start(bf16[4,32,1024]{2,1,0:T(8,128)(2,1)} %convolution_convert_fusion.7), calls=%async_computation.11 | async-start | bytes 524288 | tf_op jit(solution)/shard_map/all_to_all | solution.py:480
  259.7 3.4 %all-to-all-start.13 = ((bf16[8,32,512]{2,1,0:T(8,128)(2,1)}), bf16[8,32,512]{2,1,0:T(8,128)(2,1)S(1)}, u32[]{:S(2)}, u32[]{:S(2)}) async-start(bf16[8,32,512]{2,1,0:T(8,128)(2,1)} %reduce_sum.196), calls=%async_computation.13 | async-start | bytes 524288 | tf_op jit(solution)/shard_map/all_to_all | solution.py:493
  264.2 8.2 %all-to-all-done.13 = bf16[8,32,512]{2,1,0:T(8,128)(2,1)S(1)} async-done(((bf16[8,32,512]{2,1,0:T(8,128)(2,1)}), bf16[8,32,512]{2,1,0:T(8,128)(2,1)S(1)}, u32[]{:S(2)}, u32[]{:S(2)}) %all-to-all-start.13) | async-done | bytes 262176 | tf_op jit(solution)/shard_map/all_to_all | solution.py:493
  272.4 3.3 %all-to-all-start.8 = ((bf16[4,16,1024]{2,1,0:T(8,128)(2,1)}), bf16[4,16,1024]{2,1,0:T(8,128)(2,1)S(1)}, u32[]{:S(2)}, u32[]{:S(2)}) async-start(bf16[4,16,1024]{2,1,0:T(8,128)(2,1)} %bitcast.86), calls=%async_computation.8 | async-start | bytes 262144 | tf_op jit(solution)/shard_map/all_to_all | solution.py:472
  276.4 4.3 %all-to-all-done.8 = bf16[4,16,1024]{2,1,0:T(8,128)(2,1)S(1)} async-done(((bf16[4,16,1024]{2,1,0:T(8,128)(2,1)}), bf16[4,16,1024]{2,1,0:T(8,128)(2,1)S(1)}, u32[]{:S(2)}, u32[]{:S(2)}) %all-to-all-start.8) | async-done | bytes 131104 | tf_op jit(solution)/shard_map/all_to_all | solution.py:472
  280.7 3.4 %all-to-all-start.10 = ((bf16[8,40,384]{2,1,0:T(8,128)(2,1)}), bf16[8,40,384]{2,1,0:T(8,128)(2,1)S(1)}, u32[]{:S(2)}, u32[]{:S(2)}) async-start(bf16[8,40,384]{2,1,0:T(8,128)(2,1)} %fusion.60), calls=%async_computation.10 | async-start | bytes 491520 | tf_op jit(solution)/shard_map/all_to_all | solution.py:509
  288.8 4.0 %all-to-all-done.10 = bf16[8,40,384]{2,1,0:T(8,128)(2,1)S(1)} async-done(((bf16[8,40,384]{2,1,0:T(8,128)(2,1)}), bf16[8,40,384]{2,1,0:T(8,128)(2,1)S(1)}, u32[]{:S(2)}, u32[]{:S(2)}) %all-to-all-start.10) | async-done | bytes 245792 | tf_op jit(solution)/shard_map/all_to_all | solution.py:509
  (356 shorter events, 98.0 us)
Async XLA Ops:
  6.5 10.5 %all-to-all-start = ((bf16[4,2,16,1024]{3,2,1,0:T(8,128)(2,1)}), bf16[4,2,16,1024]{3,2,1,0:T(8,128)(2,1)S(1)}, u32[]{:S(2)}, u32[]{:S(2)}) async-start(bf16[4,2,16,1024]{3,2,1,0:T(8,128)(2,1)} %copy.104), calls=%async_computation | async-start | bytes 524288 | tf_op jit(solution)/shard_map/all_to_all | solution.py:398
  17.0 38.4 %all-to-all-start.1 = ((bf16[8,40,384]{2,1,0:T(8,128)(2,1)}), bf16[8,40,384]{2,1,0:T(8,128)(2,1)S(1)}, u32[]{:S(2)}, u32[]{:S(2)}) async-start(bf16[8,40,384]{2,1,0:T(8,128)(2,1)} %pad_maximum_fusion.6), calls=%async_computation.1 | async-start | bytes 491520 | tf_op jit(solution)/shard_map/all_to_all | solution.py:358
  21.9 12.4 %collective-permute-start.2 = (bf16[64,1024]{1,0:T(8,128)(2,1)S(1)}, bf16[64,1024]{1,0:T(8,128)(2,1)S(1)}, u32[]{:S(2)}, u32[]{:S(2)}) collective-permute-start(bf16[64,1024]{1,0:T(8,128)(2,1)S(1)} %bitcast.306), channel_id=1, source_target_pairs={{0,6},{2,4},{4,2},{6,0},{1,7},{3,5},{5,3},{7,1},{8,14},{10,12},{12... | collective-permute-start | bytes 393224 | tf_op jit(solution)/shard_map/ppermute | solution.py:286
  27.7 21.0 %collective-permute-start.1 = (bf16[64,1024]{1,0:T(8,128)(2,1)S(1)}, bf16[64,1024]{1,0:T(8,128)(2,1)S(1)}, u32[]{:S(2)}, u32[]{:S(2)}) collective-permute-start(bf16[64,1024]{1,0:T(8,128)(2,1)S(1)} %bitcast.307), channel_id=1, source_target_pairs={{0,4},{2,6},{4,0},{6,2},{1,5},{3,7},{5,1},{7,3},{8,12},{10,14},{12... | collective-permute-start | bytes 393224 | tf_op jit(solution)/shard_map/ppermute | solution.py:286
  27.7 21.0 %collective-permute-start = (bf16[64,1024]{1,0:T(8,128)(2,1)S(1)}, bf16[64,1024]{1,0:T(8,128)(2,1)S(1)}, u32[]{:S(2)}, u32[]{:S(2)}) collective-permute-start(bf16[64,1024]{1,0:T(8,128)(2,1)S(1)} %bitcast.308), channel_id=1, source_target_pairs={{0,2},{2,0},{4,6},{6,4},{1,3},{3,1},{5,7},{7,5},{8,10},{10,8},{12,... | collective-permute-start | bytes 393224 | tf_op jit(solution)/shard_map/ppermute | solution.py:286
  28.3 20.6 %collective-permute-start.18 = (bf16[64,1024]{1,0:T(8,128)(2,1)S(1)}, bf16[64,1024]{1,0:T(8,128)(2,1)S(1)}, u32[]{:S(2)}, u32[]{:S(2)}) collective-permute-start(bf16[64,1024]{1,0:T(8,128)(2,1)S(1)} %bitcast.301), channel_id=1, source_target_pairs={{0,6},{2,4},{4,2},{6,0},{1,7},{3,5},{5,3},{7,1},{8,14},{10,12},{12... | collective-permute-start | bytes 393224 | tf_op jit(solution)/shard_map/ppermute | solution.py:286
  32.1 21.8 %collective-permute-start.17 = (bf16[64,1024]{1,0:T(8,128)(2,1)S(1)}, bf16[64,1024]{1,0:T(8,128)(2,1)S(1)}, u32[]{:S(2)}, u32[]{:S(2)}) collective-permute-start(bf16[64,1024]{1,0:T(8,128)(2,1)S(1)} %bitcast.302), channel_id=1, source_target_pairs={{0,4},{2,6},{4,0},{6,2},{1,5},{3,7},{5,1},{7,3},{8,12},{10,14},{12... | collective-permute-start | bytes 393224 | tf_op jit(solution)/shard_map/ppermute | solution.py:286
  34.3 19.6 %collective-permute-start.16 = (bf16[64,1024]{1,0:T(8,128)(2,1)S(1)}, bf16[64,1024]{1,0:T(8,128)(2,1)S(1)}, u32[]{:S(2)}, u32[]{:S(2)}) collective-permute-start(bf16[64,1024]{1,0:T(8,128)(2,1)S(1)} %bitcast.303), channel_id=1, source_target_pairs={{0,2},{2,0},{4,6},{6,4},{1,3},{3,1},{5,7},{7,5},{8,10},{10,8},{12,... | collective-permute-start | bytes 393224 | tf_op jit(solution)/shard_map/ppermute | solution.py:286
  48.8 13.8 %collective-permute-start.3 = (bf16[4,64,1024]{2,1,0:T(8,128)(2,1)S(1)}, bf16[4,64,1024]{2,1,0:T(8,128)(2,1)S(1)}, u32[]{:S(2)}, u32[]{:S(2)}) collective-permute-start(bf16[4,64,1024]{2,1,0:T(8,128)(2,1)S(1)} %pad_maximum_fusion.1), channel_id=1, source_target_pairs={{0,8},{8,0},{1,9},{9,1},{2,10},{10,2},{3,11},{11,3},{4,12},{12,4},... | collective-permute-start | bytes 1572872 | tf_op jit(solution)/shard_map/ppermute | solution.py:288
  54.7 55.3 %collective-permute-start.19 = (bf16[4,64,1024]{2,1,0:T(8,128)(2,1)}, bf16[4,64,1024]{2,1,0:T(8,128)(2,1)}, u32[]{:S(2)}, u32[]{:S(2)}) collective-permute-start(bf16[4,64,1024]{2,1,0:T(8,128)(2,1)} %pad_maximum_fusion.2), channel_id=1, source_target_pairs={{0,8},{8,0},{1,9},{9,1},{2,10},{10,2},{3,11},{11,3},{4,12},{12,4},... | collective-permute-start | bytes 1572872 | tf_op jit(solution)/shard_map/ppermute | solution.py:288
  56.5 17.5 %all-to-all-start.2 = ((bf16[4,8,40,384]{3,1,2,0:T(8,128)(2,1)}), bf16[4,8,40,384]{3,1,2,0:T(8,128)(2,1)S(1)}, u32[]{:S(2)}, u32[]{:S(2)}) async-start(bf16[4,8,40,384]{3,1,2,0:T(8,128)(2,1)} %broadcast_in_dim.29), calls=%async_computation.2 | async-start | bytes 1966080 | tf_op jit(solution)/shard_map/all_to_all | solution.py:354
  74.8 11.7 %all-to-all-start.3 = ((bf16[4,32,1024]{2,1,0:T(8,128)(2,1)}), bf16[4,32,1024]{2,1,0:T(8,128)(2,1)S(1)}, u32[]{:S(2)}, u32[]{:S(2)}) async-start(bf16[4,32,1024]{2,1,0:T(8,128)(2,1)} %broadcast_in_dim.60), calls=%async_computation.3 | async-start | bytes 524288 | tf_op jit(solution)/shard_map/all_to_all | solution.py:354
  82.0 29.0 %copy-start.6 = (bf16[256,1024]{1,0:T(8,128)(2,1)}, bf16[256,1024]{1,0:T(8,128)(2,1)S(1)}, u32[]{:S(2)}) copy-start(bf16[256,1024]{1,0:T(8,128)(2,1)S(1)} %get-tuple-element.83) | copy-start | bytes 1572868
  86.5 12.7 %all-to-all-start.4 = ((bf16[8,32,512]{2,1,0:T(8,128)(2,1)}), bf16[8,32,512]{2,1,0:T(8,128)(2,1)S(1)}, u32[]{:S(2)}, u32[]{:S(2)}) async-start(bf16[8,32,512]{2,1,0:T(8,128)(2,1)} %reshape.337), calls=%async_computation.4 | async-start | bytes 524288 | tf_op jit(solution)/shard_map/all_to_all | solution.py:359
  91.0 13.5 %collective-permute-start.4 = (bf16[4,32,1024]{2,1,0:T(8,128)(2,1)}, bf16[4,32,1024]{2,1,0:T(8,128)(2,1)}, u32[]{:S(2)}, u32[]{:S(2)}) collective-permute-start(bf16[4,32,1024]{2,1,0:T(8,128)(2,1)} %bitcast.30), channel_id=1, source_target_pairs={{0,8},{8,0},{1,9},{9,1},{2,10},{10,2},{3,11},{11,3},{4,12},{12,4},... | collective-permute-start | bytes 786440 | tf_op jit(solution)/shard_map/ppermute | solution.py:297
  100.3 23.2 %all-to-all-start.5 = ((bf16[4,8,32,512]{3,2,1,0:T(8,128)(2,1)}), bf16[4,8,32,512]{3,2,1,0:T(8,128)(2,1)S(1)}, u32[]{:S(2)}, u32[]{:S(2)}) async-start(bf16[4,8,32,512]{3,2,1,0:T(8,128)(2,1)} %broadcast_in_dim.61), calls=%async_computation.5 | async-start | bytes 2097152 | tf_op jit(solution)/shard_map/all_to_all | solution.py:354
  106.4 6.1 %collective-permute-start.5 = (bf16[32,1024]{1,0:T(8,128)(2,1)S(1)}, bf16[32,1024]{1,0:T(8,128)(2,1)S(1)}, u32[]{:S(2)}, u32[]{:S(2)}) collective-permute-start(bf16[32,1024]{1,0:T(8,128)(2,1)S(1)} %get-tuple-element.66), channel_id=1, source_target_pairs={{0,2},{2,0},{4,6},{6,4},{1,3},{3,1},{5,7},{7,5},{8,10},{10,8},{12,... | collective-permute-start | bytes 196616 | tf_op jit(solution)/shard_map/ppermute | solution.py:301
  106.5 6.6 %collective-permute-start.7 = (bf16[32,1024]{1,0:T(8,128)(2,1)S(1)}, bf16[32,1024]{1,0:T(8,128)(2,1)S(1)}, u32[]{:S(2)}, u32[]{:S(2)}) collective-permute-start(bf16[32,1024]{1,0:T(8,128)(2,1)S(1)} %get-tuple-element.67), channel_id=1, source_target_pairs={{0,6},{2,4},{4,2},{6,0},{1,7},{3,5},{5,3},{7,1},{8,14},{10,12},{12... | collective-permute-start | bytes 196616 | tf_op jit(solution)/shard_map/ppermute | solution.py:301
  108.7 7.3 %collective-permute-start.6 = (bf16[32,1024]{1,0:T(8,128)(2,1)S(1)}, bf16[32,1024]{1,0:T(8,128)(2,1)}, u32[]{:S(2)}, u32[]{:S(2)}) collective-permute-start(bf16[32,1024]{1,0:T(8,128)(2,1)S(1)} %get-tuple-element.68), channel_id=1, source_target_pairs={{0,4},{2,6},{4,0},{6,2},{1,5},{3,7},{5,1},{7,3},{8,12},{10,14},{12... | collective-permute-start | bytes 196616 | tf_op jit(solution)/shard_map/ppermute | solution.py:301
  118.4 10.4 %collective-permute-start.10 = (bf16[32,1024]{1,0:T(8,128)(2,1)}, bf16[32,1024]{1,0:T(8,128)(2,1)}, u32[]{:S(2)}, u32[]{:S(2)}) collective-permute-start(bf16[32,1024]{1,0:T(8,128)(2,1)} %get-tuple-element.36), channel_id=1, source_target_pairs={{0,6},{2,4},{4,2},{6,0},{1,7},{3,5},{5,3},{7,1},{8,14},{10,12},{12... | collective-permute-start | bytes 196616 | tf_op jit(solution)/shard_map/ppermute | solution.py:286
  119.9 8.9 %collective-permute-start.9 = (bf16[32,1024]{1,0:T(8,128)(2,1)}, bf16[32,1024]{1,0:T(8,128)(2,1)}, u32[]{:S(2)}, u32[]{:S(2)}) collective-permute-start(bf16[32,1024]{1,0:T(8,128)(2,1)} %get-tuple-element.36), channel_id=1, source_target_pairs={{0,4},{2,6},{4,0},{6,2},{1,5},{3,7},{5,1},{7,3},{8,12},{10,14},{12... | collective-permute-start | bytes 196616 | tf_op jit(solution)/shard_map/ppermute | solution.py:286
  120.3 8.6 %collective-permute-start.8 = (bf16[32,1024]{1,0:T(8,128)(2,1)}, bf16[32,1024]{1,0:T(8,128)(2,1)}, u32[]{:S(2)}, u32[]{:S(2)}) collective-permute-start(bf16[32,1024]{1,0:T(8,128)(2,1)} %get-tuple-element.36), channel_id=1, source_target_pairs={{0,2},{2,0},{4,6},{6,4},{1,3},{3,1},{5,7},{7,5},{8,10},{10,8},{12,... | collective-permute-start | bytes 196616 | tf_op jit(solution)/shard_map/ppermute | solution.py:286
  124.7 16.2 %all-to-all-start.6 = ((bf16[4,128,1024]{2,1,0:T(8,128)(2,1)}), bf16[4,128,1024]{2,1,0:T(8,128)(2,1)S(1)}, u32[]{:S(2)}, u32[]{:S(2)}) async-start(bf16[4,128,1024]{2,1,0:T(8,128)(2,1)} %broadcast_in_dim.62), calls=%async_computation.6 | async-start | bytes 2097152 | tf_op jit(solution)/shard_map/all_to_all | solution.py:354
  130.2 2.6 collective-permute-start.11
  151.0 1.6 collective-permute-start.20
  152.8 4.7 %collective-permute-start.21 = (bf16[32,1152]{1,0:T(8,128)(2,1)S(1)}, bf16[32,1152]{1,0:T(8,128)(2,1)S(1)}, u32[]{:S(2)}, u32[]{:S(2)}) collective-permute-start(bf16[32,1152]{1,0:T(8,128)(2,1)S(1)} %get-tuple-element.61), channel_id=1, source_target_pairs={{0,2},{2,0},{4,6},{6,4},{1,3},{3,1},{5,7},{7,5},{8,10},{10,8},{12,... | collective-permute-start | bytes 221192 | tf_op jit(solution)/shard_map/ppermute | solution.py:301
  153.1 6.8 %collective-permute-start.23 = (bf16[32,1152]{1,0:T(8,128)(2,1)S(1)}, bf16[32,1152]{1,0:T(8,128)(2,1)S(1)}, u32[]{:S(2)}, u32[]{:S(2)}) collective-permute-start(bf16[32,1152]{1,0:T(8,128)(2,1)S(1)} %get-tuple-element.62), channel_id=1, source_target_pairs={{0,6},{2,4},{4,2},{6,0},{1,7},{3,5},{5,3},{7,1},{8,14},{10,12},{12... | collective-permute-start | bytes 221192 | tf_op jit(solution)/shard_map/ppermute | solution.py:301
  155.3 7.9 %collective-permute-start.22 = (bf16[32,1152]{1,0:T(8,128)(2,1)S(1)}, bf16[32,1152]{1,0:T(8,128)(2,1)S(1)}, u32[]{:S(2)}, u32[]{:S(2)}) collective-permute-start(bf16[32,1152]{1,0:T(8,128)(2,1)S(1)} %get-tuple-element.63), channel_id=1, source_target_pairs={{0,4},{2,6},{4,0},{6,2},{1,5},{3,7},{5,1},{7,3},{8,12},{10,14},{12... | collective-permute-start | bytes 221192 | tf_op jit(solution)/shard_map/ppermute | solution.py:301
  157.4 15.2 %collective-permute-start.12 = (bf16[4,64,1024]{2,1,0:T(8,128)(2,1)S(1)}, bf16[4,64,1024]{2,1,0:T(8,128)(2,1)S(1)}, u32[]{:S(2)}, u32[]{:S(2)}) collective-permute-start(bf16[4,64,1024]{2,1,0:T(8,128)(2,1)S(1)} %bitcast.324), channel_id=1, source_target_pairs={{0,8},{8,0},{1,9},{9,1},{2,10},{10,2},{3,11},{11,3},{4,12},{12,4},... | collective-permute-start | bytes 1572872 | tf_op jit(solution)/shard_map/ppermute | solution.py:297
  164.5 6.7 %collective-permute-start.26 = (bf16[32,1024]{1,0:T(8,128)(2,1)S(1)}, bf16[32,1024]{1,0:T(8,128)(2,1)S(1)}, u32[]{:S(2)}, u32[]{:S(2)}) collective-permute-start(bf16[32,1024]{1,0:T(8,128)(2,1)S(1)} %get-tuple-element.32), channel_id=1, source_target_pairs={{0,6},{2,4},{4,2},{6,0},{1,7},{3,5},{5,3},{7,1},{8,14},{10,12},{12... | collective-permute-start | bytes 196616 | tf_op jit(solution)/shard_map/ppermute | solution.py:286
  166.6 5.9 %collective-permute-start.25 = (bf16[32,1024]{1,0:T(8,128)(2,1)S(1)}, bf16[32,1024]{1,0:T(8,128)(2,1)S(1)}, u32[]{:S(2)}, u32[]{:S(2)}) collective-permute-start(bf16[32,1024]{1,0:T(8,128)(2,1)S(1)} %get-tuple-element.32), channel_id=1, source_target_pairs={{0,4},{2,6},{4,0},{6,2},{1,5},{3,7},{5,1},{7,3},{8,12},{10,14},{12... | collective-permute-start | bytes 196616 | tf_op jit(solution)/shard_map/ppermute | solution.py:286
  166.6 5.9 %collective-permute-start.24 = (bf16[32,1024]{1,0:T(8,128)(2,1)S(1)}, bf16[32,1024]{1,0:T(8,128)(2,1)S(1)}, u32[]{:S(2)}, u32[]{:S(2)}) collective-permute-start(bf16[32,1024]{1,0:T(8,128)(2,1)S(1)} %get-tuple-element.32), channel_id=1, source_target_pairs={{0,2},{2,0},{4,6},{6,4},{1,3},{3,1},{5,7},{7,5},{8,10},{10,8},{12,... | collective-permute-start | bytes 196616 | tf_op jit(solution)/shard_map/ppermute | solution.py:286
  172.5 22.6 %collective-permute-start.27 = (bf16[4,32,1024]{2,1,0:T(8,128)(2,1)S(1)}, bf16[4,32,1024]{2,1,0:T(8,128)(2,1)}, u32[]{:S(2)}, u32[]{:S(2)}) collective-permute-start(bf16[4,32,1024]{2,1,0:T(8,128)(2,1)S(1)} %pad_maximum_fusion.5), channel_id=1, source_target_pairs={{0,8},{8,0},{1,9},{9,1},{2,10},{10,2},{3,11},{11,3},{4,12},{12,4},... | collective-permute-start | bytes 786440 | tf_op jit(solution)/shard_map/ppermute | solution.py:288
  174.8 5.9 %collective-permute-start.13 = (bf16[64,1024]{1,0:T(8,128)(2,1)S(1)}, bf16[64,1024]{1,0:T(8,128)(2,1)S(1)}, u32[]{:S(2)}, u32[]{:S(2)}) collective-permute-start(bf16[64,1024]{1,0:T(8,128)(2,1)S(1)} %get-tuple-element.58), channel_id=1, source_target_pairs={{0,2},{2,0},{4,6},{6,4},{1,3},{3,1},{5,7},{7,5},{8,10},{10,8},{12,... | collective-permute-start | bytes 393224 | tf_op jit(solution)/shard_map/ppermute | solution.py:301
  175.5 9.3 %collective-permute-start.15 = (bf16[64,1024]{1,0:T(8,128)(2,1)S(1)}, bf16[64,1024]{1,0:T(8,128)(2,1)S(1)}, u32[]{:S(2)}, u32[]{:S(2)}) collective-permute-start(bf16[64,1024]{1,0:T(8,128)(2,1)S(1)} %get-tuple-element.59), channel_id=1, source_target_pairs={{0,6},{2,4},{4,2},{6,0},{1,7},{3,5},{5,3},{7,1},{8,14},{10,12},{12... | collective-permute-start | bytes 393224 | tf_op jit(solution)/shard_map/ppermute | solution.py:301
  177.6 12.7 %collective-permute-start.14 = (bf16[64,1024]{1,0:T(8,128)(2,1)S(1)}, bf16[64,1024]{1,0:T(8,128)(2,1)S(1)}, u32[]{:S(2)}, u32[]{:S(2)}) collective-permute-start(bf16[64,1024]{1,0:T(8,128)(2,1)S(1)} %get-tuple-element.60), channel_id=1, source_target_pairs={{0,4},{2,6},{4,0},{6,2},{1,5},{3,7},{5,1},{7,3},{8,12},{10,14},{12... | collective-permute-start | bytes 393224 | tf_op jit(solution)/shard_map/ppermute | solution.py:301
  191.1 10.2 %all-to-all-start.7 = ((bf16[4,16,1024]{2,1,0:T(8,128)(2,1)}), bf16[4,16,1024]{2,1,0:T(8,128)(2,1)}, u32[]{:S(2)}, u32[]{:S(2)}) async-start(bf16[4,16,1024]{2,1,0:T(8,128)(2,1)} %bitcast.51), calls=%async_computation.7 | async-start | bytes 262144 | tf_op jit(solution)/shard_map/all_to_all | solution.py:472
  201.3 17.2 %all-to-all-start.12 = ((bf16[4,8,32,512]{3,2,1,0:T(8,128)(2,1)}), bf16[4,8,32,512]{3,2,1,0:T(8,128)(2,1)S(1)}, u32[]{:S(2)}, u32[]{:S(2)}) async-start(bf16[4,8,32,512]{3,2,1,0:T(8,128)(2,1)} %bitcast.107), calls=%async_computation.12 | async-start | bytes 2097152 | tf_op jit(solution)/shard_map/all_to_all | solution.py:480
  218.5 16.6 %all-to-all-start.14 = ((bf16[4,128,1024]{2,1,0:T(8,128)(2,1)}), bf16[4,128,1024]{2,1,0:T(8,128)(2,1)S(1)}, u32[]{:S(2)}, u32[]{:S(2)}) async-start(bf16[4,128,1024]{2,1,0:T(8,128)(2,1)} %bitcast.109), calls=%async_computation.14 | async-start | bytes 2097152 | tf_op jit(solution)/shard_map/all_to_all | solution.py:480
  223.2 15.3 %collective-permute-start.28 = (bf16[4,64,1024]{2,1,0:T(8,128)(2,1)}, bf16[4,64,1024]{2,1,0:T(8,128)(2,1)}, u32[]{:S(2)}, u32[]{:S(2)}) collective-permute-start(bf16[4,64,1024]{2,1,0:T(8,128)(2,1)} %bitcast.81), channel_id=1, source_target_pairs={{0,8},{8,0},{1,9},{9,1},{2,10},{10,2},{3,11},{11,3},{4,12},{12,4},... | collective-permute-start | bytes 1572872 | tf_op jit(solution)/shard_map/ppermute | solution.py:297
  235.0 15.9 %all-to-all-start.9 = ((bf16[4,8,40,384]{3,2,1,0:T(8,128)(2,1)}), bf16[4,8,40,384]{3,2,1,0:T(8,128)(2,1)S(1)}, u32[]{:S(2)}, u32[]{:S(2)}) async-start(bf16[4,8,40,384]{3,2,1,0:T(8,128)(2,1)} %fusion.29), calls=%async_computation.9 | async-start | bytes 1966080 | tf_op jit(solution)/shard_map/all_to_all | solution.py:480
  241.7 12.6 %collective-permute-start.29 = (bf16[64,1024]{1,0:T(8,128)(2,1)}, bf16[64,1024]{1,0:T(8,128)(2,1)S(1)}, u32[]{:S(2)}, u32[]{:S(2)}) collective-permute-start(bf16[64,1024]{1,0:T(8,128)(2,1)} %get-tuple-element.53), channel_id=1, source_target_pairs={{0,2},{2,0},{4,6},{6,4},{1,3},{3,1},{5,7},{7,5},{8,10},{10,8},{12,... | collective-permute-start | bytes 393224 | tf_op jit(solution)/shard_map/ppermute | solution.py:301
  241.7 12.6 %collective-permute-start.31 = (bf16[64,1024]{1,0:T(8,128)(2,1)}, bf16[64,1024]{1,0:T(8,128)(2,1)S(1)}, u32[]{:S(2)}, u32[]{:S(2)}) collective-permute-start(bf16[64,1024]{1,0:T(8,128)(2,1)} %get-tuple-element.54), channel_id=1, source_target_pairs={{0,6},{2,4},{4,2},{6,0},{1,7},{3,5},{5,3},{7,1},{8,14},{10,12},{12... | collective-permute-start | bytes 393224 | tf_op jit(solution)/shard_map/ppermute | solution.py:301
  243.6 12.4 %collective-permute-start.30 = (bf16[64,1024]{1,0:T(8,128)(2,1)S(1)}, bf16[64,1024]{1,0:T(8,128)(2,1)}, u32[]{:S(2)}, u32[]{:S(2)}) collective-permute-start(bf16[64,1024]{1,0:T(8,128)(2,1)S(1)} %get-tuple-element.55), channel_id=1, source_target_pairs={{0,4},{2,6},{4,0},{6,2},{1,5},{3,7},{5,1},{7,3},{8,12},{10,14},{12... | collective-permute-start | bytes 393224 | tf_op jit(solution)/shard_map/ppermute | solution.py:301
  250.9 8.8 %all-to-all-start.11 = ((bf16[4,32,1024]{2,1,0:T(8,128)(2,1)}), bf16[4,32,1024]{2,1,0:T(8,128)(2,1)S(1)}, u32[]{:S(2)}, u32[]{:S(2)}) async-start(bf16[4,32,1024]{2,1,0:T(8,128)(2,1)} %convolution_convert_fusion.7), calls=%async_computation.11 | async-start | bytes 524288 | tf_op jit(solution)/shard_map/all_to_all | solution.py:480
  259.7 12.7 %all-to-all-start.13 = ((bf16[8,32,512]{2,1,0:T(8,128)(2,1)}), bf16[8,32,512]{2,1,0:T(8,128)(2,1)S(1)}, u32[]{:S(2)}, u32[]{:S(2)}) async-start(bf16[8,32,512]{2,1,0:T(8,128)(2,1)} %reduce_sum.196), calls=%async_computation.13 | async-start | bytes 524288 | tf_op jit(solution)/shard_map/all_to_all | solution.py:493
  272.4 8.3 %all-to-all-start.8 = ((bf16[4,16,1024]{2,1,0:T(8,128)(2,1)}), bf16[4,16,1024]{2,1,0:T(8,128)(2,1)S(1)}, u32[]{:S(2)}, u32[]{:S(2)}) async-start(bf16[4,16,1024]{2,1,0:T(8,128)(2,1)} %bitcast.86), calls=%async_computation.8 | async-start | bytes 262144 | tf_op jit(solution)/shard_map/all_to_all | solution.py:472
  280.7 12.1 %all-to-all-start.10 = ((bf16[8,40,384]{2,1,0:T(8,128)(2,1)}), bf16[8,40,384]{2,1,0:T(8,128)(2,1)S(1)}, u32[]{:S(2)}, u32[]{:S(2)}) async-start(bf16[8,40,384]{2,1,0:T(8,128)(2,1)} %fusion.60), calls=%async_computation.10 | async-start | bytes 491520 | tf_op jit(solution)/shard_map/all_to_all | solution.py:509
  (68 other events, 256.8 us)

commit v2 on v0

--- a/solution.py
+++ b/solution.py
@@ -1,6 +1,11 @@
+import math
+from functools import partial
+
 import jax
 import jax.numpy as jnp
 from jax import lax
+from jax.experimental import pallas as pl
+from jax.experimental.pallas import tpu as pltpu
 from jax.sharding import PartitionSpec as P
 
 HEADS = 16
@@ -276,28 +281,614 @@
     )
 
 
+F32, BF16 = jnp.float32, jnp.bfloat16
+NN = (((1,), (0,)), ((), ()))
+NT = (((1,), (1,)), ((), ()))
+TN = (((0,), (0,)), ((), ()))
+
+
+def mm(left, right, dims=NN):
+    return lax.dot_general(left, right, dims, preferred_element_type=F32)
+
+
+def local_call(body, outs, args, flops=0, scratch=(), scalars=0):
+    shapes = [jax.ShapeDtypeStruct(s, d) for s, d in outs]
+    spaces = [pltpu.SMEM] * scalars + [pltpu.VMEM] * (len(args) - scalars)
+    size = sum(math.prod(a.shape) * a.dtype.itemsize for a in list(args) + shapes)
+    return pl.pallas_call(
+        body,
+        out_shape=shapes,
+        in_specs=[pl.BlockSpec(memory_space=s) for s in spaces],
+        out_specs=[pl.BlockSpec(memory_space=pltpu.VMEM)] * len(shapes),
+        scratch_shapes=list(scratch),
+        compiler_params=pltpu.CompilerParams(vmem_limit_bytes=32 * 2**20),
+        cost_estimate=pl.CostEstimate(flops=int(flops), bytes_accessed=size, transcendentals=0),
+    )(*args)
+
+
+def flips(count):
+    return [[(i, i ^ k) for i in range(count)] for k in range(count)]
+
+
+def send_z(blocks):
+    return [lax.ppermute(b, "z", f) for b, f in zip(blocks, flips(lax.axis_size("z"))[1:])]
+
+
+def send_c(block):
+    return lax.ppermute(block, "c", flips(2)[1])
+
+
+def gather_group(own):
+    blocks = [own] + send_z([own] * (lax.axis_size("z") - 1))
+    return blocks + [send_c(b) for b in blocks]
+
+
+def half_sum_kernel(near, far, mine, *low):
+    for k in range(near.shape[0]):
+        total = near[k].astype(F32) + far[k].astype(F32)
+        if k == 0:
+            mine[...] = total
+        else:
+            low[k - 1][...] = total.astype(BF16)
+
+
+def scatter_group(near, far):
+    depth, rows, lanes = near.shape
+    outs = [((rows, lanes), F32)] + [((rows, lanes), BF16)] * (depth - 1)
+    mine, *low = local_call(half_sum_kernel, outs, (near, send_c(far)))
+    return [mine] + send_z(low)
+
+
+def add_up(refs):
+    total = refs[0][...]
+    for ref in refs[1:]:
+        total = total + ref[...].astype(F32)
+    return total
+
+
+def xor_order(blocks, index):
+    step = 1
+    while step < len(blocks):
+        swap = (index & step) != 0
+        blocks = [jnp.where(swap, blocks[b ^ step], blocks[b]) for b in range(len(blocks))]
+        step *= 2
+    return blocks
+
+
+def columns_kernel(dims, w_qkv, w_up, vecs, out):
+    ny, members, nx, ff_rows = dims
+    cols = 3 * ny * HDIM
+    for g in range(members):
+        parts = []
+        for t in range(3):
+            for y in range(ny):
+                at = (t * HEADS + y * members + g) * HDIM
+                parts.append(w_qkv[:, at : at + HDIM])
+        out[g, :, :cols] = jnp.concatenate(parts, 1)
+        out[g, :, cols : cols + 128] = vecs[...]
+        for y in range(ny):
+            for x in range(nx):
+                at = ((y * members + g) * nx + x) * ff_rows
+                to = cols + 128 + (y * nx + x) * ff_rows
+                out[g, :, to : to + ff_rows] = w_up[:, at : at + ff_rows]
+
+
+def pick_kernel(cap, where, chosen_t, tokens, cot, rows, pick):
+    seq_count, seg_len = tokens.shape[:2]
+    base = where[4] * seg_len
+    places = base + lax.broadcasted_iota(jnp.int32, (chosen_t.shape[0], seg_len), 1)
+    slots = lax.broadcasted_iota(jnp.int32, (cap, seg_len), 0)
+    for s in range(seq_count):
+        at = chosen_t[:, s : s + 1]
+        present = jnp.sum((at == places).astype(F32), 0, keepdims=True)
+        rank = jnp.sum(((at >= base) & (at < places)).astype(F32), 0, keepdims=True)
+        hot = jnp.where(rank.astype(jnp.int32) == slots, present, 0.0).astype(BF16)
+        pick[s] = hot
+        rows[s, :cap] = mm(hot, tokens[s]).astype(BF16)
+        rows[s, cap:] = mm(hot, cot[s]).astype(BF16)
+
+
+def spread_kernel(dims, where, chosen, chosen_t, spread):
+    ny, nc, nz, nx, seg_len, cap = dims
+    c, z, line = where[0], where[1], where[2]
+    routed = chosen_t.shape[0]
+    members = nc * nz
+
+    def owner_of(mine):
+        return lax.div(mine, jnp.int32(seg_len))
+
+    mine_col = chosen_t[:, 0:1]
+    mine_row = chosen[0:1, :]
+    for s in range(1, chosen.shape[0]):
+        mine_col = jnp.where(line == s, chosen_t[:, s : s + 1], mine_col)
+        mine_row = jnp.where(line == s, chosen[s : s + 1, :], mine_row)
+    owner, owner_row = owner_of(mine_col), owner_of(mine_row)
+    order = lax.broadcasted_iota(jnp.int32, (routed, routed), 0)
+    other = lax.broadcasted_iota(jnp.int32, (routed, routed), 1)
+    same = (owner == owner_row) & (other < order)
+    slot = jnp.sum(same.astype(F32), 1, keepdims=True).astype(jnp.int32)
+    ox, rest = lax.rem(owner, jnp.int32(nx)), lax.div(owner, jnp.int32(nx))
+    oz, rest = lax.rem(rest, jnp.int32(nz)), lax.div(rest, jnp.int32(nz))
+    oc, oy = lax.rem(rest, jnp.int32(nc)), lax.div(rest, jnp.int32(nc))
+    cell = ((((oc ^ c) * nz + (oz ^ z)) * ny + oy) * nx + ox) * cap + slot
+    own = routed // members
+    cells = [cell[b * own : (b + 1) * own] for b in range(members)]
+    for b, block in enumerate(xor_order(cells, where[3])):
+        lanes = lax.broadcasted_iota(jnp.int32, (own, spread.shape[1]), 1)
+        spread[b * own : (b + 1) * own] = (block == lanes).astype(F32).astype(BF16)
+
+
+def kept_pairs(member, routed, own):
+    down = lax.broadcasted_iota(jnp.int32, (routed, routed), 0)
+    across = lax.broadcasted_iota(jnp.int32, (routed, routed), 1)
+    shift = own.bit_length() - 1
+    first = ((down >> shift) ^ member) * own + (down & (own - 1))
+    second = ((across >> shift) ^ member) * own + (across & (own - 1))
+    return second <= first
+
+
+def probabilities(queries, keys, kept):
+    scores = jnp.where(kept, mm(queries, keys, NT) * HDIM ** (-0.5), neg_large)
+    top = jnp.max(scores, 1, keepdims=True)
+    probs = jnp.where(kept, jnp.exp(scores - top), 0.0)
+    return probs, jnp.sum(probs, 1, keepdims=True)
+
+
+def inverse_rms(values):
+    return lax.rsqrt(jnp.mean(values * values, 1, keepdims=True) + epsilon)
+
+
+def line_rows(got, first, count):
+    return jnp.concatenate([got[q, first : first + count] for q in range(got.shape[0])], 0)
+
+
+def natural_rows(got, dims, first, count, out):
+    ny, members, nx, rows = dims
+    for y in range(ny):
+        for g in range(members):
+            for x in range(nx):
+                to = ((y * members + g) * nx + x) * rows
+                out[to : to + rows] = got[y * nx + x, g, :, first : first + count]
+
+
+def attention_kernel(dims, members, where, spread, got_rows, got_qkv, *refs):
+    ny, nx, rows, cap, ff_rows = dims
+    blocks, outs = refs[:members], refs[members:]
+    picked_o, normed_o, w_o, vecs_o, joined_o, att_o, exact_o, near_o, far_o, vec_s = outs
+    heads = ny
+    cols = 3 * heads * HDIM
+    routed, width = picked_o.shape
+    own = routed // members
+    spots = jnp.concatenate(
+        [b[q, :cap] for b in blocks for q in range(b.shape[0])], 0
+    )
+    picked_low = mm(spread[...], spots).astype(BF16)
+    picked_o[...] = picked_low
+    picked = picked_low.astype(F32)
+    natural_rows(got_qkv, (ny, members, nx, rows), 0, cols, w_o)
+    natural_rows(got_qkv, (ny, members, nx, rows), cols, 128, vec_s)
+    eye = lax.broadcasted_iota(jnp.int32, (8, 128), 0)
+    eye = (eye == lax.broadcasted_iota(jnp.int32, (8, 128), 1)).astype(F32).astype(BF16)
+    vecs = mm(eye, vec_s[...], NT)
+    vecs_o[...] = vecs
+    normed = (picked * inverse_rms(picked) * vecs[0:1]).astype(BF16)
+    normed_o[...] = normed
+    joined = mm(normed, w_o[...]).astype(BF16)
+    joined_o[...] = joined
+    kept = kept_pairs(where[3], routed, own)
+    parts = []
+    for h in range(heads):
+        queries, keys, values = (
+            joined[:, (t * heads + h) * HDIM : (t * heads + h + 1) * HDIM] for t in range(3)
+        )
+        probs, total = probabilities(queries, keys, kept)
+        parts.append(mm(probs.astype(BF16), values) / total)
+    exact = jnp.concatenate(parts, 1)
+    exact_o[...] = exact
+    attended = exact.astype(BF16)
+    att_o[...] = attended
+    branch = mm(attended, line_rows(got_rows, ff_rows, rows)).astype(BF16)
+    put_halves(branch, near_o, far_o)
+
+
+def put_halves(values, near, far):
+    depth, own = near.shape[:2]
+    for k in range(depth):
+        near[k] = values[k * own : (k + 1) * own]
+        far[k] = values[(depth + k) * own : (depth + k + 1) * own]
+
+
+def update_kernel(dims, members, spread, got_rows, picked, vecs, *refs):
+    cap, ff_rows = dims
+    blocks, (cot_o, gate_o, d_result_o, d_active_o) = refs[:members], refs[members:]
+    spots = jnp.concatenate(
+        [b[q, cap:] for b in blocks for q in range(b.shape[0])], 0
+    )
+    cot_low = mm(spread[...], spots).astype(BF16)
+    cot_o[...] = cot_low
+    logit = jnp.sum(picked[...].astype(F32) * vecs[2:3, :], 1, keepdims=True)
+    gate = 1.0 / (1.0 + jnp.exp(-logit))
+    gate_o[...] = gate
+    d_result = (gate * cot_low.astype(F32)).astype(BF16)
+    d_result_o[...] = d_result
+    d_active_o[...] = mm(d_result, line_rows(got_rows, 0, ff_rows), NT)
+
+
+def hidden_kernel(own, picked, vecs, *refs):
+    *terms, hidden_o, normed_o = refs
+    hidden = picked[:own, :].astype(F32) + add_up(terms)
+    hidden_o[...] = hidden
+    normed_o[...] = (hidden * inverse_rms(hidden) * vecs[1:2, :]).astype(BF16)
+
+
+def forward_kernel(dims, members, got_up, d_active, *refs):
+    blocks, (active_o, d_upper_o, near_o, far_o, w_s) = refs[:members], refs[members:]
+    natural_rows(got_up, dims, 0, got_up.shape[3], w_s)
+    normed = jnp.concatenate([b[...] for b in blocks], 0)
+    upper = mm(normed, w_s[...])
+    below = 0.5 * (1.0 + lax.erf(upper * (0.5**0.5)))
+    active_o[...] = (upper * below).astype(BF16)
+    slope = below + upper * jnp.exp(-0.5 * upper * upper) * ((2.0 * math.pi) ** -0.5)
+    d_upper = (d_active[...] * slope).astype(BF16)
+    d_upper_o[...] = d_upper
+    put_halves(mm(d_upper, w_s[...], NT).astype(BF16), near_o, far_o)
+
+
+def ff_grads_kernel(dims, members, active, d_upper, d_result, *refs):
+    ny, nx, rows, ff_rows = dims
+    blocks, (sums_o,) = refs[:members], refs[members:]
+    lines = ny * nx
+    normed = jnp.concatenate([b[...] for b in blocks], 0)
+    down = mm(active[...], d_result[...], TN).astype(BF16)
+    up = mm(normed, d_upper[...], TN).astype(BF16)
+    wide = up.shape[1]
+    each = ff_rows + members * rows // 2
+    for y in range(ny):
+        for x in range(nx):
+            q = y * nx + x
+            sums_o[q * each : q * each + ff_rows] = down[q * ff_rows : (q + 1) * ff_rows]
+            for g in range(members):
+                at = ((y * members + g) * nx + x) * rows
+                half, row = divmod(g * rows, members * rows // 2)
+                to = q * each + ff_rows + row
+                sums_o[to : to + rows, half * wide : (half + 1) * wide] = up[at : at + rows]
+
+
+def result_kernel(dims, active, attended, got_rows, cot, gate, spread, logit_o, near_o, far_o):
+    rows, ff_rows = dims
+    result = mm(active[...], line_rows(got_rows, 0, ff_rows))
+    combined = result + mm(attended[...], line_rows(got_rows, ff_rows, rows))
+    logit = jnp.sum(cot[...].astype(F32) * combined, 1, keepdims=True)
+    logit_o[...] = logit * gate[...] * (1.0 - gate[...])
+    update = (gate[...] * combined).astype(BF16)
+    put_halves(mm(spread[...], update, TN).astype(BF16), near_o, far_o)
+
+
+def hidden_back_kernel(own, hidden_r, vecs, gate, cot, *refs):
+    *terms, d_branch_o, d_hidden_o, gain_o = refs
+    d_normed = add_up(terms)
+    hidden = hidden_r[...]
+    inv = inverse_rms(hidden)
+    u = d_normed * vecs[1:2, :]
+    d_hidden = inv * u - hidden * (inv * inv * inv * jnp.mean(u * hidden, 1, keepdims=True))
+    d_hidden_o[...] = d_hidden
+    gain_o[...] = (d_normed * hidden * inv).astype(BF16)
+    d_update = gate[:own, :] * cot[:own, :].astype(F32)
+    d_branch_o[...] = (d_update + d_hidden).astype(BF16)
+
+
+def attention_back_kernel(dims, members, where, *refs):
+    rows, ff_rows = dims
+    got_rows, joined_r, exact_r, w, vecs, picked_r, logit, d_hidden, spread = refs[:9]
+    blocks = refs[9 : 9 + members]
+    near_o, far_o, d_joined_o, gain_o = refs[9 + members :]
+    routed, width = picked_r.shape
+    own = routed // members
+    heads = joined_r.shape[1] // (3 * HDIM)
+    d_branch = jnp.concatenate([b[...] for b in blocks], 0)
+    d_attended = mm(d_branch, line_rows(got_rows, ff_rows, rows), NT).astype(BF16)
+    joined = joined_r[...]
+    exact = exact_r[...]
+    kept = kept_pairs(where[3], routed, own)
+    grads = [[], [], []]
+    for h in range(heads):
+        queries, keys, values = (
+            joined[:, (t * heads + h) * HDIM : (t * heads + h + 1) * HDIM] for t in range(3)
+        )
+        probs, total = probabilities(queries, keys, kept)
+        d_att = d_attended[:, h * HDIM : (h + 1) * HDIM]
+        d_wide = d_att.astype(F32)
+        delta = jnp.sum(d_wide * exact[:, h * HDIM : (h + 1) * HDIM], 1, keepdims=True)
+        d_scores = (probs / total * (mm(d_att, values, NT) - delta)).astype(BF16)
+        grads[0].append(mm(d_scores, keys) * HDIM ** (-0.5))
+        grads[1].append(mm(d_scores, queries, TN) * HDIM ** (-0.5))
+        grads[2].append(mm(probs.astype(BF16), (d_wide / total).astype(BF16), TN))
+    d_joined = jnp.concatenate(grads[0] + grads[1] + grads[2], 1).astype(BF16)
+    d_joined_o[...] = d_joined
+    d_normed = mm(d_joined, w[...], NT)
+    picked = picked_r[...].astype(F32)
+    inv = inverse_rms(picked)
+    gain_o[...] = (d_normed * picked * inv).astype(BF16)
+    v = d_normed * vecs[0:1, :]
+    d_picked = inv * v - picked * (inv * inv * inv * jnp.mean(v * picked, 1, keepdims=True))
+    d_picked = d_picked + logit[...] * vecs[2:3, :]
+    first = d_picked[:own] + d_hidden[...]
+    d_picked = jnp.concatenate([first, d_picked[own:]], 0).astype(BF16)
+    put_halves(mm(spread[...], d_picked, TN).astype(BF16), near_o, far_o)
+
+
+def grads_kernel(dims, members, normed, d_joined, attended, gain_a, gain_m, picked, logit, *refs):
+    ny, nx, rows = dims
+    blocks, (sums_o,) = refs[:members], refs[members:]
+    cols = d_joined.shape[1]
+    routed, width = normed.shape
+    own = gain_m.shape[0]
+    main = mm(normed[...], d_joined[...], TN).astype(BF16)
+    lanes = lax.broadcasted_iota(jnp.int32, (routed, 128), 1)
+
+    def lane(k, count):
+        return (lanes[:count] == k).astype(F32)
+
+    vec = mm(gain_a[...], lane(0, routed).astype(BF16), TN)
+    vec = vec + mm(gain_m[...], lane(1, own).astype(BF16), TN)
+    high = logit[...].astype(BF16)
+    low = (logit[...] - high.astype(F32)).astype(BF16)
+    vec = vec + mm(picked[...], (lane(2, routed) * high.astype(F32)).astype(BF16), TN)
+    vec = vec + mm(picked[...], (lane(2, routed) * low.astype(F32)).astype(BF16), TN)
+    vec = vec.astype(BF16)
+    out = mm(attended[...], jnp.concatenate([b[...] for b in blocks], 0), TN).astype(BF16)
+    for y in range(ny):
+        for x in range(nx):
+            q = y * nx + x
+            for g in range(members):
+                at = ((y * members + g) * nx + x) * rows
+                sums_o[q, g * rows : (g + 1) * rows, :cols] = main[at : at + rows]
+                sums_o[q, g * rows : (g + 1) * rows, cols:] = vec[at : at + rows]
+            half = width // 2
+            end = members * rows
+            for k in range(2):
+                piece = out[q * rows : (q + 1) * rows, k * half : (k + 1) * half]
+                sums_o[q, end + k * rows : end + (k + 1) * rows, :] = piece
+
+
+def join_slots_kernel(cap, *refs):
+    *terms, rows_o = refs
+    half = len(terms) // 2
+    for k in range(2):
+        total = add_up(terms[k * half : (k + 1) * half]).astype(BF16)
+        for q in range(rows_o.shape[0]):
+            rows_o[q, k * cap : (k + 1) * cap] = total[q * cap : (q + 1) * cap]
+
+
+def place_kernel(cap, got, pick, tokens, cot, out_o, grad_o):
+    for s in range(tokens.shape[0]):
+        hot = pick[s]
+        out_o[s] = (tokens[s].astype(F32) + mm(hot, got[s, :cap], TN)).astype(BF16)
+        grad_o[s] = (cot[s].astype(F32) + mm(hot, got[s, cap:], TN)).astype(BF16)
+
+
+def line_sums_kernel(dims, got, ff, send_o, out_o, down_o):
+    members, rows, ff_rows = dims
+    cols = got.shape[2]
+    wide = ff.shape[1] // 2
+    total = got[0].astype(F32)
+    for q in range(1, got.shape[0]):
+        total = total + got[q].astype(F32)
+    for g in range(members):
+        send_o[g, :, :cols] = total[g * rows : (g + 1) * rows].astype(BF16)
+        half, row = divmod(g * rows, members * rows // 2)
+        at = ff_rows + row
+        send_o[g, :, cols:] = ff[at : at + rows, half * wide : (half + 1) * wide]
+    end = members * rows
+    out_o[...] = jnp.concatenate([total[end : end + rows], total[end + rows :]], 1)
+    down_o[...] = ff[:ff_rows, :].astype(F32)
+
+
+def unpack_kernel(dims, got, qkv_o, up_o, vec_o):
+    ny, members, nx, ff_rows = dims
+    cols = 3 * ny * HDIM
+    for t in range(3):
+        for y in range(ny):
+            from_ = (t * ny + y) * HDIM
+            row = [got[g, :, from_ : from_ + HDIM] for g in range(members)]
+            at = (t * HEADS + y * members) * HDIM
+            qkv_o[:, at : at + members * HDIM] = jnp.concatenate(row, 1).astype(F32)
+    for y in range(ny):
+        for g in range(members):
+            for x in range(nx):
+                at = ((y * members + g) * nx + x) * ff_rows
+                from_ = cols + 128 + (y * nx + x) * ff_rows
+                up_o[:, at : at + ff_rows] = got[g, :, from_ : from_ + ff_rows].astype(F32)
+    vec = got[0, :, cols : cols + 128].astype(F32)
+    for g in range(1, members):
+        vec = vec + got[g, :, cols : cols + 128].astype(F32)
+    vec_o[...] = vec
+
+
+def grouped(
+    tokens, chosen, w_qkv, w_out, w_up, w_down, gain_attn, gain_mlp, router, cotangent
+):
+    ny, nc, nz, nx = (lax.axis_size(a) for a in ("y", "c", "z", "x"))
+    y, c, z, x = (lax.axis_index(a) for a in ("y", "c", "z", "x"))
+    seq_count, seg_len, width = tokens.shape
+    cap = seg_len // 4
+    routed = chosen.shape[1]
+    members, lines = nc * nz, ny * nx
+    member, line = c * nz + z, y * nx + x
+    shard = ((y * nc + c) * nz + z) * nx + x
+    rows, ff_rows = w_qkv.shape[0], w_down.shape[0]
+    heads = HEADS // members
+    own = routed // members
+    cols, wide = 3 * heads * HDIM, lines * ff_rows
+    line_axes, group_axes = ("y", "x"), ("c", "z")
+    where = jnp.stack([c, z, line, member, shard]).astype(jnp.int32)
+    chosen_t = chosen.T
+    block = (own, width)
+    halves = [((nz, own, width), BF16)] * 2
+    slot_halves = [((nz, lines * cap, width), BF16)] * 2
+
+    vecs = jnp.pad(jnp.stack([gain_attn, gain_mlp, router], 1), ((0, 0), (0, 125)))
+    (columns,) = local_call(
+        partial(columns_kernel, (ny, members, nx, ff_rows)),
+        [((members, rows, cols + 128 + wide), BF16)],
+        (w_qkv, w_up, vecs),
+    )
+    got_rows = lax.all_gather(jnp.concatenate([w_down, w_out]), line_axes)
+    got_cols = lax.all_to_all(columns, group_axes, 0, 0, tiled=True)
+    got_qkv = got_cols[:, :, : cols + 128]
+    got_qkv = lax.all_to_all(
+        jnp.broadcast_to(got_qkv, (lines,) + got_qkv.shape), line_axes, 0, 0, tiled=True
+    )
+    got_up = lax.all_gather(got_cols[:, :, cols + 128 :], line_axes)
+
+    picked_rows, pick = local_call(
+        partial(pick_kernel, cap),
+        [((seq_count, 2 * cap, width), BF16), ((seq_count, cap, seg_len), BF16)],
+        (where, chosen_t, tokens, cotangent),
+        scalars=1,
+    )
+    (spread,) = local_call(
+        partial(spread_kernel, (ny, nc, nz, nx, seg_len, cap)),
+        [((routed, members * lines * cap), BF16)],
+        (where, chosen, chosen_t),
+        scalars=1,
+    )
+    slots = gather_group(lax.all_to_all(picked_rows, line_axes, 0, 0, tiled=True))
+
+    picked, normed, full_qkv, full_vecs, joined, attended, exact, near, far = local_call(
+        partial(attention_kernel, (ny, nx, rows, cap, ff_rows), members),
+        [
+            ((routed, width), BF16),
+            ((routed, width), BF16),
+            ((width, cols), BF16),
+            ((8, width), F32),
+            ((routed, cols), BF16),
+            ((routed, heads * HDIM), BF16),
+            ((routed, heads * HDIM), F32),
+        ]
+        + halves,
+        (where, spread, got_rows, got_qkv, *slots),
+        flops=1.2e9,
+        scratch=[pltpu.VMEM((width, 128), BF16)],
+        scalars=1,
+    )
+    terms = scatter_group(near, far)
+    cot, gate, d_result, d_active = local_call(
+        partial(update_kernel, (cap, ff_rows), members),
+        [
+            ((routed, width), BF16),
+            ((routed, 1), F32),
+            ((routed, width), BF16),
+            ((routed, wide), F32),
+        ],
+        (spread, got_rows, picked, full_vecs, *slots),
+        flops=8e8,
+    )
+    hidden, normed_own = local_call(
+        partial(hidden_kernel, own), [(block, F32), (block, BF16)], (picked, full_vecs, *terms)
+    )
+    normed_mlp = gather_group(normed_own)
+
+    active, d_upper, near, far = local_call(
+        partial(forward_kernel, (ny, members, nx, rows), members),
+        [((routed, wide), BF16)] * 2 + halves,
+        (got_up, d_active, *normed_mlp),
+        flops=6e8,
+        scratch=[pltpu.VMEM((width, wide), BF16)],
+    )
+    terms = scatter_group(near, far)
+    (ff_part,) = local_call(
+        partial(ff_grads_kernel, (ny, nx, rows, ff_rows), members),
+        [((lines * (ff_rows + members * rows // 2), width), BF16)],
+        (active, d_upper, d_result, *normed_mlp),
+        flops=6e8,
+    )
+    ff_sum = lax.psum_scatter(ff_part, line_axes, tiled=True)
+    logit, up_near, up_far = local_call(
+        partial(result_kernel, (rows, ff_rows)),
+        [((routed, 1), F32)] + slot_halves,
+        (active, attended, got_rows, cot, gate, spread),
+        flops=8e8,
+    )
+    d_branch_own, d_hidden, gain_m = local_call(
+        partial(hidden_back_kernel, own),
+        [(block, BF16), (block, F32), (block, BF16)],
+        (hidden, full_vecs, gate, cot, *terms),
+    )
+    d_branch = gather_group(d_branch_own)
+    update_terms = scatter_group(up_near, up_far)
+
+    near, far, d_joined, gain_a = local_call(
+        partial(attention_back_kernel, (rows, ff_rows), members),
+        slot_halves + [((routed, cols), BF16), ((routed, width), BF16)],
+        (where, got_rows, joined, exact, full_qkv, full_vecs, picked, logit, d_hidden, spread)
+        + tuple(d_branch),
+        flops=1.2e9,
+        scalars=1,
+    )
+    picked_terms = scatter_group(near, far)
+    (part,) = local_call(
+        partial(grads_kernel, (ny, nx, rows), members),
+        [((lines, members * rows + 2 * rows, cols + 128), BF16)],
+        (normed, d_joined, attended, gain_a, gain_m, picked, logit, *d_branch),
+        flops=5e8,
+    )
+    got_part = lax.all_to_all(part, line_axes, 0, 0, tiled=True)
+    (slot_rows,) = local_call(
+        partial(join_slots_kernel, cap),
+        [((lines, 2 * cap, width), BF16)],
+        (*update_terms, *picked_terms),
+    )
+    slot_rows = lax.all_to_all(slot_rows, line_axes, 0, 0, tiled=True)
+    send, grad_out, grad_down = local_call(
+        partial(line_sums_kernel, (members, rows, ff_rows)),
+        [
+            ((members, rows, cols + 128 + wide), BF16),
+            ((rows, width), F32),
+            ((ff_rows, width), F32),
+        ],
+        (got_part, ff_sum),
+    )
+    got = lax.all_to_all(send, group_axes, 0, 0, tiled=True)
+    output, grad_tokens = local_call(
+        partial(place_kernel, cap),
+        [(tokens.shape, BF16), (tokens.shape, BF16)],
+        (slot_rows, pick, tokens, cotangent),
+    )
+    grad_qkv, grad_up, grad_vecs = local_call(
+        partial(unpack_kernel, (ny, members, nx, ff_rows)),
+        [(w_qkv.shape, F32), (w_up.shape, F32), ((rows, 128), F32)],
+        (got,),
+    )
+    return (
+        output,
+        grad_tokens,
+        grad_qkv,
+        grad_out,
+        grad_up,
+        grad_down,
+        grad_vecs[:, 0],
+        grad_vecs[:, 1],
+        grad_vecs[:, 2],
+    )
+
+
+def fits(mesh):
+    head_count, block_count = mesh.devices.shape
+    members = (head_count // 2) * (block_count // 2)
+    power = members & (members - 1) == 0
+    return power and head_count == 4 and HEADS == 2 * members
+
+
 def solution(mesh):
-    in_specs = (
-        P(None, ("head", "blk"), None),
-        P(),
-        P(("head", "blk"), None),
-        P(("head", "blk"), None),
-        P(("head", "blk"), None),
-        P(("head", "blk"), None),
-        P(("head", "blk")),
-        P(("head", "blk")),
-        P(("head", "blk")),
-        P(None, ("head", "blk"), None),
-    )
-    out_specs = (
-        P(None, ("head", "blk"), None),
-        P(None, ("head", "blk"), None),
-        P(("head", "blk"), None),
-        P(("head", "blk"), None),
-        P(("head", "blk"), None),
-        P(("head", "blk"), None),
-        P(("head", "blk")),
-        P(("head", "blk")),
-        P(("head", "blk")),
-    )
-    return jax.shard_map(shards, mesh=mesh, in_specs=in_specs, out_specs=out_specs, check_vma=False)
+    if fits(mesh):
+        head_count, block_count = mesh.devices.shape
+        devices = mesh.devices.reshape(2, head_count // 2, block_count // 2, 2)
+        mesh = jax.sharding.Mesh(devices, ("y", "c", "z", "x"))
+        body, all_axes = grouped, ("y", "c", "z", "x")
+    else:
+        body, all_axes = shards, ("head", "blk")
+    seqs, mats, vecs = P(None, all_axes, None), P(all_axes, None), P(all_axes)
+    in_specs = (seqs, P(), mats, mats, mats, mats, vecs, vecs, vecs, seqs)
+    out_specs = (seqs, seqs, mats, mats, mats, mats, vecs, vecs, vecs)
+    return jax.shard_map(body, mesh=mesh, in_specs=in_specs, out_specs=out_specs, check_vma=False)

time: 1530 us -> 237 us (0.15)
  waiting for transfers between devices: 1060 us -> 74.2 us
  blocking collectives: 240 us -> 31 us
  matrix products: 77 us -> 0 us
  local copies, waits for them, and re-layouts: 103 us -> 43.3 us
  starting transfers between devices: 3.98 us -> 50.8 us
  other arithmetic: 23.7 us -> 2.44 us
  Pallas kernels: 0 us -> 19.3 us
    reduce_scatter x4 -> x1, waiting for transfers between devices: 818 us -> 0.01 us  [grouped(): ff_sum = lax.psum_scatter(ff_part, line_axes, tiled=True)]
    all_gather x7 -> x2, waiting for transfers between devices: 234 us -> 0.01 us  [the longest x1 0.01 us: grouped(): got_rows = lax.all_gather(jnp.concatenate([w_down, w_out]), line_axes)]
    all_gather x4 -> x0, blocking collectives: 129 us -> none  [the longest x1 32.5 us: shards(): piece_delta_low = lax.all_gather(delta_low, 'blk', axis=1, tiled=True)]
    unnamed x2 -> x0, blocking collectives: 80.6 us -> none
    dot_general x20 -> x0, matrix products: 77 us -> none  [the longest x1 8.22 us: shards(): jnp.einsum('scd,sci->di', normed_mlp, d_upper, preferred_element_type=jnp...]
    ppermute x0 -> x37, waiting for transfers between devices: none -> 57.4 us  [the longest x21 52.9 us: send_z(): lax.ppermute(b, 'z', f)]
    gather x23 -> x0, local copies, waits for them, and re-layouts: 45.5 us -> none  [the longest x18 24.8 us: shards(): jnp.searchsorted(chosen_row, bounds, side='left')]
    ppermute x0 -> x37, starting transfers between devices: none -> 34.6 us  [the longest x21 31.6 us: send_z(): lax.ppermute(b, 'z', f)]
  transfers between devices with their start and end apart: 12 -> 44, of which waited for: 8 -> 20; matrix products, arithmetic and copies ran while one was open for 12% -> 1% of each run, Pallas kernels for 0% -> 7%
where the time goes in v2:
time: 237 us; the launch traced here: 235 us
  waiting for transfers between devices  74.2 us (31%)
  starting transfers between devices  50.8 us (21%)
  local copies, waits for them, and re-layouts  43.3 us (18%)
  blocking collectives  31 us (13%)
  Pallas kernels  19.3 us (8%)
  between operations  14.3 us (6%)
  other arithmetic  2.44 us (1%)
    ppermute x21, waiting for transfers between devices, send_z(): lax.ppermute(b, 'z', f)  52.9 us
    unnamed x147, local copies, waits for them, and re-layouts  40.5 us
    ppermute x21, starting transfers between devices, send_z(): lax.ppermute(b, 'z', f)  31.6 us
    all_to_all x1, blocking collectives, grouped(): got_cols = lax.all_to_all(columns, group_axes, 0, 0, tiled=True)  21.3 us
    pallas_call x20, Pallas kernels, local_call(): pl.pallas_call(body, out_shape=shapes, in_specs=[pl.BlockSpec(memory_spac...  19.3 us
    all_to_all x1, waiting for transfers between devices, grouped(): got = lax.all_to_all(send, group_axes, 0, 0, tiled=True)  13.5 us
    all_to_all x1, blocking collectives, grouped(): lax.all_to_all(picked_rows, line_axes, 0, 0, tiled=True)  9.74 us
  transfers between devices with their start and end apart: 44, of which 20 were waited for; matrix products, arithmetic and copies ran while one was open for 1% of the time, Pallas kernels for 7%

profile of v2, /device:TPU:0, one launch (start us, length us, event | category | flops | bytes accessed | tf_op | source)
XLA Modules:
  0.0 235.3 jit_solution(5231242969262056464)
XLA Ops:
  7.2 1.7 pad_maximum_fusion
  11.9 21.3 %all_to_all.30 = bf16[8,32,1024]{2,1,0:T(8,128)(2,1)S(1)} all-to-all(bf16[8,32,1024]{2,1,0:T(8,128)(2,1)S(1)} %shard_map.169), channel_id=1, replica_groups=mesh['y'=2,'c'=2,'z'=4,'x'=2] {'c','z'}, dimensions={0} | all-to-all | bytes 1048576 | tf_op jit(solution)/shard_map/all_to_all | solution.py:737
  35.3 9.7 %all_to_all.31.refs_0_ = bf16[4,32,1024]{2,1,0:T(8,128)(2,1)S(1)} all-to-all(bf16[4,32,1024]{2,1,0:T(8,128)(2,1)S(1)} %get-tuple-element.64), channel_id=1, replica_groups=mesh['y'=2,'c'=2,'z'=4,'x'=2] {'y','x'}, dimensions={0} | all-to-all | bytes 524288 | tf_op jit(solution)/shard_map/all_to_all | solution.py:756
  46.1 3.5 %all-to-all-start.1 = ((bf16[4,8,32,512]{3,2,1,0:T(8,128)(2,1)}), bf16[4,8,32,512]{3,2,1,0:T(8,128)(2,1)S(1)}, u32[]{:S(2)}, u32[]{:S(2)}) async-start(bf16[4,8,32,512]{3,2,1,0:T(8,128)(2,1)} %broadcast_in_dim.3), calls=%async_computation.1 | async-start | bytes 2097152 | tf_op jit(solution)/shard_map/all_to_all | solution.py:739
  49.7 1.4 collective-permute-start
  51.1 2.1 collective-permute-start.1
  54.1 7.6 %collective-permute-done.refs_1_ = bf16[4,32,1024]{2,1,0:T(8,128)(2,1)S(1)} collective-permute-done((bf16[4,32,1024]{2,1,0:T(8,128)(2,1)S(1)}, bf16[4,32,1024]{2,1,0:T(8,128)(2,1)S(1)}, u32[]{:S(2)}, u32[]{:S(2)}) %collective-permute-start) | collective-permute-done | bytes 262176 | tf_op jit(solution)/shard_map/ppermute | solution.py:314
  61.7 10.8 %collective-permute-done.1.refs_2_ = bf16[4,32,1024]{2,1,0:T(8,128)(2,1)S(1)} collective-permute-done((bf16[4,32,1024]{2,1,0:T(8,128)(2,1)S(1)}, bf16[4,32,1024]{2,1,0:T(8,128)(2,1)S(1)}, u32[]{:S(2)}, u32[]{:S(2)}) %collective-permute-start.1) | collective-permute-done | bytes 262176 | tf_op jit(solution)/shard_map/ppermute | solution.py:314
  74.4 1.1 shard_map.170.spread.refs_8_
  78.4 1.3 copy-done
  86.4 2.4 %shard_map.172 = (bf16[256,1024]{1,0:T(8,128)(2,1)S(1)}, bf16[256,1024]{1,0:T(8,128)(2,1)S(1)}, bf16[1024,384]{1,0:T(8,128)(2,1)S(1)}, f32[8,1024]{1,0:T(8,128)S...) custom-call(s32[5]{0:T(128)S(1)} %stack.39.where, ...), custom_call_target="tpu_custom_call" | custom-call | flops 1200000000 | bytes 7503892 | tf_op jit(solution)/shard_map/pallas_call | solution.py:298
  90.4 1.5 collective-permute-done.7.far
  92.0 2.6 %collective-permute-start.10 = (bf16[32,1024]{1,0:T(8,128)(2,1)S(1)}, bf16[32,1024]{1,0:T(8,128)(2,1)S(1)}, u32[]{:S(2)}, u32[]{:S(2)}) collective-permute-start(bf16[32,1024]{1,0:T(8,128)(2,1)S(1)} %get-tuple-element.73), channel_id=1, source_target_pairs={{0,6},{2,4},{4,2},{6,0},{1,7},{3,5},{5,3},{7,1},{8,14},{10,12},{12... | collective-permute-start | bytes 196616 | tf_op jit(solution)/shard_map/ppermute | solution.py:314
  94.5 2.2 collective-permute-start.8
  96.9 1.2 collective-permute-done.10.refs_3_
  98.1 1.4 collective-permute-done.8.refs_1_
  99.5 3.1 %collective-permute-done.9.refs_2_ = bf16[32,1024]{1,0:T(8,128)(2,1)S(1)} collective-permute-done((bf16[32,1024]{1,0:T(8,128)(2,1)S(1)}, bf16[32,1024]{1,0:T(8,128)(2,1)S(1)}, u32[]{:S(2)}, u32[]{:S(2)}) %collective-permute-start.9) | collective-permute-done | bytes 65568 | tf_op jit(solution)/shard_map/ppermute | solution.py:314
  103.4 2.7 %collective-permute-start.12 = (bf16[32,1024]{1,0:T(8,128)(2,1)S(1)}, bf16[32,1024]{1,0:T(8,128)(2,1)S(1)}, u32[]{:S(2)}, u32[]{:S(2)}) collective-permute-start(bf16[32,1024]{1,0:T(8,128)(2,1)S(1)} %get-tuple-element.74.refs_0_), channel_id=1, source_target_pairs={{0,4},{2,6},{4,0},{6,2},{1,5},{3,7},{5,1},{7,3},{8,12},{10,14},{12... | collective-permute-start | bytes 196616 | tf_op jit(solution)/shard_map/ppermute | solution.py:314
  106.1 1.7 collective-permute-start.13
  109.3 2.9 %collective-permute-done.13.refs_3_ = bf16[32,1024]{1,0:T(8,128)(2,1)S(1)} collective-permute-done((bf16[32,1024]{1,0:T(8,128)(2,1)S(1)}, bf16[32,1024]{1,0:T(8,128)(2,1)S(1)}, u32[]{:S(2)}, u32[]{:S(2)}) %collective-permute-start.13) | collective-permute-done | bytes 65568 | tf_op jit(solution)/shard_map/ppermute | solution.py:314
  125.5 1.2 copy-done.61
  130.1 2.0 shard_map.186
  132.7 1.4 collective-permute-done.22.far
  135.2 2.3 collective-permute-start.24
  137.5 2.1 collective-permute-start.25
  139.6 1.1 collective-permute-done.23.refs_1_
  140.7 3.0 %collective-permute-done.24.refs_2_ = bf16[32,1024]{1,0:T(8,128)(2,1)S(1)} collective-permute-done((bf16[32,1024]{1,0:T(8,128)(2,1)S(1)}, bf16[32,1024]{1,0:T(8,128)(2,1)S(1)}, u32[]{:S(2)}, u32[]{:S(2)}) %collective-permute-start.24) | collective-permute-done | bytes 65568 | tf_op jit(solution)/shard_map/ppermute | solution.py:314
  146.7 1.7 collective-permute-start.26
  148.5 1.5 collective-permute-start.27
  150.0 1.2 collective-permute-start.28
  151.7 4.8 %collective-permute-done.27.refs_11_.refs_2_ = bf16[32,1024]{1,0:T(8,128)(2,1)S(1)} collective-permute-done((bf16[32,1024]{1,0:T(8,128)(2,1)S(1)}, bf16[32,1024]{1,0:T(8,128)(2,1)S(1)}, u32[]{:S(2)}, u32[]{:S(2)}) %collective-permute-start.27) | collective-permute-done | bytes 65568 | tf_op jit(solution)/shard_map/ppermute | solution.py:314
  159.5 2.9 %shard_map.181 = (bf16[4,64,1024]{2,1,0:T(8,128)(2,1)S(1)}, bf16[4,64,1024]{2,1,0:T(8,128)(2,1)S(1)}, bf16[256,384]{1,0:T(8,128)(2,1)S(1)}, bf16[256,1024]{1,0:T(8,128)(2,1)S(1)}) custom-call(s32[5]{0:T(128)S(1)} %stack.39.where, bf16[4,160,1024]{2,1,0:T(8,128)(2,1)S(1)} %bitcast.14, bf16[256,384]{1,0:T(8,128)(2,1)S(1)} %copy-done.70, ...), custom_call_target="tpu_custom_call" | custom-call | flops 1200000000 | bytes 5669908 | tf_op jit(solution)/shard_map/pallas_call | solution.py:298
  164.0 2.1 shard_map.185
  166.1 4.2 %all-to-all-start.4 = ((bf16[4,320,512]{2,1,0:T(8,128)(2,1)}), bf16[4,320,512]{2,1,0:T(8,128)(2,1)S(1)}, u32[]{:S(2)}, u32[]{:S(2)}) async-start(bf16[4,320,512]{2,1,0:T(8,128)(2,1)} %shard_map.185), calls=%async_computation.4 | async-start | bytes 2621440 | tf_op jit(solution)/shard_map/all_to_all | solution.py:836
  170.9 1.6 collective-permute-done.18.far
  173.4 1.8 collective-permute-start.20
  175.2 1.8 collective-permute-start.21
  177.2 2.6 %collective-permute-start.35 = (bf16[64,1024]{1,0:T(8,128)(2,1)S(1)}, bf16[64,1024]{1,0:T(8,128)(2,1)S(1)}, u32[]{:S(2)}, u32[]{:S(2)}) collective-permute-start(bf16[64,1024]{1,0:T(8,128)(2,1)S(1)} %get-tuple-element.102), channel_id=1, source_target_pairs={{0,4},{2,6},{4,0},{6,2},{1,5},{3,7},{5,1},{7,3},{8,12},{10,14},{12... | collective-permute-start | bytes 393224 | tf_op jit(solution)/shard_map/ppermute | solution.py:314
  179.8 1.2 collective-permute-done.19.refs_1_
  181.0 1.8 collective-permute-start.36
  182.9 3.5 %collective-permute-done.20.refs_2_ = bf16[64,1024]{1,0:T(8,128)(2,1)S(1)} collective-permute-done((bf16[64,1024]{1,0:T(8,128)(2,1)S(1)}, bf16[64,1024]{1,0:T(8,128)(2,1)S(1)}, u32[]{:S(2)}, u32[]{:S(2)}) %collective-permute-start.20) | collective-permute-done | bytes 131104 | tf_op jit(solution)/shard_map/ppermute | solution.py:314
  186.6 11.0 %collective-permute-done.35.refs_6_ = bf16[64,1024]{1,0:T(8,128)(2,1)S(1)} collective-permute-done((bf16[64,1024]{1,0:T(8,128)(2,1)S(1)}, bf16[64,1024]{1,0:T(8,128)(2,1)S(1)}, u32[]{:S(2)}, u32[]{:S(2)}) %collective-permute-start.35) | collective-permute-done | bytes 131104 | tf_op jit(solution)/shard_map/ppermute | solution.py:314
  198.4 4.2 %all-to-all-start.3 = ((bf16[4,32,1024]{2,1,0:T(8,128)(2,1)}), bf16[4,32,1024]{2,1,0:T(8,128)(2,1)S(1)}, u32[]{:S(2)}, u32[]{:S(2)}) async-start(bf16[4,32,1024]{2,1,0:T(8,128)(2,1)} %shard_map.183), calls=%async_computation.3 | async-start | bytes 524288 | tf_op jit(solution)/shard_map/all_to_all | solution.py:842
  203.7 1.1 shard_map.187
  204.8 3.2 %all-to-all-done.3.got = bf16[4,32,1024]{2,1,0:T(8,128)(2,1)S(1)} async-done(((bf16[4,32,1024]{2,1,0:T(8,128)(2,1)}), bf16[4,32,1024]{2,1,0:T(8,128)(2,1)S(1)}, u32[]{:S(2)}, u32[]{:S(2)}) %all-to-all-start.3) | async-done | bytes 262176 | tf_op jit(solution)/shard_map/all_to_all | solution.py:842
  208.0 4.1 %all-to-all-start.5 = ((bf16[8,32,1024]{2,1,0:T(8,128)(2,1)}), bf16[8,32,1024]{2,1,0:T(8,128)(2,1)S(1)}, u32[]{:S(2)}, u32[]{:S(2)}) async-start(bf16[8,32,1024]{2,1,0:T(8,128)(2,1)} %get-tuple-element.113), calls=%async_computation.6 | async-start | bytes 1048576 | tf_op jit(solution)/shard_map/all_to_all | solution.py:852
  212.1 1.4 shard_map.184
  213.5 13.5 %all-to-all-done.5.got = bf16[8,32,1024]{2,1,0:T(8,128)(2,1)S(1)} async-done(((bf16[8,32,1024]{2,1,0:T(8,128)(2,1)}), bf16[8,32,1024]{2,1,0:T(8,128)(2,1)S(1)}, u32[]{:S(2)}, u32[]{:S(2)}) %all-to-all-start.5) | async-done | bytes 524320 | tf_op jit(solution)/shard_map/all_to_all | solution.py:852
  (220 shorter events, 54.3 us)
Async XLA Ops:
  7.2 71.2 %all-gather.7.cloned.1.call-start = ((), (), s32[]{:S(2)}) async-start(), calls=%async_computation.9 | async-start | bytes 1638400 | tf_op jit(solution)/shard_map/all_gather | solution.py:736
  9.0 109.7 %all-gather.5.cloned.1.call-start = ((), (), s32[]{:S(2)}) async-start(), calls=%async_computation.8 | async-start | bytes 1310720 | tf_op jit(solution)/shard_map/all_gather | solution.py:742
  46.1 32.3 %all-to-all-start.1 = ((bf16[4,8,32,512]{3,2,1,0:T(8,128)(2,1)}), bf16[4,8,32,512]{3,2,1,0:T(8,128)(2,1)S(1)}, u32[]{:S(2)}, u32[]{:S(2)}) async-start(bf16[4,8,32,512]{3,2,1,0:T(8,128)(2,1)} %broadcast_in_dim.3), calls=%async_computation.1 | async-start | bytes 2097152 | tf_op jit(solution)/shard_map/all_to_all | solution.py:739
  49.6 153.0 %reduce-scatter.2.cloned.1.call-start = ((), (), s32[]{:S(2)}) async-start(), calls=%async_computation.7 | async-start | bytes 2621440 | tf_op jit(solution)/shard_map/reduce_scatter | solution.py:806
  49.7 12.0 %collective-permute-start = (bf16[4,32,1024]{2,1,0:T(8,128)(2,1)S(1)}, bf16[4,32,1024]{2,1,0:T(8,128)(2,1)S(1)}, u32[]{:S(2)}, u32[]{:S(2)}) collective-permute-start(bf16[4,32,1024]{2,1,0:T(8,128)(2,1)S(1)} %all_to_all.31.refs_0_), channel_id=1, source_target_pairs={{0,2},{2,0},{4,6},{6,4},{1,3},{3,1},{5,7},{7,5},{8,10},{10,8},{12,... | collective-permute-start | bytes 786440 | tf_op jit(solution)/shard_map/ppermute | solution.py:314
  51.1 21.4 %collective-permute-start.1 = (bf16[4,32,1024]{2,1,0:T(8,128)(2,1)S(1)}, bf16[4,32,1024]{2,1,0:T(8,128)(2,1)S(1)}, u32[]{:S(2)}, u32[]{:S(2)}) collective-permute-start(bf16[4,32,1024]{2,1,0:T(8,128)(2,1)S(1)} %all_to_all.31.refs_0_), channel_id=1, source_target_pairs={{0,4},{2,6},{4,0},{6,2},{1,5},{3,7},{5,1},{7,3},{8,12},{10,14},{12... | collective-permute-start | bytes 786440 | tf_op jit(solution)/shard_map/ppermute | solution.py:314
  53.2 20.0 %collective-permute-start.2 = (bf16[4,32,1024]{2,1,0:T(8,128)(2,1)S(1)}, bf16[4,32,1024]{2,1,0:T(8,128)(2,1)S(1)}, u32[]{:S(2)}, u32[]{:S(2)}) collective-permute-start(bf16[4,32,1024]{2,1,0:T(8,128)(2,1)S(1)} %all_to_all.31.refs_0_), channel_id=1, source_target_pairs={{0,6},{2,4},{4,2},{6,0},{1,7},{3,5},{5,3},{7,1},{8,14},{10,12},{12... | collective-permute-start | bytes 786440 | tf_op jit(solution)/shard_map/ppermute | solution.py:314
  54.1 21.4 %collective-permute-start.3 = (bf16[4,32,1024]{2,1,0:T(8,128)(2,1)S(1)}, bf16[4,32,1024]{2,1,0:T(8,128)(2,1)S(1)}, u32[]{:S(2)}, u32[]{:S(2)}) collective-permute-start(bf16[4,32,1024]{2,1,0:T(8,128)(2,1)S(1)} %all_to_all.31.refs_0_), channel_id=1, source_target_pairs={{0,8},{8,0},{1,9},{9,1},{2,10},{10,2},{3,11},{11,3},{4,12},{12,4},... | collective-permute-start | bytes 786440 | tf_op jit(solution)/shard_map/ppermute | solution.py:318
  61.7 14.5 %collective-permute-start.4 = (bf16[4,32,1024]{2,1,0:T(8,128)(2,1)S(1)}, bf16[4,32,1024]{2,1,0:T(8,128)(2,1)S(1)}, u32[]{:S(2)}, u32[]{:S(2)}) collective-permute-start(bf16[4,32,1024]{2,1,0:T(8,128)(2,1)S(1)} %collective-permute-done.refs_1_), channel_id=1, source_target_pairs={{0,8},{8,0},{1,9},{9,1},{2,10},{10,2},{3,11},{11,3},{4,12},{12,4},... | collective-permute-start | bytes 786440 | tf_op jit(solution)/shard_map/ppermute | solution.py:318
  72.5 4.5 %collective-permute-start.5 = (bf16[4,32,1024]{2,1,0:T(8,128)(2,1)S(1)}, bf16[4,32,1024]{2,1,0:T(8,128)(2,1)S(1)}, u32[]{:S(2)}, u32[]{:S(2)}) collective-permute-start(bf16[4,32,1024]{2,1,0:T(8,128)(2,1)S(1)} %collective-permute-done.1.refs_2_), channel_id=1, source_target_pairs={{0,8},{8,0},{1,9},{9,1},{2,10},{10,2},{3,11},{11,3},{4,12},{12,4},... | collective-permute-start | bytes 786440 | tf_op jit(solution)/shard_map/ppermute | solution.py:318
  73.2 4.5 %collective-permute-start.6 = (bf16[4,32,1024]{2,1,0:T(8,128)(2,1)S(1)}, bf16[4,32,1024]{2,1,0:T(8,128)(2,1)S(1)}, u32[]{:S(2)}, u32[]{:S(2)}) collective-permute-start(bf16[4,32,1024]{2,1,0:T(8,128)(2,1)S(1)} %collective-permute-done.2.refs_3_), channel_id=1, source_target_pairs={{0,8},{8,0},{1,9},{9,1},{2,10},{10,2},{3,11},{11,3},{4,12},{12,4},... | collective-permute-start | bytes 786440 | tf_op jit(solution)/shard_map/ppermute | solution.py:318
  86.4 25.9 %copy-start.12 = (bf16[4,32,1024]{2,1,0:T(8,128)(2,1)S(1)}, bf16[4,32,1024]{2,1,0:T(8,128)(2,1)}, u32[]{:S(2)}) copy-start(bf16[4,32,1024]{2,1,0:T(8,128)(2,1)} %copy-done.10) | copy-start | bytes 786436
  86.4 25.9 %copy-start.15 = (bf16[4,32,1024]{2,1,0:T(8,128)(2,1)S(1)}, bf16[4,32,1024]{2,1,0:T(8,128)(2,1)}, u32[]{:S(2)}) copy-start(bf16[4,32,1024]{2,1,0:T(8,128)(2,1)} %copy-done.13) | copy-start | bytes 786436
  86.4 25.9 %copy-start.20 = (bf16[4,32,1024]{2,1,0:T(8,128)(2,1)S(1)}, bf16[4,32,1024]{2,1,0:T(8,128)(2,1)}, u32[]{:S(2)}) copy-start(bf16[4,32,1024]{2,1,0:T(8,128)(2,1)} %copy-done.18) | copy-start | bytes 786436
  86.4 25.9 %copy-start.23 = (bf16[4,32,1024]{2,1,0:T(8,128)(2,1)S(1)}, bf16[4,32,1024]{2,1,0:T(8,128)(2,1)}, u32[]{:S(2)}) copy-start(bf16[4,32,1024]{2,1,0:T(8,128)(2,1)} %copy-done.21) | copy-start | bytes 786436
  90.4 1.5 collective-permute-start.7
  92.0 6.2 %collective-permute-start.10 = (bf16[32,1024]{1,0:T(8,128)(2,1)S(1)}, bf16[32,1024]{1,0:T(8,128)(2,1)S(1)}, u32[]{:S(2)}, u32[]{:S(2)}) collective-permute-start(bf16[32,1024]{1,0:T(8,128)(2,1)S(1)} %get-tuple-element.73), channel_id=1, source_target_pairs={{0,6},{2,4},{4,2},{6,0},{1,7},{3,5},{5,3},{7,1},{8,14},{10,12},{12... | collective-permute-start | bytes 196616 | tf_op jit(solution)/shard_map/ppermute | solution.py:314
  94.5 5.0 %collective-permute-start.8 = (bf16[32,1024]{1,0:T(8,128)(2,1)S(1)}, bf16[32,1024]{1,0:T(8,128)(2,1)S(1)}, u32[]{:S(2)}, u32[]{:S(2)}) collective-permute-start(bf16[32,1024]{1,0:T(8,128)(2,1)S(1)} %get-tuple-element.71), channel_id=1, source_target_pairs={{0,2},{2,0},{4,6},{6,4},{1,3},{3,1},{5,7},{7,5},{8,10},{10,8},{12,... | collective-permute-start | bytes 196616 | tf_op jit(solution)/shard_map/ppermute | solution.py:314
  96.7 5.9 %collective-permute-start.9 = (bf16[32,1024]{1,0:T(8,128)(2,1)S(1)}, bf16[32,1024]{1,0:T(8,128)(2,1)S(1)}, u32[]{:S(2)}, u32[]{:S(2)}) collective-permute-start(bf16[32,1024]{1,0:T(8,128)(2,1)S(1)} %get-tuple-element.72), channel_id=1, source_target_pairs={{0,4},{2,6},{4,0},{6,2},{1,5},{3,7},{5,1},{7,3},{8,12},{10,14},{12... | collective-permute-start | bytes 196616 | tf_op jit(solution)/shard_map/ppermute | solution.py:314
  103.4 4.5 %collective-permute-start.11 = (bf16[32,1024]{1,0:T(8,128)(2,1)S(1)}, bf16[32,1024]{1,0:T(8,128)(2,1)S(1)}, u32[]{:S(2)}, u32[]{:S(2)}) collective-permute-start(bf16[32,1024]{1,0:T(8,128)(2,1)S(1)} %get-tuple-element.74.refs_0_), channel_id=1, source_target_pairs={{0,2},{2,0},{4,6},{6,4},{1,3},{3,1},{5,7},{7,5},{8,10},{10,8},{12,... | collective-permute-start | bytes 196616 | tf_op jit(solution)/shard_map/ppermute | solution.py:314
  103.4 5.9 %collective-permute-start.12 = (bf16[32,1024]{1,0:T(8,128)(2,1)S(1)}, bf16[32,1024]{1,0:T(8,128)(2,1)S(1)}, u32[]{:S(2)}, u32[]{:S(2)}) collective-permute-start(bf16[32,1024]{1,0:T(8,128)(2,1)S(1)} %get-tuple-element.74.refs_0_), channel_id=1, source_target_pairs={{0,4},{2,6},{4,0},{6,2},{1,5},{3,7},{5,1},{7,3},{8,12},{10,14},{12... | collective-permute-start | bytes 196616 | tf_op jit(solution)/shard_map/ppermute | solution.py:314
  106.1 6.1 %collective-permute-start.13 = (bf16[32,1024]{1,0:T(8,128)(2,1)S(1)}, bf16[32,1024]{1,0:T(8,128)(2,1)S(1)}, u32[]{:S(2)}, u32[]{:S(2)}) collective-permute-start(bf16[32,1024]{1,0:T(8,128)(2,1)S(1)} %get-tuple-element.74.refs_0_), channel_id=1, source_target_pairs={{0,6},{2,4},{4,2},{6,0},{1,7},{3,5},{5,3},{7,1},{8,14},{10,12},{12... | collective-permute-start | bytes 196616 | tf_op jit(solution)/shard_map/ppermute | solution.py:314
  107.8 8.3 %collective-permute-start.14 = (bf16[32,1024]{1,0:T(8,128)(2,1)S(1)}, bf16[32,1024]{1,0:T(8,128)(2,1)S(1)}, u32[]{:S(2)}, u32[]{:S(2)}) collective-permute-start(bf16[32,1024]{1,0:T(8,128)(2,1)S(1)} %get-tuple-element.74.refs_0_), channel_id=1, source_target_pairs={{0,8},{8,0},{1,9},{9,1},{2,10},{10,2},{3,11},{11,3},{4,12},{12,4},... | collective-permute-start | bytes 196616 | tf_op jit(solution)/shard_map/ppermute | solution.py:318
  107.9 8.9 %collective-permute-start.15 = (bf16[32,1024]{1,0:T(8,128)(2,1)S(1)}, bf16[32,1024]{1,0:T(8,128)(2,1)S(1)}, u32[]{:S(2)}, u32[]{:S(2)}) collective-permute-start(bf16[32,1024]{1,0:T(8,128)(2,1)S(1)} %collective-permute-done.11.refs_1_), channel_id=1, source_target_pairs={{0,8},{8,0},{1,9},{9,1},{2,10},{10,2},{3,11},{11,3},{4,12},{12,4},... | collective-permute-start | bytes 196616 | tf_op jit(solution)/shard_map/ppermute | solution.py:318
  109.3 8.1 %collective-permute-start.16 = (bf16[32,1024]{1,0:T(8,128)(2,1)S(1)}, bf16[32,1024]{1,0:T(8,128)(2,1)S(1)}, u32[]{:S(2)}, u32[]{:S(2)}) collective-permute-start(bf16[32,1024]{1,0:T(8,128)(2,1)S(1)} %collective-permute-done.12.refs_2_), channel_id=1, source_target_pairs={{0,8},{8,0},{1,9},{9,1},{2,10},{10,2},{3,11},{11,3},{4,12},{12,4},... | collective-permute-start | bytes 196616 | tf_op jit(solution)/shard_map/ppermute | solution.py:318
  112.2 5.8 %collective-permute-start.17 = (bf16[32,1024]{1,0:T(8,128)(2,1)S(1)}, bf16[32,1024]{1,0:T(8,128)(2,1)S(1)}, u32[]{:S(2)}, u32[]{:S(2)}) collective-permute-start(bf16[32,1024]{1,0:T(8,128)(2,1)S(1)} %collective-permute-done.13.refs_3_), channel_id=1, source_target_pairs={{0,8},{8,0},{1,9},{9,1},{2,10},{10,2},{3,11},{11,3},{4,12},{12,4},... | collective-permute-start | bytes 196616 | tf_op jit(solution)/shard_map/ppermute | solution.py:318
  132.2 1.9 collective-permute-start.22
  135.1 5.6 %collective-permute-start.23 = (bf16[32,1024]{1,0:T(8,128)(2,1)S(1)}, bf16[32,1024]{1,0:T(8,128)(2,1)S(1)}, u32[]{:S(2)}, u32[]{:S(2)}) collective-permute-start(bf16[32,1024]{1,0:T(8,128)(2,1)S(1)} %get-tuple-element.93), channel_id=1, source_target_pairs={{0,2},{2,0},{4,6},{6,4},{1,3},{3,1},{5,7},{7,5},{8,10},{10,8},{12,... | collective-permute-start | bytes 196616 | tf_op jit(solution)/shard_map/ppermute | solution.py:314
  135.2 8.5 %collective-permute-start.24 = (bf16[32,1024]{1,0:T(8,128)(2,1)S(1)}, bf16[32,1024]{1,0:T(8,128)(2,1)S(1)}, u32[]{:S(2)}, u32[]{:S(2)}) collective-permute-start(bf16[32,1024]{1,0:T(8,128)(2,1)S(1)} %get-tuple-element.94), channel_id=1, source_target_pairs={{0,4},{2,6},{4,0},{6,2},{1,5},{3,7},{5,1},{7,3},{8,12},{10,14},{12... | collective-permute-start | bytes 196616 | tf_op jit(solution)/shard_map/ppermute | solution.py:314
  137.5 6.2 %collective-permute-start.25 = (bf16[32,1024]{1,0:T(8,128)(2,1)S(1)}, bf16[32,1024]{1,0:T(8,128)(2,1)S(1)}, u32[]{:S(2)}, u32[]{:S(2)}) collective-permute-start(bf16[32,1024]{1,0:T(8,128)(2,1)S(1)} %get-tuple-element.95), channel_id=1, source_target_pairs={{0,6},{2,4},{4,2},{6,0},{1,7},{3,5},{5,3},{7,1},{8,14},{10,12},{12... | collective-permute-start | bytes 196616 | tf_op jit(solution)/shard_map/ppermute | solution.py:314
  146.7 4.5 %collective-permute-start.26 = (bf16[32,1024]{1,0:T(8,128)(2,1)S(1)}, bf16[32,1024]{1,0:T(8,128)(2,1)S(1)}, u32[]{:S(2)}, u32[]{:S(2)}) collective-permute-start(bf16[32,1024]{1,0:T(8,128)(2,1)S(1)} %get-tuple-element.97.refs_9_.refs_0_), channel_id=1, source_target_pairs={{0,2},{2,0},{4,6},{6,4},{1,3},{3,1},{5,7},{7,5},{8,10},{10,8},{12,... | collective-permute-start | bytes 196616 | tf_op jit(solution)/shard_map/ppermute | solution.py:314
  148.5 8.0 %collective-permute-start.27 = (bf16[32,1024]{1,0:T(8,128)(2,1)S(1)}, bf16[32,1024]{1,0:T(8,128)(2,1)S(1)}, u32[]{:S(2)}, u32[]{:S(2)}) collective-permute-start(bf16[32,1024]{1,0:T(8,128)(2,1)S(1)} %get-tuple-element.97.refs_9_.refs_0_), channel_id=1, source_target_pairs={{0,4},{2,6},{4,0},{6,2},{1,5},{3,7},{5,1},{7,3},{8,12},{10,14},{12... | collective-permute-start | bytes 196616 | tf_op jit(solution)/shard_map/ppermute | solution.py:314
  150.0 6.5 %collective-permute-start.28 = (bf16[32,1024]{1,0:T(8,128)(2,1)S(1)}, bf16[32,1024]{1,0:T(8,128)(2,1)S(1)}, u32[]{:S(2)}, u32[]{:S(2)}) collective-permute-start(bf16[32,1024]{1,0:T(8,128)(2,1)S(1)} %get-tuple-element.97.refs_9_.refs_0_), channel_id=1, source_target_pairs={{0,6},{2,4},{4,2},{6,0},{1,7},{3,5},{5,3},{7,1},{8,14},{10,12},{12... | collective-permute-start | bytes 196616 | tf_op jit(solution)/shard_map/ppermute | solution.py:314
  151.2 8.3 %collective-permute-start.29 = (bf16[32,1024]{1,0:T(8,128)(2,1)S(1)}, bf16[32,1024]{1,0:T(8,128)(2,1)S(1)}, u32[]{:S(2)}, u32[]{:S(2)}) collective-permute-start(bf16[32,1024]{1,0:T(8,128)(2,1)S(1)} %get-tuple-element.97.refs_9_.refs_0_), channel_id=1, source_target_pairs={{0,8},{8,0},{1,9},{9,1},{2,10},{10,2},{3,11},{11,3},{4,12},{12,4},... | collective-permute-start | bytes 196616 | tf_op jit(solution)/shard_map/ppermute | solution.py:318
  151.2 8.3 %collective-permute-start.30 = (bf16[32,1024]{1,0:T(8,128)(2,1)S(1)}, bf16[32,1024]{1,0:T(8,128)(2,1)S(1)}, u32[]{:S(2)}, u32[]{:S(2)}) collective-permute-start(bf16[32,1024]{1,0:T(8,128)(2,1)S(1)} %collective-permute-done.26.refs_10_.refs_1_), channel_id=1, source_target_pairs={{0,8},{8,0},{1,9},{9,1},{2,10},{10,2},{3,11},{11,3},{4,12},{12,4},... | collective-permute-start | bytes 196616 | tf_op jit(solution)/shard_map/ppermute | solution.py:318
  156.5 3.0 %collective-permute-start.31 = (bf16[32,1024]{1,0:T(8,128)(2,1)S(1)}, bf16[32,1024]{1,0:T(8,128)(2,1)S(1)}, u32[]{:S(2)}, u32[]{:S(2)}) collective-permute-start(bf16[32,1024]{1,0:T(8,128)(2,1)S(1)} %collective-permute-done.27.refs_11_.refs_2_), channel_id=1, source_target_pairs={{0,8},{8,0},{1,9},{9,1},{2,10},{10,2},{3,11},{11,3},{4,12},{12,4},... | collective-permute-start | bytes 196616 | tf_op jit(solution)/shard_map/ppermute | solution.py:318
  156.5 3.0 %collective-permute-start.32 = (bf16[32,1024]{1,0:T(8,128)(2,1)S(1)}, bf16[32,1024]{1,0:T(8,128)(2,1)S(1)}, u32[]{:S(2)}, u32[]{:S(2)}) collective-permute-start(bf16[32,1024]{1,0:T(8,128)(2,1)S(1)} %collective-permute-done.28.refs_12_.refs_3_), channel_id=1, source_target_pairs={{0,8},{8,0},{1,9},{9,1},{2,10},{10,2},{3,11},{11,3},{4,12},{12,4},... | collective-permute-start | bytes 196616 | tf_op jit(solution)/shard_map/ppermute | solution.py:318
  166.1 32.3 %all-to-all-start.4 = ((bf16[4,320,512]{2,1,0:T(8,128)(2,1)}), bf16[4,320,512]{2,1,0:T(8,128)(2,1)S(1)}, u32[]{:S(2)}, u32[]{:S(2)}) async-start(bf16[4,320,512]{2,1,0:T(8,128)(2,1)} %shard_map.185), calls=%async_computation.4 | async-start | bytes 2621440 | tf_op jit(solution)/shard_map/all_to_all | solution.py:836
  170.3 2.1 collective-permute-start.18
  170.3 6.7 %collective-permute-start.33 = (bf16[4,64,1024]{2,1,0:T(8,128)(2,1)}, bf16[4,64,1024]{2,1,0:T(8,128)(2,1)S(1)}, u32[]{:S(2)}, u32[]{:S(2)}) collective-permute-start(bf16[4,64,1024]{2,1,0:T(8,128)(2,1)} %copy-done.64), channel_id=1, source_target_pairs={{0,8},{8,0},{1,9},{9,1},{2,10},{10,2},{3,11},{11,3},{4,12},{12,4},... | collective-permute-start | bytes 1572872 | tf_op jit(solution)/shard_map/ppermute | solution.py:318
  172.6 8.4 %collective-permute-start.19 = (bf16[64,1024]{1,0:T(8,128)(2,1)S(1)}, bf16[64,1024]{1,0:T(8,128)(2,1)S(1)}, u32[]{:S(2)}, u32[]{:S(2)}) collective-permute-start(bf16[64,1024]{1,0:T(8,128)(2,1)S(1)} %get-tuple-element.82), channel_id=1, source_target_pairs={{0,2},{2,0},{4,6},{6,4},{1,3},{3,1},{5,7},{7,5},{8,10},{10,8},{12,... | collective-permute-start | bytes 393224 | tf_op jit(solution)/shard_map/ppermute | solution.py:314
  173.4 12.9 %collective-permute-start.20 = (bf16[64,1024]{1,0:T(8,128)(2,1)S(1)}, bf16[64,1024]{1,0:T(8,128)(2,1)S(1)}, u32[]{:S(2)}, u32[]{:S(2)}) collective-permute-start(bf16[64,1024]{1,0:T(8,128)(2,1)S(1)} %get-tuple-element.83), channel_id=1, source_target_pairs={{0,4},{2,6},{4,0},{6,2},{1,5},{3,7},{5,1},{7,3},{8,12},{10,14},{12... | collective-permute-start | bytes 393224 | tf_op jit(solution)/shard_map/ppermute | solution.py:314
  175.2 11.1 %collective-permute-start.21 = (bf16[64,1024]{1,0:T(8,128)(2,1)S(1)}, bf16[64,1024]{1,0:T(8,128)(2,1)S(1)}, u32[]{:S(2)}, u32[]{:S(2)}) collective-permute-start(bf16[64,1024]{1,0:T(8,128)(2,1)S(1)} %get-tuple-element.84), channel_id=1, source_target_pairs={{0,6},{2,4},{4,2},{6,0},{1,7},{3,5},{5,3},{7,1},{8,14},{10,12},{12... | collective-permute-start | bytes 393224 | tf_op jit(solution)/shard_map/ppermute | solution.py:314
  177.2 9.4 %collective-permute-start.34 = (bf16[64,1024]{1,0:T(8,128)(2,1)S(1)}, bf16[64,1024]{1,0:T(8,128)(2,1)S(1)}, u32[]{:S(2)}, u32[]{:S(2)}) collective-permute-start(bf16[64,1024]{1,0:T(8,128)(2,1)S(1)} %get-tuple-element.101), channel_id=1, source_target_pairs={{0,2},{2,0},{4,6},{6,4},{1,3},{3,1},{5,7},{7,5},{8,10},{10,8},{12,... | collective-permute-start | bytes 393224 | tf_op jit(solution)/shard_map/ppermute | solution.py:314
  177.2 20.3 %collective-permute-start.35 = (bf16[64,1024]{1,0:T(8,128)(2,1)S(1)}, bf16[64,1024]{1,0:T(8,128)(2,1)S(1)}, u32[]{:S(2)}, u32[]{:S(2)}) collective-permute-start(bf16[64,1024]{1,0:T(8,128)(2,1)S(1)} %get-tuple-element.102), channel_id=1, source_target_pairs={{0,4},{2,6},{4,0},{6,2},{1,5},{3,7},{5,1},{7,3},{8,12},{10,14},{12... | collective-permute-start | bytes 393224 | tf_op jit(solution)/shard_map/ppermute | solution.py:314
  181.0 16.6 %collective-permute-start.36 = (bf16[64,1024]{1,0:T(8,128)(2,1)S(1)}, bf16[64,1024]{1,0:T(8,128)(2,1)S(1)}, u32[]{:S(2)}, u32[]{:S(2)}) collective-permute-start(bf16[64,1024]{1,0:T(8,128)(2,1)S(1)} %get-tuple-element.103), channel_id=1, source_target_pairs={{0,6},{2,4},{4,2},{6,0},{1,7},{3,5},{5,3},{7,1},{8,14},{10,12},{12... | collective-permute-start | bytes 393224 | tf_op jit(solution)/shard_map/ppermute | solution.py:314
  198.4 9.6 %all-to-all-start.3 = ((bf16[4,32,1024]{2,1,0:T(8,128)(2,1)}), bf16[4,32,1024]{2,1,0:T(8,128)(2,1)S(1)}, u32[]{:S(2)}, u32[]{:S(2)}) async-start(bf16[4,32,1024]{2,1,0:T(8,128)(2,1)} %shard_map.183), calls=%async_computation.3 | async-start | bytes 524288 | tf_op jit(solution)/shard_map/all_to_all | solution.py:842
  208.0 19.0 %all-to-all-start.5 = ((bf16[8,32,1024]{2,1,0:T(8,128)(2,1)}), bf16[8,32,1024]{2,1,0:T(8,128)(2,1)S(1)}, u32[]{:S(2)}, u32[]{:S(2)}) async-start(bf16[8,32,1024]{2,1,0:T(8,128)(2,1)} %get-tuple-element.113), calls=%async_computation.6 | async-start | bytes 1048576 | tf_op jit(solution)/shard_map/all_to_all | solution.py:852
  (69 other events, 324.9 us)
Sparse Core Ops, SparseCore 0:
  10.4 31.6 all-gather.6
  44.5 34.1 all-gather.4
  132.3 35.1 reduce-scatter.1

commit v3 on v2

--- a/solution.py
+++ b/solution.py
@@ -291,19 +291,25 @@
     return lax.dot_general(left, right, dims, preferred_element_type=F32)
 
 
-def local_call(body, outs, args, flops=0, scratch=(), scalars=0):
+def local_call(body, outs, args, flops=0, scratch=(), scalars=0, after=()):
     shapes = [jax.ShapeDtypeStruct(s, d) for s, d in outs]
-    spaces = [pltpu.SMEM] * scalars + [pltpu.VMEM] * (len(args) - scalars)
+    spaces = [pltpu.SMEM] * scalars + [pltpu.VMEM] * (len(args) - scalars) + [pl.ANY] * len(after)
+    count = len(args)
+    args = tuple(args) + tuple(after)
+
+    def run(*refs):
+        body(*refs[:count], *refs[len(args) :])
+
     size = sum(math.prod(a.shape) * a.dtype.itemsize for a in list(args) + shapes)
-    return pl.pallas_call(
-        body,
+    return list(pl.pallas_call(
+        run,
         out_shape=shapes,
         in_specs=[pl.BlockSpec(memory_space=s) for s in spaces],
         out_specs=[pl.BlockSpec(memory_space=pltpu.VMEM)] * len(shapes),
         scratch_shapes=list(scratch),
         compiler_params=pltpu.CompilerParams(vmem_limit_bytes=32 * 2**20),
         cost_estimate=pl.CostEstimate(flops=int(flops), bytes_accessed=size, transcendentals=0),
-    )(*args)
+    )(*args))
 
 
 def flips(count):
@@ -314,12 +320,22 @@
     return [lax.ppermute(b, "z", f) for b, f in zip(blocks, flips(lax.axis_size("z"))[1:])]
 
 
+def send_lines(blocks):
+    count = lax.axis_size("y") * lax.axis_size("x")
+    return [lax.ppermute(b, ("y", "x"), f) for b, f in zip(blocks, flips(count)[1:])]
+
+
+def gather_lines(own):
+    return [own] + send_lines([own] * (lax.axis_size("y") * lax.axis_size("x") - 1))
+
+
 def send_c(block):
     return lax.ppermute(block, "c", flips(2)[1])
 
 
 def gather_group(own):
-    blocks = [own] + send_z([own] * (lax.axis_size("z") - 1))
+    lists = [own] + [list(t) for t in zip(*[send_z([o] * (lax.axis_size("z") - 1)) for o in own])]
+    blocks = [b for one in lists for b in one]
     return blocks + [send_c(b) for b in blocks]
 
 
@@ -332,10 +348,10 @@
             low[k - 1][...] = total.astype(BF16)
 
 
-def scatter_group(near, far):
+def scatter_group(near, far, after=()):
     depth, rows, lanes = near.shape
     outs = [((rows, lanes), F32)] + [((rows, lanes), BF16)] * (depth - 1)
-    mine, *low = local_call(half_sum_kernel, outs, (near, send_c(far)))
+    mine, *low = local_call(half_sum_kernel, outs, (near, send_c(far)), after=after)
     return [mine] + send_z(low)
 
 
@@ -355,9 +371,13 @@
     return blocks
 
 
-def columns_kernel(dims, w_qkv, w_up, vecs, out):
+def columns_kernel(dims, w_qkv, w_up, gain_attn, gain_mlp, router, out, vec_s):
     ny, members, nx, ff_rows = dims
     cols = 3 * ny * HDIM
+    vec_s[...] = jnp.zeros_like(vec_s)
+    for k, vec in enumerate((gain_attn, gain_mlp, router)):
+        vec_s[k : k + 1] = vec[...].astype(F32)
+    vecs = mm(vec_s[...].astype(BF16), eye_rows(), TN).astype(BF16)
     for g in range(members):
         parts = []
         for t in range(3):
@@ -365,7 +385,7 @@
                 at = (t * HEADS + y * members + g) * HDIM
                 parts.append(w_qkv[:, at : at + HDIM])
         out[g, :, :cols] = jnp.concatenate(parts, 1)
-        out[g, :, cols : cols + 128] = vecs[...]
+        out[g, :, cols : cols + 128] = vecs
         for y in range(ny):
             for x in range(nx):
                 at = ((y * members + g) * nx + x) * ff_rows
@@ -373,7 +393,13 @@
                 out[g, :, to : to + ff_rows] = w_up[:, at : at + ff_rows]
 
 
-def pick_kernel(cap, where, chosen_t, tokens, cot, rows, pick):
+def eye_rows():
+    down = lax.broadcasted_iota(jnp.int32, (8, 128), 0)
+    return (down == lax.broadcasted_iota(jnp.int32, (8, 128), 1)).astype(F32).astype(BF16)
+
+
+def pick_kernel(cap, where, chosen_t, tokens, cot, pick, *refs):
+    *outs, rows = refs
     seq_count, seg_len = tokens.shape[:2]
     base = where[4] * seg_len
     places = base + lax.broadcasted_iota(jnp.int32, (chosen_t.shape[0], seg_len), 1)
@@ -386,6 +412,29 @@
         pick[s] = hot
         rows[s, :cap] = mm(hot, tokens[s]).astype(BF16)
         rows[s, cap:] = mm(hot, cot[s]).astype(BF16)
+    for k, out in enumerate(outs):
+        out[...] = rows[where[2] ^ k]
+
+
+def stack_kernel(cap, *refs):
+    *blocks, out = refs
+    for k, block in enumerate(blocks):
+        for j in range(2):
+            to = (j * len(blocks) + k) * cap
+            out[to : to + cap] = block[j * cap : (j + 1) * cap]
+
+
+def relay_kernel(got, w_out, w_down, first, second):
+    members, rows, lanes = got.shape
+    half, width = lanes // 2, w_down.shape[1]
+    for g in range(members):
+        first[g * rows : (g + 1) * rows] = got[g, :, :half]
+        second[g * rows : (g + 1) * rows] = got[g, :, half:]
+    for out, block in ((first, w_out), (second, w_down)):
+        size = block.shape[0]
+        for j in range(2):
+            to = members * rows + j * size
+            out[to : to + size] = block[:, j * (width // 2) : (j + 1) * (width // 2)]
 
 
 def spread_kernel(dims, where, chosen, chosen_t, spread):
@@ -410,7 +459,7 @@
     ox, rest = lax.rem(owner, jnp.int32(nx)), lax.div(owner, jnp.int32(nx))
     oz, rest = lax.rem(rest, jnp.int32(nz)), lax.div(rest, jnp.int32(nz))
     oc, oy = lax.rem(rest, jnp.int32(nc)), lax.div(rest, jnp.int32(nc))
-    cell = ((((oc ^ c) * nz + (oz ^ z)) * ny + oy) * nx + ox) * cap + slot
+    cell = (((oc ^ c) * nz + (oz ^ z)) * (ny * nx) + ((oy * nx + ox) ^ line)) * cap + slot
     own = routed // members
     cells = [cell[b * own : (b + 1) * own] for b in range(members)]
     for b, block in enumerate(xor_order(cells, where[3])):
@@ -438,38 +487,48 @@
     return lax.rsqrt(jnp.mean(values * values, 1, keepdims=True) + epsilon)
 
 
-def line_rows(got, first, count):
-    return jnp.concatenate([got[q, first : first + count] for q in range(got.shape[0])], 0)
-
-
-def natural_rows(got, dims, first, count, out):
+def line_rows(where, blocks, start, out):
+    lines, half = len(blocks), out.shape[1] // 2
+    size = out.shape[0] // lines
+    for k, block in enumerate(blocks):
+        to = pl.ds(pl.multiple_of((where[2] ^ k) * size, size), size)
+        for j in range(2):
+            piece = block[start + j * size : start + (j + 1) * size]
+            out[to, j * half : (j + 1) * half] = piece
+
+
+def natural_rows(where, blocks, dims, first, count, out):
     ny, members, nx, rows = dims
-    for y in range(ny):
+    for k, block in enumerate(blocks):
+        line = where[2] ^ k
+        y, x = lax.div(line, jnp.int32(nx)), lax.rem(line, jnp.int32(nx))
         for g in range(members):
-            for x in range(nx):
-                to = ((y * members + g) * nx + x) * rows
-                out[to : to + rows] = got[y * nx + x, g, :, first : first + count]
-
-
-def attention_kernel(dims, members, where, spread, got_rows, got_qkv, *refs):
-    ny, nx, rows, cap, ff_rows = dims
+            to = pl.multiple_of(((y * members + g) * nx + x) * rows, rows)
+            out[pl.ds(to, rows)] = block[g * rows : (g + 1) * rows, first : first + count]
+
+
+def slot_rows(blocks, first, count):
+    return jnp.concatenate([b[first : first + count] for b in blocks], 0)
+
+
+def attention_kernel(dims, members, where, spread, *refs):
+    ny, nx, rows, cap = dims
+    lines = ny * nx
+    qkv_blocks, refs = refs[:lines], refs[lines:]
     blocks, outs = refs[:members], refs[members:]
-    picked_o, normed_o, w_o, vecs_o, joined_o, att_o, exact_o, near_o, far_o, vec_s = outs
+    picked_o, normed_o, w_o, wo_o, vecs_o, joined_o, att_o, exact_o, near_o, far_o, vec_s = outs
     heads = ny
     cols = 3 * heads * HDIM
     routed, width = picked_o.shape
     own = routed // members
-    spots = jnp.concatenate(
-        [b[q, :cap] for b in blocks for q in range(b.shape[0])], 0
-    )
+    spots = slot_rows(blocks, 0, lines * cap)
     picked_low = mm(spread[...], spots).astype(BF16)
     picked_o[...] = picked_low
     picked = picked_low.astype(F32)
-    natural_rows(got_qkv, (ny, members, nx, rows), 0, cols, w_o)
-    natural_rows(got_qkv, (ny, members, nx, rows), cols, 128, vec_s)
-    eye = lax.broadcasted_iota(jnp.int32, (8, 128), 0)
-    eye = (eye == lax.broadcasted_iota(jnp.int32, (8, 128), 1)).astype(F32).astype(BF16)
-    vecs = mm(eye, vec_s[...], NT)
+    natural_rows(where, qkv_blocks, (ny, members, nx, rows), 0, cols, w_o)
+    natural_rows(where, qkv_blocks, (ny, members, nx, rows), cols, 128, vec_s)
+    line_rows(where, qkv_blocks, members * rows, wo_o)
+    vecs = mm(eye_rows(), vec_s[...], NT)
     vecs_o[...] = vecs
     normed = (picked * inverse_rms(picked) * vecs[0:1]).astype(BF16)
     normed_o[...] = normed
@@ -487,7 +546,7 @@
     exact_o[...] = exact
     attended = exact.astype(BF16)
     att_o[...] = attended
-    branch = mm(attended, line_rows(got_rows, ff_rows, rows)).astype(BF16)
+    branch = mm(attended, wo_o[...]).astype(BF16)
     put_halves(branch, near_o, far_o)
 
 
@@ -498,12 +557,11 @@
         far[k] = values[(depth + k) * own : (depth + k + 1) * own]
 
 
-def update_kernel(dims, members, spread, got_rows, picked, vecs, *refs):
-    cap, ff_rows = dims
-    blocks, (cot_o, gate_o, d_result_o, d_active_o) = refs[:members], refs[members:]
-    spots = jnp.concatenate(
-        [b[q, cap:] for b in blocks for q in range(b.shape[0])], 0
-    )
+def update_kernel(dims, members, where, spread, picked, vecs, *refs):
+    lines, cap, start = dims
+    downs, refs = refs[:lines], refs[lines:]
+    blocks, (cot_o, gate_o, d_result_o, d_active_o, w_o) = refs[:members], refs[members:]
+    spots = slot_rows(blocks, lines * cap, lines * cap)
     cot_low = mm(spread[...], spots).astype(BF16)
     cot_o[...] = cot_low
     logit = jnp.sum(picked[...].astype(F32) * vecs[2:3, :], 1, keepdims=True)
@@ -511,7 +569,8 @@
     gate_o[...] = gate
     d_result = (gate * cot_low.astype(F32)).astype(BF16)
     d_result_o[...] = d_result
-    d_active_o[...] = mm(d_result, line_rows(got_rows, 0, ff_rows), NT)
+    line_rows(where, downs, start, w_o)
+    d_active_o[...] = mm(d_result, w_o[...], NT)
 
 
 def hidden_kernel(own, picked, vecs, *refs):
@@ -521,9 +580,11 @@
     normed_o[...] = (hidden * inverse_rms(hidden) * vecs[1:2, :]).astype(BF16)
 
 
-def forward_kernel(dims, members, got_up, d_active, *refs):
+def forward_kernel(dims, members, where, d_active, *refs):
+    lines = dims[0] * dims[2]
+    ups, refs = refs[:lines], refs[lines:]
     blocks, (active_o, d_upper_o, near_o, far_o, w_s) = refs[:members], refs[members:]
-    natural_rows(got_up, dims, 0, got_up.shape[3], w_s)
+    natural_rows(where, ups, dims, 0, ups[0].shape[1], w_s)
     normed = jnp.concatenate([b[...] for b in blocks], 0)
     upper = mm(normed, w_s[...])
     below = 0.5 * (1.0 + lax.erf(upper * (0.5**0.5)))
@@ -534,30 +595,27 @@
     put_halves(mm(d_upper, w_s[...], NT).astype(BF16), near_o, far_o)
 
 
-def ff_grads_kernel(dims, members, active, d_upper, d_result, *refs):
+def ff_grads_kernel(dims, members, where, active, d_upper, d_result, *refs):
     ny, nx, rows, ff_rows = dims
-    blocks, (sums_o,) = refs[:members], refs[members:]
     lines = ny * nx
+    blocks, sums, (down, up) = refs[:members], refs[members : members + lines], refs[-2:]
     normed = jnp.concatenate([b[...] for b in blocks], 0)
-    down = mm(active[...], d_result[...], TN).astype(BF16)
-    up = mm(normed, d_upper[...], TN).astype(BF16)
+    down[...] = mm(active[...], d_result[...], TN).astype(BF16)
+    up[...] = mm(normed, d_upper[...], TN).astype(BF16)
     wide = up.shape[1]
-    each = ff_rows + members * rows // 2
-    for y in range(ny):
-        for x in range(nx):
-            q = y * nx + x
-            sums_o[q * each : q * each + ff_rows] = down[q * ff_rows : (q + 1) * ff_rows]
-            for g in range(members):
-                at = ((y * members + g) * nx + x) * rows
-                half, row = divmod(g * rows, members * rows // 2)
-                to = q * each + ff_rows + row
-                sums_o[to : to + rows, half * wide : (half + 1) * wide] = up[at : at + rows]
-
-
-def result_kernel(dims, active, attended, got_rows, cot, gate, spread, logit_o, near_o, far_o):
-    rows, ff_rows = dims
-    result = mm(active[...], line_rows(got_rows, 0, ff_rows))
-    combined = result + mm(attended[...], line_rows(got_rows, ff_rows, rows))
+    for k in range(lines):
+        line = where[2] ^ k
+        y, x = lax.div(line, jnp.int32(nx)), lax.rem(line, jnp.int32(nx))
+        sums[k][:ff_rows] = down[pl.ds(pl.multiple_of(line * ff_rows, ff_rows), ff_rows)]
+        for g in range(members):
+            at = pl.multiple_of(((y * members + g) * nx + x) * rows, rows)
+            half, row = divmod(g * rows, members * rows // 2)
+            to = ff_rows + row
+            sums[k][to : to + rows, half * wide : (half + 1) * wide] = up[pl.ds(at, rows)]
+
+
+def result_kernel(active, attended, w_down, w_out, cot, gate, spread, logit_o, near_o, far_o):
+    combined = mm(active[...], w_down[...]) + mm(attended[...], w_out[...])
     logit = jnp.sum(cot[...].astype(F32) * combined, 1, keepdims=True)
     logit_o[...] = logit * gate[...] * (1.0 - gate[...])
     update = (gate[...] * combined).astype(BF16)
@@ -577,16 +635,15 @@
     d_branch_o[...] = (d_update + d_hidden).astype(BF16)
 
 
-def attention_back_kernel(dims, members, where, *refs):
-    rows, ff_rows = dims
-    got_rows, joined_r, exact_r, w, vecs, picked_r, logit, d_hidden, spread = refs[:9]
+def attention_back_kernel(members, where, *refs):
+    w_out, joined_r, exact_r, w, vecs, picked_r, logit, d_hidden, spread = refs[:9]
     blocks = refs[9 : 9 + members]
     near_o, far_o, d_joined_o, gain_o = refs[9 + members :]
     routed, width = picked_r.shape
     own = routed // members
     heads = joined_r.shape[1] // (3 * HDIM)
     d_branch = jnp.concatenate([b[...] for b in blocks], 0)
-    d_attended = mm(d_branch, line_rows(got_rows, ff_rows, rows), NT).astype(BF16)
+    d_attended = mm(d_branch, w_out[...], NT).astype(BF16)
     joined = joined_r[...]
     exact = exact_r[...]
     kept = kept_pairs(where[3], routed, own)
@@ -617,13 +674,15 @@
     put_halves(mm(spread[...], d_picked, TN).astype(BF16), near_o, far_o)
 
 
-def grads_kernel(dims, members, normed, d_joined, attended, gain_a, gain_m, picked, logit, *refs):
+def grads_kernel(dims, members, where, normed, d_joined, attended, gain_a, gain_m, *refs):
     ny, nx, rows = dims
-    blocks, (sums_o,) = refs[:members], refs[members:]
+    lines = ny * nx
+    picked, logit, refs = refs[0], refs[1], refs[2:]
+    blocks, sums, (main, vec_s, out) = refs[:members], refs[members : members + lines], refs[-3:]
     cols = d_joined.shape[1]
     routed, width = normed.shape
     own = gain_m.shape[0]
-    main = mm(normed[...], d_joined[...], TN).astype(BF16)
+    main[...] = mm(normed[...], d_joined[...], TN).astype(BF16)
     lanes = lax.broadcasted_iota(jnp.int32, (routed, 128), 1)
 
     def lane(k, count):
@@ -635,56 +694,66 @@
     low = (logit[...] - high.astype(F32)).astype(BF16)
     vec = vec + mm(picked[...], (lane(2, routed) * high.astype(F32)).astype(BF16), TN)
     vec = vec + mm(picked[...], (lane(2, routed) * low.astype(F32)).astype(BF16), TN)
-    vec = vec.astype(BF16)
-    out = mm(attended[...], jnp.concatenate([b[...] for b in blocks], 0), TN).astype(BF16)
-    for y in range(ny):
-        for x in range(nx):
-            q = y * nx + x
-            for g in range(members):
-                at = ((y * members + g) * nx + x) * rows
-                sums_o[q, g * rows : (g + 1) * rows, :cols] = main[at : at + rows]
-                sums_o[q, g * rows : (g + 1) * rows, cols:] = vec[at : at + rows]
-            half = width // 2
-            end = members * rows
-            for k in range(2):
-                piece = out[q * rows : (q + 1) * rows, k * half : (k + 1) * half]
-                sums_o[q, end + k * rows : end + (k + 1) * rows, :] = piece
-
-
-def join_slots_kernel(cap, *refs):
-    *terms, rows_o = refs
+    vec_s[...] = vec.astype(BF16)
+    out[...] = mm(attended[...], jnp.concatenate([b[...] for b in blocks], 0), TN).astype(BF16)
+    for k in range(lines):
+        line = where[2] ^ k
+        y, x = lax.div(line, jnp.int32(nx)), lax.rem(line, jnp.int32(nx))
+        for g in range(members):
+            at = pl.multiple_of(((y * members + g) * nx + x) * rows, rows)
+            sums[k][g * rows : (g + 1) * rows, :cols] = main[pl.ds(at, rows)]
+            sums[k][g * rows : (g + 1) * rows, cols:] = vec_s[pl.ds(at, rows)]
+        half, end = width // 2, members * rows
+        at = pl.multiple_of(line * rows, rows)
+        for j in range(2):
+            piece = out[pl.ds(at, rows), j * half : (j + 1) * half]
+            sums[k][end + j * rows : end + (j + 1) * rows, :] = piece
+
+
+def join_slots_kernel(cap, lines, *refs):
+    terms, outs = refs[:-lines], refs[-lines:]
     half = len(terms) // 2
-    for k in range(2):
-        total = add_up(terms[k * half : (k + 1) * half]).astype(BF16)
-        for q in range(rows_o.shape[0]):
-            rows_o[q, k * cap : (k + 1) * cap] = total[q * cap : (q + 1) * cap]
-
-
-def place_kernel(cap, got, pick, tokens, cot, out_o, grad_o):
+    for j in range(2):
+        total = add_up(terms[j * half : (j + 1) * half]).astype(BF16)
+        for k in range(lines):
+            outs[k][j * cap : (j + 1) * cap] = total[k * cap : (k + 1) * cap]
+
+
+def place_kernel(cap, lines, where, pick, tokens, cot, *refs):
+    blocks, (out_o, grad_o, got) = refs[:lines], refs[lines:]
+    for k, block in enumerate(blocks):
+        got[where[2] ^ k] = block[...]
     for s in range(tokens.shape[0]):
         hot = pick[s]
         out_o[s] = (tokens[s].astype(F32) + mm(hot, got[s, :cap], TN)).astype(BF16)
         grad_o[s] = (cot[s].astype(F32) + mm(hot, got[s, cap:], TN)).astype(BF16)
 
 
-def line_sums_kernel(dims, got, ff, send_o, out_o, down_o):
+def line_sums_kernel(dims, lines, *refs):
     members, rows, ff_rows = dims
-    cols = got.shape[2]
-    wide = ff.shape[1] // 2
-    total = got[0].astype(F32)
-    for q in range(1, got.shape[0]):
-        total = total + got[q].astype(F32)
+    parts, ffs, (send_o, out_o, down_o) = refs[:lines], refs[lines : 2 * lines], refs[2 * lines :]
+    cols = parts[0].shape[1]
+    wide = ffs[0].shape[1] // 2
+
+    def total(blocks):
+        sums = blocks[0][...].astype(F32)
+        for block in blocks[1:]:
+            sums = sums + block[...].astype(F32)
+        return sums
+
+    main, ff = total(parts), total(ffs)
     for g in range(members):
-        send_o[g, :, :cols] = total[g * rows : (g + 1) * rows].astype(BF16)
+        send_o[g, :, :cols] = main[g * rows : (g + 1) * rows].astype(BF16)
         half, row = divmod(g * rows, members * rows // 2)
         at = ff_rows + row
-        send_o[g, :, cols:] = ff[at : at + rows, half * wide : (half + 1) * wide]
+        piece = ff[at : at + rows, half * wide : (half + 1) * wide]
+        send_o[g, :, cols:] = piece.astype(BF16)
     end = members * rows
-    out_o[...] = jnp.concatenate([total[end : end + rows], total[end + rows :]], 1)
-    down_o[...] = ff[:ff_rows, :].astype(F32)
-
-
-def unpack_kernel(dims, got, qkv_o, up_o, vec_o):
+    out_o[...] = jnp.concatenate([main[end : end + rows], main[end + rows :]], 1)
+    down_o[...] = ff[:ff_rows]
+
+
+def unpack_kernel(dims, got, qkv_o, up_o, *vec_o):
     ny, members, nx, ff_rows = dims
     cols = 3 * ny * HDIM
     for t in range(3):
@@ -702,7 +771,11 @@
     vec = got[0, :, cols : cols + 128].astype(F32)
     for g in range(1, members):
         vec = vec + got[g, :, cols : cols + 128].astype(F32)
-    vec_o[...] = vec
+    high = vec.astype(BF16)
+    low = (vec - high.astype(F32)).astype(BF16)
+    vec = mm(eye_rows(), high, NT) + mm(eye_rows(), low, NT)
+    for k, out in enumerate(vec_o):
+        out[...] = vec[k : k + 1]
 
 
 def grouped(
@@ -720,94 +793,108 @@
     heads = HEADS // members
     own = routed // members
     cols, wide = 3 * heads * HDIM, lines * ff_rows
-    line_axes, group_axes = ("y", "x"), ("c", "z")
     where = jnp.stack([c, z, line, member, shard]).astype(jnp.int32)
     chosen_t = chosen.T
     block = (own, width)
+    slot_block = (2 * cap, width)
     halves = [((nz, own, width), BF16)] * 2
     slot_halves = [((nz, lines * cap, width), BF16)] * 2
 
-    vecs = jnp.pad(jnp.stack([gain_attn, gain_mlp, router], 1), ((0, 0), (0, 125)))
-    (columns,) = local_call(
-        partial(columns_kernel, (ny, members, nx, ff_rows)),
-        [((members, rows, cols + 128 + wide), BF16)],
-        (w_qkv, w_up, vecs),
-    )
-    got_rows = lax.all_gather(jnp.concatenate([w_down, w_out]), line_axes)
-    got_cols = lax.all_to_all(columns, group_axes, 0, 0, tiled=True)
-    got_qkv = got_cols[:, :, : cols + 128]
-    got_qkv = lax.all_to_all(
-        jnp.broadcast_to(got_qkv, (lines,) + got_qkv.shape), line_axes, 0, 0, tiled=True
-    )
-    got_up = lax.all_gather(got_cols[:, :, cols + 128 :], line_axes)
-
-    picked_rows, pick = local_call(
+    pick, *picked_rows = local_call(
         partial(pick_kernel, cap),
-        [((seq_count, 2 * cap, width), BF16), ((seq_count, cap, seg_len), BF16)],
+        [((seq_count, cap, seg_len), BF16)] + [(slot_block, BF16)] * lines,
         (where, chosen_t, tokens, cotangent),
+        scratch=[pltpu.VMEM((seq_count, 2 * cap, width), BF16)],
         scalars=1,
     )
+    line_slots = picked_rows[:1] + send_lines(picked_rows[1:])
     (spread,) = local_call(
         partial(spread_kernel, (ny, nc, nz, nx, seg_len, cap)),
         [((routed, members * lines * cap), BF16)],
         (where, chosen, chosen_t),
         scalars=1,
     )
-    slots = gather_group(lax.all_to_all(picked_rows, line_axes, 0, 0, tiled=True))
-
-    picked, normed, full_qkv, full_vecs, joined, attended, exact, near, far = local_call(
-        partial(attention_kernel, (ny, nx, rows, cap, ff_rows), members),
+    (line_slots,) = local_call(
+        partial(stack_kernel, cap), [((lines * 2 * cap, width), BF16)], line_slots
+    )
+    slots = gather_group([line_slots])
+
+    (columns,) = local_call(
+        partial(columns_kernel, (ny, members, nx, ff_rows)),
+        [((members, rows, cols + 128 + wide), BF16)],
+        (w_qkv, w_up) + tuple(v.reshape(1, rows) for v in (gain_attn, gain_mlp, router)),
+        scratch=[pltpu.VMEM((8, rows), F32)],
+    )
+    got_cols = lax.all_to_all(columns, ("c", "z"), 0, 0, tiled=True)
+    first, second = local_call(
+        relay_kernel,
+        [
+            ((members * rows + 2 * rows, width // 2), BF16),
+            ((members * rows + 2 * ff_rows, width // 2), BF16),
+        ],
+        (got_cols, w_out, w_down),
+    )
+    first, second = gather_lines(first), gather_lines(second)
+
+    picked, normed, full_qkv, full_out, full_vecs, joined, attended, exact, near, far = local_call(
+        partial(attention_kernel, (ny, nx, rows, cap), members),
         [
             ((routed, width), BF16),
             ((routed, width), BF16),
             ((width, cols), BF16),
+            ((heads * HDIM, width), BF16),
             ((8, width), F32),
             ((routed, cols), BF16),
             ((routed, heads * HDIM), BF16),
             ((routed, heads * HDIM), F32),
         ]
         + halves,
-        (where, spread, got_rows, got_qkv, *slots),
+        (where, spread, *first, *slots),
         flops=1.2e9,
         scratch=[pltpu.VMEM((width, 128), BF16)],
         scalars=1,
     )
     terms = scatter_group(near, far)
-    cot, gate, d_result, d_active = local_call(
-        partial(update_kernel, (cap, ff_rows), members),
+    cot, gate, d_result, d_active, full_down = local_call(
+        partial(update_kernel, (lines, cap, members * rows), members),
         [
             ((routed, width), BF16),
             ((routed, 1), F32),
             ((routed, width), BF16),
             ((routed, wide), F32),
+            ((wide, width), BF16),
         ],
-        (spread, got_rows, picked, full_vecs, *slots),
+        (where, spread, picked, full_vecs, *second, *slots),
         flops=8e8,
+        scalars=1,
     )
     hidden, normed_own = local_call(
         partial(hidden_kernel, own), [(block, F32), (block, BF16)], (picked, full_vecs, *terms)
     )
-    normed_mlp = gather_group(normed_own)
+    normed_mlp = gather_group([normed_own])
 
     active, d_upper, near, far = local_call(
         partial(forward_kernel, (ny, members, nx, rows), members),
         [((routed, wide), BF16)] * 2 + halves,
-        (got_up, d_active, *normed_mlp),
+        (where, d_active, *second, *normed_mlp),
         flops=6e8,
         scratch=[pltpu.VMEM((width, wide), BF16)],
+        scalars=1,
     )
     terms = scatter_group(near, far)
-    (ff_part,) = local_call(
+    ff_parts = local_call(
         partial(ff_grads_kernel, (ny, nx, rows, ff_rows), members),
-        [((lines * (ff_rows + members * rows // 2), width), BF16)],
-        (active, d_upper, d_result, *normed_mlp),
+        [((ff_rows + members * rows // 2, width), BF16)] * lines,
+        (where, active, d_upper, d_result, *normed_mlp),
         flops=6e8,
-    )
-    ff_sum = lax.psum_scatter(ff_part, line_axes, tiled=True)
+        scratch=[pltpu.VMEM((wide, width), BF16), pltpu.VMEM((width, wide), BF16)],
+        scalars=1,
+    )
+    ff_parts = ff_parts[:1] + send_lines(ff_parts[1:])
     logit, up_near, up_far = local_call(
-        partial(result_kernel, (rows, ff_rows)),
+        result_kernel,
         [((routed, 1), F32)] + slot_halves,
-        (active, attended, got_rows, cot, gate, spread),
+        (active, attended, full_down, full_out, cot, gate, spread),
         flops=8e8,
     )
     d_branch_own, d_hidden, gain_m = local_call(
@@ -815,49 +902,58 @@
         [(block, BF16), (block, F32), (block, BF16)],
         (hidden, full_vecs, gate, cot, *terms),
     )
-    d_branch = gather_group(d_branch_own)
+    d_branch = gather_group([d_branch_own])
     update_terms = scatter_group(up_near, up_far)
 
     near, far, d_joined, gain_a = local_call(
-        partial(attention_back_kernel, (rows, ff_rows), members),
+        partial(attention_back_kernel, members),
         slot_halves + [((routed, cols), BF16), ((routed, width), BF16)],
-        (where, got_rows, joined, exact, full_qkv, full_vecs, picked, logit, d_hidden, spread)
+        (where, full_out, joined, exact, full_qkv, full_vecs, picked, logit, d_hidden, spread)
         + tuple(d_branch),
         flops=1.2e9,
         scalars=1,
     )
-    picked_terms = scatter_group(near, far)
-    (part,) = local_call(
+    picked_terms = scatter_group(near, far, after=update_terms[1:])
+    parts = local_call(
         partial(grads_kernel, (ny, nx, rows), members),
-        [((lines, members * rows + 2 * rows, cols + 128), BF16)],
-        (normed, d_joined, attended, gain_a, gain_m, picked, logit, *d_branch),
+        [((members * rows + 2 * rows, cols + 128), BF16)] * lines,
+        (where, normed, d_joined, attended, gain_a, gain_m, picked, logit, *d_branch),
         flops=5e8,
-    )
-    got_part = lax.all_to_all(part, line_axes, 0, 0, tiled=True)
-    (slot_rows,) = local_call(
-        partial(join_slots_kernel, cap),
-        [((lines, 2 * cap, width), BF16)],
+        scratch=[
+            pltpu.VMEM((width, cols), BF16),
+            pltpu.VMEM((width, 128), BF16),
+            pltpu.VMEM((heads * HDIM, width), BF16),
+        ],
+        scalars=1,
+    )
+    parts = parts[:1] + send_lines(parts[1:])
+    back_rows = local_call(
+        partial(join_slots_kernel, cap, lines),
+        [(slot_block, BF16)] * lines,
         (*update_terms, *picked_terms),
     )
-    slot_rows = lax.all_to_all(slot_rows, line_axes, 0, 0, tiled=True)
+    back_rows = back_rows[:1] + send_lines(back_rows[1:])
     send, grad_out, grad_down = local_call(
-        partial(line_sums_kernel, (members, rows, ff_rows)),
+        partial(line_sums_kernel, (members, rows, ff_rows), lines),
         [
             ((members, rows, cols + 128 + wide), BF16),
             ((rows, width), F32),
             ((ff_rows, width), F32),
         ],
-        (got_part, ff_sum),
-    )
-    got = lax.all_to_all(send, group_axes, 0, 0, tiled=True)
+        (*parts, *ff_parts),
+        after=back_rows[:1],
+    )
+    got = lax.all_to_all(send, ("c", "z"), 0, 0, tiled=True)
     output, grad_tokens = local_call(
-        partial(place_kernel, cap),
+        partial(place_kernel, cap, lines),
         [(tokens.shape, BF16), (tokens.shape, BF16)],
-        (slot_rows, pick, tokens, cotangent),
-    )
-    grad_qkv, grad_up, grad_vecs = local_call(
+        (where, pick, tokens, cotangent, *back_rows),
+        scratch=[pltpu.VMEM((seq_count, 2 * cap, width), BF16)],
+        scalars=1,
+    )
+    grad_qkv, grad_up, *grad_vecs = local_call(
         partial(unpack_kernel, (ny, members, nx, ff_rows)),
-        [(w_qkv.shape, F32), (w_up.shape, F32), ((rows, 128), F32)],
+        [(w_qkv.shape, F32), (w_up.shape, F32)] + [((1, rows), F32)] * 3,
         (got,),
     )
     return (
@@ -867,9 +963,7 @@
         grad_out,
         grad_up,
         grad_down,
-        grad_vecs[:, 0],
-        grad_vecs[:, 1],
-        grad_vecs[:, 2],
+        *(v.reshape(rows) for v in grad_vecs),
     )
 
 

time: 237 us -> 182 us (0.77)
  local copies, waits for them, and re-layouts: 43.3 us -> 4.89 us
  blocking collectives: 31 us -> 0 us
  waiting for transfers between devices: 74.2 us -> 93.1 us
  between operations: 14.3 us -> 0.98 us
  starting transfers between devices: 50.8 us -> 61.6 us
  other arithmetic: 2.44 us -> 0 us
    unnamed x147 -> x25, local copies, waits for them, and re-layouts: 40.5 us -> 4.8 us
    all_to_all x2 -> x0, blocking collectives: 31 us -> none  [the longest x1 21.3 us: grouped(): got_cols = lax.all_to_all(columns, group_axes, 0, 0, tiled=True)]
    ppermute x0 -> x18, waiting for transfers between devices: none -> 28.5 us  [send_lines(): lax.ppermute(b, ('y', 'x'), f)]
    ppermute x0 -> x18, starting transfers between devices: none -> 21.4 us  [send_lines(): lax.ppermute(b, ('y', 'x'), f)]
    all_to_all x4 -> x2, waiting for transfers between devices: 16.7 us -> 6.2 us  [the longest x1 6.2 us: grouped(): got = lax.all_to_all(send, ('c', 'z'), 0, 0, tiled=True)]
    all_to_all x4 -> x2, starting transfers between devices: 16.1 us -> 10.2 us  [the longest x1 6.46 us: grouped(): got_cols = lax.all_to_all(columns, ('c', 'z'), 0, 0, tiled=True)]
    ppermute x21, starting transfers between devices: 31.6 us -> 27 us  [send_z(): lax.ppermute(b, 'z', f)]
    pallas_call x20 -> x22, Pallas kernels: 19.3 us -> 20.6 us  [local_call(): pl.pallas_call(run, out_shape=shapes, in_specs=[pl.BlockSpec(memory_space...]
  transfers between devices with their start and end apart: 44 -> 57, of which waited for: 20 -> 28; matrix products, arithmetic and copies ran while one was open for 1% -> 0% of each run, Pallas kernels for 7% -> 9%
where the time goes in v3:
time: 182 us; the launch traced here: 181 us
  waiting for transfers between devices  93.1 us (51%)
  starting transfers between devices  61.6 us (34%)
  Pallas kernels  20.6 us (11%)
  local copies, waits for them, and re-layouts  4.89 us (3%)
    ppermute x21, waiting for transfers between devices, send_z(): lax.ppermute(b, 'z', f)  54.7 us
    ppermute x18, waiting for transfers between devices, send_lines(): lax.ppermute(b, ('y', 'x'), f)  28.5 us
    ppermute x21, starting transfers between devices, send_z(): lax.ppermute(b, 'z', f)  27 us
    ppermute x18, starting transfers between devices, send_lines(): lax.ppermute(b, ('y', 'x'), f)  21.4 us
    pallas_call x22, Pallas kernels, local_call(): pl.pallas_call(run, out_shape=shapes, in_specs=[pl.BlockSpec(memory_space...  20.6 us
    all_to_all x1, starting transfers between devices, grouped(): got_cols = lax.all_to_all(columns, ('c', 'z'), 0, 0, tiled=True)  6.46 us
    all_to_all x1, waiting for transfers between devices, grouped(): got = lax.all_to_all(send, ('c', 'z'), 0, 0, tiled=True)  6.2 us
    unnamed x25, local copies, waits for them, and re-layouts  4.8 us
  transfers between devices with their start and end apart: 57, of which 28 were waited for; matrix products, arithmetic and copies ran while one was open for 0% of the time, Pallas kernels for 9%

profile of v3, /device:TPU:0, one launch (start us, length us, event | category | flops | bytes accessed | tf_op | source)
XLA Modules:
  0.0 181.2 jit_solution(2067170505681305344)
XLA Ops:
  4.2 6.5 %all-to-all-start = ((bf16[8,32,1024]{2,1,0:T(8,128)(2,1)}), bf16[8,32,1024]{2,1,0:T(8,128)(2,1)S(1)}, u32[]{:S(2)}, u32[]{:S(2)}) async-start(bf16[8,32,1024]{2,1,0:T(8,128)(2,1)} %shard_map.171), calls=%async_computation | async-start | bytes 1048576 | tf_op jit(solution)/shard_map/all_to_all | solution.py:828
  13.3 1.5 collective-permute-start.3
  14.8 1.5 collective-permute-start.4
  19.0 2.4 %collective-permute-done.5.refs_3_ = bf16[32,1024]{1,0:T(8,128)(2,1)S(1)} collective-permute-done((bf16[32,1024]{1,0:T(8,128)(2,1)S(1)}, bf16[32,1024]{1,0:T(8,128)(2,1)S(1)}, u32[]{:S(2)}, u32[]{:S(2)}) %collective-permute-start.5) | collective-permute-done | bytes 65568 | tf_op jit(solution)/shard_map/ppermute | solution.py:325
  21.5 2.1 %collective-permute-start.6 = (bf16[128,1024]{1,0:T(8,128)(2,1)S(1)}, bf16[128,1024]{1,0:T(8,128)(2,1)S(1)}, u32[]{:S(2)}, u32[]{:S(2)}) collective-permute-start(bf16[128,1024]{1,0:T(8,128)(2,1)S(1)} %shard_map.173.refs_6_.refs_8_), channel_id=1, source_target_pairs={{0,2},{2,0},{4,6},{6,4},{1,3},{3,1},{5,7},{7,5},{8,10},{10,8},{12,... | collective-permute-start | bytes 786440 | tf_op jit(solution)/shard_map/ppermute | solution.py:320
  23.6 2.4 %collective-permute-start.7 = (bf16[128,1024]{1,0:T(8,128)(2,1)S(1)}, bf16[128,1024]{1,0:T(8,128)(2,1)S(1)}, u32[]{:S(2)}, u32[]{:S(2)}) collective-permute-start(bf16[128,1024]{1,0:T(8,128)(2,1)S(1)} %shard_map.173.refs_6_.refs_8_), channel_id=1, source_target_pairs={{0,4},{2,6},{4,0},{6,2},{1,5},{3,7},{5,1},{7,3},{8,12},{10,14},{12... | collective-permute-start | bytes 786440 | tf_op jit(solution)/shard_map/ppermute | solution.py:320
  26.0 11.8 %collective-permute-done.6.refs_7_.refs_9_ = bf16[128,1024]{1,0:T(8,128)(2,1)S(1)} collective-permute-done((bf16[128,1024]{1,0:T(8,128)(2,1)S(1)}, bf16[128,1024]{1,0:T(8,128)(2,1)S(1)}, u32[]{:S(2)}, u32[]{:S(2)}) %collective-permute-start.6) | collective-permute-done | bytes 262176 | tf_op jit(solution)/shard_map/ppermute | solution.py:320
  38.7 1.6 collective-permute-start
  40.3 4.6 %collective-permute-done.7.refs_8_.refs_10_ = bf16[128,1024]{1,0:T(8,128)(2,1)S(1)} collective-permute-done((bf16[128,1024]{1,0:T(8,128)(2,1)S(1)}, bf16[128,1024]{1,0:T(8,128)(2,1)S(1)}, u32[]{:S(2)}, u32[]{:S(2)}) %collective-permute-start.7) | collective-permute-done | bytes 262176 | tf_op jit(solution)/shard_map/ppermute | solution.py:320
  45.5 1.5 collective-permute-start.2
  48.5 1.5 collective-permute-start.13
  51.7 1.5 collective-permute-start.15
  53.2 7.9 %collective-permute-done.1.refs_4_ = bf16[320,512]{1,0:T(8,128)(2,1)S(1)} collective-permute-done((bf16[320,512]{1,0:T(8,128)(2,1)S(1)}, bf16[320,512]{1,0:T(8,128)(2,1)S(1)}, u32[]{:S(2)}, u32[]{:S(2)}) %collective-permute-start.1) | collective-permute-done | bytes 327712 | tf_op jit(solution)/shard_map/ppermute | solution.py:325
  61.0 2.4 %shard_map.174 = (bf16[256,1024]{1,0:T(8,128)(2,1)S(1)}, bf16[256,1024]{1,0:T(8,128)(2,1)S(1)}, bf16[1024,384]{1,0:T(8,128)(2,1)S(1)}, bf16[128,1024]{1,0:T(8,12...) custom-call(s32[5]{0:T(128)S(1)} %stack.23.refs_0_, ...), custom_call_target="tpu_custom_call" | custom-call | flops 1200000000 | bytes 6717460 | tf_op jit(solution)/shard_map/pallas_call | solution.py:304
  63.5 1.5 collective-permute-done.16.refs_1_
  65.3 5.2 %collective-permute-done.17.refs_3_ = bf16[32,1024]{1,0:T(8,128)(2,1)S(1)} collective-permute-done((bf16[32,1024]{1,0:T(8,128)(2,1)S(1)}, bf16[32,1024]{1,0:T(8,128)(2,1)S(1)}, u32[]{:S(2)}, u32[]{:S(2)}) %collective-permute-start.17) | collective-permute-done | bytes 65568 | tf_op jit(solution)/shard_map/ppermute | solution.py:320
  70.5 1.3 collective-permute-done.18.refs_4_
  71.8 5.3 %collective-permute-done.19.refs_5_ = bf16[32,1024]{1,0:T(8,128)(2,1)S(1)} collective-permute-done((bf16[32,1024]{1,0:T(8,128)(2,1)S(1)}, bf16[32,1024]{1,0:T(8,128)(2,1)S(1)}, u32[]{:S(2)}, u32[]{:S(2)}) %collective-permute-start.19) | collective-permute-done | bytes 65568 | tf_op jit(solution)/shard_map/ppermute | solution.py:320
  77.4 4.3 %collective-permute-start.22 = (bf16[32,1024]{1,0:T(8,128)(2,1)S(1)}, bf16[32,1024]{1,0:T(8,128)(2,1)S(1)}, u32[]{:S(2)}, u32[]{:S(2)}) collective-permute-start(bf16[32,1024]{1,0:T(8,128)(2,1)S(1)} %get-tuple-element.101.refs_6_.refs_4_), channel_id=1, source_target_pairs={{0,6},{2,4},{4,2},{6,0},{1,7},{3,5},{5,3},{7,1},{8,14},{10,12},{12... | collective-permute-start | bytes 196616 | tf_op jit(solution)/shard_map/ppermute | solution.py:320
  82.5 2.1 %collective-permute-done.22.refs_9_.refs_7_ = bf16[32,1024]{1,0:T(8,128)(2,1)S(1)} collective-permute-done((bf16[32,1024]{1,0:T(8,128)(2,1)S(1)}, bf16[32,1024]{1,0:T(8,128)(2,1)S(1)}, u32[]{:S(2)}, u32[]{:S(2)}) %collective-permute-start.22) | collective-permute-done | bytes 65568 | tf_op jit(solution)/shard_map/ppermute | solution.py:320
  84.6 1.4 shard_map.175
  86.1 1.6 shard_map.178
  89.8 3.4 %collective-permute-start.33 = (bf16[32,1024]{1,0:T(8,128)(2,1)S(1)}, bf16[32,1024]{1,0:T(8,128)(2,1)S(1)}, u32[]{:S(2)}, u32[]{:S(2)}) collective-permute-start(bf16[32,1024]{1,0:T(8,128)(2,1)S(1)} %get-tuple-element.123), channel_id=1, source_target_pairs={{0,4},{2,6},{4,0},{6,2},{1,5},{3,7},{5,1},{7,3},{8,12},{10,14},{12... | collective-permute-start | bytes 196616 | tf_op jit(solution)/shard_map/ppermute | solution.py:320
  93.9 3.4 %collective-permute-done.33.refs_6_ = bf16[32,1024]{1,0:T(8,128)(2,1)S(1)} collective-permute-done((bf16[32,1024]{1,0:T(8,128)(2,1)S(1)}, bf16[32,1024]{1,0:T(8,128)(2,1)S(1)}, u32[]{:S(2)}, u32[]{:S(2)}) %collective-permute-start.33) | collective-permute-done | bytes 65568 | tf_op jit(solution)/shard_map/ppermute | solution.py:320
  97.3 2.0 %collective-permute-done.34.refs_7_ = bf16[32,1024]{1,0:T(8,128)(2,1)S(1)} collective-permute-done((bf16[32,1024]{1,0:T(8,128)(2,1)S(1)}, bf16[32,1024]{1,0:T(8,128)(2,1)S(1)}, u32[]{:S(2)}, u32[]{:S(2)}) %collective-permute-start.34) | collective-permute-done | bytes 65568 | tf_op jit(solution)/shard_map/ppermute | solution.py:320
  100.6 1.6 collective-permute-start.36
  102.1 1.8 collective-permute-start.37
  104.5 4.0 %collective-permute-done.36.refs_12_.refs_10_ = bf16[32,1024]{1,0:T(8,128)(2,1)S(1)} collective-permute-done((bf16[32,1024]{1,0:T(8,128)(2,1)S(1)}, bf16[32,1024]{1,0:T(8,128)(2,1)S(1)}, u32[]{:S(2)}, u32[]{:S(2)}) %collective-permute-start.36) | collective-permute-done | bytes 65568 | tf_op jit(solution)/shard_map/ppermute | solution.py:320
  109.9 2.9 %shard_map.183 = (bf16[4,64,1024]{2,1,0:T(8,128)(2,1)S(1)}, bf16[4,64,1024]{2,1,0:T(8,128)(2,1)S(1)}, bf16[256,384]{1,0:T(8,128)(2,1)S(1)}, bf16[256,1024]{1,0:T(8,128)(2,1)S(1)}) custom-call(s32[5]{0:T(128)S(1)} %stack.23.refs_0_, bf16[128,1024]{1,0:T(8,128)(2,1)S(1)} %get-tuple-element.105.refs_3_.refs_1_, ...), custom_call_target="tpu_custom_call" | custom-call | flops 1200000000 | bytes 4621332 | tf_op jit(solution)/shard_map/pallas_call | solution.py:304
  113.3 1.4 shard_map.188
  114.7 2.3 %collective-permute-start.52 = (bf16[256,1024]{1,0:T(8,128)(2,1)S(1)}, bf16[256,1024]{1,0:T(8,128)(2,1)S(1)}, u32[]{:S(2)}, u32[]{:S(2)}) collective-permute-start(bf16[256,1024]{1,0:T(8,128)(2,1)S(1)} %get-tuple-element.150), channel_id=1, source_target_pairs={{0,1},{1,0},{16,17},{17,16},{2,3},{3,2},{18,19},{19,18},{4,5},{5,4... | collective-permute-start | bytes 1572872 | tf_op jit(solution)/shard_map/ppermute | solution.py:325
  118.0 1.8 %collective-permute-start.29 = (bf16[64,1024]{1,0:T(8,128)(2,1)S(1)}, bf16[64,1024]{1,0:T(8,128)(2,1)S(1)}, u32[]{:S(2)}, u32[]{:S(2)}) collective-permute-start(bf16[64,1024]{1,0:T(8,128)(2,1)S(1)} %get-tuple-element.112), channel_id=1, source_target_pairs={{0,4},{2,6},{4,0},{6,2},{1,5},{3,7},{5,1},{7,3},{8,12},{10,14},{12... | collective-permute-start | bytes 393224 | tf_op jit(solution)/shard_map/ppermute | solution.py:320
  119.8 1.8 collective-permute-start.30
  121.6 2.7 %collective-permute-done.28.refs_2_.refs_1_ = bf16[64,1024]{1,0:T(8,128)(2,1)S(1)} collective-permute-done((bf16[64,1024]{1,0:T(8,128)(2,1)S(1)}, bf16[64,1024]{1,0:T(8,128)(2,1)S(1)}, u32[]{:S(2)}, u32[]{:S(2)}) %collective-permute-start.28) | collective-permute-done | bytes 131104 | tf_op jit(solution)/shard_map/ppermute | solution.py:320
  125.1 5.7 %collective-permute-done.29.refs_3_.refs_2_ = bf16[64,1024]{1,0:T(8,128)(2,1)S(1)} collective-permute-done((bf16[64,1024]{1,0:T(8,128)(2,1)S(1)}, bf16[64,1024]{1,0:T(8,128)(2,1)S(1)}, u32[]{:S(2)}, u32[]{:S(2)}) %collective-permute-start.29) | collective-permute-done | bytes 131104 | tf_op jit(solution)/shard_map/ppermute | solution.py:320
  132.0 1.4 collective-permute-start.43
  133.4 1.3 collective-permute-start.44
  134.7 1.8 collective-permute-start.45
  136.5 1.9 %shard_map.187 = (bf16[320,512]{1,0:T(8,128)(2,1)S(1)}, bf16[320,512]{1,0:T(8,128)(2,1)S(1)}, bf16[320,512]{1,0:T(8,128)(2,1)S(1)}, bf16[320,512]{1,0:T(8,128)(2,1)S(1)}) custom-call(s32[5]{0:T(128)S(1)} %stack.23.refs_0_, bf16[256,1024]{1,0:T(8,128)(2,1)S(1)} %get-tuple-element.139.refs_1_, bf16[256,384]{1,0:T(8,128)(2,1)S(1)} %get-tuple-element.140.refs_2_, ...), custom_call_target="tpu_custom_call" | custom-call | flops 500000000 | bytes 3736596 | tf_op jit(solution)/shard_map/pallas_call | solution.py:304
  139.7 5.7 %collective-permute-done.44.refs_6_ = bf16[64,1024]{1,0:T(8,128)(2,1)S(1)} collective-permute-done((bf16[64,1024]{1,0:T(8,128)(2,1)S(1)}, bf16[64,1024]{1,0:T(8,128)(2,1)S(1)}, u32[]{:S(2)}, u32[]{:S(2)}) %collective-permute-start.44) | collective-permute-done | bytes 131104 | tf_op jit(solution)/shard_map/ppermute | solution.py:320
  147.6 9.2 %collective-permute-done.53.refs_6_ = bf16[256,1024]{1,0:T(8,128)(2,1)S(1)} collective-permute-done((bf16[256,1024]{1,0:T(8,128)(2,1)S(1)}, bf16[256,1024]{1,0:T(8,128)(2,1)S(1)}, u32[]{:S(2)}, u32[]{:S(2)}) %collective-permute-start.53) | collective-permute-done | bytes 524320 | tf_op jit(solution)/shard_map/ppermute | solution.py:325
  156.8 3.5 %collective-permute-done.50.refs_2_ = bf16[320,512]{1,0:T(8,128)(2,1)S(1)} collective-permute-done((bf16[320,512]{1,0:T(8,128)(2,1)S(1)}, bf16[320,512]{1,0:T(8,128)(2,1)S(1)}, u32[]{:S(2)}, u32[]{:S(2)}) %collective-permute-start.50) | collective-permute-done | bytes 327712 | tf_op jit(solution)/shard_map/ppermute | solution.py:325
  160.3 1.3 shard_map.189
  161.6 3.7 %all-to-all-start.1 = ((bf16[8,32,1024]{2,1,0:T(8,128)(2,1)}), bf16[8,32,1024]{2,1,0:T(8,128)(2,1)S(1)}, u32[]{:S(2)}, u32[]{:S(2)}) async-start(bf16[8,32,1024]{2,1,0:T(8,128)(2,1)} %get-tuple-element.153), calls=%async_computation.1 | async-start | bytes 1048576 | tf_op jit(solution)/shard_map/all_to_all | solution.py:946
  166.9 1.9 %collective-permute-start.48 = (bf16[32,1024]{1,0:T(8,128)(2,1)S(1)}, bf16[32,1024]{1,0:T(8,128)(2,1)S(1)}, u32[]{:S(2)}, u32[]{:S(2)}) collective-permute-start(bf16[32,1024]{1,0:T(8,128)(2,1)S(1)} %get-tuple-element.136), channel_id=1, source_target_pairs={{0,17},{1,16},{16,1},{17,0},{2,19},{3,18},{18,3},{19,2},{4,21},{5,... | collective-permute-start | bytes 196616 | tf_op jit(solution)/shard_map/ppermute | solution.py:325
  170.2 1.8 %collective-permute-done.48.refs_7_ = bf16[32,1024]{1,0:T(8,128)(2,1)S(1)} collective-permute-done((bf16[32,1024]{1,0:T(8,128)(2,1)S(1)}, bf16[32,1024]{1,0:T(8,128)(2,1)S(1)}, u32[]{:S(2)}, u32[]{:S(2)}) %collective-permute-start.48) | collective-permute-done | bytes 65568 | tf_op jit(solution)/shard_map/ppermute | solution.py:325
  172.1 1.9 %shard_map.186 = (bf16[4,64,1024]{2,1,0:T(8,128)(2,1)}, bf16[4,64,1024]{2,1,0:T(8,128)(2,1)}) custom-call(s32[5]{0:T(128)S(1)} %stack.23.refs_0_, bf16[4,16,64]{2,1,0:T(8,128)(2,1)S(1)} %copy-done.7, bf16[4,64,1024]{2,1,0:T(8,128)(2,1)S(1)} %copy-done, bf16[4,64,1024]{2,1,0:T(8,128)(2,1)S(1)} %copy-done.1, ...), custom_call_target="tpu_custom_call" | custom-call | bytes 2367508 | tf_op jit(solution)/shard_map/pallas_call | solution.py:304
  174.0 6.2 %all-to-all-done.1.refs_0_ = bf16[8,32,1024]{2,1,0:T(8,128)(2,1)S(1)} async-done(((bf16[8,32,1024]{2,1,0:T(8,128)(2,1)}), bf16[8,32,1024]{2,1,0:T(8,128)(2,1)S(1)}, u32[]{:S(2)}, u32[]{:S(2)}) %all-to-all-start.1) | async-done | bytes 524320 | tf_op jit(solution)/shard_map/all_to_all | solution.py:946
  (114 shorter events, 32.1 us)
Async XLA Ops:
  4.2 33.6 %all-to-all-start = ((bf16[8,32,1024]{2,1,0:T(8,128)(2,1)}), bf16[8,32,1024]{2,1,0:T(8,128)(2,1)S(1)}, u32[]{:S(2)}, u32[]{:S(2)}) async-start(bf16[8,32,1024]{2,1,0:T(8,128)(2,1)} %shard_map.171), calls=%async_computation | async-start | bytes 1048576 | tf_op jit(solution)/shard_map/all_to_all | solution.py:828
  13.3 4.5 %collective-permute-start.3 = (bf16[32,1024]{1,0:T(8,128)(2,1)S(1)}, bf16[32,1024]{1,0:T(8,128)(2,1)S(1)}, u32[]{:S(2)}, u32[]{:S(2)}) collective-permute-start(bf16[32,1024]{1,0:T(8,128)(2,1)S(1)} %get-tuple-element.88), channel_id=1, source_target_pairs={{0,1},{1,0},{16,17},{17,16},{2,3},{3,2},{18,19},{19,18},{4,5},{5,4... | collective-permute-start | bytes 196616 | tf_op jit(solution)/shard_map/ppermute | solution.py:325
  16.3 5.2 %collective-permute-start.5 = (bf16[32,1024]{1,0:T(8,128)(2,1)S(1)}, bf16[32,1024]{1,0:T(8,128)(2,1)S(1)}, u32[]{:S(2)}, u32[]{:S(2)}) collective-permute-start(bf16[32,1024]{1,0:T(8,128)(2,1)S(1)} %get-tuple-element.90), channel_id=1, source_target_pairs={{0,17},{1,16},{16,1},{17,0},{2,19},{3,18},{18,3},{19,2},{4,21},{5,... | collective-permute-start | bytes 196616 | tf_op jit(solution)/shard_map/ppermute | solution.py:325
  21.5 16.3 %collective-permute-start.6 = (bf16[128,1024]{1,0:T(8,128)(2,1)S(1)}, bf16[128,1024]{1,0:T(8,128)(2,1)S(1)}, u32[]{:S(2)}, u32[]{:S(2)}) collective-permute-start(bf16[128,1024]{1,0:T(8,128)(2,1)S(1)} %shard_map.173.refs_6_.refs_8_), channel_id=1, source_target_pairs={{0,2},{2,0},{4,6},{6,4},{1,3},{3,1},{5,7},{7,5},{8,10},{10,8},{12,... | collective-permute-start | bytes 786440 | tf_op jit(solution)/shard_map/ppermute | solution.py:320
  23.6 21.4 %collective-permute-start.7 = (bf16[128,1024]{1,0:T(8,128)(2,1)S(1)}, bf16[128,1024]{1,0:T(8,128)(2,1)S(1)}, u32[]{:S(2)}, u32[]{:S(2)}) collective-permute-start(bf16[128,1024]{1,0:T(8,128)(2,1)S(1)} %shard_map.173.refs_6_.refs_8_), channel_id=1, source_target_pairs={{0,4},{2,6},{4,0},{6,2},{1,5},{3,7},{5,1},{7,3},{8,12},{10,14},{12... | collective-permute-start | bytes 786440 | tf_op jit(solution)/shard_map/ppermute | solution.py:320
  25.9 19.5 %collective-permute-start.8 = (bf16[128,1024]{1,0:T(8,128)(2,1)S(1)}, bf16[128,1024]{1,0:T(8,128)(2,1)S(1)}, u32[]{:S(2)}, u32[]{:S(2)}) collective-permute-start(bf16[128,1024]{1,0:T(8,128)(2,1)S(1)} %shard_map.173.refs_6_.refs_8_), channel_id=1, source_target_pairs={{0,6},{2,4},{4,2},{6,0},{1,7},{3,5},{5,3},{7,1},{8,14},{10,12},{12... | collective-permute-start | bytes 786440 | tf_op jit(solution)/shard_map/ppermute | solution.py:320
  26.0 20.9 %collective-permute-start.9 = (bf16[128,1024]{1,0:T(8,128)(2,1)S(1)}, bf16[128,1024]{1,0:T(8,128)(2,1)S(1)}, u32[]{:S(2)}, u32[]{:S(2)}) collective-permute-start(bf16[128,1024]{1,0:T(8,128)(2,1)S(1)} %shard_map.173.refs_6_.refs_8_), channel_id=1, source_target_pairs={{0,8},{8,0},{1,9},{9,1},{2,10},{10,2},{3,11},{11,3},{4,12},{12,4},... | collective-permute-start | bytes 786440 | tf_op jit(solution)/shard_map/ppermute | solution.py:333
  37.8 9.2 %collective-permute-start.10 = (bf16[128,1024]{1,0:T(8,128)(2,1)S(1)}, bf16[128,1024]{1,0:T(8,128)(2,1)S(1)}, u32[]{:S(2)}, u32[]{:S(2)}) collective-permute-start(bf16[128,1024]{1,0:T(8,128)(2,1)S(1)} %collective-permute-done.6.refs_7_.refs_9_), channel_id=1, source_target_pairs={{0,8},{8,0},{1,9},{9,1},{2,10},{10,2},{3,11},{11,3},{4,12},{12,4},... | collective-permute-start | bytes 786440 | tf_op jit(solution)/shard_map/ppermute | solution.py:333
  38.7 13.0 %collective-permute-start = (bf16[320,512]{1,0:T(8,128)(2,1)S(1)}, bf16[320,512]{1,0:T(8,128)(2,1)S(1)}, u32[]{:S(2)}, u32[]{:S(2)}) collective-permute-start(bf16[320,512]{1,0:T(8,128)(2,1)S(1)} %get-tuple-element.86.refs_2_), channel_id=1, source_target_pairs={{0,1},{1,0},{16,17},{17,16},{2,3},{3,2},{18,19},{19,18},{4,5},{5,4... | collective-permute-start | bytes 983048 | tf_op jit(solution)/shard_map/ppermute | solution.py:325
  44.9 16.1 %collective-permute-start.1 = (bf16[320,512]{1,0:T(8,128)(2,1)S(1)}, bf16[320,512]{1,0:T(8,128)(2,1)S(1)}, u32[]{:S(2)}, u32[]{:S(2)}) collective-permute-start(bf16[320,512]{1,0:T(8,128)(2,1)S(1)} %get-tuple-element.86.refs_2_), channel_id=1, source_target_pairs={{0,16},{1,17},{16,0},{17,1},{2,18},{3,19},{18,2},{19,3},{4,20},{5,... | collective-permute-start | bytes 983048 | tf_op jit(solution)/shard_map/ppermute | solution.py:325
  45.5 15.6 %collective-permute-start.2 = (bf16[320,512]{1,0:T(8,128)(2,1)S(1)}, bf16[320,512]{1,0:T(8,128)(2,1)S(1)}, u32[]{:S(2)}, u32[]{:S(2)}) collective-permute-start(bf16[320,512]{1,0:T(8,128)(2,1)S(1)} %get-tuple-element.86.refs_2_), channel_id=1, source_target_pairs={{0,17},{1,16},{16,1},{17,0},{2,19},{3,18},{18,3},{19,2},{4,21},{5,... | collective-permute-start | bytes 983048 | tf_op jit(solution)/shard_map/ppermute | solution.py:325
  48.5 28.9 %collective-permute-start.13 = (bf16[512,512]{1,0:T(8,128)(2,1)S(1)}, bf16[512,512]{1,0:T(8,128)(2,1)S(1)}, u32[]{:S(2)}, u32[]{:S(2)}) collective-permute-start(bf16[512,512]{1,0:T(8,128)(2,1)S(1)} %get-tuple-element.93.refs_4_.refs_2_), channel_id=1, source_target_pairs={{0,1},{1,0},{16,17},{17,16},{2,3},{3,2},{18,19},{19,18},{4,5},{5,4... | collective-permute-start | bytes 1572872 | tf_op jit(solution)/shard_map/ppermute | solution.py:325
  51.1 30.6 %collective-permute-start.14 = (bf16[512,512]{1,0:T(8,128)(2,1)S(1)}, bf16[512,512]{1,0:T(8,128)(2,1)S(1)}, u32[]{:S(2)}, u32[]{:S(2)}) collective-permute-start(bf16[512,512]{1,0:T(8,128)(2,1)S(1)} %get-tuple-element.93.refs_4_.refs_2_), channel_id=1, source_target_pairs={{0,16},{1,17},{16,0},{17,1},{2,18},{3,19},{18,2},{19,3},{4,20},{5,... | collective-permute-start | bytes 1572872 | tf_op jit(solution)/shard_map/ppermute | solution.py:325
  51.7 33.0 %collective-permute-start.15 = (bf16[512,512]{1,0:T(8,128)(2,1)S(1)}, bf16[512,512]{1,0:T(8,128)(2,1)S(1)}, u32[]{:S(2)}, u32[]{:S(2)}) collective-permute-start(bf16[512,512]{1,0:T(8,128)(2,1)S(1)} %get-tuple-element.93.refs_4_.refs_2_), channel_id=1, source_target_pairs={{0,17},{1,16},{16,1},{17,0},{2,19},{3,18},{18,3},{19,2},{4,21},{5,... | collective-permute-start | bytes 1572872 | tf_op jit(solution)/shard_map/ppermute | solution.py:325
  65.1 5.4 %collective-permute-start.17 = (bf16[32,1024]{1,0:T(8,128)(2,1)S(1)}, bf16[32,1024]{1,0:T(8,128)(2,1)S(1)}, u32[]{:S(2)}, u32[]{:S(2)}) collective-permute-start(bf16[32,1024]{1,0:T(8,128)(2,1)S(1)} %get-tuple-element.98), channel_id=1, source_target_pairs={{0,2},{2,0},{4,6},{6,4},{1,3},{3,1},{5,7},{7,5},{8,10},{10,8},{12,... | collective-permute-start | bytes 196616 | tf_op jit(solution)/shard_map/ppermute | solution.py:320
  65.2 6.6 %collective-permute-start.18 = (bf16[32,1024]{1,0:T(8,128)(2,1)S(1)}, bf16[32,1024]{1,0:T(8,128)(2,1)S(1)}, u32[]{:S(2)}, u32[]{:S(2)}) collective-permute-start(bf16[32,1024]{1,0:T(8,128)(2,1)S(1)} %get-tuple-element.99), channel_id=1, source_target_pairs={{0,4},{2,6},{4,0},{6,2},{1,5},{3,7},{5,1},{7,3},{8,12},{10,14},{12... | collective-permute-start | bytes 196616 | tf_op jit(solution)/shard_map/ppermute | solution.py:320
  70.5 6.6 %collective-permute-start.19 = (bf16[32,1024]{1,0:T(8,128)(2,1)S(1)}, bf16[32,1024]{1,0:T(8,128)(2,1)S(1)}, u32[]{:S(2)}, u32[]{:S(2)}) collective-permute-start(bf16[32,1024]{1,0:T(8,128)(2,1)S(1)} %get-tuple-element.100), channel_id=1, source_target_pairs={{0,6},{2,4},{4,2},{6,0},{1,7},{3,5},{5,3},{7,1},{8,14},{10,12},{12... | collective-permute-start | bytes 196616 | tf_op jit(solution)/shard_map/ppermute | solution.py:320
  77.2 4.5 %collective-permute-start.20 = (bf16[32,1024]{1,0:T(8,128)(2,1)S(1)}, bf16[32,1024]{1,0:T(8,128)(2,1)S(1)}, u32[]{:S(2)}, u32[]{:S(2)}) collective-permute-start(bf16[32,1024]{1,0:T(8,128)(2,1)S(1)} %get-tuple-element.101.refs_6_.refs_4_), channel_id=1, source_target_pairs={{0,2},{2,0},{4,6},{6,4},{1,3},{3,1},{5,7},{7,5},{8,10},{10,8},{12,... | collective-permute-start | bytes 196616 | tf_op jit(solution)/shard_map/ppermute | solution.py:320
  77.3 5.2 %collective-permute-start.21 = (bf16[32,1024]{1,0:T(8,128)(2,1)S(1)}, bf16[32,1024]{1,0:T(8,128)(2,1)S(1)}, u32[]{:S(2)}, u32[]{:S(2)}) collective-permute-start(bf16[32,1024]{1,0:T(8,128)(2,1)S(1)} %get-tuple-element.101.refs_6_.refs_4_), channel_id=1, source_target_pairs={{0,4},{2,6},{4,0},{6,2},{1,5},{3,7},{5,1},{7,3},{8,12},{10,14},{12... | collective-permute-start | bytes 196616 | tf_op jit(solution)/shard_map/ppermute | solution.py:320
  77.4 7.2 %collective-permute-start.22 = (bf16[32,1024]{1,0:T(8,128)(2,1)S(1)}, bf16[32,1024]{1,0:T(8,128)(2,1)S(1)}, u32[]{:S(2)}, u32[]{:S(2)}) collective-permute-start(bf16[32,1024]{1,0:T(8,128)(2,1)S(1)} %get-tuple-element.101.refs_6_.refs_4_), channel_id=1, source_target_pairs={{0,6},{2,4},{4,2},{6,0},{1,7},{3,5},{5,3},{7,1},{8,14},{10,12},{12... | collective-permute-start | bytes 196616 | tf_op jit(solution)/shard_map/ppermute | solution.py:320
  81.7 4.3 %collective-permute-start.23 = (bf16[32,1024]{1,0:T(8,128)(2,1)S(1)}, bf16[32,1024]{1,0:T(8,128)(2,1)S(1)}, u32[]{:S(2)}, u32[]{:S(2)}) collective-permute-start(bf16[32,1024]{1,0:T(8,128)(2,1)S(1)} %get-tuple-element.101.refs_6_.refs_4_), channel_id=1, source_target_pairs={{0,8},{8,0},{1,9},{9,1},{2,10},{10,2},{3,11},{11,3},{4,12},{12,4},... | collective-permute-start | bytes 196616 | tf_op jit(solution)/shard_map/ppermute | solution.py:333
  81.7 4.3 %collective-permute-start.24 = (bf16[32,1024]{1,0:T(8,128)(2,1)S(1)}, bf16[32,1024]{1,0:T(8,128)(2,1)S(1)}, u32[]{:S(2)}, u32[]{:S(2)}) collective-permute-start(bf16[32,1024]{1,0:T(8,128)(2,1)S(1)} %collective-permute-done.20.refs_7_.refs_5_), channel_id=1, source_target_pairs={{0,8},{8,0},{1,9},{9,1},{2,10},{10,2},{3,11},{11,3},{4,12},{12,4},... | collective-permute-start | bytes 196616 | tf_op jit(solution)/shard_map/ppermute | solution.py:333
  89.5 4.5 %collective-permute-start.32 = (bf16[32,1024]{1,0:T(8,128)(2,1)S(1)}, bf16[32,1024]{1,0:T(8,128)(2,1)S(1)}, u32[]{:S(2)}, u32[]{:S(2)}) collective-permute-start(bf16[32,1024]{1,0:T(8,128)(2,1)S(1)} %get-tuple-element.122), channel_id=1, source_target_pairs={{0,2},{2,0},{4,6},{6,4},{1,3},{3,1},{5,7},{7,5},{8,10},{10,8},{12,... | collective-permute-start | bytes 196616 | tf_op jit(solution)/shard_map/ppermute | solution.py:320
  89.8 7.5 %collective-permute-start.33 = (bf16[32,1024]{1,0:T(8,128)(2,1)S(1)}, bf16[32,1024]{1,0:T(8,128)(2,1)S(1)}, u32[]{:S(2)}, u32[]{:S(2)}) collective-permute-start(bf16[32,1024]{1,0:T(8,128)(2,1)S(1)} %get-tuple-element.123), channel_id=1, source_target_pairs={{0,4},{2,6},{4,0},{6,2},{1,5},{3,7},{5,1},{7,3},{8,12},{10,14},{12... | collective-permute-start | bytes 196616 | tf_op jit(solution)/shard_map/ppermute | solution.py:320
  93.2 6.1 %collective-permute-start.34 = (bf16[32,1024]{1,0:T(8,128)(2,1)S(1)}, bf16[32,1024]{1,0:T(8,128)(2,1)S(1)}, u32[]{:S(2)}, u32[]{:S(2)}) collective-permute-start(bf16[32,1024]{1,0:T(8,128)(2,1)S(1)} %get-tuple-element.124), channel_id=1, source_target_pairs={{0,6},{2,4},{4,2},{6,0},{1,7},{3,5},{5,3},{7,1},{8,14},{10,12},{12... | collective-permute-start | bytes 196616 | tf_op jit(solution)/shard_map/ppermute | solution.py:320
  99.5 4.7 %collective-permute-start.35 = (bf16[32,1024]{1,0:T(8,128)(2,1)S(1)}, bf16[32,1024]{1,0:T(8,128)(2,1)S(1)}, u32[]{:S(2)}, u32[]{:S(2)}) collective-permute-start(bf16[32,1024]{1,0:T(8,128)(2,1)S(1)} %get-tuple-element.126.refs_10_.refs_8_), channel_id=1, source_target_pairs={{0,2},{2,0},{4,6},{6,4},{1,3},{3,1},{5,7},{7,5},{8,10},{10,8},{12,... | collective-permute-start | bytes 196616 | tf_op jit(solution)/shard_map/ppermute | solution.py:320
  100.6 7.9 %collective-permute-start.36 = (bf16[32,1024]{1,0:T(8,128)(2,1)S(1)}, bf16[32,1024]{1,0:T(8,128)(2,1)S(1)}, u32[]{:S(2)}, u32[]{:S(2)}) collective-permute-start(bf16[32,1024]{1,0:T(8,128)(2,1)S(1)} %get-tuple-element.126.refs_10_.refs_8_), channel_id=1, source_target_pairs={{0,4},{2,6},{4,0},{6,2},{1,5},{3,7},{5,1},{7,3},{8,12},{10,14},{12... | collective-permute-start | bytes 196616 | tf_op jit(solution)/shard_map/ppermute | solution.py:320
  102.1 6.3 %collective-permute-start.37 = (bf16[32,1024]{1,0:T(8,128)(2,1)S(1)}, bf16[32,1024]{1,0:T(8,128)(2,1)S(1)}, u32[]{:S(2)}, u32[]{:S(2)}) collective-permute-start(bf16[32,1024]{1,0:T(8,128)(2,1)S(1)} %get-tuple-element.126.refs_10_.refs_8_), channel_id=1, source_target_pairs={{0,6},{2,4},{4,2},{6,0},{1,7},{3,5},{5,3},{7,1},{8,14},{10,12},{12... | collective-permute-start | bytes 196616 | tf_op jit(solution)/shard_map/ppermute | solution.py:320
  104.0 5.9 %collective-permute-start.38 = (bf16[32,1024]{1,0:T(8,128)(2,1)S(1)}, bf16[32,1024]{1,0:T(8,128)(2,1)S(1)}, u32[]{:S(2)}, u32[]{:S(2)}) collective-permute-start(bf16[32,1024]{1,0:T(8,128)(2,1)S(1)} %get-tuple-element.126.refs_10_.refs_8_), channel_id=1, source_target_pairs={{0,8},{8,0},{1,9},{9,1},{2,10},{10,2},{3,11},{11,3},{4,12},{12,4},... | collective-permute-start | bytes 196616 | tf_op jit(solution)/shard_map/ppermute | solution.py:333
  104.2 5.7 %collective-permute-start.39 = (bf16[32,1024]{1,0:T(8,128)(2,1)S(1)}, bf16[32,1024]{1,0:T(8,128)(2,1)S(1)}, u32[]{:S(2)}, u32[]{:S(2)}) collective-permute-start(bf16[32,1024]{1,0:T(8,128)(2,1)S(1)} %collective-permute-done.35.refs_11_.refs_9_), channel_id=1, source_target_pairs={{0,8},{8,0},{1,9},{9,1},{2,10},{10,2},{3,11},{11,3},{4,12},{12,4},... | collective-permute-start | bytes 196616 | tf_op jit(solution)/shard_map/ppermute | solution.py:333
  109.8 7.2 %collective-permute-start.27 = (bf16[4,64,1024]{2,1,0:T(8,128)(2,1)S(1)}, bf16[4,64,1024]{2,1,0:T(8,128)(2,1)S(1)}, u32[]{:S(2)}, u32[]{:S(2)}) collective-permute-start(bf16[4,64,1024]{2,1,0:T(8,128)(2,1)S(1)} %get-tuple-element.109), channel_id=1, source_target_pairs={{0,8},{8,0},{1,9},{9,1},{2,10},{10,2},{3,11},{11,3},{4,12},{12,4},... | collective-permute-start | bytes 1572872 | tf_op jit(solution)/shard_map/ppermute | solution.py:333
  112.8 19.1 %collective-permute-start.42 = (bf16[4,64,1024]{2,1,0:T(8,128)(2,1)S(1)}, bf16[4,64,1024]{2,1,0:T(8,128)(2,1)S(1)}, u32[]{:S(2)}, u32[]{:S(2)}) collective-permute-start(bf16[4,64,1024]{2,1,0:T(8,128)(2,1)S(1)} %get-tuple-element.128), channel_id=1, source_target_pairs={{0,8},{8,0},{1,9},{9,1},{2,10},{10,2},{3,11},{11,3},{4,12},{12,4},... | collective-permute-start | bytes 1572872 | tf_op jit(solution)/shard_map/ppermute | solution.py:333
  114.7 19.9 %collective-permute-start.52 = (bf16[256,1024]{1,0:T(8,128)(2,1)S(1)}, bf16[256,1024]{1,0:T(8,128)(2,1)S(1)}, u32[]{:S(2)}, u32[]{:S(2)}) collective-permute-start(bf16[256,1024]{1,0:T(8,128)(2,1)S(1)} %get-tuple-element.150), channel_id=1, source_target_pairs={{0,1},{1,0},{16,17},{17,16},{2,3},{3,2},{18,19},{19,18},{4,5},{5,4... | collective-permute-start | bytes 1572872 | tf_op jit(solution)/shard_map/ppermute | solution.py:325
  117.1 7.2 %collective-permute-start.28 = (bf16[64,1024]{1,0:T(8,128)(2,1)S(1)}, bf16[64,1024]{1,0:T(8,128)(2,1)S(1)}, u32[]{:S(2)}, u32[]{:S(2)}) collective-permute-start(bf16[64,1024]{1,0:T(8,128)(2,1)S(1)} %get-tuple-element.111), channel_id=1, source_target_pairs={{0,2},{2,0},{4,6},{6,4},{1,3},{3,1},{5,7},{7,5},{8,10},{10,8},{12,... | collective-permute-start | bytes 393224 | tf_op jit(solution)/shard_map/ppermute | solution.py:320
  118.0 12.9 %collective-permute-start.29 = (bf16[64,1024]{1,0:T(8,128)(2,1)S(1)}, bf16[64,1024]{1,0:T(8,128)(2,1)S(1)}, u32[]{:S(2)}, u32[]{:S(2)}) collective-permute-start(bf16[64,1024]{1,0:T(8,128)(2,1)S(1)} %get-tuple-element.112), channel_id=1, source_target_pairs={{0,4},{2,6},{4,0},{6,2},{1,5},{3,7},{5,1},{7,3},{8,12},{10,14},{12... | collective-permute-start | bytes 393224 | tf_op jit(solution)/shard_map/ppermute | solution.py:320
  119.8 12.1 %collective-permute-start.30 = (bf16[64,1024]{1,0:T(8,128)(2,1)S(1)}, bf16[64,1024]{1,0:T(8,128)(2,1)S(1)}, u32[]{:S(2)}, u32[]{:S(2)}) collective-permute-start(bf16[64,1024]{1,0:T(8,128)(2,1)S(1)} %get-tuple-element.113), channel_id=1, source_target_pairs={{0,6},{2,4},{4,2},{6,0},{1,7},{3,5},{5,3},{7,1},{8,14},{10,12},{12... | collective-permute-start | bytes 393224 | tf_op jit(solution)/shard_map/ppermute | solution.py:320
  124.3 32.5 %collective-permute-start.53 = (bf16[256,1024]{1,0:T(8,128)(2,1)S(1)}, bf16[256,1024]{1,0:T(8,128)(2,1)S(1)}, u32[]{:S(2)}, u32[]{:S(2)}) collective-permute-start(bf16[256,1024]{1,0:T(8,128)(2,1)S(1)} %get-tuple-element.151), channel_id=1, source_target_pairs={{0,16},{1,17},{16,0},{17,1},{2,18},{3,19},{18,2},{19,3},{4,20},{5,... | collective-permute-start | bytes 1572872 | tf_op jit(solution)/shard_map/ppermute | solution.py:325
  130.9 25.9 %collective-permute-start.54 = (bf16[256,1024]{1,0:T(8,128)(2,1)S(1)}, bf16[256,1024]{1,0:T(8,128)(2,1)S(1)}, u32[]{:S(2)}, u32[]{:S(2)}) collective-permute-start(bf16[256,1024]{1,0:T(8,128)(2,1)S(1)} %get-tuple-element.152), channel_id=1, source_target_pairs={{0,17},{1,16},{16,1},{17,0},{2,19},{3,18},{18,3},{19,2},{4,21},{5,... | collective-permute-start | bytes 1572872 | tf_op jit(solution)/shard_map/ppermute | solution.py:325
  132.0 6.6 %collective-permute-start.43 = (bf16[64,1024]{1,0:T(8,128)(2,1)S(1)}, bf16[64,1024]{1,0:T(8,128)(2,1)S(1)}, u32[]{:S(2)}, u32[]{:S(2)}) collective-permute-start(bf16[64,1024]{1,0:T(8,128)(2,1)S(1)} %get-tuple-element.130), channel_id=1, source_target_pairs={{0,2},{2,0},{4,6},{6,4},{1,3},{3,1},{5,7},{7,5},{8,10},{10,8},{12,... | collective-permute-start | bytes 393224 | tf_op jit(solution)/shard_map/ppermute | solution.py:320
  133.4 12.0 %collective-permute-start.44 = (bf16[64,1024]{1,0:T(8,128)(2,1)S(1)}, bf16[64,1024]{1,0:T(8,128)(2,1)S(1)}, u32[]{:S(2)}, u32[]{:S(2)}) collective-permute-start(bf16[64,1024]{1,0:T(8,128)(2,1)S(1)} %get-tuple-element.131), channel_id=1, source_target_pairs={{0,4},{2,6},{4,0},{6,2},{1,5},{3,7},{5,1},{7,3},{8,12},{10,14},{12... | collective-permute-start | bytes 393224 | tf_op jit(solution)/shard_map/ppermute | solution.py:320
  134.7 11.6 %collective-permute-start.45 = (bf16[64,1024]{1,0:T(8,128)(2,1)S(1)}, bf16[64,1024]{1,0:T(8,128)(2,1)S(1)}, u32[]{:S(2)}, u32[]{:S(2)}) collective-permute-start(bf16[64,1024]{1,0:T(8,128)(2,1)S(1)} %get-tuple-element.132), channel_id=1, source_target_pairs={{0,6},{2,4},{4,2},{6,0},{1,7},{3,5},{5,3},{7,1},{8,14},{10,12},{12... | collective-permute-start | bytes 393224 | tf_op jit(solution)/shard_map/ppermute | solution.py:320
  138.6 18.2 %collective-permute-start.49 = (bf16[320,512]{1,0:T(8,128)(2,1)S(1)}, bf16[320,512]{1,0:T(8,128)(2,1)S(1)}, u32[]{:S(2)}, u32[]{:S(2)}) collective-permute-start(bf16[320,512]{1,0:T(8,128)(2,1)S(1)} %get-tuple-element.144), channel_id=1, source_target_pairs={{0,1},{1,0},{16,17},{17,16},{2,3},{3,2},{18,19},{19,18},{4,5},{5,4... | collective-permute-start | bytes 983048 | tf_op jit(solution)/shard_map/ppermute | solution.py:325
  145.4 14.9 %collective-permute-start.50 = (bf16[320,512]{1,0:T(8,128)(2,1)S(1)}, bf16[320,512]{1,0:T(8,128)(2,1)S(1)}, u32[]{:S(2)}, u32[]{:S(2)}) collective-permute-start(bf16[320,512]{1,0:T(8,128)(2,1)S(1)} %get-tuple-element.145), channel_id=1, source_target_pairs={{0,16},{1,17},{16,0},{17,1},{2,18},{3,19},{18,2},{19,3},{4,20},{5,... | collective-permute-start | bytes 983048 | tf_op jit(solution)/shard_map/ppermute | solution.py:325
  146.2 14.1 %collective-permute-start.51 = (bf16[320,512]{1,0:T(8,128)(2,1)S(1)}, bf16[320,512]{1,0:T(8,128)(2,1)S(1)}, u32[]{:S(2)}, u32[]{:S(2)}) collective-permute-start(bf16[320,512]{1,0:T(8,128)(2,1)S(1)} %get-tuple-element.146), channel_id=1, source_target_pairs={{0,17},{1,16},{16,1},{17,0},{2,19},{3,18},{18,3},{19,2},{4,21},{5,... | collective-permute-start | bytes 983048 | tf_op jit(solution)/shard_map/ppermute | solution.py:325
  161.6 18.6 %all-to-all-start.1 = ((bf16[8,32,1024]{2,1,0:T(8,128)(2,1)}), bf16[8,32,1024]{2,1,0:T(8,128)(2,1)S(1)}, u32[]{:S(2)}, u32[]{:S(2)}) async-start(bf16[8,32,1024]{2,1,0:T(8,128)(2,1)} %get-tuple-element.153), calls=%async_computation.1 | async-start | bytes 1048576 | tf_op jit(solution)/shard_map/all_to_all | solution.py:946
  165.3 4.5 %collective-permute-start.46 = (bf16[32,1024]{1,0:T(8,128)(2,1)S(1)}, bf16[32,1024]{1,0:T(8,128)(2,1)S(1)}, u32[]{:S(2)}, u32[]{:S(2)}) collective-permute-start(bf16[32,1024]{1,0:T(8,128)(2,1)S(1)} %get-tuple-element.134), channel_id=1, source_target_pairs={{0,1},{1,0},{16,17},{17,16},{2,3},{3,2},{18,19},{19,18},{4,5},{5,4... | collective-permute-start | bytes 196616 | tf_op jit(solution)/shard_map/ppermute | solution.py:325
  166.0 4.3 %collective-permute-start.47 = (bf16[32,1024]{1,0:T(8,128)(2,1)S(1)}, bf16[32,1024]{1,0:T(8,128)(2,1)S(1)}, u32[]{:S(2)}, u32[]{:S(2)}) collective-permute-start(bf16[32,1024]{1,0:T(8,128)(2,1)S(1)} %get-tuple-element.135), channel_id=1, source_target_pairs={{0,16},{1,17},{16,0},{17,1},{2,18},{3,19},{18,2},{19,3},{4,20},{5,... | collective-permute-start | bytes 196616 | tf_op jit(solution)/shard_map/ppermute | solution.py:325
  166.9 5.2 %collective-permute-start.48 = (bf16[32,1024]{1,0:T(8,128)(2,1)S(1)}, bf16[32,1024]{1,0:T(8,128)(2,1)S(1)}, u32[]{:S(2)}, u32[]{:S(2)}) collective-permute-start(bf16[32,1024]{1,0:T(8,128)(2,1)S(1)} %get-tuple-element.136), channel_id=1, source_target_pairs={{0,17},{1,16},{16,1},{17,0},{2,19},{3,18},{18,3},{19,2},{4,21},{5,... | collective-permute-start | bytes 196616 | tf_op jit(solution)/shard_map/ppermute | solution.py:325
  (21 other events, 68.7 us)

commit v4 on v3

--- a/solution.py
+++ b/solution.py
@@ -291,25 +291,103 @@
     return lax.dot_general(left, right, dims, preferred_element_type=F32)
 
 
+class Far:
+    def __init__(self, item, rows=None, start=0):
+        self.item, self.rows, self.start = item, rows, start
+
+
+class Loaded:
+    def __init__(self, copy, ref):
+        self.copy, self.ref, self.shape, self.waited = copy, ref, ref.shape, False
+
+    def __getitem__(self, index):
+        self.wait()
+        return self.ref[index]
+
+    def wait(self):
+        if not self.waited:
+            self.copy.wait()
+        self.waited = True
+
+
+class Stored:
+    def __init__(self, copy, ref):
+        self.copy, self.ref, self.shape, self.started = copy, ref, ref.shape, False
+
+    def __getitem__(self, index):
+        return self.ref[index]
+
+    def __setitem__(self, index, value):
+        self.ref[index] = value
+        if index is Ellipsis:
+            self.start()
+
+    def start(self):
+        if not self.started:
+            self.copy.start()
+        self.started = True
+
+
 def local_call(body, outs, args, flops=0, scratch=(), scalars=0, after=()):
-    shapes = [jax.ShapeDtypeStruct(s, d) for s, d in outs]
-    spaces = [pltpu.SMEM] * scalars + [pltpu.VMEM] * (len(args) - scalars) + [pl.ANY] * len(after)
-    count = len(args)
-    args = tuple(args) + tuple(after)
+    far_in = [a if isinstance(a, Far) else None for a in args]
+    far_out = [isinstance(o, Far) for o in outs]
+    outs = [o.item if f else o for o, f in zip(outs, far_out)]
+    args = [pltpu.with_memory_space_constraint(f.item, pltpu.HBM) if f else a for a, f in zip(args, far_in)]
+    shapes = [pltpu.HBM(s, d) if f else jax.ShapeDtypeStruct(s, d) for (s, d), f in zip(outs, far_out)]
+    spaces = [pltpu.SMEM] * scalars
+    spaces += [pltpu.HBM if f else pltpu.VMEM for f in far_in[scalars:]]
+    spaces += [pl.ANY] * len(after)
+    stages = []
+    for f in far_in:
+        if f:
+            shape = f.item.shape if f.rows is None else (f.rows,) + f.item.shape[1:]
+            stages.append(pltpu.VMEM(shape, f.item.dtype))
+    stages += [pltpu.VMEM(s, d) for (s, d), f in zip(outs, far_out) if f]
+    n_in, n_out, n_far = len(args), len(outs), len(stages)
+    first_out = n_in + len(after)
+    if n_far:
+        stages.append(pltpu.SemaphoreType.DMA((n_far,)))
 
     def run(*refs):
-        body(*refs[:count], *refs[len(args) :])
-
-    size = sum(math.prod(a.shape) * a.dtype.itemsize for a in list(args) + shapes)
-    return list(pl.pallas_call(
-        run,
-        out_shape=shapes,
-        in_specs=[pl.BlockSpec(memory_space=s) for s in spaces],
-        out_specs=[pl.BlockSpec(memory_space=pltpu.VMEM)] * len(shapes),
-        scratch_shapes=list(scratch),
-        compiler_params=pltpu.CompilerParams(vmem_limit_bytes=32 * 2**20),
-        cost_estimate=pl.CostEstimate(flops=int(flops), bytes_accessed=size, transcendentals=0),
-    )(*args))
+        ins, results = list(refs[:n_in]), list(refs[first_out : first_out + n_out])
+        rest = refs[first_out + n_out :]
+        own, stage = rest[: len(scratch)], rest[len(scratch) :]
+        at, loads, stores = 0, [], []
+        for i, f in enumerate(far_in):
+            if f:
+                source = ins[i] if f.rows is None else ins[i].at[pl.ds(f.start, f.rows)]
+                copy = pltpu.make_async_copy(source, stage[at], stage[-1].at[at])
+                copy.start()
+                ins[i] = Loaded(copy, stage[at])
+                loads.append(ins[i])
+                at += 1
+        for i, f in enumerate(far_out):
+            if f:
+                copy = pltpu.make_async_copy(stage[at], results[i], stage[-1].at[at])
+                results[i] = Stored(copy, stage[at])
+                stores.append(results[i])
+                at += 1
+        body(*ins, *results, *own)
+        for load in loads:
+            load.wait()
+        for store in stores:
+            store.start()
+        for store in stores:
+            store.copy.wait()
+
+    return list(
+        pl.pallas_call(
+            run,
+            out_shape=shapes,
+            in_specs=[pl.BlockSpec(memory_space=s) for s in spaces],
+            out_specs=[
+                pl.BlockSpec(memory_space=pltpu.HBM if f else pltpu.VMEM) for f in far_out
+            ],
+            scratch_shapes=list(scratch) + stages,
+            compiler_params=pltpu.CompilerParams(vmem_limit_bytes=32 * 2**20),
+            cost_estimate=pl.CostEstimate(flops=int(flops), bytes_accessed=0, transcendentals=0),
+        )(*args, *after)
+    )
 
 
 def flips(count):
@@ -346,6 +424,20 @@
             mine[...] = total
         else:
             low[k - 1][...] = total.astype(BF16)
+
+
+def slot_sum_kernel(*refs):
+    pairs, (mine, *low) = refs[:4], refs[4:]
+    size = pairs[0].shape[1]
+    for j in range(2):
+        near, far = pairs[2 * j], pairs[2 * j + 1]
+        rows = slice(j * size, (j + 1) * size)
+        for k in range(near.shape[0]):
+            total = near[k].astype(F32) + far[k].astype(F32)
+            if k == 0:
+                mine[rows] = total
+            else:
+                low[k - 1][rows] = total.astype(BF16)
 
 
 def scatter_group(near, far, after=()):
@@ -426,15 +518,19 @@
 
 def relay_kernel(got, w_out, w_down, first, second):
     members, rows, lanes = got.shape
-    half, width = lanes // 2, w_down.shape[1]
+    half = lanes // 2
+    for line in range(first.shape[0]):
+        for g in range(members):
+            first[line, g * rows : (g + 1) * rows] = got[g, :, :half]
+        for j in range(2):
+            to = (members + j) * rows
+            first[line, to : to + rows] = w_out[:, j * half : (j + 1) * half]
+    size = w_down.shape[0]
     for g in range(members):
-        first[g * rows : (g + 1) * rows] = got[g, :, :half]
         second[g * rows : (g + 1) * rows] = got[g, :, half:]
-    for out, block in ((first, w_out), (second, w_down)):
-        size = block.shape[0]
-        for j in range(2):
-            to = members * rows + j * size
-            out[to : to + size] = block[:, j * (width // 2) : (j + 1) * (width // 2)]
+    for j in range(2):
+        to = members * rows + j * size
+        second[to : to + size] = w_down[:, j * half : (j + 1) * half]
 
 
 def spread_kernel(dims, where, chosen, chosen_t, spread):
@@ -487,9 +583,18 @@
     return lax.rsqrt(jnp.mean(values * values, 1, keepdims=True) + epsilon)
 
 
-def line_rows(where, blocks, start, out):
-    lines, half = len(blocks), out.shape[1] // 2
-    size = out.shape[0] // lines
+def line_rows(blocks, start, out):
+    half = out.shape[1] // 2
+    size = out.shape[0] // blocks.shape[0]
+    for q in range(blocks.shape[0]):
+        for j in range(2):
+            piece = blocks[q, start + j * size : start + (j + 1) * size]
+            out[q * size : (q + 1) * size, j * half : (j + 1) * half] = piece
+
+
+def own_line_rows(where, blocks, start, out):
+    half = out.shape[1] // 2
+    size = out.shape[0] // len(blocks)
     for k, block in enumerate(blocks):
         to = pl.ds(pl.multiple_of((where[2] ^ k) * size, size), size)
         for j in range(2):
@@ -497,37 +602,42 @@
             out[to, j * half : (j + 1) * half] = piece
 
 
-def natural_rows(where, blocks, dims, first, count, out):
+def own_order_rows(where, blocks, dims, out):
     ny, members, nx, rows = dims
     for k, block in enumerate(blocks):
         line = where[2] ^ k
         y, x = lax.div(line, jnp.int32(nx)), lax.rem(line, jnp.int32(nx))
         for g in range(members):
             to = pl.multiple_of(((y * members + g) * nx + x) * rows, rows)
-            out[pl.ds(to, rows)] = block[g * rows : (g + 1) * rows, first : first + count]
-
-
-def slot_rows(blocks, first, count):
-    return jnp.concatenate([b[first : first + count] for b in blocks], 0)
-
-
-def attention_kernel(dims, members, where, spread, *refs):
+            out[pl.ds(to, rows)] = block[g * rows : (g + 1) * rows, :]
+
+
+def natural_rows(blocks, dims, first, count, out):
+    ny, members, nx, rows = dims
+    for y in range(ny):
+        for g in range(members):
+            for x in range(nx):
+                to = ((y * members + g) * nx + x) * rows
+                piece = blocks[y * nx + x, g * rows : (g + 1) * rows, first : first + count]
+                out[to : to + rows] = piece
+
+
+def attention_kernel(dims, members, where, spread, qkv_blocks, *refs):
     ny, nx, rows, cap = dims
-    lines = ny * nx
-    qkv_blocks, refs = refs[:lines], refs[lines:]
     blocks, outs = refs[:members], refs[members:]
-    picked_o, normed_o, w_o, wo_o, vecs_o, joined_o, att_o, exact_o, near_o, far_o, vec_s = outs
+    picked_o, normed_o, w_o, first_o, wo_o, vecs_o = outs[:6]
+    joined_o, att_o, exact_o, near_o, far_o, vec_s = outs[6:]
     heads = ny
     cols = 3 * heads * HDIM
     routed, width = picked_o.shape
     own = routed // members
-    spots = slot_rows(blocks, 0, lines * cap)
-    picked_low = mm(spread[...], spots).astype(BF16)
+    picked_low = mm(spread[...], jnp.concatenate([b[...] for b in blocks], 0)).astype(BF16)
     picked_o[...] = picked_low
     picked = picked_low.astype(F32)
-    natural_rows(where, qkv_blocks, (ny, members, nx, rows), 0, cols, w_o)
-    natural_rows(where, qkv_blocks, (ny, members, nx, rows), cols, 128, vec_s)
-    line_rows(where, qkv_blocks, members * rows, wo_o)
+    first_o[...] = picked_low[:own]
+    natural_rows(qkv_blocks, (ny, members, nx, rows), 0, cols, w_o)
+    natural_rows(qkv_blocks, (ny, members, nx, rows), cols, 128, vec_s)
+    line_rows(qkv_blocks, members * rows, wo_o)
     vecs = mm(eye_rows(), vec_s[...], NT)
     vecs_o[...] = vecs
     normed = (picked * inverse_rms(picked) * vecs[0:1]).astype(BF16)
@@ -557,25 +667,26 @@
         far[k] = values[(depth + k) * own : (depth + k + 1) * own]
 
 
-def update_kernel(dims, members, where, spread, picked, vecs, *refs):
-    lines, cap, start = dims
+def update_kernel(dims, where, spread, picked, vecs, *refs):
+    lines, members, start = dims
     downs, refs = refs[:lines], refs[lines:]
-    blocks, (cot_o, gate_o, d_result_o, d_active_o, w_o) = refs[:members], refs[members:]
-    spots = slot_rows(blocks, lines * cap, lines * cap)
-    cot_low = mm(spread[...], spots).astype(BF16)
-    cot_o[...] = cot_low
+    blocks, outs = refs[:members], refs[members:]
+    gate_o, cot_o, first_o, d_result_o, d_active_o, w_o = outs
     logit = jnp.sum(picked[...].astype(F32) * vecs[2:3, :], 1, keepdims=True)
     gate = 1.0 / (1.0 + jnp.exp(-logit))
     gate_o[...] = gate
-    d_result = (gate * cot_low.astype(F32)).astype(BF16)
+    cot = mm(spread[...], jnp.concatenate([b[...] for b in blocks], 0)).astype(BF16)
+    cot_o[...] = cot
+    first_o[...] = cot[: first_o.shape[0]]
+    d_result = (gate * cot.astype(F32)).astype(BF16)
     d_result_o[...] = d_result
-    line_rows(where, downs, start, w_o)
+    own_line_rows(where, downs, start, w_o)
     d_active_o[...] = mm(d_result, w_o[...], NT)
 
 
-def hidden_kernel(own, picked, vecs, *refs):
+def hidden_kernel(picked, vecs, *refs):
     *terms, hidden_o, normed_o = refs
-    hidden = picked[:own, :].astype(F32) + add_up(terms)
+    hidden = picked[...].astype(F32) + add_up(terms)
     hidden_o[...] = hidden
     normed_o[...] = (hidden * inverse_rms(hidden) * vecs[1:2, :]).astype(BF16)
 
@@ -584,7 +695,7 @@
     lines = dims[0] * dims[2]
     ups, refs = refs[:lines], refs[lines:]
     blocks, (active_o, d_upper_o, near_o, far_o, w_s) = refs[:members], refs[members:]
-    natural_rows(where, ups, dims, 0, ups[0].shape[1], w_s)
+    own_order_rows(where, ups, dims, w_s)
     normed = jnp.concatenate([b[...] for b in blocks], 0)
     upper = mm(normed, w_s[...])
     below = 0.5 * (1.0 + lax.erf(upper * (0.5**0.5)))
@@ -597,21 +708,32 @@
 
 def ff_grads_kernel(dims, members, where, active, d_upper, d_result, *refs):
     ny, nx, rows, ff_rows = dims
-    lines = ny * nx
-    blocks, sums, (down, up) = refs[:members], refs[members : members + lines], refs[-2:]
+    blocks, (keep, by_x, by_y, down, up) = refs[:members], refs[members:]
     normed = jnp.concatenate([b[...] for b in blocks], 0)
     down[...] = mm(active[...], d_result[...], TN).astype(BF16)
     up[...] = mm(normed, d_upper[...], TN).astype(BF16)
     wide = up.shape[1]
-    for k in range(lines):
+    part = members * rows // 2
+    for k in range(ny * nx):
         line = where[2] ^ k
         y, x = lax.div(line, jnp.int32(nx)), lax.rem(line, jnp.int32(nx))
-        sums[k][:ff_rows] = down[pl.ds(pl.multiple_of(line * ff_rows, ff_rows), ff_rows)]
+        first = by_x.at[k // 2] if k % 2 else keep.at[k // 2]
+        second = by_y.at[k % 2] if k // 2 else keep.at[2 + k % 2]
+        first[...] = down[pl.ds(pl.multiple_of(line * ff_rows, ff_rows), ff_rows)]
         for g in range(members):
             at = pl.multiple_of(((y * members + g) * nx + x) * rows, rows)
-            half, row = divmod(g * rows, members * rows // 2)
-            to = ff_rows + row
-            sums[k][to : to + rows, half * wide : (half + 1) * wide] = up[pl.ds(at, rows)]
+            half, row = divmod(g * rows, part)
+            second[row : row + rows, half * wide : (half + 1) * wide] = up[pl.ds(at, rows)]
+
+
+def add_halves_kernel(keep, got_x, got_y, mine, to_y, to_x):
+    def both(index, got):
+        return keep[index].astype(F32) + got.astype(F32)
+
+    mine[0] = both(0, got_x[0])
+    mine[1] = both(2, got_y[0])
+    to_y[...] = both(1, got_x[1]).astype(BF16)
+    to_x[...] = both(3, got_y[1]).astype(BF16)
 
 
 def result_kernel(active, attended, w_down, w_out, cot, gate, spread, logit_o, near_o, far_o):
@@ -631,7 +753,7 @@
     d_hidden = inv * u - hidden * (inv * inv * inv * jnp.mean(u * hidden, 1, keepdims=True))
     d_hidden_o[...] = d_hidden
     gain_o[...] = (d_normed * hidden * inv).astype(BF16)
-    d_update = gate[:own, :] * cot[:own, :].astype(F32)
+    d_update = gate[:own, :] * cot[...].astype(F32)
     d_branch_o[...] = (d_update + d_hidden).astype(BF16)
 
 
@@ -712,11 +834,11 @@
 
 def join_slots_kernel(cap, lines, *refs):
     terms, outs = refs[:-lines], refs[-lines:]
-    half = len(terms) // 2
+    total = add_up(terms).astype(BF16)
     for j in range(2):
-        total = add_up(terms[j * half : (j + 1) * half]).astype(BF16)
         for k in range(lines):
-            outs[k][j * cap : (j + 1) * cap] = total[k * cap : (k + 1) * cap]
+            at = (j * lines + k) * cap
+            outs[k][j * cap : (j + 1) * cap] = total[at : at + cap]
 
 
 def place_kernel(cap, lines, where, pick, tokens, cot, *refs):
@@ -729,32 +851,44 @@
         grad_o[s] = (cot[s].astype(F32) + mm(hot, got[s, cap:], TN)).astype(BF16)
 
 
-def line_sums_kernel(dims, lines, *refs):
+def line_sums_kernel(dims, where, mine, got_down, got_up, *refs):
     members, rows, ff_rows = dims
-    parts, ffs, (send_o, out_o, down_o) = refs[:lines], refs[lines : 2 * lines], refs[2 * lines :]
+    *parts, near_o, far_o, out_o, down_o, send = refs
     cols = parts[0].shape[1]
-    wide = ffs[0].shape[1] // 2
-
-    def total(blocks):
-        sums = blocks[0][...].astype(F32)
-        for block in blocks[1:]:
-            sums = sums + block[...].astype(F32)
-        return sums
-
-    main, ff = total(parts), total(ffs)
+    wide = mine.shape[2] // 2
+    up = mine[1] + got_up[...].astype(F32)
+    main = parts[0][...].astype(F32)
+    for part in parts[1:]:
+        main = main + part[...].astype(F32)
     for g in range(members):
-        send_o[g, :, :cols] = main[g * rows : (g + 1) * rows].astype(BF16)
+        send[g, :, :cols] = main[g * rows : (g + 1) * rows].astype(BF16)
         half, row = divmod(g * rows, members * rows // 2)
-        at = ff_rows + row
-        piece = ff[at : at + rows, half * wide : (half + 1) * wide]
-        send_o[g, :, cols:] = piece.astype(BF16)
+        piece = up[row : row + rows, half * wide : (half + 1) * wide]
+        send[g, :, cols:] = piece.astype(BF16)
+    depth = near_o.shape[0]
+    for k in range(depth):
+        near_o[k] = send[where[3] ^ k]
+        far_o[k] = send[where[3] ^ (depth + k)]
     end = members * rows
     out_o[...] = jnp.concatenate([main[end : end + rows], main[end + rows :]], 1)
-    down_o[...] = ff[:ff_rows]
-
-
-def unpack_kernel(dims, got, qkv_o, up_o, *vec_o):
+    down_o[...] = mine[0] + got_down[...].astype(F32)
+
+
+def pair_kernel(near, far, *outs):
+    rows = near.shape[1]
+    for k, out in enumerate(outs):
+        out[:rows] = near[k]
+        out[rows:] = far[k]
+
+
+def unpack_kernel(dims, where, *refs):
     ny, members, nx, ff_rows = dims
+    depth = members // 2
+    pairs, (qkv_o, up_o, *vec_o, got) = refs[:depth], refs[depth:]
+    rows = got.shape[1]
+    for k, pair in enumerate(pairs):
+        got[where[3] ^ k] = pair[:rows]
+        got[where[3] ^ (depth + k)] = pair[rows:]
     cols = 3 * ny * HDIM
     for t in range(3):
         for y in range(ny):
@@ -802,74 +936,86 @@
 
     pick, *picked_rows = local_call(
         partial(pick_kernel, cap),
-        [((seq_count, cap, seg_len), BF16)] + [(slot_block, BF16)] * lines,
+        [Far(((seq_count, cap, seg_len), BF16))] + [(slot_block, BF16)] * lines,
         (where, chosen_t, tokens, cotangent),
         scratch=[pltpu.VMEM((seq_count, 2 * cap, width), BF16)],
         scalars=1,
     )
     line_slots = picked_rows[:1] + send_lines(picked_rows[1:])
-    (spread,) = local_call(
+    (hot,) = local_call(
         partial(spread_kernel, (ny, nc, nz, nx, seg_len, cap)),
-        [((routed, members * lines * cap), BF16)],
+        [Far(((routed, members * lines * cap), BF16))],
         (where, chosen, chosen_t),
         scalars=1,
     )
+    spread = Far(hot)
     (line_slots,) = local_call(
-        partial(stack_kernel, cap), [((lines * 2 * cap, width), BF16)], line_slots
+        partial(stack_kernel, cap), [((2 * lines * cap, width), BF16)], line_slots, after=(hot,)
     )
     slots = gather_group([line_slots])
-
+    half = lines * cap
+    picked_slots, cot_slots = [Far(b, half) for b in slots], [Far(b, half, half) for b in slots]
+
+    vecs = [v.reshape(1, rows) for v in (gain_attn, gain_mlp, router)]
     (columns,) = local_call(
         partial(columns_kernel, (ny, members, nx, ff_rows)),
         [((members, rows, cols + 128 + wide), BF16)],
-        (w_qkv, w_up) + tuple(v.reshape(1, rows) for v in (gain_attn, gain_mlp, router)),
+        tuple(Far(v) for v in (w_qkv, w_up, *vecs)),
         scratch=[pltpu.VMEM((8, rows), F32)],
     )
     got_cols = lax.all_to_all(columns, ("c", "z"), 0, 0, tiled=True)
     first, second = local_call(
         relay_kernel,
         [
-            ((members * rows + 2 * rows, width // 2), BF16),
+            Far(((lines, members * rows + 2 * rows, width // 2), BF16)),
             ((members * rows + 2 * ff_rows, width // 2), BF16),
         ],
         (got_cols, w_out, w_down),
-    )
-    first, second = gather_lines(first), gather_lines(second)
-
-    picked, normed, full_qkv, full_out, full_vecs, joined, attended, exact, near, far = local_call(
-        partial(attention_kernel, (ny, nx, rows, cap), members),
+        after=(line_slots,),
+    )
+    first = lax.all_to_all(first, ("y", "x"), 0, 0, tiled=True)
+    second = gather_lines(second)
+
+    picked, normed, full_qkv, picked_own, full_out, full_vecs, joined, attended, exact, near, far = (
+        local_call(
+            partial(attention_kernel, (ny, nx, rows, cap), members),
+            [
+                ((routed, width), BF16),
+                ((routed, width), BF16),
+                ((width, cols), BF16),
+                (block, BF16),
+                ((heads * HDIM, width), BF16),
+                ((8, width), F32),
+                ((routed, cols), BF16),
+                ((routed, heads * HDIM), BF16),
+                ((routed, heads * HDIM), F32),
+            ]
+            + halves,
+            (where, spread, Far(first), *picked_slots),
+            flops=1.2e9,
+            scratch=[pltpu.VMEM((width, 128), BF16)],
+            scalars=1,
+        )
+    )
+    terms = scatter_group(near, far)
+    gate, cot, cot_own, d_result, d_active, full_down = local_call(
+        partial(update_kernel, (lines, members, members * rows)),
         [
+            ((routed, 1), F32),
             ((routed, width), BF16),
-            ((routed, width), BF16),
-            ((width, cols), BF16),
-            ((heads * HDIM, width), BF16),
-            ((8, width), F32),
-            ((routed, cols), BF16),
-            ((routed, heads * HDIM), BF16),
-            ((routed, heads * HDIM), F32),
-        ]
-        + halves,
-        (where, spread, *first, *slots),
-        flops=1.2e9,
-        scratch=[pltpu.VMEM((width, 128), BF16)],
-        scalars=1,
-    )
-    terms = scatter_group(near, far)
-    cot, gate, d_result, d_active, full_down = local_call(
-        partial(update_kernel, (lines, cap, members * rows), members),
-        [
-            ((routed, width), BF16),
-            ((routed, 1), F32),
+            (block, BF16),
             ((routed, width), BF16),
             ((routed, wide), F32),
             ((wide, width), BF16),
         ],
-        (where, spread, picked, full_vecs, *second, *slots),
+        (where, spread, picked, full_vecs, *second, *cot_slots),
         flops=8e8,
         scalars=1,
     )
     hidden, normed_own = local_call(
-        partial(hidden_kernel, own), [(block, F32), (block, BF16)], (picked, full_vecs, *terms)
+        hidden_kernel,
+        [(block, F32), (block, BF16)],
+        (picked_own, full_vecs, *terms),
     )
     normed_mlp = gather_group([normed_own])
 
@@ -882,15 +1028,15 @@
         scalars=1,
     )
     terms = scatter_group(near, far)
-    ff_parts = local_call(
+    half = (ff_rows, width)
+    ff_keep, ff_x, ff_y = local_call(
         partial(ff_grads_kernel, (ny, nx, rows, ff_rows), members),
-        [((ff_rows + members * rows // 2, width), BF16)] * lines,
+        [((4, *half), BF16), ((2, *half), BF16), ((2, *half), BF16)],
         (where, active, d_upper, d_result, *normed_mlp),
         flops=6e8,
         scratch=[pltpu.VMEM((wide, width), BF16), pltpu.VMEM((width, wide), BF16)],
         scalars=1,
     )
-    ff_parts = ff_parts[:1] + send_lines(ff_parts[1:])
     logit, up_near, up_far = local_call(
         result_kernel,
         [((routed, 1), F32)] + slot_halves,
@@ -900,20 +1046,28 @@
     d_branch_own, d_hidden, gain_m = local_call(
         partial(hidden_back_kernel, own),
         [(block, BF16), (block, F32), (block, BF16)],
-        (hidden, full_vecs, gate, cot, *terms),
+        (hidden, full_vecs, gate, cot_own, *terms),
+        after=(ff_x, logit),
     )
     d_branch = gather_group([d_branch_own])
-    update_terms = scatter_group(up_near, up_far)
+    up_far = send_c(up_far)
+    ff_mine, ff_y, ff_x = local_call(
+        add_halves_kernel,
+        [((2, *half), F32), (half, BF16), (half, BF16)],
+        (ff_keep, lax.ppermute(ff_x, "x", flips(nx)[1]), lax.ppermute(ff_y, "y", flips(ny)[1])),
+    )
+    ff_got = (lax.ppermute(ff_y, "y", flips(ny)[1]), lax.ppermute(ff_x, "x", flips(nx)[1]))
 
     near, far, d_joined, gain_a = local_call(
         partial(attention_back_kernel, members),
         slot_halves + [((routed, cols), BF16), ((routed, width), BF16)],
-        (where, full_out, joined, exact, full_qkv, full_vecs, picked, logit, d_hidden, spread)
-        + tuple(d_branch),
+        (where, full_out, joined, exact, full_qkv, full_vecs, picked)
+        + (logit, d_hidden, spread, *d_branch),
         flops=1.2e9,
         scalars=1,
-    )
-    picked_terms = scatter_group(near, far, after=update_terms[1:])
+        after=(ff_mine,),
+    )
+    far = send_c(far)
     parts = local_call(
         partial(grads_kernel, (ny, nx, rows), members),
         [((members * rows + 2 * rows, cols + 128), BF16)] * lines,
@@ -927,34 +1081,42 @@
         scalars=1,
     )
     parts = parts[:1] + send_lines(parts[1:])
+    both_slots = (2 * lines * cap, width)
+    mine, *low = local_call(
+        slot_sum_kernel,
+        [(both_slots, F32)] + [(both_slots, BF16)] * (nz - 1),
+        (up_near, up_far, near, far),
+    )
     back_rows = local_call(
         partial(join_slots_kernel, cap, lines),
         [(slot_block, BF16)] * lines,
-        (*update_terms, *picked_terms),
+        [mine] + send_z(low),
     )
     back_rows = back_rows[:1] + send_lines(back_rows[1:])
-    send, grad_out, grad_down = local_call(
-        partial(line_sums_kernel, (members, rows, ff_rows), lines),
-        [
-            ((members, rows, cols + 128 + wide), BF16),
-            ((rows, width), F32),
-            ((ff_rows, width), F32),
-        ],
-        (*parts, *ff_parts),
+    row_width = cols + 128 + wide
+    near, far, grad_out, grad_down = local_call(
+        partial(line_sums_kernel, (members, rows, ff_rows)),
+        [((nz, rows, row_width), BF16)] * 2 + [((rows, width), F32), ((ff_rows, width), F32)],
+        (where, ff_mine, *ff_got, *parts),
+        scratch=[pltpu.VMEM((members, rows, row_width), BF16)],
+        scalars=1,
         after=back_rows[:1],
     )
-    got = lax.all_to_all(send, ("c", "z"), 0, 0, tiled=True)
+    pairs = local_call(pair_kernel, [((2 * rows, row_width), BF16)] * nz, (near, send_c(far)))
+    pairs = pairs[:1] + send_z(pairs[1:])
     output, grad_tokens = local_call(
         partial(place_kernel, cap, lines),
         [(tokens.shape, BF16), (tokens.shape, BF16)],
-        (where, pick, tokens, cotangent, *back_rows),
+        (where, Far(pick), tokens, cotangent, *back_rows),
         scratch=[pltpu.VMEM((seq_count, 2 * cap, width), BF16)],
         scalars=1,
     )
     grad_qkv, grad_up, *grad_vecs = local_call(
         partial(unpack_kernel, (ny, members, nx, ff_rows)),
         [(w_qkv.shape, F32), (w_up.shape, F32)] + [((1, rows), F32)] * 3,
-        (got,),
+        (where, *pairs),
+        scratch=[pltpu.VMEM((members, rows, row_width), BF16)],
+        scalars=1,
     )
     return (
         output,

time: 182 us -> 174 us (0.956)
  waiting for transfers between devices: 93.1 us -> 74.1 us
  Pallas kernels: 20.6 us -> 30.8 us
  starting transfers between devices: 61.6 us -> 65.5 us
  local copies, waits for them, and re-layouts: 4.89 us -> 1.94 us
    ppermute x18 -> x12, waiting for transfers between devices: 28.5 us -> 6.58 us  [send_lines(): lax.ppermute(b, ('y', 'x'), f)]
    ppermute x21, starting transfers between devices: 27 us -> 37.8 us  [send_z(): lax.ppermute(b, 'z', f)]
    ppermute x18 -> x12, starting transfers between devices: 21.4 us -> 10.9 us  [send_lines(): lax.ppermute(b, ('y', 'x'), f)]
    pallas_call x22 -> x23, Pallas kernels: 20.6 us -> 30.8 us  [local_call(): pl.pallas_call(run, out_shape=shapes, in_specs=[pl.BlockSpec(memory_space...]
    all_to_all x1, waiting for transfers between devices: 6.2 us -> 0.01 us  [grouped(): first = lax.all_to_all(first, ('y', 'x'), 0, 0, tiled=True)]
    ppermute x0 -> x4, waiting for transfers between devices: none -> 5.88 us  [the longest x2 5.32 us: grouped(): lax.ppermute(ff_y, 'y', flips(ny)[1])]
    ppermute x0 -> x4, starting transfers between devices: none -> 4.1 us  [the longest x2 2.08 us: grouped(): lax.ppermute(ff_x, 'x', flips(nx)[1])]
    all_to_all x1, waiting for transfers between devices: 0.01 us -> 3.84 us  [grouped(): got_cols = lax.all_to_all(columns, ('c', 'z'), 0, 0, tiled=True)]
  transfers between devices with their start and end apart: 57 -> 56, of which waited for: 28 -> 27; matrix products, arithmetic and copies ran while one was open for 0% -> 0% of each run, Pallas kernels for 9% -> 12%
where the time goes in v4:
time: 174 us; the launch traced here: 173 us
  waiting for transfers between devices  74.1 us (43%)
  starting transfers between devices  65.5 us (38%)
  Pallas kernels  30.8 us (18%)
  local copies, waits for them, and re-layouts  1.94 us (1%)
    ppermute x21, waiting for transfers between devices, send_z(): lax.ppermute(b, 'z', f)  51.5 us
    ppermute x21, starting transfers between devices, send_z(): lax.ppermute(b, 'z', f)  37.8 us
    pallas_call x23, Pallas kernels, local_call(): pl.pallas_call(run, out_shape=shapes, in_specs=[pl.BlockSpec(memory_space...  30.8 us
    ppermute x12, starting transfers between devices, send_lines(): lax.ppermute(b, ('y', 'x'), f)  10.9 us
    ppermute x12, waiting for transfers between devices, send_lines(): lax.ppermute(b, ('y', 'x'), f)  6.58 us
    ppermute x17, waiting for transfers between devices, send_c(): return lax.ppermute(block, 'c', flips(2)[1])  6.37 us
    all_to_all x1, starting transfers between devices, grouped(): got_cols = lax.all_to_all(columns, ('c', 'z'), 0, 0, tiled=True)  6.34 us
    ppermute x2, waiting for transfers between devices, grouped(): lax.ppermute(ff_y, 'y', flips(ny)[1])  5.32 us
  transfers between devices with their start and end apart: 56, of which 27 were waited for; matrix products, arithmetic and copies ran while one was open for 0% of the time, Pallas kernels for 12%

profile of v4, /device:TPU:0, one launch (start us, length us, event | category | flops | bytes accessed | tf_op | source)
XLA Modules:
  0.0 173.4 jit_solution(7583441945458643126)
XLA Ops:
  0.7 2.2 %shard_map.171 = bf16[8,32,1024]{2,1,0:T(8,128)(2,1)} custom-call(bf16[32,3072]{1,0:T(8,128)(2,1)} %refs_0_.1, bf16[32,4096]{1,0:T(8,128)(2,1)} %refs_1_.4, bf16[1,32]{1,0:T(2,128)(2,1)} %bitcast.14, bf16[1,32]{1,0:T(2,128)(2,1)} %bitcast.15, bf16[1,32]{1,0:T(2,128)(2,1)} %bitcast.16), custom_call_target="tpu_custom_call" | custom-call | tf_op jit(solution)/shard_map/pallas_call | solution.py:379
  2.9 6.3 %all-to-all-start = ((bf16[8,32,1024]{2,1,0:T(8,128)(2,1)}), bf16[8,32,1024]{2,1,0:T(8,128)(2,1)S(1)}, u32[]{:S(2)}, u32[]{:S(2)}) async-start(bf16[8,32,1024]{2,1,0:T(8,128)(2,1)} %shard_map.171), calls=%async_computation | async-start | bytes 1048576 | tf_op jit(solution)/shard_map/all_to_all | solution.py:966
  9.5 1.5 shard_map.169
  11.0 1.6 collective-permute-start
  12.6 1.5 collective-permute-start.1
  14.6 1.8 %shard_map.170.refs_4_.refs_1_.refs_6_.refs_9_ = bf16[256,512]{1,0:T(8,128)(2,1)} custom-call(s32[5]{0:T(128)S(1)} %stack.23.refs_0_, s32[4,256]{1,0:T(4,128)S(1)} %copy-done.6, s32[256,4]{1,0:T(8,128)S(1)} %bitcast.13), custom_call_target="tpu_custom_call" | custom-call | tf_op jit(solution)/shard_map/pallas_call | solution.py:379
  16.8 2.4 %collective-permute-done.2.refs_3_ = bf16[32,1024]{1,0:T(8,128)(2,1)S(1)} collective-permute-done((bf16[32,1024]{1,0:T(8,128)(2,1)S(1)}, bf16[32,1024]{1,0:T(8,128)(2,1)S(1)}, u32[]{:S(2)}, u32[]{:S(2)}) %collective-permute-start.2) | collective-permute-done | bytes 65568 | tf_op jit(solution)/shard_map/ppermute | solution.py:403
  20.2 3.8 %all-to-all-done.refs_0_ = bf16[8,32,1024]{2,1,0:T(8,128)(2,1)S(1)} async-done(((bf16[8,32,1024]{2,1,0:T(8,128)(2,1)}), bf16[8,32,1024]{2,1,0:T(8,128)(2,1)S(1)}, u32[]{:S(2)}, u32[]{:S(2)}) %all-to-all-start) | async-done | bytes 524320 | tf_op jit(solution)/shard_map/all_to_all | solution.py:966
  25.2 4.3 %all-to-all-start.1 = ((bf16[4,320,512]{2,1,0:T(8,128)(2,1)}), bf16[4,320,512]{2,1,0:T(8,128)(2,1)}, u32[]{:S(2)}, u32[]{:S(2)}) async-start(bf16[4,320,512]{2,1,0:T(8,128)(2,1)} %get-tuple-element.95), calls=%async_computation.1 | async-start | bytes 2621440 | tf_op jit(solution)/shard_map/all_to_all | solution.py:976
  30.6 3.4 %collective-permute-start.5 = (bf16[128,1024]{1,0:T(8,128)(2,1)S(1)}, bf16[128,1024]{1,0:T(8,128)(2,1)S(1)}, u32[]{:S(2)}, u32[]{:S(2)}) collective-permute-start(bf16[128,1024]{1,0:T(8,128)(2,1)S(1)} %shard_map.172.refs_3_.refs_8_), channel_id=1, source_target_pairs={{0,6},{2,4},{4,2},{6,0},{1,7},{3,5},{5,3},{7,1},{8,14},{10,12},{12... | collective-permute-start | bytes 786440 | tf_op jit(solution)/shard_map/ppermute | solution.py:398
  34.0 8.9 %collective-permute-done.3.refs_4_.refs_9_ = bf16[128,1024]{1,0:T(8,128)(2,1)S(1)} collective-permute-done((bf16[128,1024]{1,0:T(8,128)(2,1)S(1)}, bf16[128,1024]{1,0:T(8,128)(2,1)S(1)}, u32[]{:S(2)}, u32[]{:S(2)}) %collective-permute-start.3) | collective-permute-done | bytes 262176 | tf_op jit(solution)/shard_map/ppermute | solution.py:398
  42.9 8.1 %collective-permute-done.4.refs_5_.refs_10_ = bf16[128,1024]{1,0:T(8,128)(2,1)S(1)} collective-permute-done((bf16[128,1024]{1,0:T(8,128)(2,1)S(1)}, bf16[128,1024]{1,0:T(8,128)(2,1)S(1)}, u32[]{:S(2)}, u32[]{:S(2)}) %collective-permute-start.4) | collective-permute-done | bytes 262176 | tf_op jit(solution)/shard_map/ppermute | solution.py:398
  51.5 1.9 %collective-permute-start.10 = (bf16[512,512]{1,0:T(8,128)(2,1)S(1)}, bf16[512,512]{1,0:T(8,128)(2,1)S(1)}, u32[]{:S(2)}, u32[]{:S(2)}) collective-permute-start(bf16[512,512]{1,0:T(8,128)(2,1)S(1)} %get-tuple-element.98.refs_4_.refs_2_), channel_id=1, source_target_pairs={{0,1},{1,0},{16,17},{17,16},{2,3},{3,2},{18,19},{19,18},{4,5},{5,4... | collective-permute-start | bytes 1572872 | tf_op jit(solution)/shard_map/ppermute | solution.py:403
  53.4 1.5 collective-permute-start.11
  55.8 4.2 %shard_map.174 = (bf16[256,1024]{1,0:T(8,128)(2,1)S(1)}, bf16[256,1024]{1,0:T(8,128)(2,1)S(1)}, bf16[1024,384]{1,0:T(8,128)(2,1)S(1)}, bf16[32,1024]{1,0:T(8,128...) custom-call(s32[5]{0:T(128)S(1)} %stack.23.refs_0_, ...), custom_call_target="tpu_custom_call" | custom-call | flops 1200000000 | tf_op jit(solution)/shard_map/pallas_call | solution.py:379
  60.1 1.5 collective-permute-done.13.refs_1_
  61.7 5.1 %collective-permute-start.14 = (bf16[32,1024]{1,0:T(8,128)(2,1)S(1)}, bf16[32,1024]{1,0:T(8,128)(2,1)S(1)}, u32[]{:S(2)}, u32[]{:S(2)}) collective-permute-start(bf16[32,1024]{1,0:T(8,128)(2,1)S(1)} %get-tuple-element.104), channel_id=1, source_target_pairs={{0,2},{2,0},{4,6},{6,4},{1,3},{3,1},{5,7},{7,5},{8,10},{10,8},{12,... | collective-permute-start | bytes 196616 | tf_op jit(solution)/shard_map/ppermute | solution.py:398
  67.2 2.0 %collective-permute-done.14.refs_3_ = bf16[32,1024]{1,0:T(8,128)(2,1)S(1)} collective-permute-done((bf16[32,1024]{1,0:T(8,128)(2,1)S(1)}, bf16[32,1024]{1,0:T(8,128)(2,1)S(1)}, u32[]{:S(2)}, u32[]{:S(2)}) %collective-permute-start.14) | collective-permute-done | bytes 65568 | tf_op jit(solution)/shard_map/ppermute | solution.py:398
  69.2 1.7 %collective-permute-start.16 = (bf16[32,1024]{1,0:T(8,128)(2,1)S(1)}, bf16[32,1024]{1,0:T(8,128)(2,1)S(1)}, u32[]{:S(2)}, u32[]{:S(2)}) collective-permute-start(bf16[32,1024]{1,0:T(8,128)(2,1)S(1)} %get-tuple-element.106), channel_id=1, source_target_pairs={{0,6},{2,4},{4,2},{6,0},{1,7},{3,5},{5,3},{7,1},{8,14},{10,12},{12... | collective-permute-start | bytes 196616 | tf_op jit(solution)/shard_map/ppermute | solution.py:398
  70.9 2.3 %collective-permute-done.15.refs_4_ = bf16[32,1024]{1,0:T(8,128)(2,1)S(1)} collective-permute-done((bf16[32,1024]{1,0:T(8,128)(2,1)S(1)}, bf16[32,1024]{1,0:T(8,128)(2,1)S(1)}, u32[]{:S(2)}, u32[]{:S(2)}) %collective-permute-start.15) | collective-permute-done | bytes 65568 | tf_op jit(solution)/shard_map/ppermute | solution.py:398
  73.2 2.1 %collective-permute-done.16.refs_5_ = bf16[32,1024]{1,0:T(8,128)(2,1)S(1)} collective-permute-done((bf16[32,1024]{1,0:T(8,128)(2,1)S(1)}, bf16[32,1024]{1,0:T(8,128)(2,1)S(1)}, u32[]{:S(2)}, u32[]{:S(2)}) %collective-permute-start.16) | collective-permute-done | bytes 65568 | tf_op jit(solution)/shard_map/ppermute | solution.py:398
  77.8 2.1 %collective-permute-start.19 = (bf16[32,1024]{1,0:T(8,128)(2,1)S(1)}, bf16[32,1024]{1,0:T(8,128)(2,1)S(1)}, u32[]{:S(2)}, u32[]{:S(2)}) collective-permute-start(bf16[32,1024]{1,0:T(8,128)(2,1)S(1)} %get-tuple-element.107.refs_6_.refs_4_), channel_id=1, source_target_pairs={{0,6},{2,4},{4,2},{6,0},{1,7},{3,5},{5,3},{7,1},{8,14},{10,12},{12... | collective-permute-start | bytes 196616 | tf_op jit(solution)/shard_map/ppermute | solution.py:398
  80.4 2.4 %collective-permute-done.18.refs_8_.refs_6_ = bf16[32,1024]{1,0:T(8,128)(2,1)S(1)} collective-permute-done((bf16[32,1024]{1,0:T(8,128)(2,1)S(1)}, bf16[32,1024]{1,0:T(8,128)(2,1)S(1)}, u32[]{:S(2)}, u32[]{:S(2)}) %collective-permute-start.18) | collective-permute-done | bytes 65568 | tf_op jit(solution)/shard_map/ppermute | solution.py:398
  84.0 2.8 %shard_map.175 = (f32[256,1]{1,0:T(8,128)S(1)}, bf16[256,1024]{1,0:T(8,128)(2,1)S(1)}, bf16[32,1024]{1,0:T(8,128)(2,1)S(1)}, bf16[256,1024]{1,0:T(8,128)(2,1)S(1...) custom-call(s32[5]{0:T(128)S(1)} %stack.23.refs_0_, ...), custom_call_target="tpu_custom_call" | custom-call | flops 800000000 | tf_op jit(solution)/shard_map/pallas_call | solution.py:379
  86.9 1.6 shard_map.178
  89.9 1.7 collective-permute-start.36
  91.6 1.5 collective-permute-start.37
  93.0 1.5 collective-permute-done.25.refs_1_
  95.4 1.8 %collective-permute-start.27 = (bf16[32,1024]{1,0:T(8,128)(2,1)S(1)}, bf16[32,1024]{1,0:T(8,128)(2,1)S(1)}, u32[]{:S(2)}, u32[]{:S(2)}) collective-permute-start(bf16[32,1024]{1,0:T(8,128)(2,1)S(1)} %get-tuple-element.126), channel_id=1, source_target_pairs={{0,4},{2,6},{4,0},{6,2},{1,5},{3,7},{5,1},{7,3},{8,12},{10,14},{12... | collective-permute-start | bytes 196616 | tf_op jit(solution)/shard_map/ppermute | solution.py:398
  97.3 1.8 %collective-permute-start.28 = (bf16[32,1024]{1,0:T(8,128)(2,1)S(1)}, bf16[32,1024]{1,0:T(8,128)(2,1)S(1)}, u32[]{:S(2)}, u32[]{:S(2)}) collective-permute-start(bf16[32,1024]{1,0:T(8,128)(2,1)S(1)} %get-tuple-element.127), channel_id=1, source_target_pairs={{0,6},{2,4},{4,2},{6,0},{1,7},{3,5},{5,3},{7,1},{8,14},{10,12},{12... | collective-permute-start | bytes 196616 | tf_op jit(solution)/shard_map/ppermute | solution.py:398
  100.6 3.2 %collective-permute-done.27.refs_6_ = bf16[32,1024]{1,0:T(8,128)(2,1)S(1)} collective-permute-done((bf16[32,1024]{1,0:T(8,128)(2,1)S(1)}, bf16[32,1024]{1,0:T(8,128)(2,1)S(1)}, u32[]{:S(2)}, u32[]{:S(2)}) %collective-permute-start.27) | collective-permute-done | bytes 65568 | tf_op jit(solution)/shard_map/ppermute | solution.py:398
  106.4 1.9 %collective-permute-start.31 = (bf16[32,1024]{1,0:T(8,128)(2,1)S(1)}, bf16[32,1024]{1,0:T(8,128)(2,1)S(1)}, u32[]{:S(2)}, u32[]{:S(2)}) collective-permute-start(bf16[32,1024]{1,0:T(8,128)(2,1)S(1)} %get-tuple-element.132.refs_10_.refs_8_), channel_id=1, source_target_pairs={{0,6},{2,4},{4,2},{6,0},{1,7},{3,5},{5,3},{7,1},{8,14},{10,12},{12... | collective-permute-start | bytes 196616 | tf_op jit(solution)/shard_map/ppermute | solution.py:398
  108.3 3.5 %collective-permute-done.30.refs_12_.refs_10_ = bf16[32,1024]{1,0:T(8,128)(2,1)S(1)} collective-permute-done((bf16[32,1024]{1,0:T(8,128)(2,1)S(1)}, bf16[32,1024]{1,0:T(8,128)(2,1)S(1)}, u32[]{:S(2)}, u32[]{:S(2)}) %collective-permute-start.30) | collective-permute-done | bytes 65568 | tf_op jit(solution)/shard_map/ppermute | solution.py:398
  114.0 3.9 %shard_map.184 = (bf16[4,64,1024]{2,1,0:T(8,128)(2,1)S(1)}, bf16[4,64,1024]{2,1,0:T(8,128)(2,1)S(1)}, bf16[256,384]{1,0:T(8,128)(2,1)S(1)}, bf16[256,1024]{1,0:T(8,128)(2,1)S(1)}) custom-call(s32[5]{0:T(128)S(1)} %stack.23.refs_0_, bf16[128,1024]{1,0:T(8,128)(2,1)S(1)} %get-tuple-element.111.refs_3_.refs_1_, ...), custom_call_target="tpu_custom_call" | custom-call | flops 1200000000 | tf_op jit(solution)/shard_map/pallas_call | solution.py:379
  118.3 1.6 collective-permute-done.38.refs_3_
  122.6 1.9 %collective-permute-start.41 = (bf16[128,1024]{1,0:T(8,128)(2,1)S(1)}, bf16[128,1024]{1,0:T(8,128)(2,1)S(1)}, u32[]{:S(2)}, u32[]{:S(2)}) collective-permute-start(bf16[128,1024]{1,0:T(8,128)(2,1)S(1)} %get-tuple-element.141), channel_id=1, source_target_pairs={{0,6},{2,4},{4,2},{6,0},{1,7},{3,5},{5,3},{7,1},{8,14},{10,12},{12... | collective-permute-start | bytes 786440 | tf_op jit(solution)/shard_map/ppermute | solution.py:398
  124.5 1.7 shard_map.188
  127.3 6.2 %collective-permute-done.39.refs_1_ = bf16[128,1024]{1,0:T(8,128)(2,1)S(1)} collective-permute-done((bf16[128,1024]{1,0:T(8,128)(2,1)S(1)}, bf16[128,1024]{1,0:T(8,128)(2,1)S(1)}, u32[]{:S(2)}, u32[]{:S(2)}) %collective-permute-start.39) | collective-permute-done | bytes 262176 | tf_op jit(solution)/shard_map/ppermute | solution.py:398
  134.0 8.7 %collective-permute-done.40.refs_2_ = bf16[128,1024]{1,0:T(8,128)(2,1)S(1)} collective-permute-done((bf16[128,1024]{1,0:T(8,128)(2,1)S(1)}, bf16[128,1024]{1,0:T(8,128)(2,1)S(1)}, u32[]{:S(2)}, u32[]{:S(2)}) %collective-permute-start.40) | collective-permute-done | bytes 262176 | tf_op jit(solution)/shard_map/ppermute | solution.py:398
  143.8 5.3 %collective-permute-done.45.refs_2_ = bf16[128,1024]{1,0:T(8,128)(2,1)S(1)} collective-permute-done((bf16[128,1024]{1,0:T(8,128)(2,1)S(1)}, bf16[128,1024]{1,0:T(8,128)(2,1)S(1)}, u32[]{:S(2)}, u32[]{:S(2)}) %collective-permute-start.45) | collective-permute-done | bytes 262176 | tf_op jit(solution)/shard_map/ppermute | solution.py:1059
  149.6 1.8 %shard_map.189 = (bf16[4,32,1024]{2,1,0:T(8,128)(2,1)S(1)}, bf16[4,32,1024]{2,1,0:T(8,128)(2,1)S(1)}, f32[32,1024]{1,0:T(8,128)}, f32[128,1024]{1,0:T(8,128)}) custom-call(s32[5]{0:T(128)S(1)} %stack.23.refs_0_, f32[2,128,1024]{2,1,0:T(8,128)S(1)} %get-tuple-element.135.refs_18_.refs_1_, bf16[128,1024]{1,0:T(8,128)(2,1)S(1)} %collective-permute-done.45.refs_2_, ...), custom_call_target="tpu_custom_call" | custom-call | tf_op jit(solution)/shard_map/pallas_call | solution.py:379
  153.0 5.9 %collective-permute-start.51 = (bf16[64,1024]{1,0:T(8,128)(2,1)S(1)}, bf16[64,1024]{1,0:T(8,128)(2,1)S(1)}, u32[]{:S(2)}, u32[]{:S(2)}) collective-permute-start(bf16[64,1024]{1,0:T(8,128)(2,1)S(1)} %get-tuple-element.161), channel_id=1, source_target_pairs={{0,2},{2,0},{4,6},{6,4},{1,3},{3,1},{5,7},{7,5},{8,10},{10,8},{12,... | collective-permute-start | bytes 393224 | tf_op jit(solution)/shard_map/ppermute | solution.py:398
  159.5 1.9 %collective-permute-start.53 = (bf16[64,1024]{1,0:T(8,128)(2,1)S(1)}, bf16[64,1024]{1,0:T(8,128)(2,1)S(1)}, u32[]{:S(2)}, u32[]{:S(2)}) collective-permute-start(bf16[64,1024]{1,0:T(8,128)(2,1)S(1)} %get-tuple-element.163), channel_id=1, source_target_pairs={{0,6},{2,4},{4,2},{6,0},{1,7},{3,5},{5,3},{7,1},{8,14},{10,12},{12... | collective-permute-start | bytes 393224 | tf_op jit(solution)/shard_map/ppermute | solution.py:398
  161.9 1.5 collective-permute-start.44
  163.4 2.7 %collective-permute-done.43.refs_6_ = bf16[32,1024]{1,0:T(8,128)(2,1)S(1)} collective-permute-done((bf16[32,1024]{1,0:T(8,128)(2,1)S(1)}, bf16[32,1024]{1,0:T(8,128)(2,1)S(1)}, u32[]{:S(2)}, u32[]{:S(2)}) %collective-permute-start.43) | collective-permute-done | bytes 65568 | tf_op jit(solution)/shard_map/ppermute | solution.py:403
  167.1 2.6 %shard_map.187 = (bf16[4,64,1024]{2,1,0:T(8,128)(2,1)}, bf16[4,64,1024]{2,1,0:T(8,128)(2,1)}) custom-call(s32[5]{0:T(128)S(1)} %stack.23.refs_0_, bf16[4,16,64]{2,1,0:T(8,128)(2,1)} %get-tuple-element.90.refs_1_, bf16[4,64,1024]{2,1,0:T(8,128)(2,1)S(1)} %copy-done.2, bf16[4,64,1024]{2,1,0:T(8,128)(2,1)S(1)} %copy-done.3, ...), custom_call_target="tpu_custom_call" | custom-call | tf_op jit(solution)/shard_map/pallas_call | solution.py:379
  169.7 2.1 %collective-permute-done.52.refs_3_ = bf16[64,1024]{1,0:T(8,128)(2,1)S(1)} collective-permute-done((bf16[64,1024]{1,0:T(8,128)(2,1)S(1)}, bf16[64,1024]{1,0:T(8,128)(2,1)S(1)}, u32[]{:S(2)}, u32[]{:S(2)}) %collective-permute-start.52) | collective-permute-done | bytes 131104 | tf_op jit(solution)/shard_map/ppermute | solution.py:398
  171.8 1.6 shard_map.191
  (111 shorter events, 29.0 us)
Async XLA Ops:
  2.9 21.2 %all-to-all-start = ((bf16[8,32,1024]{2,1,0:T(8,128)(2,1)}), bf16[8,32,1024]{2,1,0:T(8,128)(2,1)S(1)}, u32[]{:S(2)}, u32[]{:S(2)}) async-start(bf16[8,32,1024]{2,1,0:T(8,128)(2,1)} %shard_map.171), calls=%async_computation | async-start | bytes 1048576 | tf_op jit(solution)/shard_map/all_to_all | solution.py:966
  11.0 5.4 %collective-permute-start = (bf16[32,1024]{1,0:T(8,128)(2,1)S(1)}, bf16[32,1024]{1,0:T(8,128)(2,1)S(1)}, u32[]{:S(2)}, u32[]{:S(2)}) collective-permute-start(bf16[32,1024]{1,0:T(8,128)(2,1)S(1)} %get-tuple-element.92), channel_id=1, source_target_pairs={{0,1},{1,0},{16,17},{17,16},{2,3},{3,2},{18,19},{19,18},{4,5},{5,4... | collective-permute-start | bytes 196616 | tf_op jit(solution)/shard_map/ppermute | solution.py:403
  12.6 4.3 %collective-permute-start.1 = (bf16[32,1024]{1,0:T(8,128)(2,1)S(1)}, bf16[32,1024]{1,0:T(8,128)(2,1)S(1)}, u32[]{:S(2)}, u32[]{:S(2)}) collective-permute-start(bf16[32,1024]{1,0:T(8,128)(2,1)S(1)} %get-tuple-element.93), channel_id=1, source_target_pairs={{0,16},{1,17},{16,0},{17,1},{2,18},{3,19},{18,2},{19,3},{4,20},{5,... | collective-permute-start | bytes 196616 | tf_op jit(solution)/shard_map/ppermute | solution.py:403
  14.1 5.2 %collective-permute-start.2 = (bf16[32,1024]{1,0:T(8,128)(2,1)S(1)}, bf16[32,1024]{1,0:T(8,128)(2,1)S(1)}, u32[]{:S(2)}, u32[]{:S(2)}) collective-permute-start(bf16[32,1024]{1,0:T(8,128)(2,1)S(1)} %get-tuple-element.94), channel_id=1, source_target_pairs={{0,17},{1,16},{16,1},{17,0},{2,19},{3,18},{18,3},{19,2},{4,21},{5,... | collective-permute-start | bytes 196616 | tf_op jit(solution)/shard_map/ppermute | solution.py:403
  25.2 30.5 %all-to-all-start.1 = ((bf16[4,320,512]{2,1,0:T(8,128)(2,1)}), bf16[4,320,512]{2,1,0:T(8,128)(2,1)}, u32[]{:S(2)}, u32[]{:S(2)}) async-start(bf16[4,320,512]{2,1,0:T(8,128)(2,1)} %get-tuple-element.95), calls=%async_computation.1 | async-start | bytes 2621440 | tf_op jit(solution)/shard_map/all_to_all | solution.py:976
  29.6 13.4 %collective-permute-start.3 = (bf16[128,1024]{1,0:T(8,128)(2,1)S(1)}, bf16[128,1024]{1,0:T(8,128)(2,1)S(1)}, u32[]{:S(2)}, u32[]{:S(2)}) collective-permute-start(bf16[128,1024]{1,0:T(8,128)(2,1)S(1)} %shard_map.172.refs_3_.refs_8_), channel_id=1, source_target_pairs={{0,2},{2,0},{4,6},{6,4},{1,3},{3,1},{5,7},{7,5},{8,10},{10,8},{12,... | collective-permute-start | bytes 786440 | tf_op jit(solution)/shard_map/ppermute | solution.py:398
  29.6 21.4 %collective-permute-start.4 = (bf16[128,1024]{1,0:T(8,128)(2,1)S(1)}, bf16[128,1024]{1,0:T(8,128)(2,1)S(1)}, u32[]{:S(2)}, u32[]{:S(2)}) collective-permute-start(bf16[128,1024]{1,0:T(8,128)(2,1)S(1)} %shard_map.172.refs_3_.refs_8_), channel_id=1, source_target_pairs={{0,4},{2,6},{4,0},{6,2},{1,5},{3,7},{5,1},{7,3},{8,12},{10,14},{12... | collective-permute-start | bytes 786440 | tf_op jit(solution)/shard_map/ppermute | solution.py:398
  30.6 20.4 %collective-permute-start.5 = (bf16[128,1024]{1,0:T(8,128)(2,1)S(1)}, bf16[128,1024]{1,0:T(8,128)(2,1)S(1)}, u32[]{:S(2)}, u32[]{:S(2)}) collective-permute-start(bf16[128,1024]{1,0:T(8,128)(2,1)S(1)} %shard_map.172.refs_3_.refs_8_), channel_id=1, source_target_pairs={{0,6},{2,4},{4,2},{6,0},{1,7},{3,5},{5,3},{7,1},{8,14},{10,12},{12... | collective-permute-start | bytes 786440 | tf_op jit(solution)/shard_map/ppermute | solution.py:398
  34.0 19.4 %collective-permute-start.6 = (bf16[128,1024]{1,0:T(8,128)(2,1)S(1)}, bf16[128,1024]{1,0:T(8,128)(2,1)}, u32[]{:S(2)}, u32[]{:S(2)}) collective-permute-start(bf16[128,1024]{1,0:T(8,128)(2,1)S(1)} %shard_map.172.refs_3_.refs_8_), channel_id=1, source_target_pairs={{0,8},{8,0},{1,9},{9,1},{2,10},{10,2},{3,11},{11,3},{4,12},{12,4},... | collective-permute-start | bytes 786440 | tf_op jit(solution)/shard_map/ppermute | solution.py:411
  42.9 12.0 %collective-permute-start.7 = (bf16[128,1024]{1,0:T(8,128)(2,1)S(1)}, bf16[128,1024]{1,0:T(8,128)(2,1)}, u32[]{:S(2)}, u32[]{:S(2)}) collective-permute-start(bf16[128,1024]{1,0:T(8,128)(2,1)S(1)} %collective-permute-done.3.refs_4_.refs_9_), channel_id=1, source_target_pairs={{0,8},{8,0},{1,9},{9,1},{2,10},{10,2},{3,11},{11,3},{4,12},{12,4},... | collective-permute-start | bytes 786440 | tf_op jit(solution)/shard_map/ppermute | solution.py:411
  51.0 4.0 %collective-permute-start.8 = (bf16[128,1024]{1,0:T(8,128)(2,1)S(1)}, bf16[128,1024]{1,0:T(8,128)(2,1)S(1)}, u32[]{:S(2)}, u32[]{:S(2)}) collective-permute-start(bf16[128,1024]{1,0:T(8,128)(2,1)S(1)} %collective-permute-done.4.refs_5_.refs_10_), channel_id=1, source_target_pairs={{0,8},{8,0},{1,9},{9,1},{2,10},{10,2},{3,11},{11,3},{4,12},{12,4},... | collective-permute-start | bytes 786440 | tf_op jit(solution)/shard_map/ppermute | solution.py:411
  51.0 4.7 %collective-permute-start.9 = (bf16[128,1024]{1,0:T(8,128)(2,1)S(1)}, bf16[128,1024]{1,0:T(8,128)(2,1)}, u32[]{:S(2)}, u32[]{:S(2)}) collective-permute-start(bf16[128,1024]{1,0:T(8,128)(2,1)S(1)} %collective-permute-done.5.refs_6_.refs_11_), channel_id=1, source_target_pairs={{0,8},{8,0},{1,9},{9,1},{2,10},{10,2},{3,11},{11,3},{4,12},{12,4},... | collective-permute-start | bytes 786440 | tf_op jit(solution)/shard_map/ppermute | solution.py:411
  51.5 26.3 %collective-permute-start.10 = (bf16[512,512]{1,0:T(8,128)(2,1)S(1)}, bf16[512,512]{1,0:T(8,128)(2,1)S(1)}, u32[]{:S(2)}, u32[]{:S(2)}) collective-permute-start(bf16[512,512]{1,0:T(8,128)(2,1)S(1)} %get-tuple-element.98.refs_4_.refs_2_), channel_id=1, source_target_pairs={{0,1},{1,0},{16,17},{17,16},{2,3},{3,2},{18,19},{19,18},{4,5},{5,4... | collective-permute-start | bytes 1572872 | tf_op jit(solution)/shard_map/ppermute | solution.py:403
  53.4 26.5 %collective-permute-start.11 = (bf16[512,512]{1,0:T(8,128)(2,1)S(1)}, bf16[512,512]{1,0:T(8,128)(2,1)S(1)}, u32[]{:S(2)}, u32[]{:S(2)}) collective-permute-start(bf16[512,512]{1,0:T(8,128)(2,1)S(1)} %get-tuple-element.98.refs_4_.refs_2_), channel_id=1, source_target_pairs={{0,16},{1,17},{16,0},{17,1},{2,18},{3,19},{18,2},{19,3},{4,20},{5,... | collective-permute-start | bytes 1572872 | tf_op jit(solution)/shard_map/ppermute | solution.py:403
  54.9 29.1 %collective-permute-start.12 = (bf16[512,512]{1,0:T(8,128)(2,1)S(1)}, bf16[512,512]{1,0:T(8,128)(2,1)S(1)}, u32[]{:S(2)}, u32[]{:S(2)}) collective-permute-start(bf16[512,512]{1,0:T(8,128)(2,1)S(1)} %get-tuple-element.98.refs_4_.refs_2_), channel_id=1, source_target_pairs={{0,17},{1,16},{16,1},{17,0},{2,19},{3,18},{18,3},{19,2},{4,21},{5,... | collective-permute-start | bytes 1572872 | tf_op jit(solution)/shard_map/ppermute | solution.py:403
  61.7 7.5 %collective-permute-start.14 = (bf16[32,1024]{1,0:T(8,128)(2,1)S(1)}, bf16[32,1024]{1,0:T(8,128)(2,1)S(1)}, u32[]{:S(2)}, u32[]{:S(2)}) collective-permute-start(bf16[32,1024]{1,0:T(8,128)(2,1)S(1)} %get-tuple-element.104), channel_id=1, source_target_pairs={{0,2},{2,0},{4,6},{6,4},{1,3},{3,1},{5,7},{7,5},{8,10},{10,8},{12,... | collective-permute-start | bytes 196616 | tf_op jit(solution)/shard_map/ppermute | solution.py:398
  66.8 6.4 %collective-permute-start.15 = (bf16[32,1024]{1,0:T(8,128)(2,1)S(1)}, bf16[32,1024]{1,0:T(8,128)(2,1)S(1)}, u32[]{:S(2)}, u32[]{:S(2)}) collective-permute-start(bf16[32,1024]{1,0:T(8,128)(2,1)S(1)} %get-tuple-element.105), channel_id=1, source_target_pairs={{0,4},{2,6},{4,0},{6,2},{1,5},{3,7},{5,1},{7,3},{8,12},{10,14},{12... | collective-permute-start | bytes 196616 | tf_op jit(solution)/shard_map/ppermute | solution.py:398
  69.2 6.1 %collective-permute-start.16 = (bf16[32,1024]{1,0:T(8,128)(2,1)S(1)}, bf16[32,1024]{1,0:T(8,128)(2,1)S(1)}, u32[]{:S(2)}, u32[]{:S(2)}) collective-permute-start(bf16[32,1024]{1,0:T(8,128)(2,1)S(1)} %get-tuple-element.106), channel_id=1, source_target_pairs={{0,6},{2,4},{4,2},{6,0},{1,7},{3,5},{5,3},{7,1},{8,14},{10,12},{12... | collective-permute-start | bytes 196616 | tf_op jit(solution)/shard_map/ppermute | solution.py:398
  75.5 4.5 %collective-permute-start.17 = (bf16[32,1024]{1,0:T(8,128)(2,1)S(1)}, bf16[32,1024]{1,0:T(8,128)(2,1)S(1)}, u32[]{:S(2)}, u32[]{:S(2)}) collective-permute-start(bf16[32,1024]{1,0:T(8,128)(2,1)S(1)} %get-tuple-element.107.refs_6_.refs_4_), channel_id=1, source_target_pairs={{0,2},{2,0},{4,6},{6,4},{1,3},{3,1},{5,7},{7,5},{8,10},{10,8},{12,... | collective-permute-start | bytes 196616 | tf_op jit(solution)/shard_map/ppermute | solution.py:398
  76.7 6.1 %collective-permute-start.18 = (bf16[32,1024]{1,0:T(8,128)(2,1)S(1)}, bf16[32,1024]{1,0:T(8,128)(2,1)S(1)}, u32[]{:S(2)}, u32[]{:S(2)}) collective-permute-start(bf16[32,1024]{1,0:T(8,128)(2,1)S(1)} %get-tuple-element.107.refs_6_.refs_4_), channel_id=1, source_target_pairs={{0,4},{2,6},{4,0},{6,2},{1,5},{3,7},{5,1},{7,3},{8,12},{10,14},{12... | collective-permute-start | bytes 196616 | tf_op jit(solution)/shard_map/ppermute | solution.py:398
  77.8 6.2 %collective-permute-start.19 = (bf16[32,1024]{1,0:T(8,128)(2,1)S(1)}, bf16[32,1024]{1,0:T(8,128)(2,1)S(1)}, u32[]{:S(2)}, u32[]{:S(2)}) collective-permute-start(bf16[32,1024]{1,0:T(8,128)(2,1)S(1)} %get-tuple-element.107.refs_6_.refs_4_), channel_id=1, source_target_pairs={{0,6},{2,4},{4,2},{6,0},{1,7},{3,5},{5,3},{7,1},{8,14},{10,12},{12... | collective-permute-start | bytes 196616 | tf_op jit(solution)/shard_map/ppermute | solution.py:398
  79.9 6.9 %collective-permute-start.20 = (bf16[32,1024]{1,0:T(8,128)(2,1)S(1)}, bf16[32,1024]{1,0:T(8,128)(2,1)S(1)}, u32[]{:S(2)}, u32[]{:S(2)}) collective-permute-start(bf16[32,1024]{1,0:T(8,128)(2,1)S(1)} %get-tuple-element.107.refs_6_.refs_4_), channel_id=1, source_target_pairs={{0,8},{8,0},{1,9},{9,1},{2,10},{10,2},{3,11},{11,3},{4,12},{12,4},... | collective-permute-start | bytes 196616 | tf_op jit(solution)/shard_map/ppermute | solution.py:411
  80.0 6.9 %collective-permute-start.21 = (bf16[32,1024]{1,0:T(8,128)(2,1)S(1)}, bf16[32,1024]{1,0:T(8,128)(2,1)S(1)}, u32[]{:S(2)}, u32[]{:S(2)}) collective-permute-start(bf16[32,1024]{1,0:T(8,128)(2,1)S(1)} %collective-permute-done.17.refs_7_.refs_5_), channel_id=1, source_target_pairs={{0,8},{8,0},{1,9},{9,1},{2,10},{10,2},{3,11},{11,3},{4,12},{12,4},... | collective-permute-start | bytes 196616 | tf_op jit(solution)/shard_map/ppermute | solution.py:411
  82.8 4.1 %collective-permute-start.22 = (bf16[32,1024]{1,0:T(8,128)(2,1)S(1)}, bf16[32,1024]{1,0:T(8,128)(2,1)S(1)}, u32[]{:S(2)}, u32[]{:S(2)}) collective-permute-start(bf16[32,1024]{1,0:T(8,128)(2,1)S(1)} %collective-permute-done.18.refs_8_.refs_6_), channel_id=1, source_target_pairs={{0,8},{8,0},{1,9},{9,1},{2,10},{10,2},{3,11},{11,3},{4,12},{12,4},... | collective-permute-start | bytes 196616 | tf_op jit(solution)/shard_map/ppermute | solution.py:411
  89.9 22.7 %collective-permute-start.36 = (bf16[2,128,1024]{2,1,0:T(8,128)(2,1)S(1)}, bf16[2,128,1024]{2,1,0:T(8,128)(2,1)S(1)}, u32[]{:S(2)}, u32[]{:S(2)}) collective-permute-start(bf16[2,128,1024]{2,1,0:T(8,128)(2,1)S(1)} %get-tuple-element.130.refs_8_), channel_id=1, source_target_pairs={{0,1},{1,0},{2,3},{3,2},{4,5},{5,4},{6,7},{7,6},{8,9},{9,8},{10,11... | collective-permute-start | bytes 1572872 | tf_op jit(solution)/shard_map/ppermute | solution.py:1057
  91.6 21.5 %collective-permute-start.37 = (bf16[2,128,1024]{2,1,0:T(8,128)(2,1)S(1)}, bf16[2,128,1024]{2,1,0:T(8,128)(2,1)S(1)}, u32[]{:S(2)}, u32[]{:S(2)}) collective-permute-start(bf16[2,128,1024]{2,1,0:T(8,128)(2,1)S(1)} %get-tuple-element.134), channel_id=1, source_target_pairs={{0,16},{16,0},{1,17},{17,1},{2,18},{18,2},{3,19},{19,3},{4,20},{20... | collective-permute-start | bytes 1572872 | tf_op jit(solution)/shard_map/ppermute | solution.py:1057
  94.6 5.9 %collective-permute-start.26 = (bf16[32,1024]{1,0:T(8,128)(2,1)S(1)}, bf16[32,1024]{1,0:T(8,128)(2,1)S(1)}, u32[]{:S(2)}, u32[]{:S(2)}) collective-permute-start(bf16[32,1024]{1,0:T(8,128)(2,1)S(1)} %get-tuple-element.125), channel_id=1, source_target_pairs={{0,2},{2,0},{4,6},{6,4},{1,3},{3,1},{5,7},{7,5},{8,10},{10,8},{12,... | collective-permute-start | bytes 196616 | tf_op jit(solution)/shard_map/ppermute | solution.py:398
  95.4 8.3 %collective-permute-start.27 = (bf16[32,1024]{1,0:T(8,128)(2,1)S(1)}, bf16[32,1024]{1,0:T(8,128)(2,1)S(1)}, u32[]{:S(2)}, u32[]{:S(2)}) collective-permute-start(bf16[32,1024]{1,0:T(8,128)(2,1)S(1)} %get-tuple-element.126), channel_id=1, source_target_pairs={{0,4},{2,6},{4,0},{6,2},{1,5},{3,7},{5,1},{7,3},{8,12},{10,14},{12... | collective-permute-start | bytes 196616 | tf_op jit(solution)/shard_map/ppermute | solution.py:398
  97.3 6.5 %collective-permute-start.28 = (bf16[32,1024]{1,0:T(8,128)(2,1)S(1)}, bf16[32,1024]{1,0:T(8,128)(2,1)S(1)}, u32[]{:S(2)}, u32[]{:S(2)}) collective-permute-start(bf16[32,1024]{1,0:T(8,128)(2,1)S(1)} %get-tuple-element.127), channel_id=1, source_target_pairs={{0,6},{2,4},{4,2},{6,0},{1,7},{3,5},{5,3},{7,1},{8,14},{10,12},{12... | collective-permute-start | bytes 196616 | tf_op jit(solution)/shard_map/ppermute | solution.py:398
  103.9 4.5 %collective-permute-start.29 = (bf16[32,1024]{1,0:T(8,128)(2,1)S(1)}, bf16[32,1024]{1,0:T(8,128)(2,1)S(1)}, u32[]{:S(2)}, u32[]{:S(2)}) collective-permute-start(bf16[32,1024]{1,0:T(8,128)(2,1)S(1)} %get-tuple-element.132.refs_10_.refs_8_), channel_id=1, source_target_pairs={{0,2},{2,0},{4,6},{6,4},{1,3},{3,1},{5,7},{7,5},{8,10},{10,8},{12,... | collective-permute-start | bytes 196616 | tf_op jit(solution)/shard_map/ppermute | solution.py:398
  105.2 6.6 %collective-permute-start.30 = (bf16[32,1024]{1,0:T(8,128)(2,1)S(1)}, bf16[32,1024]{1,0:T(8,128)(2,1)S(1)}, u32[]{:S(2)}, u32[]{:S(2)}) collective-permute-start(bf16[32,1024]{1,0:T(8,128)(2,1)S(1)} %get-tuple-element.132.refs_10_.refs_8_), channel_id=1, source_target_pairs={{0,4},{2,6},{4,0},{6,2},{1,5},{3,7},{5,1},{7,3},{8,12},{10,14},{12... | collective-permute-start | bytes 196616 | tf_op jit(solution)/shard_map/ppermute | solution.py:398
  106.4 6.2 %collective-permute-start.31 = (bf16[32,1024]{1,0:T(8,128)(2,1)S(1)}, bf16[32,1024]{1,0:T(8,128)(2,1)S(1)}, u32[]{:S(2)}, u32[]{:S(2)}) collective-permute-start(bf16[32,1024]{1,0:T(8,128)(2,1)S(1)} %get-tuple-element.132.refs_10_.refs_8_), channel_id=1, source_target_pairs={{0,6},{2,4},{4,2},{6,0},{1,7},{3,5},{5,3},{7,1},{8,14},{10,12},{12... | collective-permute-start | bytes 196616 | tf_op jit(solution)/shard_map/ppermute | solution.py:398
  108.3 5.1 %collective-permute-start.32 = (bf16[32,1024]{1,0:T(8,128)(2,1)S(1)}, bf16[32,1024]{1,0:T(8,128)(2,1)S(1)}, u32[]{:S(2)}, u32[]{:S(2)}) collective-permute-start(bf16[32,1024]{1,0:T(8,128)(2,1)S(1)} %get-tuple-element.132.refs_10_.refs_8_), channel_id=1, source_target_pairs={{0,8},{8,0},{1,9},{9,1},{2,10},{10,2},{3,11},{11,3},{4,12},{12,4},... | collective-permute-start | bytes 196616 | tf_op jit(solution)/shard_map/ppermute | solution.py:411
  113.1 5.2 %collective-permute-start.24 = (bf16[4,64,1024]{2,1,0:T(8,128)(2,1)S(1)}, bf16[4,64,1024]{2,1,0:T(8,128)(2,1)S(1)}, u32[]{:S(2)}, u32[]{:S(2)}) collective-permute-start(bf16[4,64,1024]{2,1,0:T(8,128)(2,1)S(1)} %get-tuple-element.115), channel_id=1, source_target_pairs={{0,8},{8,0},{1,9},{9,1},{2,10},{10,2},{3,11},{11,3},{4,12},{12,4},... | collective-permute-start | bytes 1572872 | tf_op jit(solution)/shard_map/ppermute | solution.py:411
  120.1 13.5 %collective-permute-start.39 = (bf16[128,1024]{1,0:T(8,128)(2,1)S(1)}, bf16[128,1024]{1,0:T(8,128)(2,1)S(1)}, u32[]{:S(2)}, u32[]{:S(2)}) collective-permute-start(bf16[128,1024]{1,0:T(8,128)(2,1)S(1)} %get-tuple-element.139), channel_id=1, source_target_pairs={{0,2},{2,0},{4,6},{6,4},{1,3},{3,1},{5,7},{7,5},{8,10},{10,8},{12,... | collective-permute-start | bytes 786440 | tf_op jit(solution)/shard_map/ppermute | solution.py:398
  121.4 21.3 %collective-permute-start.40 = (bf16[128,1024]{1,0:T(8,128)(2,1)S(1)}, bf16[128,1024]{1,0:T(8,128)(2,1)S(1)}, u32[]{:S(2)}, u32[]{:S(2)}) collective-permute-start(bf16[128,1024]{1,0:T(8,128)(2,1)S(1)} %get-tuple-element.140), channel_id=1, source_target_pairs={{0,4},{2,6},{4,0},{6,2},{1,5},{3,7},{5,1},{7,3},{8,12},{10,14},{12... | collective-permute-start | bytes 786440 | tf_op jit(solution)/shard_map/ppermute | solution.py:398
  122.6 20.6 %collective-permute-start.41 = (bf16[128,1024]{1,0:T(8,128)(2,1)S(1)}, bf16[128,1024]{1,0:T(8,128)(2,1)S(1)}, u32[]{:S(2)}, u32[]{:S(2)}) collective-permute-start(bf16[128,1024]{1,0:T(8,128)(2,1)S(1)} %get-tuple-element.141), channel_id=1, source_target_pairs={{0,6},{2,4},{4,2},{6,0},{1,7},{3,5},{5,3},{7,1},{8,14},{10,12},{12... | collective-permute-start | bytes 786440 | tf_op jit(solution)/shard_map/ppermute | solution.py:398
  126.3 23.4 %collective-permute-start.47 = (bf16[320,512]{1,0:T(8,128)(2,1)S(1)}, bf16[320,512]{1,0:T(8,128)(2,1)S(1)}, u32[]{:S(2)}, u32[]{:S(2)}) collective-permute-start(bf16[320,512]{1,0:T(8,128)(2,1)S(1)} %get-tuple-element.155), channel_id=1, source_target_pairs={{0,1},{1,0},{16,17},{17,16},{2,3},{3,2},{18,19},{19,18},{4,5},{5,4... | collective-permute-start | bytes 983048 | tf_op jit(solution)/shard_map/ppermute | solution.py:403
  126.9 22.7 %collective-permute-start.48 = (bf16[320,512]{1,0:T(8,128)(2,1)S(1)}, bf16[320,512]{1,0:T(8,128)(2,1)S(1)}, u32[]{:S(2)}, u32[]{:S(2)}) collective-permute-start(bf16[320,512]{1,0:T(8,128)(2,1)S(1)} %get-tuple-element.156), channel_id=1, source_target_pairs={{0,16},{1,17},{16,0},{17,1},{2,18},{3,19},{18,2},{19,3},{4,20},{5,... | collective-permute-start | bytes 983048 | tf_op jit(solution)/shard_map/ppermute | solution.py:403
  133.6 16.1 %collective-permute-start.49 = (bf16[320,512]{1,0:T(8,128)(2,1)S(1)}, bf16[320,512]{1,0:T(8,128)(2,1)S(1)}, u32[]{:S(2)}, u32[]{:S(2)}) collective-permute-start(bf16[320,512]{1,0:T(8,128)(2,1)S(1)} %get-tuple-element.157), channel_id=1, source_target_pairs={{0,17},{1,16},{16,1},{17,0},{2,19},{3,18},{18,3},{19,2},{4,21},{5,... | collective-permute-start | bytes 983048 | tf_op jit(solution)/shard_map/ppermute | solution.py:403
  142.7 6.4 %collective-permute-start.45 = (bf16[128,1024]{1,0:T(8,128)(2,1)S(1)}, bf16[128,1024]{1,0:T(8,128)(2,1)S(1)}, u32[]{:S(2)}, u32[]{:S(2)}) collective-permute-start(bf16[128,1024]{1,0:T(8,128)(2,1)S(1)} %get-tuple-element.148), channel_id=1, source_target_pairs={{0,16},{16,0},{1,17},{17,1},{2,18},{18,2},{3,19},{19,3},{4,20},{20... | collective-permute-start | bytes 786440 | tf_op jit(solution)/shard_map/ppermute | solution.py:1059
  143.3 6.4 %collective-permute-start.46 = (bf16[128,1024]{1,0:T(8,128)(2,1)S(1)}, bf16[128,1024]{1,0:T(8,128)(2,1)S(1)}, u32[]{:S(2)}, u32[]{:S(2)}) collective-permute-start(bf16[128,1024]{1,0:T(8,128)(2,1)S(1)} %get-tuple-element.149), channel_id=1, source_target_pairs={{0,1},{1,0},{2,3},{3,2},{4,5},{5,4},{6,7},{7,6},{8,9},{9,8},{10,11... | collective-permute-start | bytes 786440 | tf_op jit(solution)/shard_map/ppermute | solution.py:1059
  151.5 10.4 %collective-permute-start.42 = (bf16[32,1024]{1,0:T(8,128)(2,1)S(1)}, bf16[32,1024]{1,0:T(8,128)(2,1)S(1)}, u32[]{:S(2)}, u32[]{:S(2)}) collective-permute-start(bf16[32,1024]{1,0:T(8,128)(2,1)S(1)} %get-tuple-element.143), channel_id=1, source_target_pairs={{0,1},{1,0},{16,17},{17,16},{2,3},{3,2},{18,19},{19,18},{4,5},{5,4... | collective-permute-start | bytes 196616 | tf_op jit(solution)/shard_map/ppermute | solution.py:403
  153.0 16.7 %collective-permute-start.51 = (bf16[64,1024]{1,0:T(8,128)(2,1)S(1)}, bf16[64,1024]{1,0:T(8,128)(2,1)S(1)}, u32[]{:S(2)}, u32[]{:S(2)}) collective-permute-start(bf16[64,1024]{1,0:T(8,128)(2,1)S(1)} %get-tuple-element.161), channel_id=1, source_target_pairs={{0,2},{2,0},{4,6},{6,4},{1,3},{3,1},{5,7},{7,5},{8,10},{10,8},{12,... | collective-permute-start | bytes 393224 | tf_op jit(solution)/shard_map/ppermute | solution.py:398
  158.9 12.9 %collective-permute-start.52 = (bf16[64,1024]{1,0:T(8,128)(2,1)S(1)}, bf16[64,1024]{1,0:T(8,128)(2,1)S(1)}, u32[]{:S(2)}, u32[]{:S(2)}) collective-permute-start(bf16[64,1024]{1,0:T(8,128)(2,1)S(1)} %get-tuple-element.162), channel_id=1, source_target_pairs={{0,4},{2,6},{4,0},{6,2},{1,5},{3,7},{5,1},{7,3},{8,12},{10,14},{12... | collective-permute-start | bytes 393224 | tf_op jit(solution)/shard_map/ppermute | solution.py:398
  159.5 12.3 %collective-permute-start.53 = (bf16[64,1024]{1,0:T(8,128)(2,1)S(1)}, bf16[64,1024]{1,0:T(8,128)(2,1)S(1)}, u32[]{:S(2)}, u32[]{:S(2)}) collective-permute-start(bf16[64,1024]{1,0:T(8,128)(2,1)S(1)} %get-tuple-element.163), channel_id=1, source_target_pairs={{0,6},{2,4},{4,2},{6,0},{1,7},{3,5},{5,3},{7,1},{8,14},{10,12},{12... | collective-permute-start | bytes 393224 | tf_op jit(solution)/shard_map/ppermute | solution.py:398
  161.3 4.8 %collective-permute-start.43 = (bf16[32,1024]{1,0:T(8,128)(2,1)S(1)}, bf16[32,1024]{1,0:T(8,128)(2,1)S(1)}, u32[]{:S(2)}, u32[]{:S(2)}) collective-permute-start(bf16[32,1024]{1,0:T(8,128)(2,1)S(1)} %get-tuple-element.144), channel_id=1, source_target_pairs={{0,16},{1,17},{16,0},{17,1},{2,18},{3,19},{18,2},{19,3},{4,20},{5,... | collective-permute-start | bytes 196616 | tf_op jit(solution)/shard_map/ppermute | solution.py:403
  161.9 5.2 %collective-permute-start.44 = (bf16[32,1024]{1,0:T(8,128)(2,1)S(1)}, bf16[32,1024]{1,0:T(8,128)(2,1)S(1)}, u32[]{:S(2)}, u32[]{:S(2)}) collective-permute-start(bf16[32,1024]{1,0:T(8,128)(2,1)S(1)} %get-tuple-element.145), channel_id=1, source_target_pairs={{0,17},{1,16},{16,1},{17,0},{2,19},{3,18},{18,3},{19,2},{4,21},{5,... | collective-permute-start | bytes 196616 | tf_op jit(solution)/shard_map/ppermute | solution.py:403
  (19 other events, 105.9 us)

commit v5 on v4

--- a/solution.py
+++ b/solution.py
@@ -292,8 +292,19 @@
 
 
 class Far:
-    def __init__(self, item, rows=None, start=0):
-        self.item, self.rows, self.start = item, rows, start
+    def __init__(self, item, start=0, count=None, dim=0):
+        self.item, self.start, self.count, self.dim = item, start, count, dim
+
+    def shape(self):
+        shape = list(self.item.shape)
+        if self.count is not None:
+            shape[self.dim] = self.count
+        return tuple(shape)
+
+    def source(self, ref):
+        if self.count is None:
+            return ref
+        return ref.at[(slice(None),) * self.dim + (pl.ds(self.start, self.count),)]
 
 
 class Loaded:
@@ -340,8 +351,7 @@
     stages = []
     for f in far_in:
         if f:
-            shape = f.item.shape if f.rows is None else (f.rows,) + f.item.shape[1:]
-            stages.append(pltpu.VMEM(shape, f.item.dtype))
+            stages.append(pltpu.VMEM(f.shape(), f.item.dtype))
     stages += [pltpu.VMEM(s, d) for (s, d), f in zip(outs, far_out) if f]
     n_in, n_out, n_far = len(args), len(outs), len(stages)
     first_out = n_in + len(after)
@@ -355,8 +365,7 @@
         at, loads, stores = 0, [], []
         for i, f in enumerate(far_in):
             if f:
-                source = ins[i] if f.rows is None else ins[i].at[pl.ds(f.start, f.rows)]
-                copy = pltpu.make_async_copy(source, stage[at], stage[-1].at[at])
+                copy = pltpu.make_async_copy(f.source(ins[i]), stage[at], stage[-1].at[at])
                 copy.start()
                 ins[i] = Loaded(copy, stage[at])
                 loads.append(ins[i])
@@ -516,21 +525,18 @@
             out[to : to + cap] = block[j * cap : (j + 1) * cap]
 
 
-def relay_kernel(got, w_out, w_down, first, second):
+def relay_kernel(got, w_out, w_down, first, up):
     members, rows, lanes = got.shape
     half = lanes // 2
     for line in range(first.shape[0]):
-        for g in range(members):
-            first[line, g * rows : (g + 1) * rows] = got[g, :, :half]
-        for j in range(2):
-            to = (members + j) * rows
-            first[line, to : to + rows] = w_out[:, j * half : (j + 1) * half]
-    size = w_down.shape[0]
-    for g in range(members):
-        second[g * rows : (g + 1) * rows] = got[g, :, half:]
-    for j in range(2):
-        to = members * rows + j * size
-        second[to : to + size] = w_down[:, j * half : (j + 1) * half]
+        at = members * rows
+        first[line, :at] = got[:, :, :half].reshape(at, half)
+        for block in (w_out, w_down):
+            size = block.shape[0]
+            for j in range(2):
+                first[line, at : at + size] = block[:, j * half : (j + 1) * half]
+                at += size
+    up[...] = got[:, :, half:].reshape(members * rows, half)
 
 
 def spread_kernel(dims, where, chosen, chosen_t, spread):
@@ -590,16 +596,6 @@
         for j in range(2):
             piece = blocks[q, start + j * size : start + (j + 1) * size]
             out[q * size : (q + 1) * size, j * half : (j + 1) * half] = piece
-
-
-def own_line_rows(where, blocks, start, out):
-    half = out.shape[1] // 2
-    size = out.shape[0] // len(blocks)
-    for k, block in enumerate(blocks):
-        to = pl.ds(pl.multiple_of((where[2] ^ k) * size, size), size)
-        for j in range(2):
-            piece = block[start + j * size : start + (j + 1) * size]
-            out[to, j * half : (j + 1) * half] = piece
 
 
 def own_order_rows(where, blocks, dims, out):
@@ -667,9 +663,7 @@
         far[k] = values[(depth + k) * own : (depth + k + 1) * own]
 
 
-def update_kernel(dims, where, spread, picked, vecs, *refs):
-    lines, members, start = dims
-    downs, refs = refs[:lines], refs[lines:]
+def update_kernel(members, spread, picked, vecs, downs, *refs):
     blocks, outs = refs[:members], refs[members:]
     gate_o, cot_o, first_o, d_result_o, d_active_o, w_o = outs
     logit = jnp.sum(picked[...].astype(F32) * vecs[2:3, :], 1, keepdims=True)
@@ -680,7 +674,7 @@
     first_o[...] = cot[: first_o.shape[0]]
     d_result = (gate * cot.astype(F32)).astype(BF16)
     d_result_o[...] = d_result
-    own_line_rows(where, downs, start, w_o)
+    line_rows(downs, 0, w_o)
     d_active_o[...] = mm(d_result, w_o[...], NT)
 
 
@@ -954,7 +948,7 @@
     )
     slots = gather_group([line_slots])
     half = lines * cap
-    picked_slots, cot_slots = [Far(b, half) for b in slots], [Far(b, half, half) for b in slots]
+    picked_slots, cot_slots = [Far(b, 0, half) for b in slots], [Far(b, half, half) for b in slots]
 
     vecs = [v.reshape(1, rows) for v in (gain_attn, gain_mlp, router)]
     (columns,) = local_call(
@@ -964,17 +958,17 @@
         scratch=[pltpu.VMEM((8, rows), F32)],
     )
     got_cols = lax.all_to_all(columns, ("c", "z"), 0, 0, tiled=True)
-    first, second = local_call(
+    half = width // 2
+    base = members * rows + 2 * rows
+    first, up = local_call(
         relay_kernel,
-        [
-            Far(((lines, members * rows + 2 * rows, width // 2), BF16)),
-            ((members * rows + 2 * ff_rows, width // 2), BF16),
-        ],
+        [Far(((lines, base + 2 * ff_rows, half), BF16)), ((members * rows, half), BF16)],
         (got_cols, w_out, w_down),
         after=(line_slots,),
     )
     first = lax.all_to_all(first, ("y", "x"), 0, 0, tiled=True)
-    second = gather_lines(second)
+    got_down = Far(first, base, 2 * ff_rows, 1)
+    got_up = gather_lines(up)
 
     picked, normed, full_qkv, picked_own, full_out, full_vecs, joined, attended, exact, near, far = (
         local_call(
@@ -991,7 +985,7 @@
                 ((routed, heads * HDIM), F32),
             ]
             + halves,
-            (where, spread, Far(first), *picked_slots),
+            (where, spread, Far(first, 0, base, 1), *picked_slots),
             flops=1.2e9,
             scratch=[pltpu.VMEM((width, 128), BF16)],
             scalars=1,
@@ -999,7 +993,7 @@
     )
     terms = scatter_group(near, far)
     gate, cot, cot_own, d_result, d_active, full_down = local_call(
-        partial(update_kernel, (lines, members, members * rows)),
+        partial(update_kernel, members),
         [
             ((routed, 1), F32),
             ((routed, width), BF16),
@@ -1008,21 +1002,21 @@
             ((routed, wide), F32),
             ((wide, width), BF16),
         ],
-        (where, spread, picked, full_vecs, *second, *cot_slots),
+        (spread, picked, full_vecs, got_down, *cot_slots),
         flops=8e8,
-        scalars=1,
     )
     hidden, normed_own = local_call(
         hidden_kernel,
         [(block, F32), (block, BF16)],
         (picked_own, full_vecs, *terms),
+        after=(d_active,),
     )
     normed_mlp = gather_group([normed_own])
 
     active, d_upper, near, far = local_call(
         partial(forward_kernel, (ny, members, nx, rows), members),
         [((routed, wide), BF16)] * 2 + halves,
-        (where, d_active, *second, *normed_mlp),
+        (where, d_active, *got_up, *normed_mlp),
         flops=6e8,
         scratch=[pltpu.VMEM((width, wide), BF16)],
         scalars=1,
@@ -1065,7 +1059,6 @@
         + (logit, d_hidden, spread, *d_branch),
         flops=1.2e9,
         scalars=1,
-        after=(ff_mine,),
     )
     far = send_c(far)
     parts = local_call(

time: 174 us -> 169 us (0.971)
  waiting for transfers between devices: 74.1 us -> 70.8 us
  starting transfers between devices: 65.5 us -> 63.4 us
    ppermute x21, waiting for transfers between devices: 51.5 us -> 36.8 us  [send_z(): lax.ppermute(b, 'z', f)]
    ppermute x21, starting transfers between devices: 37.8 us -> 30.7 us  [send_z(): lax.ppermute(b, 'z', f)]
    ppermute x2, waiting for transfers between devices: 0.56 us -> 6.01 us  [grouped(): lax.ppermute(ff_x, 'x', flips(nx)[1])]
    all_to_all x1, waiting for transfers between devices: 0.01 us -> 5.11 us  [grouped(): first = lax.all_to_all(first, ('y', 'x'), 0, 0, tiled=True)]
    ppermute x12, waiting for transfers between devices: 6.58 us -> 11.5 us  [send_lines(): lax.ppermute(b, ('y', 'x'), f)]
    ppermute x12, starting transfers between devices: 10.9 us -> 14.6 us  [send_lines(): lax.ppermute(b, ('y', 'x'), f)]
    ppermute x17, waiting for transfers between devices: 6.37 us -> 4.27 us  [send_c(): return lax.ppermute(block, 'c', flips(2)[1])]
  transfers between devices with their start and end apart: 56 -> 56, of which waited for: 27 -> 26; matrix products, arithmetic and copies ran while one was open for 0% -> 1% of each run, Pallas kernels for 12% -> 11%
where the time goes in v5:
time: 169 us; the launch traced here: 168 us
  waiting for transfers between devices  70.8 us (42%)
  starting transfers between devices  63.4 us (38%)
  Pallas kernels  31.1 us (18%)
  local copies, waits for them, and re-layouts  1.91 us (1%)
    ppermute x21, waiting for transfers between devices, send_z(): lax.ppermute(b, 'z', f)  36.8 us
    pallas_call x23, Pallas kernels, local_call(): pl.pallas_call(run, out_shape=shapes, in_specs=[pl.BlockSpec(memory_space...  31.1 us
    ppermute x21, starting transfers between devices, send_z(): lax.ppermute(b, 'z', f)  30.7 us
    ppermute x12, starting transfers between devices, send_lines(): lax.ppermute(b, ('y', 'x'), f)  14.6 us
    ppermute x12, waiting for transfers between devices, send_lines(): lax.ppermute(b, ('y', 'x'), f)  11.5 us
    all_to_all x1, starting transfers between devices, grouped(): got_cols = lax.all_to_all(columns, ('c', 'z'), 0, 0, tiled=True)  6.34 us
    ppermute x2, waiting for transfers between devices, grouped(): lax.ppermute(ff_x, 'x', flips(nx)[1])  6.01 us
    all_to_all x1, waiting for transfers between devices, grouped(): first = lax.all_to_all(first, ('y', 'x'), 0, 0, tiled=True)  5.11 us
  transfers between devices with their start and end apart: 56, of which 26 were waited for; matrix products, arithmetic and copies ran while one was open for 1% of the time, Pallas kernels for 11%

profile of v5, /device:TPU:0, one launch (start us, length us, event | category | flops | bytes accessed | tf_op | source)
XLA Modules:
  0.0 168.3 jit_solution(6542419791816714711)
XLA Ops:
  0.7 2.2 %shard_map.171 = bf16[8,32,1024]{2,1,0:T(8,128)(2,1)} custom-call(bf16[32,3072]{1,0:T(8,128)(2,1)} %refs_0_.1, bf16[32,4096]{1,0:T(8,128)(2,1)} %refs_1_.4, bf16[1,32]{1,0:T(2,128)(2,1)} %bitcast.14, bf16[1,32]{1,0:T(2,128)(2,1)} %bitcast.15, bf16[1,32]{1,0:T(2,128)(2,1)} %bitcast.16), custom_call_target="tpu_custom_call" | custom-call | tf_op jit(solution)/shard_map/pallas_call | solution.py:388
  2.9 6.3 %all-to-all-start = ((bf16[8,32,1024]{2,1,0:T(8,128)(2,1)}), bf16[8,32,1024]{2,1,0:T(8,128)(2,1)S(1)}, u32[]{:S(2)}, u32[]{:S(2)}) async-start(bf16[8,32,1024]{2,1,0:T(8,128)(2,1)} %shard_map.171), calls=%async_computation | async-start | bytes 1048576 | tf_op jit(solution)/shard_map/all_to_all | solution.py:960
  10.1 1.5 shard_map.169
  11.7 1.6 collective-permute-start
  13.2 1.5 collective-permute-start.1
  15.2 1.8 %shard_map.170.refs_4_.refs_1_.refs_0_.refs_6_.refs_9_ = bf16[256,512]{1,0:T(8,128)(2,1)} custom-call(s32[5]{0:T(128)S(1)} %stack.23.refs_0_, s32[4,256]{1,0:T(4,128)S(1)} %copy-done.6, s32[256,4]{1,0:T(8,128)S(1)} %bitcast.13), custom_call_target="tpu_custom_call" | custom-call | tf_op jit(solution)/shard_map/pallas_call | solution.py:388
  17.5 2.4 %collective-permute-done.2.refs_3_ = bf16[32,1024]{1,0:T(8,128)(2,1)S(1)} collective-permute-done((bf16[32,1024]{1,0:T(8,128)(2,1)S(1)}, bf16[32,1024]{1,0:T(8,128)(2,1)S(1)}, u32[]{:S(2)}, u32[]{:S(2)}) %collective-permute-start.2) | collective-permute-done | bytes 65568 | tf_op jit(solution)/shard_map/ppermute | solution.py:412
  20.9 3.2 %all-to-all-done.refs_0_ = bf16[8,32,1024]{2,1,0:T(8,128)(2,1)S(1)} async-done(((bf16[8,32,1024]{2,1,0:T(8,128)(2,1)}), bf16[8,32,1024]{2,1,0:T(8,128)(2,1)S(1)}, u32[]{:S(2)}, u32[]{:S(2)}) %all-to-all-start) | async-done | bytes 524320 | tf_op jit(solution)/shard_map/all_to_all | solution.py:960
  24.1 1.6 shard_map.173
  25.7 4.5 %all-to-all-start.1 = ((bf16[4,576,512]{2,1,0:T(8,128)(2,1)}), bf16[4,576,512]{2,1,0:T(8,128)(2,1)}, u32[]{:S(2)}, u32[]{:S(2)}) async-start(bf16[4,576,512]{2,1,0:T(8,128)(2,1)} %get-tuple-element.95), calls=%async_computation.1 | async-start | bytes 4718592 | tf_op jit(solution)/shard_map/all_to_all | solution.py:969
  31.5 3.2 %collective-permute-start.5 = (bf16[128,1024]{1,0:T(8,128)(2,1)S(1)}, bf16[128,1024]{1,0:T(8,128)(2,1)S(1)}, u32[]{:S(2)}, u32[]{:S(2)}) collective-permute-start(bf16[128,1024]{1,0:T(8,128)(2,1)S(1)} %shard_map.172.refs_3_.refs_4_), channel_id=1, source_target_pairs={{0,6},{2,4},{4,2},{6,0},{1,7},{3,5},{5,3},{7,1},{8,14},{10,12},{12... | collective-permute-start | bytes 786440 | tf_op jit(solution)/shard_map/ppermute | solution.py:407
  34.7 8.9 %collective-permute-done.3.refs_4_.refs_5_ = bf16[128,1024]{1,0:T(8,128)(2,1)S(1)} collective-permute-done((bf16[128,1024]{1,0:T(8,128)(2,1)S(1)}, bf16[128,1024]{1,0:T(8,128)(2,1)S(1)}, u32[]{:S(2)}, u32[]{:S(2)}) %collective-permute-start.3) | collective-permute-done | bytes 262176 | tf_op jit(solution)/shard_map/ppermute | solution.py:407
  43.6 8.1 %collective-permute-done.4.refs_5_.refs_6_ = bf16[128,1024]{1,0:T(8,128)(2,1)S(1)} collective-permute-done((bf16[128,1024]{1,0:T(8,128)(2,1)S(1)}, bf16[128,1024]{1,0:T(8,128)(2,1)S(1)}, u32[]{:S(2)}, u32[]{:S(2)}) %collective-permute-start.4) | collective-permute-done | bytes 262176 | tf_op jit(solution)/shard_map/ppermute | solution.py:407
  53.6 5.1 %all-to-all-done.1.refs_2_.refs_3_ = bf16[4,576,512]{2,1,0:T(8,128)(2,1)} async-done(((bf16[4,576,512]{2,1,0:T(8,128)(2,1)}), bf16[4,576,512]{2,1,0:T(8,128)(2,1)}, u32[]{:S(2)}, u32[]{:S(2)}) %all-to-all-start.1) | async-done | bytes 2359328 | tf_op jit(solution)/shard_map/all_to_all | solution.py:969
  58.8 4.2 %shard_map.174 = (bf16[256,1024]{1,0:T(8,128)(2,1)S(1)}, bf16[256,1024]{1,0:T(8,128)(2,1)S(1)}, bf16[1024,384]{1,0:T(8,128)(2,1)S(1)}, bf16[32,1024]{1,0:T(8,128...) custom-call(s32[5]{0:T(128)S(1)} %stack.23.refs_0_, ...), custom_call_target="tpu_custom_call" | custom-call | flops 1200000000 | tf_op jit(solution)/shard_map/pallas_call | solution.py:388
  63.1 1.5 collective-permute-start.10
  65.2 1.9 %collective-permute-start.14 = (bf16[32,1024]{1,0:T(8,128)(2,1)S(1)}, bf16[32,1024]{1,0:T(8,128)(2,1)S(1)}, u32[]{:S(2)}, u32[]{:S(2)}) collective-permute-start(bf16[32,1024]{1,0:T(8,128)(2,1)S(1)} %get-tuple-element.104), channel_id=1, source_target_pairs={{0,2},{2,0},{4,6},{6,4},{1,3},{3,1},{5,7},{7,5},{8,10},{10,8},{12,... | collective-permute-start | bytes 196616 | tf_op jit(solution)/shard_map/ppermute | solution.py:407
  69.5 1.6 collective-permute-start.16
  71.2 2.7 %shard_map.175 = (f32[256,1]{1,0:T(8,128)S(1)}, bf16[256,1024]{1,0:T(8,128)(2,1)S(1)}, bf16[32,1024]{1,0:T(8,128)(2,1)S(1)}, bf16[256,1024]{1,0:T(8,128)(2,1)S(1...) custom-call(bf16[256,512]{1,0:T(8,128)(2,1)} %shard_map.170.refs_4_.refs_1_.refs_0_.refs_6_.refs_9_, ...), custom_call_target="tpu_custom_call" | custom-call | flops 800000000 | tf_op jit(solution)/shard_map/pallas_call | solution.py:388
  73.9 2.0 %collective-permute-done.15.refs_4_ = bf16[32,1024]{1,0:T(8,128)(2,1)S(1)} collective-permute-done((bf16[32,1024]{1,0:T(8,128)(2,1)S(1)}, bf16[32,1024]{1,0:T(8,128)(2,1)S(1)}, u32[]{:S(2)}, u32[]{:S(2)}) %collective-permute-start.15) | collective-permute-done | bytes 65568 | tf_op jit(solution)/shard_map/ppermute | solution.py:407
  78.3 2.2 %collective-permute-start.19 = (bf16[32,1024]{1,0:T(8,128)(2,1)S(1)}, bf16[32,1024]{1,0:T(8,128)(2,1)S(1)}, u32[]{:S(2)}, u32[]{:S(2)}) collective-permute-start(bf16[32,1024]{1,0:T(8,128)(2,1)S(1)} %get-tuple-element.107.refs_6_.refs_4_), channel_id=1, source_target_pairs={{0,6},{2,4},{4,2},{6,0},{1,7},{3,5},{5,3},{7,1},{8,14},{10,12},{12... | collective-permute-start | bytes 196616 | tf_op jit(solution)/shard_map/ppermute | solution.py:407
  81.0 3.8 %collective-permute-done.18.refs_8_.refs_6_ = bf16[32,1024]{1,0:T(8,128)(2,1)S(1)} collective-permute-done((bf16[32,1024]{1,0:T(8,128)(2,1)S(1)}, bf16[32,1024]{1,0:T(8,128)(2,1)S(1)}, u32[]{:S(2)}, u32[]{:S(2)}) %collective-permute-start.18) | collective-permute-done | bytes 65568 | tf_op jit(solution)/shard_map/ppermute | solution.py:407
  86.2 1.6 shard_map.178
  90.6 1.4 collective-permute-start.27
  92.0 1.9 %collective-permute-start.28 = (bf16[32,1024]{1,0:T(8,128)(2,1)S(1)}, bf16[32,1024]{1,0:T(8,128)(2,1)S(1)}, u32[]{:S(2)}, u32[]{:S(2)}) collective-permute-start(bf16[32,1024]{1,0:T(8,128)(2,1)S(1)} %get-tuple-element.127), channel_id=1, source_target_pairs={{0,6},{2,4},{4,2},{6,0},{1,7},{3,5},{5,3},{7,1},{8,14},{10,12},{12... | collective-permute-start | bytes 196616 | tf_op jit(solution)/shard_map/ppermute | solution.py:407
  93.9 1.4 shard_map.179
  96.8 2.1 %collective-permute-done.27.refs_6_ = bf16[32,1024]{1,0:T(8,128)(2,1)S(1)} collective-permute-done((bf16[32,1024]{1,0:T(8,128)(2,1)S(1)}, bf16[32,1024]{1,0:T(8,128)(2,1)S(1)}, u32[]{:S(2)}, u32[]{:S(2)}) %collective-permute-start.27) | collective-permute-done | bytes 65568 | tf_op jit(solution)/shard_map/ppermute | solution.py:407
  101.6 1.9 %collective-permute-start.31 = (bf16[32,1024]{1,0:T(8,128)(2,1)S(1)}, bf16[32,1024]{1,0:T(8,128)(2,1)S(1)}, u32[]{:S(2)}, u32[]{:S(2)}) collective-permute-start(bf16[32,1024]{1,0:T(8,128)(2,1)S(1)} %get-tuple-element.132.refs_10_.refs_8_), channel_id=1, source_target_pairs={{0,6},{2,4},{4,2},{6,0},{1,7},{3,5},{5,3},{7,1},{8,14},{10,12},{12... | collective-permute-start | bytes 196616 | tf_op jit(solution)/shard_map/ppermute | solution.py:407
  104.0 2.8 %collective-permute-done.30.refs_12_.refs_10_ = bf16[32,1024]{1,0:T(8,128)(2,1)S(1)} collective-permute-done((bf16[32,1024]{1,0:T(8,128)(2,1)S(1)}, bf16[32,1024]{1,0:T(8,128)(2,1)S(1)}, u32[]{:S(2)}, u32[]{:S(2)}) %collective-permute-start.30) | collective-permute-done | bytes 65568 | tf_op jit(solution)/shard_map/ppermute | solution.py:407
  109.1 3.9 %shard_map.183 = (bf16[4,64,1024]{2,1,0:T(8,128)(2,1)S(1)}, bf16[4,64,1024]{2,1,0:T(8,128)(2,1)S(1)}, bf16[256,384]{1,0:T(8,128)(2,1)S(1)}, bf16[256,1024]{1,0:T(8,128)(2,1)S(1)}) custom-call(s32[5]{0:T(128)S(1)} %stack.23.refs_0_, bf16[128,1024]{1,0:T(8,128)(2,1)S(1)} %get-tuple-element.111.refs_3_.refs_1_, ...), custom_call_target="tpu_custom_call" | custom-call | flops 1200000000 | tf_op jit(solution)/shard_map/pallas_call | solution.py:388
  113.4 1.4 collective-permute-start.44
  116.2 1.9 %collective-permute-start.38 = (bf16[128,1024]{1,0:T(8,128)(2,1)S(1)}, bf16[128,1024]{1,0:T(8,128)(2,1)S(1)}, u32[]{:S(2)}, u32[]{:S(2)}) collective-permute-start(bf16[128,1024]{1,0:T(8,128)(2,1)S(1)} %get-tuple-element.137), channel_id=1, source_target_pairs={{0,4},{2,6},{4,0},{6,2},{1,5},{3,7},{5,1},{7,3},{8,12},{10,14},{12... | collective-permute-start | bytes 786440 | tf_op jit(solution)/shard_map/ppermute | solution.py:407
  118.1 1.5 collective-permute-start.39
  119.6 1.7 %shard_map.188 = (bf16[320,512]{1,0:T(8,128)(2,1)S(1)}, bf16[320,512]{1,0:T(8,128)(2,1)S(1)}, bf16[320,512]{1,0:T(8,128)(2,1)S(1)}, bf16[320,512]{1,0:T(8,128)(2,1)S(1)}) custom-call(s32[5]{0:T(128)S(1)} %stack.23.refs_0_, bf16[256,1024]{1,0:T(8,128)(2,1)S(1)} %get-tuple-element.150.refs_1_, bf16[256,384]{1,0:T(8,128)(2,1)S(1)} %get-tuple-element.151.refs_2_, ...), custom_call_target="tpu_custom_call" | custom-call | flops 500000000 | tf_op jit(solution)/shard_map/pallas_call | solution.py:388
  121.3 6.0 %collective-permute-done.43.refs_1_ = bf16[2,128,1024]{2,1,0:T(8,128)(2,1)S(1)} collective-permute-done((bf16[2,128,1024]{2,1,0:T(8,128)(2,1)S(1)}, bf16[2,128,1024]{2,1,0:T(8,128)(2,1)S(1)}, u32[]{:S(2)}, u32[]{:S(2)}) %collective-permute-start.43) | collective-permute-done | bytes 524320 | tf_op jit(solution)/shard_map/ppermute | solution.py:1051
  129.0 1.8 %collective-permute-start.49 = (bf16[320,512]{1,0:T(8,128)(2,1)S(1)}, bf16[320,512]{1,0:T(8,128)(2,1)S(1)}, u32[]{:S(2)}, u32[]{:S(2)}) collective-permute-start(bf16[320,512]{1,0:T(8,128)(2,1)S(1)} %get-tuple-element.157), channel_id=1, source_target_pairs={{0,17},{1,16},{16,1},{17,0},{2,19},{3,18},{18,3},{19,2},{4,21},{5,... | collective-permute-start | bytes 983048 | tf_op jit(solution)/shard_map/ppermute | solution.py:412
  131.1 6.5 %collective-permute-done.38.refs_2_ = bf16[128,1024]{1,0:T(8,128)(2,1)S(1)} collective-permute-done((bf16[128,1024]{1,0:T(8,128)(2,1)S(1)}, bf16[128,1024]{1,0:T(8,128)(2,1)S(1)}, u32[]{:S(2)}, u32[]{:S(2)}) %collective-permute-start.38) | collective-permute-done | bytes 262176 | tf_op jit(solution)/shard_map/ppermute | solution.py:407
  138.3 1.5 collective-permute-start.46
  140.0 5.3 %collective-permute-done.48.refs_6_ = bf16[320,512]{1,0:T(8,128)(2,1)S(1)} collective-permute-done((bf16[320,512]{1,0:T(8,128)(2,1)S(1)}, bf16[320,512]{1,0:T(8,128)(2,1)S(1)}, u32[]{:S(2)}, u32[]{:S(2)}) %collective-permute-start.48) | collective-permute-done | bytes 327712 | tf_op jit(solution)/shard_map/ppermute | solution.py:412
  145.3 3.9 %collective-permute-done.45.refs_2_ = bf16[128,1024]{1,0:T(8,128)(2,1)S(1)} collective-permute-done((bf16[128,1024]{1,0:T(8,128)(2,1)S(1)}, bf16[128,1024]{1,0:T(8,128)(2,1)S(1)}, u32[]{:S(2)}, u32[]{:S(2)}) %collective-permute-start.45) | collective-permute-done | bytes 262176 | tf_op jit(solution)/shard_map/ppermute | solution.py:1053
  149.2 1.8 %shard_map.189 = (bf16[4,32,1024]{2,1,0:T(8,128)(2,1)S(1)}, bf16[4,32,1024]{2,1,0:T(8,128)(2,1)S(1)}, f32[32,1024]{1,0:T(8,128)}, f32[128,1024]{1,0:T(8,128)}) custom-call(s32[5]{0:T(128)S(1)} %stack.23.refs_0_, f32[2,128,1024]{2,1,0:T(8,128)S(1)} %get-tuple-element.147.refs_1_, bf16[128,1024]{1,0:T(8,128)(2,1)S(1)} %collective-permute-done.45.refs_2_, ...), custom_call_target="tpu_custom_call" | custom-call | tf_op jit(solution)/shard_map/pallas_call | solution.py:388
  151.0 1.7 %collective-permute-start.40 = (bf16[32,1024]{1,0:T(8,128)(2,1)S(1)}, bf16[32,1024]{1,0:T(8,128)(2,1)S(1)}, u32[]{:S(2)}, u32[]{:S(2)}) collective-permute-start(bf16[32,1024]{1,0:T(8,128)(2,1)S(1)} %get-tuple-element.140), channel_id=1, source_target_pairs={{0,1},{1,0},{16,17},{17,16},{2,3},{3,2},{18,19},{19,18},{4,5},{5,4... | collective-permute-start | bytes 196616 | tf_op jit(solution)/shard_map/ppermute | solution.py:412
  153.8 1.4 collective-permute-start.52
  155.3 1.9 %collective-permute-start.53 = (bf16[64,1024]{1,0:T(8,128)(2,1)S(1)}, bf16[64,1024]{1,0:T(8,128)(2,1)S(1)}, u32[]{:S(2)}, u32[]{:S(2)}) collective-permute-start(bf16[64,1024]{1,0:T(8,128)(2,1)S(1)} %get-tuple-element.163), channel_id=1, source_target_pairs={{0,6},{2,4},{4,2},{6,0},{1,7},{3,5},{5,3},{7,1},{8,14},{10,12},{12... | collective-permute-start | bytes 393224 | tf_op jit(solution)/shard_map/ppermute | solution.py:407
  158.4 1.8 %collective-permute-start.42 = (bf16[32,1024]{1,0:T(8,128)(2,1)S(1)}, bf16[32,1024]{1,0:T(8,128)(2,1)S(1)}, u32[]{:S(2)}, u32[]{:S(2)}) collective-permute-start(bf16[32,1024]{1,0:T(8,128)(2,1)S(1)} %get-tuple-element.142), channel_id=1, source_target_pairs={{0,17},{1,16},{16,1},{17,0},{2,19},{3,18},{18,3},{19,2},{4,21},{5,... | collective-permute-start | bytes 196616 | tf_op jit(solution)/shard_map/ppermute | solution.py:412
  160.2 2.0 %collective-permute-done.41.refs_6_ = bf16[32,1024]{1,0:T(8,128)(2,1)S(1)} collective-permute-done((bf16[32,1024]{1,0:T(8,128)(2,1)S(1)}, bf16[32,1024]{1,0:T(8,128)(2,1)S(1)}, u32[]{:S(2)}, u32[]{:S(2)}) %collective-permute-start.41) | collective-permute-done | bytes 65568 | tf_op jit(solution)/shard_map/ppermute | solution.py:412
  163.5 2.7 %shard_map.186 = (bf16[4,64,1024]{2,1,0:T(8,128)(2,1)}, bf16[4,64,1024]{2,1,0:T(8,128)(2,1)}) custom-call(s32[5]{0:T(128)S(1)} %stack.23.refs_0_, bf16[4,16,64]{2,1,0:T(8,128)(2,1)} %get-tuple-element.90.refs_1_, bf16[4,64,1024]{2,1,0:T(8,128)(2,1)S(1)} %copy-done.2, bf16[4,64,1024]{2,1,0:T(8,128)(2,1)S(1)} %copy-done.3, ...), custom_call_target="tpu_custom_call" | custom-call | tf_op jit(solution)/shard_map/pallas_call | solution.py:388
  166.7 1.6 shard_map.191
  (117 shorter events, 31.9 us)
Async XLA Ops:
  2.9 21.2 %all-to-all-start = ((bf16[8,32,1024]{2,1,0:T(8,128)(2,1)}), bf16[8,32,1024]{2,1,0:T(8,128)(2,1)S(1)}, u32[]{:S(2)}, u32[]{:S(2)}) async-start(bf16[8,32,1024]{2,1,0:T(8,128)(2,1)} %shard_map.171), calls=%async_computation | async-start | bytes 1048576 | tf_op jit(solution)/shard_map/all_to_all | solution.py:960
  11.7 5.4 %collective-permute-start = (bf16[32,1024]{1,0:T(8,128)(2,1)S(1)}, bf16[32,1024]{1,0:T(8,128)(2,1)S(1)}, u32[]{:S(2)}, u32[]{:S(2)}) collective-permute-start(bf16[32,1024]{1,0:T(8,128)(2,1)S(1)} %get-tuple-element.92), channel_id=1, source_target_pairs={{0,1},{1,0},{16,17},{17,16},{2,3},{3,2},{18,19},{19,18},{4,5},{5,4... | collective-permute-start | bytes 196616 | tf_op jit(solution)/shard_map/ppermute | solution.py:412
  13.2 4.3 %collective-permute-start.1 = (bf16[32,1024]{1,0:T(8,128)(2,1)S(1)}, bf16[32,1024]{1,0:T(8,128)(2,1)S(1)}, u32[]{:S(2)}, u32[]{:S(2)}) collective-permute-start(bf16[32,1024]{1,0:T(8,128)(2,1)S(1)} %get-tuple-element.93), channel_id=1, source_target_pairs={{0,16},{1,17},{16,0},{17,1},{2,18},{3,19},{18,2},{19,3},{4,20},{5,... | collective-permute-start | bytes 196616 | tf_op jit(solution)/shard_map/ppermute | solution.py:412
  14.8 5.2 %collective-permute-start.2 = (bf16[32,1024]{1,0:T(8,128)(2,1)S(1)}, bf16[32,1024]{1,0:T(8,128)(2,1)S(1)}, u32[]{:S(2)}, u32[]{:S(2)}) collective-permute-start(bf16[32,1024]{1,0:T(8,128)(2,1)S(1)} %get-tuple-element.94), channel_id=1, source_target_pairs={{0,17},{1,16},{16,1},{17,0},{2,19},{3,18},{18,3},{19,2},{4,21},{5,... | collective-permute-start | bytes 196616 | tf_op jit(solution)/shard_map/ppermute | solution.py:412
  25.7 33.0 %all-to-all-start.1 = ((bf16[4,576,512]{2,1,0:T(8,128)(2,1)}), bf16[4,576,512]{2,1,0:T(8,128)(2,1)}, u32[]{:S(2)}, u32[]{:S(2)}) async-start(bf16[4,576,512]{2,1,0:T(8,128)(2,1)} %get-tuple-element.95), calls=%async_computation.1 | async-start | bytes 4718592 | tf_op jit(solution)/shard_map/all_to_all | solution.py:969
  30.2 13.4 %collective-permute-start.3 = (bf16[128,1024]{1,0:T(8,128)(2,1)S(1)}, bf16[128,1024]{1,0:T(8,128)(2,1)S(1)}, u32[]{:S(2)}, u32[]{:S(2)}) collective-permute-start(bf16[128,1024]{1,0:T(8,128)(2,1)S(1)} %shard_map.172.refs_3_.refs_4_), channel_id=1, source_target_pairs={{0,2},{2,0},{4,6},{6,4},{1,3},{3,1},{5,7},{7,5},{8,10},{10,8},{12,... | collective-permute-start | bytes 786440 | tf_op jit(solution)/shard_map/ppermute | solution.py:407
  30.3 21.4 %collective-permute-start.4 = (bf16[128,1024]{1,0:T(8,128)(2,1)S(1)}, bf16[128,1024]{1,0:T(8,128)(2,1)S(1)}, u32[]{:S(2)}, u32[]{:S(2)}) collective-permute-start(bf16[128,1024]{1,0:T(8,128)(2,1)S(1)} %shard_map.172.refs_3_.refs_4_), channel_id=1, source_target_pairs={{0,4},{2,6},{4,0},{6,2},{1,5},{3,7},{5,1},{7,3},{8,12},{10,14},{12... | collective-permute-start | bytes 786440 | tf_op jit(solution)/shard_map/ppermute | solution.py:407
  31.5 20.2 %collective-permute-start.5 = (bf16[128,1024]{1,0:T(8,128)(2,1)S(1)}, bf16[128,1024]{1,0:T(8,128)(2,1)S(1)}, u32[]{:S(2)}, u32[]{:S(2)}) collective-permute-start(bf16[128,1024]{1,0:T(8,128)(2,1)S(1)} %shard_map.172.refs_3_.refs_4_), channel_id=1, source_target_pairs={{0,6},{2,4},{4,2},{6,0},{1,7},{3,5},{5,3},{7,1},{8,14},{10,12},{12... | collective-permute-start | bytes 786440 | tf_op jit(solution)/shard_map/ppermute | solution.py:407
  34.7 17.5 %collective-permute-start.6 = (bf16[128,1024]{1,0:T(8,128)(2,1)S(1)}, bf16[128,1024]{1,0:T(8,128)(2,1)S(1)}, u32[]{:S(2)}, u32[]{:S(2)}) collective-permute-start(bf16[128,1024]{1,0:T(8,128)(2,1)S(1)} %shard_map.172.refs_3_.refs_4_), channel_id=1, source_target_pairs={{0,8},{8,0},{1,9},{9,1},{2,10},{10,2},{3,11},{11,3},{4,12},{12,4},... | collective-permute-start | bytes 786440 | tf_op jit(solution)/shard_map/ppermute | solution.py:420
  43.6 8.6 %collective-permute-start.7 = (bf16[128,1024]{1,0:T(8,128)(2,1)S(1)}, bf16[128,1024]{1,0:T(8,128)(2,1)S(1)}, u32[]{:S(2)}, u32[]{:S(2)}) collective-permute-start(bf16[128,1024]{1,0:T(8,128)(2,1)S(1)} %collective-permute-done.3.refs_4_.refs_5_), channel_id=1, source_target_pairs={{0,8},{8,0},{1,9},{9,1},{2,10},{10,2},{3,11},{11,3},{4,12},{12,4},... | collective-permute-start | bytes 786440 | tf_op jit(solution)/shard_map/ppermute | solution.py:420
  63.0 2.1 %collective-permute-start.13 = (bf16[4,32,1024]{2,1,0:T(8,128)(2,1)S(1)}, bf16[4,32,1024]{2,1,0:T(8,128)(2,1)S(1)}, u32[]{:S(2)}, u32[]{:S(2)}) collective-permute-start(bf16[4,32,1024]{2,1,0:T(8,128)(2,1)S(1)} %get-tuple-element.102), channel_id=1, source_target_pairs={{0,8},{8,0},{1,9},{9,1},{2,10},{10,2},{3,11},{11,3},{4,12},{12,4},... | collective-permute-start | bytes 786440 | tf_op jit(solution)/shard_map/ppermute | solution.py:420
  63.1 15.2 %collective-permute-start.10 = (bf16[256,512]{1,0:T(8,128)(2,1)S(1)}, bf16[256,512]{1,0:T(8,128)(2,1)S(1)}, u32[]{:S(2)}, u32[]{:S(2)}) collective-permute-start(bf16[256,512]{1,0:T(8,128)(2,1)S(1)} %get-tuple-element.99.refs_2_), channel_id=1, source_target_pairs={{0,1},{1,0},{16,17},{17,16},{2,3},{3,2},{18,19},{19,18},{4,5},{5,4... | collective-permute-start | bytes 786440 | tf_op jit(solution)/shard_map/ppermute | solution.py:412
  64.6 15.9 %collective-permute-start.11 = (bf16[256,512]{1,0:T(8,128)(2,1)S(1)}, bf16[256,512]{1,0:T(8,128)(2,1)S(1)}, u32[]{:S(2)}, u32[]{:S(2)}) collective-permute-start(bf16[256,512]{1,0:T(8,128)(2,1)S(1)} %get-tuple-element.99.refs_2_), channel_id=1, source_target_pairs={{0,16},{1,17},{16,0},{17,1},{2,18},{3,19},{18,2},{19,3},{4,20},{5,... | collective-permute-start | bytes 786440 | tf_op jit(solution)/shard_map/ppermute | solution.py:412
  65.2 4.3 %collective-permute-start.14 = (bf16[32,1024]{1,0:T(8,128)(2,1)S(1)}, bf16[32,1024]{1,0:T(8,128)(2,1)S(1)}, u32[]{:S(2)}, u32[]{:S(2)}) collective-permute-start(bf16[32,1024]{1,0:T(8,128)(2,1)S(1)} %get-tuple-element.104), channel_id=1, source_target_pairs={{0,2},{2,0},{4,6},{6,4},{1,3},{3,1},{5,7},{7,5},{8,10},{10,8},{12,... | collective-permute-start | bytes 196616 | tf_op jit(solution)/shard_map/ppermute | solution.py:407
  67.1 18.2 %collective-permute-start.12 = (bf16[256,512]{1,0:T(8,128)(2,1)S(1)}, bf16[256,512]{1,0:T(8,128)(2,1)S(1)}, u32[]{:S(2)}, u32[]{:S(2)}) collective-permute-start(bf16[256,512]{1,0:T(8,128)(2,1)S(1)} %get-tuple-element.99.refs_2_), channel_id=1, source_target_pairs={{0,17},{1,16},{16,1},{17,0},{2,19},{3,18},{18,3},{19,2},{4,21},{5,... | collective-permute-start | bytes 786440 | tf_op jit(solution)/shard_map/ppermute | solution.py:412
  67.9 8.0 %collective-permute-start.15 = (bf16[32,1024]{1,0:T(8,128)(2,1)S(1)}, bf16[32,1024]{1,0:T(8,128)(2,1)S(1)}, u32[]{:S(2)}, u32[]{:S(2)}) collective-permute-start(bf16[32,1024]{1,0:T(8,128)(2,1)S(1)} %get-tuple-element.105), channel_id=1, source_target_pairs={{0,4},{2,6},{4,0},{6,2},{1,5},{3,7},{5,1},{7,3},{8,12},{10,14},{12... | collective-permute-start | bytes 196616 | tf_op jit(solution)/shard_map/ppermute | solution.py:407
  69.5 6.4 %collective-permute-start.16 = (bf16[32,1024]{1,0:T(8,128)(2,1)S(1)}, bf16[32,1024]{1,0:T(8,128)(2,1)S(1)}, u32[]{:S(2)}, u32[]{:S(2)}) collective-permute-start(bf16[32,1024]{1,0:T(8,128)(2,1)S(1)} %get-tuple-element.106), channel_id=1, source_target_pairs={{0,6},{2,4},{4,2},{6,0},{1,7},{3,5},{5,3},{7,1},{8,14},{10,12},{12... | collective-permute-start | bytes 196616 | tf_op jit(solution)/shard_map/ppermute | solution.py:407
  76.0 4.5 %collective-permute-start.17 = (bf16[32,1024]{1,0:T(8,128)(2,1)S(1)}, bf16[32,1024]{1,0:T(8,128)(2,1)S(1)}, u32[]{:S(2)}, u32[]{:S(2)}) collective-permute-start(bf16[32,1024]{1,0:T(8,128)(2,1)S(1)} %get-tuple-element.107.refs_6_.refs_4_), channel_id=1, source_target_pairs={{0,2},{2,0},{4,6},{6,4},{1,3},{3,1},{5,7},{7,5},{8,10},{10,8},{12,... | collective-permute-start | bytes 196616 | tf_op jit(solution)/shard_map/ppermute | solution.py:407
  77.4 7.4 %collective-permute-start.18 = (bf16[32,1024]{1,0:T(8,128)(2,1)S(1)}, bf16[32,1024]{1,0:T(8,128)(2,1)S(1)}, u32[]{:S(2)}, u32[]{:S(2)}) collective-permute-start(bf16[32,1024]{1,0:T(8,128)(2,1)S(1)} %get-tuple-element.107.refs_6_.refs_4_), channel_id=1, source_target_pairs={{0,4},{2,6},{4,0},{6,2},{1,5},{3,7},{5,1},{7,3},{8,12},{10,14},{12... | collective-permute-start | bytes 196616 | tf_op jit(solution)/shard_map/ppermute | solution.py:407
  78.3 6.5 %collective-permute-start.19 = (bf16[32,1024]{1,0:T(8,128)(2,1)S(1)}, bf16[32,1024]{1,0:T(8,128)(2,1)S(1)}, u32[]{:S(2)}, u32[]{:S(2)}) collective-permute-start(bf16[32,1024]{1,0:T(8,128)(2,1)S(1)} %get-tuple-element.107.refs_6_.refs_4_), channel_id=1, source_target_pairs={{0,6},{2,4},{4,2},{6,0},{1,7},{3,5},{5,3},{7,1},{8,14},{10,12},{12... | collective-permute-start | bytes 196616 | tf_op jit(solution)/shard_map/ppermute | solution.py:407
  80.5 4.8 %collective-permute-start.20 = (bf16[32,1024]{1,0:T(8,128)(2,1)S(1)}, bf16[32,1024]{1,0:T(8,128)(2,1)S(1)}, u32[]{:S(2)}, u32[]{:S(2)}) collective-permute-start(bf16[32,1024]{1,0:T(8,128)(2,1)S(1)} %get-tuple-element.107.refs_6_.refs_4_), channel_id=1, source_target_pairs={{0,8},{8,0},{1,9},{9,1},{2,10},{10,2},{3,11},{11,3},{4,12},{12,4},... | collective-permute-start | bytes 196616 | tf_op jit(solution)/shard_map/ppermute | solution.py:420
  80.5 4.8 %collective-permute-start.21 = (bf16[32,1024]{1,0:T(8,128)(2,1)S(1)}, bf16[32,1024]{1,0:T(8,128)(2,1)S(1)}, u32[]{:S(2)}, u32[]{:S(2)}) collective-permute-start(bf16[32,1024]{1,0:T(8,128)(2,1)S(1)} %collective-permute-done.17.refs_7_.refs_5_), channel_id=1, source_target_pairs={{0,8},{8,0},{1,9},{9,1},{2,10},{10,2},{3,11},{11,3},{4,12},{12,4},... | collective-permute-start | bytes 196616 | tf_op jit(solution)/shard_map/ppermute | solution.py:420
  89.4 7.3 %collective-permute-start.26 = (bf16[32,1024]{1,0:T(8,128)(2,1)S(1)}, bf16[32,1024]{1,0:T(8,128)(2,1)S(1)}, u32[]{:S(2)}, u32[]{:S(2)}) collective-permute-start(bf16[32,1024]{1,0:T(8,128)(2,1)S(1)} %get-tuple-element.125), channel_id=1, source_target_pairs={{0,2},{2,0},{4,6},{6,4},{1,3},{3,1},{5,7},{7,5},{8,10},{10,8},{12,... | collective-permute-start | bytes 196616 | tf_op jit(solution)/shard_map/ppermute | solution.py:407
  90.6 8.3 %collective-permute-start.27 = (bf16[32,1024]{1,0:T(8,128)(2,1)S(1)}, bf16[32,1024]{1,0:T(8,128)(2,1)S(1)}, u32[]{:S(2)}, u32[]{:S(2)}) collective-permute-start(bf16[32,1024]{1,0:T(8,128)(2,1)S(1)} %get-tuple-element.126), channel_id=1, source_target_pairs={{0,4},{2,6},{4,0},{6,2},{1,5},{3,7},{5,1},{7,3},{8,12},{10,14},{12... | collective-permute-start | bytes 196616 | tf_op jit(solution)/shard_map/ppermute | solution.py:407
  92.0 6.9 %collective-permute-start.28 = (bf16[32,1024]{1,0:T(8,128)(2,1)S(1)}, bf16[32,1024]{1,0:T(8,128)(2,1)S(1)}, u32[]{:S(2)}, u32[]{:S(2)}) collective-permute-start(bf16[32,1024]{1,0:T(8,128)(2,1)S(1)} %get-tuple-element.127), channel_id=1, source_target_pairs={{0,6},{2,4},{4,2},{6,0},{1,7},{3,5},{5,3},{7,1},{8,14},{10,12},{12... | collective-permute-start | bytes 196616 | tf_op jit(solution)/shard_map/ppermute | solution.py:407
  99.1 4.5 %collective-permute-start.29 = (bf16[32,1024]{1,0:T(8,128)(2,1)S(1)}, bf16[32,1024]{1,0:T(8,128)(2,1)S(1)}, u32[]{:S(2)}, u32[]{:S(2)}) collective-permute-start(bf16[32,1024]{1,0:T(8,128)(2,1)S(1)} %get-tuple-element.132.refs_10_.refs_8_), channel_id=1, source_target_pairs={{0,2},{2,0},{4,6},{6,4},{1,3},{3,1},{5,7},{7,5},{8,10},{10,8},{12,... | collective-permute-start | bytes 196616 | tf_op jit(solution)/shard_map/ppermute | solution.py:407
  100.4 6.5 %collective-permute-start.30 = (bf16[32,1024]{1,0:T(8,128)(2,1)S(1)}, bf16[32,1024]{1,0:T(8,128)(2,1)S(1)}, u32[]{:S(2)}, u32[]{:S(2)}) collective-permute-start(bf16[32,1024]{1,0:T(8,128)(2,1)S(1)} %get-tuple-element.132.refs_10_.refs_8_), channel_id=1, source_target_pairs={{0,4},{2,6},{4,0},{6,2},{1,5},{3,7},{5,1},{7,3},{8,12},{10,14},{12... | collective-permute-start | bytes 196616 | tf_op jit(solution)/shard_map/ppermute | solution.py:407
  101.6 6.2 %collective-permute-start.31 = (bf16[32,1024]{1,0:T(8,128)(2,1)S(1)}, bf16[32,1024]{1,0:T(8,128)(2,1)S(1)}, u32[]{:S(2)}, u32[]{:S(2)}) collective-permute-start(bf16[32,1024]{1,0:T(8,128)(2,1)S(1)} %get-tuple-element.132.refs_10_.refs_8_), channel_id=1, source_target_pairs={{0,6},{2,4},{4,2},{6,0},{1,7},{3,5},{5,3},{7,1},{8,14},{10,12},{12... | collective-permute-start | bytes 196616 | tf_op jit(solution)/shard_map/ppermute | solution.py:407
  103.5 4.8 %collective-permute-start.32 = (bf16[32,1024]{1,0:T(8,128)(2,1)S(1)}, bf16[32,1024]{1,0:T(8,128)(2,1)S(1)}, u32[]{:S(2)}, u32[]{:S(2)}) collective-permute-start(bf16[32,1024]{1,0:T(8,128)(2,1)S(1)} %get-tuple-element.132.refs_10_.refs_8_), channel_id=1, source_target_pairs={{0,8},{8,0},{1,9},{9,1},{2,10},{10,2},{3,11},{11,3},{4,12},{12,4},... | collective-permute-start | bytes 196616 | tf_op jit(solution)/shard_map/ppermute | solution.py:420
  103.5 4.8 %collective-permute-start.33 = (bf16[32,1024]{1,0:T(8,128)(2,1)S(1)}, bf16[32,1024]{1,0:T(8,128)(2,1)S(1)}, u32[]{:S(2)}, u32[]{:S(2)}) collective-permute-start(bf16[32,1024]{1,0:T(8,128)(2,1)S(1)} %collective-permute-done.29.refs_11_.refs_9_), channel_id=1, source_target_pairs={{0,8},{8,0},{1,9},{9,1},{2,10},{10,2},{3,11},{11,3},{4,12},{12,4},... | collective-permute-start | bytes 196616 | tf_op jit(solution)/shard_map/ppermute | solution.py:420
  107.8 7.0 %collective-permute-start.24 = (bf16[4,64,1024]{2,1,0:T(8,128)(2,1)S(1)}, bf16[4,64,1024]{2,1,0:T(8,128)(2,1)S(1)}, u32[]{:S(2)}, u32[]{:S(2)}) collective-permute-start(bf16[4,64,1024]{2,1,0:T(8,128)(2,1)S(1)} %get-tuple-element.115), channel_id=1, source_target_pairs={{0,8},{8,0},{1,9},{9,1},{2,10},{10,2},{3,11},{11,3},{4,12},{12,4},... | collective-permute-start | bytes 1572872 | tf_op jit(solution)/shard_map/ppermute | solution.py:420
  112.9 2.0 %collective-permute-start.36 = (bf16[4,64,1024]{2,1,0:T(8,128)(2,1)S(1)}, bf16[4,64,1024]{2,1,0:T(8,128)(2,1)S(1)}, u32[]{:S(2)}, u32[]{:S(2)}) collective-permute-start(bf16[4,64,1024]{2,1,0:T(8,128)(2,1)S(1)} %get-tuple-element.134), channel_id=1, source_target_pairs={{0,8},{8,0},{1,9},{9,1},{2,10},{10,2},{3,11},{11,3},{4,12},{12,4},... | collective-permute-start | bytes 1572872 | tf_op jit(solution)/shard_map/ppermute | solution.py:420
  113.1 14.2 %collective-permute-start.43 = (bf16[2,128,1024]{2,1,0:T(8,128)(2,1)S(1)}, bf16[2,128,1024]{2,1,0:T(8,128)(2,1)S(1)}, u32[]{:S(2)}, u32[]{:S(2)}) collective-permute-start(bf16[2,128,1024]{2,1,0:T(8,128)(2,1)S(1)} %get-tuple-element.130.refs_8_), channel_id=1, source_target_pairs={{0,1},{1,0},{2,3},{3,2},{4,5},{5,4},{6,7},{7,6},{8,9},{9,8},{10,11... | collective-permute-start | bytes 1572872 | tf_op jit(solution)/shard_map/ppermute | solution.py:1051
  113.4 14.2 %collective-permute-start.44 = (bf16[2,128,1024]{2,1,0:T(8,128)(2,1)S(1)}, bf16[2,128,1024]{2,1,0:T(8,128)(2,1)S(1)}, u32[]{:S(2)}, u32[]{:S(2)}) collective-permute-start(bf16[2,128,1024]{2,1,0:T(8,128)(2,1)S(1)} %get-tuple-element.146), channel_id=1, source_target_pairs={{0,16},{16,0},{1,17},{17,1},{2,18},{18,2},{3,19},{19,3},{4,20},{20... | collective-permute-start | bytes 1572872 | tf_op jit(solution)/shard_map/ppermute | solution.py:1051
  115.1 13.9 %collective-permute-start.37 = (bf16[128,1024]{1,0:T(8,128)(2,1)S(1)}, bf16[128,1024]{1,0:T(8,128)(2,1)S(1)}, u32[]{:S(2)}, u32[]{:S(2)}) collective-permute-start(bf16[128,1024]{1,0:T(8,128)(2,1)S(1)} %get-tuple-element.136), channel_id=1, source_target_pairs={{0,2},{2,0},{4,6},{6,4},{1,3},{3,1},{5,7},{7,5},{8,10},{10,8},{12,... | collective-permute-start | bytes 786440 | tf_op jit(solution)/shard_map/ppermute | solution.py:407
  116.2 21.3 %collective-permute-start.38 = (bf16[128,1024]{1,0:T(8,128)(2,1)S(1)}, bf16[128,1024]{1,0:T(8,128)(2,1)S(1)}, u32[]{:S(2)}, u32[]{:S(2)}) collective-permute-start(bf16[128,1024]{1,0:T(8,128)(2,1)S(1)} %get-tuple-element.137), channel_id=1, source_target_pairs={{0,4},{2,6},{4,0},{6,2},{1,5},{3,7},{5,1},{7,3},{8,12},{10,14},{12... | collective-permute-start | bytes 786440 | tf_op jit(solution)/shard_map/ppermute | solution.py:407
  118.1 20.3 %collective-permute-start.39 = (bf16[128,1024]{1,0:T(8,128)(2,1)S(1)}, bf16[128,1024]{1,0:T(8,128)(2,1)S(1)}, u32[]{:S(2)}, u32[]{:S(2)}) collective-permute-start(bf16[128,1024]{1,0:T(8,128)(2,1)S(1)} %get-tuple-element.138), channel_id=1, source_target_pairs={{0,6},{2,4},{4,2},{6,0},{1,7},{3,5},{5,3},{7,1},{8,14},{10,12},{12... | collective-permute-start | bytes 786440 | tf_op jit(solution)/shard_map/ppermute | solution.py:407
  127.3 12.7 %collective-permute-start.47 = (bf16[320,512]{1,0:T(8,128)(2,1)S(1)}, bf16[320,512]{1,0:T(8,128)(2,1)S(1)}, u32[]{:S(2)}, u32[]{:S(2)}) collective-permute-start(bf16[320,512]{1,0:T(8,128)(2,1)S(1)} %get-tuple-element.155), channel_id=1, source_target_pairs={{0,1},{1,0},{16,17},{17,16},{2,3},{3,2},{18,19},{19,18},{4,5},{5,4... | collective-permute-start | bytes 983048 | tf_op jit(solution)/shard_map/ppermute | solution.py:412
  127.6 17.7 %collective-permute-start.48 = (bf16[320,512]{1,0:T(8,128)(2,1)S(1)}, bf16[320,512]{1,0:T(8,128)(2,1)S(1)}, u32[]{:S(2)}, u32[]{:S(2)}) collective-permute-start(bf16[320,512]{1,0:T(8,128)(2,1)S(1)} %get-tuple-element.156), channel_id=1, source_target_pairs={{0,16},{1,17},{16,0},{17,1},{2,18},{3,19},{18,2},{19,3},{4,20},{5,... | collective-permute-start | bytes 983048 | tf_op jit(solution)/shard_map/ppermute | solution.py:412
  129.0 16.3 %collective-permute-start.49 = (bf16[320,512]{1,0:T(8,128)(2,1)S(1)}, bf16[320,512]{1,0:T(8,128)(2,1)S(1)}, u32[]{:S(2)}, u32[]{:S(2)}) collective-permute-start(bf16[320,512]{1,0:T(8,128)(2,1)S(1)} %get-tuple-element.157), channel_id=1, source_target_pairs={{0,17},{1,16},{16,1},{17,0},{2,19},{3,18},{18,3},{19,2},{4,21},{5,... | collective-permute-start | bytes 983048 | tf_op jit(solution)/shard_map/ppermute | solution.py:412
  137.5 11.7 %collective-permute-start.45 = (bf16[128,1024]{1,0:T(8,128)(2,1)S(1)}, bf16[128,1024]{1,0:T(8,128)(2,1)S(1)}, u32[]{:S(2)}, u32[]{:S(2)}) collective-permute-start(bf16[128,1024]{1,0:T(8,128)(2,1)S(1)} %get-tuple-element.148), channel_id=1, source_target_pairs={{0,16},{16,0},{1,17},{17,1},{2,18},{18,2},{3,19},{19,3},{4,20},{20... | collective-permute-start | bytes 786440 | tf_op jit(solution)/shard_map/ppermute | solution.py:1053
  138.3 10.8 %collective-permute-start.46 = (bf16[128,1024]{1,0:T(8,128)(2,1)S(1)}, bf16[128,1024]{1,0:T(8,128)(2,1)S(1)}, u32[]{:S(2)}, u32[]{:S(2)}) collective-permute-start(bf16[128,1024]{1,0:T(8,128)(2,1)S(1)} %get-tuple-element.149), channel_id=1, source_target_pairs={{0,1},{1,0},{2,3},{3,2},{4,5},{5,4},{6,7},{7,6},{8,9},{9,8},{10,11... | collective-permute-start | bytes 786440 | tf_op jit(solution)/shard_map/ppermute | solution.py:1053
  151.0 7.4 %collective-permute-start.40 = (bf16[32,1024]{1,0:T(8,128)(2,1)S(1)}, bf16[32,1024]{1,0:T(8,128)(2,1)S(1)}, u32[]{:S(2)}, u32[]{:S(2)}) collective-permute-start(bf16[32,1024]{1,0:T(8,128)(2,1)S(1)} %get-tuple-element.140), channel_id=1, source_target_pairs={{0,1},{1,0},{16,17},{17,16},{2,3},{3,2},{18,19},{19,18},{4,5},{5,4... | collective-permute-start | bytes 196616 | tf_op jit(solution)/shard_map/ppermute | solution.py:412
  152.7 13.5 %collective-permute-start.51 = (bf16[64,1024]{1,0:T(8,128)(2,1)S(1)}, bf16[64,1024]{1,0:T(8,128)(2,1)S(1)}, u32[]{:S(2)}, u32[]{:S(2)}) collective-permute-start(bf16[64,1024]{1,0:T(8,128)(2,1)S(1)} %get-tuple-element.161), channel_id=1, source_target_pairs={{0,2},{2,0},{4,6},{6,4},{1,3},{3,1},{5,7},{7,5},{8,10},{10,8},{12,... | collective-permute-start | bytes 393224 | tf_op jit(solution)/shard_map/ppermute | solution.py:407
  153.8 12.9 %collective-permute-start.52 = (bf16[64,1024]{1,0:T(8,128)(2,1)S(1)}, bf16[64,1024]{1,0:T(8,128)(2,1)S(1)}, u32[]{:S(2)}, u32[]{:S(2)}) collective-permute-start(bf16[64,1024]{1,0:T(8,128)(2,1)S(1)} %get-tuple-element.162), channel_id=1, source_target_pairs={{0,4},{2,6},{4,0},{6,2},{1,5},{3,7},{5,1},{7,3},{8,12},{10,14},{12... | collective-permute-start | bytes 393224 | tf_op jit(solution)/shard_map/ppermute | solution.py:407
  155.3 11.4 %collective-permute-start.53 = (bf16[64,1024]{1,0:T(8,128)(2,1)S(1)}, bf16[64,1024]{1,0:T(8,128)(2,1)S(1)}, u32[]{:S(2)}, u32[]{:S(2)}) collective-permute-start(bf16[64,1024]{1,0:T(8,128)(2,1)S(1)} %get-tuple-element.163), channel_id=1, source_target_pairs={{0,6},{2,4},{4,2},{6,0},{1,7},{3,5},{5,3},{7,1},{8,14},{10,12},{12... | collective-permute-start | bytes 393224 | tf_op jit(solution)/shard_map/ppermute | solution.py:407
  157.2 5.0 %collective-permute-start.41 = (bf16[32,1024]{1,0:T(8,128)(2,1)S(1)}, bf16[32,1024]{1,0:T(8,128)(2,1)S(1)}, u32[]{:S(2)}, u32[]{:S(2)}) collective-permute-start(bf16[32,1024]{1,0:T(8,128)(2,1)S(1)} %get-tuple-element.141), channel_id=1, source_target_pairs={{0,16},{1,17},{16,0},{17,1},{2,18},{3,19},{18,2},{19,3},{4,20},{5,... | collective-permute-start | bytes 196616 | tf_op jit(solution)/shard_map/ppermute | solution.py:412
  158.4 5.2 %collective-permute-start.42 = (bf16[32,1024]{1,0:T(8,128)(2,1)S(1)}, bf16[32,1024]{1,0:T(8,128)(2,1)S(1)}, u32[]{:S(2)}, u32[]{:S(2)}) collective-permute-start(bf16[32,1024]{1,0:T(8,128)(2,1)S(1)} %get-tuple-element.142), channel_id=1, source_target_pairs={{0,17},{1,16},{16,1},{17,0},{2,19},{3,18},{18,3},{19,2},{4,21},{5,... | collective-permute-start | bytes 196616 | tf_op jit(solution)/shard_map/ppermute | solution.py:412
  (22 other events, 160.2 us)

commit v6 on v5

--- a/solution.py
+++ b/solution.py
@@ -702,32 +702,29 @@
 
 def ff_grads_kernel(dims, members, where, active, d_upper, d_result, *refs):
     ny, nx, rows, ff_rows = dims
-    blocks, (keep, by_x, by_y, down, up) = refs[:members], refs[members:]
+    blocks, (keep, send, down, up) = refs[:members], refs[members:]
     normed = jnp.concatenate([b[...] for b in blocks], 0)
     down[...] = mm(active[...], d_result[...], TN).astype(BF16)
     up[...] = mm(normed, d_upper[...], TN).astype(BF16)
     wide = up.shape[1]
-    part = members * rows // 2
+    each = ff_rows + members * rows // 2
     for k in range(ny * nx):
         line = where[2] ^ k
+        out, start = (keep, send)[k % 2], (k // 2) * each
         y, x = lax.div(line, jnp.int32(nx)), lax.rem(line, jnp.int32(nx))
-        first = by_x.at[k // 2] if k % 2 else keep.at[k // 2]
-        second = by_y.at[k % 2] if k // 2 else keep.at[2 + k % 2]
-        first[...] = down[pl.ds(pl.multiple_of(line * ff_rows, ff_rows), ff_rows)]
+        piece = down[pl.ds(pl.multiple_of(line * ff_rows, ff_rows), ff_rows)]
+        out[start : start + ff_rows] = piece
         for g in range(members):
             at = pl.multiple_of(((y * members + g) * nx + x) * rows, rows)
-            half, row = divmod(g * rows, part)
-            second[row : row + rows, half * wide : (half + 1) * wide] = up[pl.ds(at, rows)]
-
-
-def add_halves_kernel(keep, got_x, got_y, mine, to_y, to_x):
-    def both(index, got):
-        return keep[index].astype(F32) + got.astype(F32)
-
-    mine[0] = both(0, got_x[0])
-    mine[1] = both(2, got_y[0])
-    to_y[...] = both(1, got_x[1]).astype(BF16)
-    to_x[...] = both(3, got_y[1]).astype(BF16)
+            half, row = divmod(g * rows, members * rows // 2)
+            to = start + ff_rows + row
+            out[to : to + rows, half * wide : (half + 1) * wide] = up[pl.ds(at, rows)]
+
+
+def add_halves_kernel(keep, got, mine, send):
+    half = mine.shape[0]
+    mine[...] = keep[:half].astype(F32) + got[:half].astype(F32)
+    send[...] = (keep[half:].astype(F32) + got[half:].astype(F32)).astype(BF16)
 
 
 def result_kernel(active, attended, w_down, w_out, cot, gate, spread, logit_o, near_o, far_o):
@@ -845,12 +842,13 @@
         grad_o[s] = (cot[s].astype(F32) + mm(hot, got[s, cap:], TN)).astype(BF16)
 
 
-def line_sums_kernel(dims, where, mine, got_down, got_up, *refs):
+def line_sums_kernel(dims, where, mine, got, *refs):
     members, rows, ff_rows = dims
     *parts, near_o, far_o, out_o, down_o, send = refs
     cols = parts[0].shape[1]
-    wide = mine.shape[2] // 2
-    up = mine[1] + got_up[...].astype(F32)
+    wide = mine.shape[1] // 2
+    ff = mine[...] + got[...].astype(F32)
+    up = ff[ff_rows:]
     main = parts[0][...].astype(F32)
     for part in parts[1:]:
         main = main + part[...].astype(F32)
@@ -865,7 +863,7 @@
         far_o[k] = send[where[3] ^ (depth + k)]
     end = members * rows
     out_o[...] = jnp.concatenate([main[end : end + rows], main[end + rows :]], 1)
-    down_o[...] = mine[0] + got_down[...].astype(F32)
+    down_o[...] = ff[:ff_rows]
 
 
 def pair_kernel(near, far, *outs):
@@ -1022,15 +1020,16 @@
         scalars=1,
     )
     terms = scatter_group(near, far)
-    half = (ff_rows, width)
-    ff_keep, ff_x, ff_y = local_call(
+    half_rows = 2 * (ff_rows + members * rows // 2)
+    ff_keep, ff_send = local_call(
         partial(ff_grads_kernel, (ny, nx, rows, ff_rows), members),
-        [((4, *half), BF16), ((2, *half), BF16), ((2, *half), BF16)],
+        [((half_rows, width), BF16)] * 2,
         (where, active, d_upper, d_result, *normed_mlp),
         flops=6e8,
         scratch=[pltpu.VMEM((wide, width), BF16), pltpu.VMEM((width, wide), BF16)],
         scalars=1,
     )
+    ff_got = lax.ppermute(ff_send, "x", flips(nx)[1])
     logit, up_near, up_far = local_call(
         result_kernel,
         [((routed, 1), F32)] + slot_halves,
@@ -1041,16 +1040,16 @@
         partial(hidden_back_kernel, own),
         [(block, BF16), (block, F32), (block, BF16)],
         (hidden, full_vecs, gate, cot_own, *terms),
-        after=(ff_x, logit),
+        after=(ff_send, logit),
     )
     d_branch = gather_group([d_branch_own])
     up_far = send_c(up_far)
-    ff_mine, ff_y, ff_x = local_call(
+    ff_mine, ff_send = local_call(
         add_halves_kernel,
-        [((2, *half), F32), (half, BF16), (half, BF16)],
-        (ff_keep, lax.ppermute(ff_x, "x", flips(nx)[1]), lax.ppermute(ff_y, "y", flips(ny)[1])),
-    )
-    ff_got = (lax.ppermute(ff_y, "y", flips(ny)[1]), lax.ppermute(ff_x, "x", flips(nx)[1]))
+        [((half_rows // 2, width), F32), ((half_rows // 2, width), BF16)],
+        (ff_keep, ff_got),
+    )
+    ff_got = lax.ppermute(ff_send, "y", flips(ny)[1])
 
     near, far, d_joined, gain_a = local_call(
         partial(attention_back_kernel, members),
@@ -1079,6 +1078,7 @@
         slot_sum_kernel,
         [(both_slots, F32)] + [(both_slots, BF16)] * (nz - 1),
         (up_near, up_far, near, far),
+        after=(ff_mine,),
     )
     back_rows = local_call(
         partial(join_slots_kernel, cap, lines),
@@ -1090,7 +1090,7 @@
     near, far, grad_out, grad_down = local_call(
         partial(line_sums_kernel, (members, rows, ff_rows)),
         [((nz, rows, row_width), BF16)] * 2 + [((rows, width), F32), ((ff_rows, width), F32)],
-        (where, ff_mine, *ff_got, *parts),
+        (where, ff_mine, ff_got, *parts),
         scratch=[pltpu.VMEM((members, rows, row_width), BF16)],
         scalars=1,
         after=back_rows[:1],

time: 169 us -> 165 us (0.976)
  waiting for transfers between devices: 70.8 us -> 67.6 us
    ppermute x4 -> x2, waiting for transfers between devices: 9.91 us -> 1.44 us  [the longest x1 1.44 us: grouped(): ff_got = lax.ppermute(ff_send, 'x', flips(nx)[1])]
    ppermute x21, waiting for transfers between devices: 36.8 us -> 43.4 us  [send_z(): lax.ppermute(b, 'z', f)]
    ppermute x4 -> x2, starting transfers between devices: 4.03 us -> 2.31 us  [the longest x1 1.85 us: grouped(): ff_got = lax.ppermute(ff_send, 'y', flips(ny)[1])]
  transfers between devices with their start and end apart: 56 -> 54, of which waited for: 26 -> 26; matrix products, arithmetic and copies ran while one was open for 1% -> 1% of each run, Pallas kernels for 11% -> 11%
where the time goes in v6:
time: 165 us
  waiting for transfers between devices  67.6 us (41%)
  starting transfers between devices  62.2 us (38%)
  Pallas kernels  31 us (19%)
  local copies, waits for them, and re-layouts  2.95 us (2%)
    ppermute x21, waiting for transfers between devices, send_z(): lax.ppermute(b, 'z', f)  43.4 us
    pallas_call x23, Pallas kernels, local_call(): pl.pallas_call(run, out_shape=shapes, in_specs=[pl.BlockSpec(memory_space...  31 us
    ppermute x21, starting transfers between devices, send_z(): lax.ppermute(b, 'z', f)  30.8 us
    ppermute x12, starting transfers between devices, send_lines(): lax.ppermute(b, ('y', 'x'), f)  14.9 us
    ppermute x12, waiting for transfers between devices, send_lines(): lax.ppermute(b, ('y', 'x'), f)  12.5 us
    all_to_all x1, starting transfers between devices, grouped(): got_cols = lax.all_to_all(columns, ('c', 'z'), 0, 0, tiled=True)  6.34 us
    all_to_all x1, starting transfers between devices, grouped(): first = lax.all_to_all(first, ('y', 'x'), 0, 0, tiled=True)  4.53 us
    all_to_all x1, waiting for transfers between devices, grouped(): first = lax.all_to_all(first, ('y', 'x'), 0, 0, tiled=True)  4.07 us
  transfers between devices with their start and end apart: 54, of which 26 were waited for; matrix products, arithmetic and copies ran while one was open for 1% of the time, Pallas kernels for 11%

profile of v6, /device:TPU:0, one launch (start us, length us, event | category | flops | bytes accessed | tf_op | source)
XLA Modules:
  0.0 164.8 jit_solution(9817315119873469307)
XLA Ops:
  0.7 2.2 %shard_map.171 = bf16[8,32,1024]{2,1,0:T(8,128)(2,1)} custom-call(bf16[32,3072]{1,0:T(8,128)(2,1)} %refs_0_.1, bf16[32,4096]{1,0:T(8,128)(2,1)} %refs_1_.4, bf16[1,32]{1,0:T(2,128)(2,1)} %bitcast.14, bf16[1,32]{1,0:T(2,128)(2,1)} %bitcast.15, bf16[1,32]{1,0:T(2,128)(2,1)} %bitcast.16), custom_call_target="tpu_custom_call" | custom-call | tf_op jit(solution)/shard_map/pallas_call | solution.py:388
  2.9 6.3 %all-to-all-start = ((bf16[8,32,1024]{2,1,0:T(8,128)(2,1)}), bf16[8,32,1024]{2,1,0:T(8,128)(2,1)S(1)}, u32[]{:S(2)}, u32[]{:S(2)}) async-start(bf16[8,32,1024]{2,1,0:T(8,128)(2,1)} %shard_map.171), calls=%async_computation | async-start | bytes 1048576 | tf_op jit(solution)/shard_map/all_to_all | solution.py:958
  10.1 1.5 shard_map.169
  11.7 1.6 collective-permute-start
  13.2 1.5 collective-permute-start.1
  15.2 1.8 %shard_map.170.refs_4_.refs_1_.refs_0_.refs_6_.refs_9_ = bf16[256,512]{1,0:T(8,128)(2,1)} custom-call(s32[5]{0:T(128)S(1)} %stack.23.refs_0_, s32[4,256]{1,0:T(4,128)S(1)} %copy-done.6, s32[256,4]{1,0:T(8,128)S(1)} %bitcast.13), custom_call_target="tpu_custom_call" | custom-call | tf_op jit(solution)/shard_map/pallas_call | solution.py:388
  17.5 2.4 %collective-permute-done.2.refs_3_ = bf16[32,1024]{1,0:T(8,128)(2,1)S(1)} collective-permute-done((bf16[32,1024]{1,0:T(8,128)(2,1)S(1)}, bf16[32,1024]{1,0:T(8,128)(2,1)S(1)}, u32[]{:S(2)}, u32[]{:S(2)}) %collective-permute-start.2) | collective-permute-done | bytes 65568 | tf_op jit(solution)/shard_map/ppermute | solution.py:412
  20.9 3.2 %all-to-all-done.refs_0_ = bf16[8,32,1024]{2,1,0:T(8,128)(2,1)S(1)} async-done(((bf16[8,32,1024]{2,1,0:T(8,128)(2,1)}), bf16[8,32,1024]{2,1,0:T(8,128)(2,1)S(1)}, u32[]{:S(2)}, u32[]{:S(2)}) %all-to-all-start) | async-done | bytes 524320 | tf_op jit(solution)/shard_map/all_to_all | solution.py:958
  24.1 1.6 shard_map.173
  25.7 4.5 %all-to-all-start.1 = ((bf16[4,576,512]{2,1,0:T(8,128)(2,1)}), bf16[4,576,512]{2,1,0:T(8,128)(2,1)}, u32[]{:S(2)}, u32[]{:S(2)}) async-start(bf16[4,576,512]{2,1,0:T(8,128)(2,1)} %get-tuple-element.93), calls=%async_computation.1 | async-start | bytes 4718592 | tf_op jit(solution)/shard_map/all_to_all | solution.py:967
  31.5 3.2 %collective-permute-start.5 = (bf16[128,1024]{1,0:T(8,128)(2,1)S(1)}, bf16[128,1024]{1,0:T(8,128)(2,1)S(1)}, u32[]{:S(2)}, u32[]{:S(2)}) collective-permute-start(bf16[128,1024]{1,0:T(8,128)(2,1)S(1)} %shard_map.172.refs_3_.refs_4_), channel_id=1, source_target_pairs={{0,6},{2,4},{4,2},{6,0},{1,7},{3,5},{5,3},{7,1},{8,14},{10,12},{12... | collective-permute-start | bytes 786440 | tf_op jit(solution)/shard_map/ppermute | solution.py:407
  34.7 8.9 %collective-permute-done.3.refs_4_.refs_5_ = bf16[128,1024]{1,0:T(8,128)(2,1)S(1)} collective-permute-done((bf16[128,1024]{1,0:T(8,128)(2,1)S(1)}, bf16[128,1024]{1,0:T(8,128)(2,1)S(1)}, u32[]{:S(2)}, u32[]{:S(2)}) %collective-permute-start.3) | collective-permute-done | bytes 262176 | tf_op jit(solution)/shard_map/ppermute | solution.py:407
  43.6 8.1 %collective-permute-done.4.refs_5_.refs_6_ = bf16[128,1024]{1,0:T(8,128)(2,1)S(1)} collective-permute-done((bf16[128,1024]{1,0:T(8,128)(2,1)S(1)}, bf16[128,1024]{1,0:T(8,128)(2,1)S(1)}, u32[]{:S(2)}, u32[]{:S(2)}) %collective-permute-start.4) | collective-permute-done | bytes 262176 | tf_op jit(solution)/shard_map/ppermute | solution.py:407
  54.6 4.1 %all-to-all-done.1.refs_2_.refs_3_ = bf16[4,576,512]{2,1,0:T(8,128)(2,1)} async-done(((bf16[4,576,512]{2,1,0:T(8,128)(2,1)}), bf16[4,576,512]{2,1,0:T(8,128)(2,1)}, u32[]{:S(2)}, u32[]{:S(2)}) %all-to-all-start.1) | async-done | bytes 2359328 | tf_op jit(solution)/shard_map/all_to_all | solution.py:967
  58.7 4.2 %shard_map.174 = (bf16[256,1024]{1,0:T(8,128)(2,1)S(1)}, bf16[256,1024]{1,0:T(8,128)(2,1)S(1)}, bf16[1024,384]{1,0:T(8,128)(2,1)S(1)}, bf16[32,1024]{1,0:T(8,128...) custom-call(s32[5]{0:T(128)S(1)} %stack.23.refs_0_, ...), custom_call_target="tpu_custom_call" | custom-call | flops 1200000000 | tf_op jit(solution)/shard_map/pallas_call | solution.py:388
  63.0 1.5 collective-permute-start.10
  65.2 2.0 %collective-permute-start.14 = (bf16[32,1024]{1,0:T(8,128)(2,1)S(1)}, bf16[32,1024]{1,0:T(8,128)(2,1)S(1)}, u32[]{:S(2)}, u32[]{:S(2)}) collective-permute-start(bf16[32,1024]{1,0:T(8,128)(2,1)S(1)} %get-tuple-element.102), channel_id=1, source_target_pairs={{0,2},{2,0},{4,6},{6,4},{1,3},{3,1},{5,7},{7,5},{8,10},{10,8},{12,... | collective-permute-start | bytes 196616 | tf_op jit(solution)/shard_map/ppermute | solution.py:407
  69.5 1.7 %collective-permute-start.16 = (bf16[32,1024]{1,0:T(8,128)(2,1)S(1)}, bf16[32,1024]{1,0:T(8,128)(2,1)S(1)}, u32[]{:S(2)}, u32[]{:S(2)}) collective-permute-start(bf16[32,1024]{1,0:T(8,128)(2,1)S(1)} %get-tuple-element.104), channel_id=1, source_target_pairs={{0,6},{2,4},{4,2},{6,0},{1,7},{3,5},{5,3},{7,1},{8,14},{10,12},{12... | collective-permute-start | bytes 196616 | tf_op jit(solution)/shard_map/ppermute | solution.py:407
  71.2 2.7 %shard_map.175 = (f32[256,1]{1,0:T(8,128)S(1)}, bf16[256,1024]{1,0:T(8,128)(2,1)S(1)}, bf16[32,1024]{1,0:T(8,128)(2,1)S(1)}, bf16[256,1024]{1,0:T(8,128)(2,1)S(1...) custom-call(bf16[256,512]{1,0:T(8,128)(2,1)} %shard_map.170.refs_4_.refs_1_.refs_0_.refs_6_.refs_9_, ...), custom_call_target="tpu_custom_call" | custom-call | flops 800000000 | tf_op jit(solution)/shard_map/pallas_call | solution.py:388
  73.9 2.0 %collective-permute-done.15.refs_4_ = bf16[32,1024]{1,0:T(8,128)(2,1)S(1)} collective-permute-done((bf16[32,1024]{1,0:T(8,128)(2,1)S(1)}, bf16[32,1024]{1,0:T(8,128)(2,1)S(1)}, u32[]{:S(2)}, u32[]{:S(2)}) %collective-permute-start.15) | collective-permute-done | bytes 65568 | tf_op jit(solution)/shard_map/ppermute | solution.py:407
  78.3 2.2 %collective-permute-start.19 = (bf16[32,1024]{1,0:T(8,128)(2,1)S(1)}, bf16[32,1024]{1,0:T(8,128)(2,1)S(1)}, u32[]{:S(2)}, u32[]{:S(2)}) collective-permute-start(bf16[32,1024]{1,0:T(8,128)(2,1)S(1)} %get-tuple-element.105.refs_6_.refs_4_), channel_id=1, source_target_pairs={{0,6},{2,4},{4,2},{6,0},{1,7},{3,5},{5,3},{7,1},{8,14},{10,12},{12... | collective-permute-start | bytes 196616 | tf_op jit(solution)/shard_map/ppermute | solution.py:407
  81.1 3.8 %collective-permute-done.18.refs_8_.refs_6_ = bf16[32,1024]{1,0:T(8,128)(2,1)S(1)} collective-permute-done((bf16[32,1024]{1,0:T(8,128)(2,1)S(1)}, bf16[32,1024]{1,0:T(8,128)(2,1)S(1)}, u32[]{:S(2)}, u32[]{:S(2)}) %collective-permute-start.18) | collective-permute-done | bytes 65568 | tf_op jit(solution)/shard_map/ppermute | solution.py:407
  86.2 1.6 shard_map.178
  90.8 2.3 %collective-permute-start.27 = (bf16[32,1024]{1,0:T(8,128)(2,1)S(1)}, bf16[32,1024]{1,0:T(8,128)(2,1)S(1)}, u32[]{:S(2)}, u32[]{:S(2)}) collective-permute-start(bf16[32,1024]{1,0:T(8,128)(2,1)S(1)} %get-tuple-element.124), channel_id=1, source_target_pairs={{0,4},{2,6},{4,0},{6,2},{1,5},{3,7},{5,1},{7,3},{8,12},{10,14},{12... | collective-permute-start | bytes 196616 | tf_op jit(solution)/shard_map/ppermute | solution.py:407
  93.0 1.6 collective-permute-start.28
  94.6 1.4 shard_map.179
  96.1 3.2 %collective-permute-done.27.refs_6_ = bf16[32,1024]{1,0:T(8,128)(2,1)S(1)} collective-permute-done((bf16[32,1024]{1,0:T(8,128)(2,1)S(1)}, bf16[32,1024]{1,0:T(8,128)(2,1)S(1)}, u32[]{:S(2)}, u32[]{:S(2)}) %collective-permute-start.27) | collective-permute-done | bytes 65568 | tf_op jit(solution)/shard_map/ppermute | solution.py:407
  102.0 1.9 %collective-permute-start.31 = (bf16[32,1024]{1,0:T(8,128)(2,1)S(1)}, bf16[32,1024]{1,0:T(8,128)(2,1)S(1)}, u32[]{:S(2)}, u32[]{:S(2)}) collective-permute-start(bf16[32,1024]{1,0:T(8,128)(2,1)S(1)} %get-tuple-element.130.refs_10_.refs_8_), channel_id=1, source_target_pairs={{0,6},{2,4},{4,2},{6,0},{1,7},{3,5},{5,3},{7,1},{8,14},{10,12},{12... | collective-permute-start | bytes 196616 | tf_op jit(solution)/shard_map/ppermute | solution.py:407
  104.4 3.0 %collective-permute-done.30.refs_12_.refs_10_ = bf16[32,1024]{1,0:T(8,128)(2,1)S(1)} collective-permute-done((bf16[32,1024]{1,0:T(8,128)(2,1)S(1)}, bf16[32,1024]{1,0:T(8,128)(2,1)S(1)}, u32[]{:S(2)}, u32[]{:S(2)}) %collective-permute-start.30) | collective-permute-done | bytes 65568 | tf_op jit(solution)/shard_map/ppermute | solution.py:407
  109.4 3.8 %shard_map.183 = (bf16[4,64,1024]{2,1,0:T(8,128)(2,1)S(1)}, bf16[4,64,1024]{2,1,0:T(8,128)(2,1)S(1)}, bf16[256,384]{1,0:T(8,128)(2,1)S(1)}, bf16[256,1024]{1,0:T(8,128)(2,1)S(1)}) custom-call(s32[5]{0:T(128)S(1)} %stack.23.refs_0_, bf16[128,1024]{1,0:T(8,128)(2,1)S(1)} %get-tuple-element.109.refs_3_.refs_1_, ...), custom_call_target="tpu_custom_call" | custom-call | flops 1200000000 | tf_op jit(solution)/shard_map/pallas_call | solution.py:388
  118.0 1.9 %collective-permute-start.44 = (bf16[256,1024]{1,0:T(8,128)(2,1)S(1)}, bf16[256,1024]{1,0:T(8,128)(2,1)S(1)}, u32[]{:S(2)}, u32[]{:S(2)}) collective-permute-start(bf16[256,1024]{1,0:T(8,128)(2,1)S(1)} %get-tuple-element.145), channel_id=1, source_target_pairs={{0,16},{16,0},{1,17},{17,1},{2,18},{18,2},{3,19},{19,3},{4,20},{20... | collective-permute-start | bytes 1572872 | tf_op jit(solution)/shard_map/ppermute | solution.py:1052
  119.8 1.7 %shard_map.188 = (bf16[320,512]{1,0:T(8,128)(2,1)S(1)}, bf16[320,512]{1,0:T(8,128)(2,1)S(1)}, bf16[320,512]{1,0:T(8,128)(2,1)S(1)}, bf16[320,512]{1,0:T(8,128)(2,1)S(1)}) custom-call(s32[5]{0:T(128)S(1)} %stack.23.refs_0_, bf16[256,1024]{1,0:T(8,128)(2,1)S(1)} %get-tuple-element.146.refs_1_, bf16[256,384]{1,0:T(8,128)(2,1)S(1)} %get-tuple-element.147.refs_2_, ...), custom_call_target="tpu_custom_call" | custom-call | flops 500000000 | tf_op jit(solution)/shard_map/pallas_call | solution.py:388
  121.7 2.0 %collective-permute-start.46 = (bf16[320,512]{1,0:T(8,128)(2,1)S(1)}, bf16[320,512]{1,0:T(8,128)(2,1)S(1)}, u32[]{:S(2)}, u32[]{:S(2)}) collective-permute-start(bf16[320,512]{1,0:T(8,128)(2,1)S(1)} %get-tuple-element.152), channel_id=1, source_target_pairs={{0,16},{1,17},{16,0},{17,1},{2,18},{3,19},{18,2},{19,3},{4,20},{5,... | collective-permute-start | bytes 983048 | tf_op jit(solution)/shard_map/ppermute | solution.py:412
  123.7 5.2 %collective-permute-done.38.refs_1_ = bf16[128,1024]{1,0:T(8,128)(2,1)S(1)} collective-permute-done((bf16[128,1024]{1,0:T(8,128)(2,1)S(1)}, bf16[128,1024]{1,0:T(8,128)(2,1)S(1)}, u32[]{:S(2)}, u32[]{:S(2)}) %collective-permute-start.38) | collective-permute-done | bytes 262176 | tf_op jit(solution)/shard_map/ppermute | solution.py:407
  128.9 1.6 collective-permute-start.47
  131.4 1.9 %collective-permute-start.40 = (bf16[128,1024]{1,0:T(8,128)(2,1)S(1)}, bf16[128,1024]{1,0:T(8,128)(2,1)S(1)}, u32[]{:S(2)}, u32[]{:S(2)}) collective-permute-start(bf16[128,1024]{1,0:T(8,128)(2,1)S(1)} %get-tuple-element.138), channel_id=1, source_target_pairs={{0,6},{2,4},{4,2},{6,0},{1,7},{3,5},{5,3},{7,1},{8,14},{10,12},{12... | collective-permute-start | bytes 786440 | tf_op jit(solution)/shard_map/ppermute | solution.py:407
  133.3 6.3 %collective-permute-done.40.refs_3_ = bf16[128,1024]{1,0:T(8,128)(2,1)S(1)} collective-permute-done((bf16[128,1024]{1,0:T(8,128)(2,1)S(1)}, bf16[128,1024]{1,0:T(8,128)(2,1)S(1)}, u32[]{:S(2)}, u32[]{:S(2)}) %collective-permute-start.40) | collective-permute-done | bytes 262176 | tf_op jit(solution)/shard_map/ppermute | solution.py:407
  139.8 6.0 %collective-permute-done.46.refs_5_ = bf16[320,512]{1,0:T(8,128)(2,1)S(1)} collective-permute-done((bf16[320,512]{1,0:T(8,128)(2,1)S(1)}, bf16[320,512]{1,0:T(8,128)(2,1)S(1)}, u32[]{:S(2)}, u32[]{:S(2)}) %collective-permute-start.46) | collective-permute-done | bytes 327712 | tf_op jit(solution)/shard_map/ppermute | solution.py:412
  145.8 1.7 %shard_map.189 = (bf16[4,32,1024]{2,1,0:T(8,128)(2,1)S(1)}, bf16[4,32,1024]{2,1,0:T(8,128)(2,1)S(1)}, f32[32,1024]{1,0:T(8,128)}, f32[128,1024]{1,0:T(8,128)}) custom-call(s32[5]{0:T(128)S(1)} %stack.23.refs_0_, f32[256,1024]{1,0:T(8,128)S(1)} %get-tuple-element.134.refs_4_.refs_1_, bf16[256,1024]{1,0:T(8,128)(2,1)S(1)} %collective-permute-done.44.refs_2_, ...), custom_call_target="tpu_custom_call" | custom-call | tf_op jit(solution)/shard_map/pallas_call | solution.py:388
  147.5 1.8 %collective-permute-start.41 = (bf16[32,1024]{1,0:T(8,128)(2,1)S(1)}, bf16[32,1024]{1,0:T(8,128)(2,1)S(1)}, u32[]{:S(2)}, u32[]{:S(2)}) collective-permute-start(bf16[32,1024]{1,0:T(8,128)(2,1)S(1)} %get-tuple-element.140), channel_id=1, source_target_pairs={{0,1},{1,0},{16,17},{17,16},{2,3},{3,2},{18,19},{19,18},{4,5},{5,4... | collective-permute-start | bytes 196616 | tf_op jit(solution)/shard_map/ppermute | solution.py:412
  150.3 1.6 collective-permute-start.50
  151.9 1.9 %collective-permute-start.51 = (bf16[64,1024]{1,0:T(8,128)(2,1)S(1)}, bf16[64,1024]{1,0:T(8,128)(2,1)S(1)}, u32[]{:S(2)}, u32[]{:S(2)}) collective-permute-start(bf16[64,1024]{1,0:T(8,128)(2,1)S(1)} %get-tuple-element.159), channel_id=1, source_target_pairs={{0,6},{2,4},{4,2},{6,0},{1,7},{3,5},{5,3},{7,1},{8,14},{10,12},{12... | collective-permute-start | bytes 393224 | tf_op jit(solution)/shard_map/ppermute | solution.py:407
  153.8 1.5 collective-permute-start.42
  155.2 1.5 collective-permute-start.43
  156.8 2.0 %collective-permute-done.42.refs_6_ = bf16[32,1024]{1,0:T(8,128)(2,1)S(1)} collective-permute-done((bf16[32,1024]{1,0:T(8,128)(2,1)S(1)}, bf16[32,1024]{1,0:T(8,128)(2,1)S(1)}, u32[]{:S(2)}, u32[]{:S(2)}) %collective-permute-start.42) | collective-permute-done | bytes 65568 | tf_op jit(solution)/shard_map/ppermute | solution.py:412
  158.7 1.7 %collective-permute-done.43.refs_7_ = bf16[32,1024]{1,0:T(8,128)(2,1)S(1)} collective-permute-done((bf16[32,1024]{1,0:T(8,128)(2,1)S(1)}, bf16[32,1024]{1,0:T(8,128)(2,1)S(1)}, u32[]{:S(2)}, u32[]{:S(2)}) %collective-permute-start.43) | collective-permute-done | bytes 65568 | tf_op jit(solution)/shard_map/ppermute | solution.py:412
  160.4 2.7 %shard_map.187 = (bf16[4,64,1024]{2,1,0:T(8,128)(2,1)}, bf16[4,64,1024]{2,1,0:T(8,128)(2,1)}) custom-call(s32[5]{0:T(128)S(1)} %stack.23.refs_0_, bf16[4,16,64]{2,1,0:T(8,128)(2,1)} %get-tuple-element.88.refs_1_, bf16[4,64,1024]{2,1,0:T(8,128)(2,1)S(1)} %copy-done.2, bf16[4,64,1024]{2,1,0:T(8,128)(2,1)S(1)} %copy-done.3, ...), custom_call_target="tpu_custom_call" | custom-call | tf_op jit(solution)/shard_map/pallas_call | solution.py:388
  163.2 1.6 shard_map.191
  (113 shorter events, 29.7 us)
Async XLA Ops:
  2.9 21.2 %all-to-all-start = ((bf16[8,32,1024]{2,1,0:T(8,128)(2,1)}), bf16[8,32,1024]{2,1,0:T(8,128)(2,1)S(1)}, u32[]{:S(2)}, u32[]{:S(2)}) async-start(bf16[8,32,1024]{2,1,0:T(8,128)(2,1)} %shard_map.171), calls=%async_computation | async-start | bytes 1048576 | tf_op jit(solution)/shard_map/all_to_all | solution.py:958
  11.7 5.4 %collective-permute-start = (bf16[32,1024]{1,0:T(8,128)(2,1)S(1)}, bf16[32,1024]{1,0:T(8,128)(2,1)S(1)}, u32[]{:S(2)}, u32[]{:S(2)}) collective-permute-start(bf16[32,1024]{1,0:T(8,128)(2,1)S(1)} %get-tuple-element.90), channel_id=1, source_target_pairs={{0,1},{1,0},{16,17},{17,16},{2,3},{3,2},{18,19},{19,18},{4,5},{5,4... | collective-permute-start | bytes 196616 | tf_op jit(solution)/shard_map/ppermute | solution.py:412
  13.2 4.3 %collective-permute-start.1 = (bf16[32,1024]{1,0:T(8,128)(2,1)S(1)}, bf16[32,1024]{1,0:T(8,128)(2,1)S(1)}, u32[]{:S(2)}, u32[]{:S(2)}) collective-permute-start(bf16[32,1024]{1,0:T(8,128)(2,1)S(1)} %get-tuple-element.91), channel_id=1, source_target_pairs={{0,16},{1,17},{16,0},{17,1},{2,18},{3,19},{18,2},{19,3},{4,20},{5,... | collective-permute-start | bytes 196616 | tf_op jit(solution)/shard_map/ppermute | solution.py:412
  14.8 5.2 %collective-permute-start.2 = (bf16[32,1024]{1,0:T(8,128)(2,1)S(1)}, bf16[32,1024]{1,0:T(8,128)(2,1)S(1)}, u32[]{:S(2)}, u32[]{:S(2)}) collective-permute-start(bf16[32,1024]{1,0:T(8,128)(2,1)S(1)} %get-tuple-element.92), channel_id=1, source_target_pairs={{0,17},{1,16},{16,1},{17,0},{2,19},{3,18},{18,3},{19,2},{4,21},{5,... | collective-permute-start | bytes 196616 | tf_op jit(solution)/shard_map/ppermute | solution.py:412
  25.7 33.0 %all-to-all-start.1 = ((bf16[4,576,512]{2,1,0:T(8,128)(2,1)}), bf16[4,576,512]{2,1,0:T(8,128)(2,1)}, u32[]{:S(2)}, u32[]{:S(2)}) async-start(bf16[4,576,512]{2,1,0:T(8,128)(2,1)} %get-tuple-element.93), calls=%async_computation.1 | async-start | bytes 4718592 | tf_op jit(solution)/shard_map/all_to_all | solution.py:967
  30.2 13.4 %collective-permute-start.3 = (bf16[128,1024]{1,0:T(8,128)(2,1)S(1)}, bf16[128,1024]{1,0:T(8,128)(2,1)S(1)}, u32[]{:S(2)}, u32[]{:S(2)}) collective-permute-start(bf16[128,1024]{1,0:T(8,128)(2,1)S(1)} %shard_map.172.refs_3_.refs_4_), channel_id=1, source_target_pairs={{0,2},{2,0},{4,6},{6,4},{1,3},{3,1},{5,7},{7,5},{8,10},{10,8},{12,... | collective-permute-start | bytes 786440 | tf_op jit(solution)/shard_map/ppermute | solution.py:407
  30.3 21.4 %collective-permute-start.4 = (bf16[128,1024]{1,0:T(8,128)(2,1)S(1)}, bf16[128,1024]{1,0:T(8,128)(2,1)S(1)}, u32[]{:S(2)}, u32[]{:S(2)}) collective-permute-start(bf16[128,1024]{1,0:T(8,128)(2,1)S(1)} %shard_map.172.refs_3_.refs_4_), channel_id=1, source_target_pairs={{0,4},{2,6},{4,0},{6,2},{1,5},{3,7},{5,1},{7,3},{8,12},{10,14},{12... | collective-permute-start | bytes 786440 | tf_op jit(solution)/shard_map/ppermute | solution.py:407
  31.5 20.2 %collective-permute-start.5 = (bf16[128,1024]{1,0:T(8,128)(2,1)S(1)}, bf16[128,1024]{1,0:T(8,128)(2,1)S(1)}, u32[]{:S(2)}, u32[]{:S(2)}) collective-permute-start(bf16[128,1024]{1,0:T(8,128)(2,1)S(1)} %shard_map.172.refs_3_.refs_4_), channel_id=1, source_target_pairs={{0,6},{2,4},{4,2},{6,0},{1,7},{3,5},{5,3},{7,1},{8,14},{10,12},{12... | collective-permute-start | bytes 786440 | tf_op jit(solution)/shard_map/ppermute | solution.py:407
  34.7 17.5 %collective-permute-start.6 = (bf16[128,1024]{1,0:T(8,128)(2,1)S(1)}, bf16[128,1024]{1,0:T(8,128)(2,1)S(1)}, u32[]{:S(2)}, u32[]{:S(2)}) collective-permute-start(bf16[128,1024]{1,0:T(8,128)(2,1)S(1)} %shard_map.172.refs_3_.refs_4_), channel_id=1, source_target_pairs={{0,8},{8,0},{1,9},{9,1},{2,10},{10,2},{3,11},{11,3},{4,12},{12,4},... | collective-permute-start | bytes 786440 | tf_op jit(solution)/shard_map/ppermute | solution.py:420
  43.6 8.6 %collective-permute-start.7 = (bf16[128,1024]{1,0:T(8,128)(2,1)S(1)}, bf16[128,1024]{1,0:T(8,128)(2,1)S(1)}, u32[]{:S(2)}, u32[]{:S(2)}) collective-permute-start(bf16[128,1024]{1,0:T(8,128)(2,1)S(1)} %collective-permute-done.3.refs_4_.refs_5_), channel_id=1, source_target_pairs={{0,8},{8,0},{1,9},{9,1},{2,10},{10,2},{3,11},{11,3},{4,12},{12,4},... | collective-permute-start | bytes 786440 | tf_op jit(solution)/shard_map/ppermute | solution.py:420
  51.7 1.9 %collective-permute-start.9 = (bf16[128,1024]{1,0:T(8,128)(2,1)S(1)}, bf16[128,1024]{1,0:T(8,128)(2,1)S(1)}, u32[]{:S(2)}, u32[]{:S(2)}) collective-permute-start(bf16[128,1024]{1,0:T(8,128)(2,1)S(1)} %collective-permute-done.5.refs_6_.refs_7_), channel_id=1, source_target_pairs={{0,8},{8,0},{1,9},{9,1},{2,10},{10,2},{3,11},{11,3},{4,12},{12,4},... | collective-permute-start | bytes 786440 | tf_op jit(solution)/shard_map/ppermute | solution.py:420
  63.0 2.1 %collective-permute-start.13 = (bf16[4,32,1024]{2,1,0:T(8,128)(2,1)S(1)}, bf16[4,32,1024]{2,1,0:T(8,128)(2,1)S(1)}, u32[]{:S(2)}, u32[]{:S(2)}) collective-permute-start(bf16[4,32,1024]{2,1,0:T(8,128)(2,1)S(1)} %get-tuple-element.100), channel_id=1, source_target_pairs={{0,8},{8,0},{1,9},{9,1},{2,10},{10,2},{3,11},{11,3},{4,12},{12,4},... | collective-permute-start | bytes 786440 | tf_op jit(solution)/shard_map/ppermute | solution.py:420
  63.0 15.3 %collective-permute-start.10 = (bf16[256,512]{1,0:T(8,128)(2,1)S(1)}, bf16[256,512]{1,0:T(8,128)(2,1)S(1)}, u32[]{:S(2)}, u32[]{:S(2)}) collective-permute-start(bf16[256,512]{1,0:T(8,128)(2,1)S(1)} %get-tuple-element.97.refs_2_), channel_id=1, source_target_pairs={{0,1},{1,0},{16,17},{17,16},{2,3},{3,2},{18,19},{19,18},{4,5},{5,4... | collective-permute-start | bytes 786440 | tf_op jit(solution)/shard_map/ppermute | solution.py:412
  64.5 16.0 %collective-permute-start.11 = (bf16[256,512]{1,0:T(8,128)(2,1)S(1)}, bf16[256,512]{1,0:T(8,128)(2,1)S(1)}, u32[]{:S(2)}, u32[]{:S(2)}) collective-permute-start(bf16[256,512]{1,0:T(8,128)(2,1)S(1)} %get-tuple-element.97.refs_2_), channel_id=1, source_target_pairs={{0,16},{1,17},{16,0},{17,1},{2,18},{3,19},{18,2},{19,3},{4,20},{5,... | collective-permute-start | bytes 786440 | tf_op jit(solution)/shard_map/ppermute | solution.py:412
  65.2 4.3 %collective-permute-start.14 = (bf16[32,1024]{1,0:T(8,128)(2,1)S(1)}, bf16[32,1024]{1,0:T(8,128)(2,1)S(1)}, u32[]{:S(2)}, u32[]{:S(2)}) collective-permute-start(bf16[32,1024]{1,0:T(8,128)(2,1)S(1)} %get-tuple-element.102), channel_id=1, source_target_pairs={{0,2},{2,0},{4,6},{6,4},{1,3},{3,1},{5,7},{7,5},{8,10},{10,8},{12,... | collective-permute-start | bytes 196616 | tf_op jit(solution)/shard_map/ppermute | solution.py:407
  67.1 18.2 %collective-permute-start.12 = (bf16[256,512]{1,0:T(8,128)(2,1)S(1)}, bf16[256,512]{1,0:T(8,128)(2,1)S(1)}, u32[]{:S(2)}, u32[]{:S(2)}) collective-permute-start(bf16[256,512]{1,0:T(8,128)(2,1)S(1)} %get-tuple-element.97.refs_2_), channel_id=1, source_target_pairs={{0,17},{1,16},{16,1},{17,0},{2,19},{3,18},{18,3},{19,2},{4,21},{5,... | collective-permute-start | bytes 786440 | tf_op jit(solution)/shard_map/ppermute | solution.py:412
  68.0 8.0 %collective-permute-start.15 = (bf16[32,1024]{1,0:T(8,128)(2,1)S(1)}, bf16[32,1024]{1,0:T(8,128)(2,1)S(1)}, u32[]{:S(2)}, u32[]{:S(2)}) collective-permute-start(bf16[32,1024]{1,0:T(8,128)(2,1)S(1)} %get-tuple-element.103), channel_id=1, source_target_pairs={{0,4},{2,6},{4,0},{6,2},{1,5},{3,7},{5,1},{7,3},{8,12},{10,14},{12... | collective-permute-start | bytes 196616 | tf_op jit(solution)/shard_map/ppermute | solution.py:407
  69.5 6.4 %collective-permute-start.16 = (bf16[32,1024]{1,0:T(8,128)(2,1)S(1)}, bf16[32,1024]{1,0:T(8,128)(2,1)S(1)}, u32[]{:S(2)}, u32[]{:S(2)}) collective-permute-start(bf16[32,1024]{1,0:T(8,128)(2,1)S(1)} %get-tuple-element.104), channel_id=1, source_target_pairs={{0,6},{2,4},{4,2},{6,0},{1,7},{3,5},{5,3},{7,1},{8,14},{10,12},{12... | collective-permute-start | bytes 196616 | tf_op jit(solution)/shard_map/ppermute | solution.py:407
  76.1 4.5 %collective-permute-start.17 = (bf16[32,1024]{1,0:T(8,128)(2,1)S(1)}, bf16[32,1024]{1,0:T(8,128)(2,1)S(1)}, u32[]{:S(2)}, u32[]{:S(2)}) collective-permute-start(bf16[32,1024]{1,0:T(8,128)(2,1)S(1)} %get-tuple-element.105.refs_6_.refs_4_), channel_id=1, source_target_pairs={{0,2},{2,0},{4,6},{6,4},{1,3},{3,1},{5,7},{7,5},{8,10},{10,8},{12,... | collective-permute-start | bytes 196616 | tf_op jit(solution)/shard_map/ppermute | solution.py:407
  77.4 7.4 %collective-permute-start.18 = (bf16[32,1024]{1,0:T(8,128)(2,1)S(1)}, bf16[32,1024]{1,0:T(8,128)(2,1)S(1)}, u32[]{:S(2)}, u32[]{:S(2)}) collective-permute-start(bf16[32,1024]{1,0:T(8,128)(2,1)S(1)} %get-tuple-element.105.refs_6_.refs_4_), channel_id=1, source_target_pairs={{0,4},{2,6},{4,0},{6,2},{1,5},{3,7},{5,1},{7,3},{8,12},{10,14},{12... | collective-permute-start | bytes 196616 | tf_op jit(solution)/shard_map/ppermute | solution.py:407
  78.3 6.5 %collective-permute-start.19 = (bf16[32,1024]{1,0:T(8,128)(2,1)S(1)}, bf16[32,1024]{1,0:T(8,128)(2,1)S(1)}, u32[]{:S(2)}, u32[]{:S(2)}) collective-permute-start(bf16[32,1024]{1,0:T(8,128)(2,1)S(1)} %get-tuple-element.105.refs_6_.refs_4_), channel_id=1, source_target_pairs={{0,6},{2,4},{4,2},{6,0},{1,7},{3,5},{5,3},{7,1},{8,14},{10,12},{12... | collective-permute-start | bytes 196616 | tf_op jit(solution)/shard_map/ppermute | solution.py:407
  80.5 4.8 %collective-permute-start.20 = (bf16[32,1024]{1,0:T(8,128)(2,1)S(1)}, bf16[32,1024]{1,0:T(8,128)(2,1)S(1)}, u32[]{:S(2)}, u32[]{:S(2)}) collective-permute-start(bf16[32,1024]{1,0:T(8,128)(2,1)S(1)} %get-tuple-element.105.refs_6_.refs_4_), channel_id=1, source_target_pairs={{0,8},{8,0},{1,9},{9,1},{2,10},{10,2},{3,11},{11,3},{4,12},{12,4},... | collective-permute-start | bytes 196616 | tf_op jit(solution)/shard_map/ppermute | solution.py:420
  80.5 4.8 %collective-permute-start.21 = (bf16[32,1024]{1,0:T(8,128)(2,1)S(1)}, bf16[32,1024]{1,0:T(8,128)(2,1)S(1)}, u32[]{:S(2)}, u32[]{:S(2)}) collective-permute-start(bf16[32,1024]{1,0:T(8,128)(2,1)S(1)} %collective-permute-done.17.refs_7_.refs_5_), channel_id=1, source_target_pairs={{0,8},{8,0},{1,9},{9,1},{2,10},{10,2},{3,11},{11,3},{4,12},{12,4},... | collective-permute-start | bytes 196616 | tf_op jit(solution)/shard_map/ppermute | solution.py:420
  87.8 2.3 %collective-permute-start.25 = (bf16[4,32,1024]{2,1,0:T(8,128)(2,1)S(1)}, bf16[4,32,1024]{2,1,0:T(8,128)(2,1)S(1)}, u32[]{:S(2)}, u32[]{:S(2)}) collective-permute-start(bf16[4,32,1024]{2,1,0:T(8,128)(2,1)S(1)} %get-tuple-element.121), channel_id=1, source_target_pairs={{0,8},{8,0},{1,9},{9,1},{2,10},{10,2},{3,11},{11,3},{4,12},{12,4},... | collective-permute-start | bytes 786440 | tf_op jit(solution)/shard_map/ppermute | solution.py:420
  89.6 25.3 %collective-permute-start.37 = (bf16[512,1024]{1,0:T(8,128)(2,1)S(1)}, bf16[512,1024]{1,0:T(8,128)(2,1)S(1)}, u32[]{:S(2)}, u32[]{:S(2)}) collective-permute-start(bf16[512,1024]{1,0:T(8,128)(2,1)S(1)} %get-tuple-element.128.refs_8_), channel_id=1, source_target_pairs={{0,1},{1,0},{2,3},{3,2},{4,5},{5,4},{6,7},{7,6},{8,9},{9,8},{10,11... | collective-permute-start | bytes 3145736 | tf_op jit(solution)/shard_map/ppermute | solution.py:1032
  90.1 5.9 %collective-permute-start.26 = (bf16[32,1024]{1,0:T(8,128)(2,1)S(1)}, bf16[32,1024]{1,0:T(8,128)(2,1)S(1)}, u32[]{:S(2)}, u32[]{:S(2)}) collective-permute-start(bf16[32,1024]{1,0:T(8,128)(2,1)S(1)} %get-tuple-element.123), channel_id=1, source_target_pairs={{0,2},{2,0},{4,6},{6,4},{1,3},{3,1},{5,7},{7,5},{8,10},{10,8},{12,... | collective-permute-start | bytes 196616 | tf_op jit(solution)/shard_map/ppermute | solution.py:407
  90.8 8.5 %collective-permute-start.27 = (bf16[32,1024]{1,0:T(8,128)(2,1)S(1)}, bf16[32,1024]{1,0:T(8,128)(2,1)S(1)}, u32[]{:S(2)}, u32[]{:S(2)}) collective-permute-start(bf16[32,1024]{1,0:T(8,128)(2,1)S(1)} %get-tuple-element.124), channel_id=1, source_target_pairs={{0,4},{2,6},{4,0},{6,2},{1,5},{3,7},{5,1},{7,3},{8,12},{10,14},{12... | collective-permute-start | bytes 196616 | tf_op jit(solution)/shard_map/ppermute | solution.py:407
  93.0 6.2 %collective-permute-start.28 = (bf16[32,1024]{1,0:T(8,128)(2,1)S(1)}, bf16[32,1024]{1,0:T(8,128)(2,1)S(1)}, u32[]{:S(2)}, u32[]{:S(2)}) collective-permute-start(bf16[32,1024]{1,0:T(8,128)(2,1)S(1)} %get-tuple-element.125), channel_id=1, source_target_pairs={{0,6},{2,4},{4,2},{6,0},{1,7},{3,5},{5,3},{7,1},{8,14},{10,12},{12... | collective-permute-start | bytes 196616 | tf_op jit(solution)/shard_map/ppermute | solution.py:407
  99.4 4.5 %collective-permute-start.29 = (bf16[32,1024]{1,0:T(8,128)(2,1)S(1)}, bf16[32,1024]{1,0:T(8,128)(2,1)S(1)}, u32[]{:S(2)}, u32[]{:S(2)}) collective-permute-start(bf16[32,1024]{1,0:T(8,128)(2,1)S(1)} %get-tuple-element.130.refs_10_.refs_8_), channel_id=1, source_target_pairs={{0,2},{2,0},{4,6},{6,4},{1,3},{3,1},{5,7},{7,5},{8,10},{10,8},{12,... | collective-permute-start | bytes 196616 | tf_op jit(solution)/shard_map/ppermute | solution.py:407
  100.7 6.7 %collective-permute-start.30 = (bf16[32,1024]{1,0:T(8,128)(2,1)S(1)}, bf16[32,1024]{1,0:T(8,128)(2,1)S(1)}, u32[]{:S(2)}, u32[]{:S(2)}) collective-permute-start(bf16[32,1024]{1,0:T(8,128)(2,1)S(1)} %get-tuple-element.130.refs_10_.refs_8_), channel_id=1, source_target_pairs={{0,4},{2,6},{4,0},{6,2},{1,5},{3,7},{5,1},{7,3},{8,12},{10,14},{12... | collective-permute-start | bytes 196616 | tf_op jit(solution)/shard_map/ppermute | solution.py:407
  102.0 6.2 %collective-permute-start.31 = (bf16[32,1024]{1,0:T(8,128)(2,1)S(1)}, bf16[32,1024]{1,0:T(8,128)(2,1)S(1)}, u32[]{:S(2)}, u32[]{:S(2)}) collective-permute-start(bf16[32,1024]{1,0:T(8,128)(2,1)S(1)} %get-tuple-element.130.refs_10_.refs_8_), channel_id=1, source_target_pairs={{0,6},{2,4},{4,2},{6,0},{1,7},{3,5},{5,3},{7,1},{8,14},{10,12},{12... | collective-permute-start | bytes 196616 | tf_op jit(solution)/shard_map/ppermute | solution.py:407
  103.9 4.3 %collective-permute-start.32 = (bf16[32,1024]{1,0:T(8,128)(2,1)S(1)}, bf16[32,1024]{1,0:T(8,128)(2,1)S(1)}, u32[]{:S(2)}, u32[]{:S(2)}) collective-permute-start(bf16[32,1024]{1,0:T(8,128)(2,1)S(1)} %get-tuple-element.130.refs_10_.refs_8_), channel_id=1, source_target_pairs={{0,8},{8,0},{1,9},{9,1},{2,10},{10,2},{3,11},{11,3},{4,12},{12,4},... | collective-permute-start | bytes 196616 | tf_op jit(solution)/shard_map/ppermute | solution.py:420
  103.9 4.8 %collective-permute-start.33 = (bf16[32,1024]{1,0:T(8,128)(2,1)S(1)}, bf16[32,1024]{1,0:T(8,128)(2,1)S(1)}, u32[]{:S(2)}, u32[]{:S(2)}) collective-permute-start(bf16[32,1024]{1,0:T(8,128)(2,1)S(1)} %collective-permute-done.29.refs_11_.refs_9_), channel_id=1, source_target_pairs={{0,8},{8,0},{1,9},{9,1},{2,10},{10,2},{3,11},{11,3},{4,12},{12,4},... | collective-permute-start | bytes 196616 | tf_op jit(solution)/shard_map/ppermute | solution.py:420
  108.2 7.0 %collective-permute-start.24 = (bf16[4,64,1024]{2,1,0:T(8,128)(2,1)S(1)}, bf16[4,64,1024]{2,1,0:T(8,128)(2,1)S(1)}, u32[]{:S(2)}, u32[]{:S(2)}) collective-permute-start(bf16[4,64,1024]{2,1,0:T(8,128)(2,1)S(1)} %get-tuple-element.113), channel_id=1, source_target_pairs={{0,8},{8,0},{1,9},{9,1},{2,10},{10,2},{3,11},{11,3},{4,12},{12,4},... | collective-permute-start | bytes 1572872 | tf_op jit(solution)/shard_map/ppermute | solution.py:420
  113.3 2.0 %collective-permute-start.36 = (bf16[4,64,1024]{2,1,0:T(8,128)(2,1)S(1)}, bf16[4,64,1024]{2,1,0:T(8,128)(2,1)S(1)}, u32[]{:S(2)}, u32[]{:S(2)}) collective-permute-start(bf16[4,64,1024]{2,1,0:T(8,128)(2,1)S(1)} %get-tuple-element.132), channel_id=1, source_target_pairs={{0,8},{8,0},{1,9},{9,1},{2,10},{10,2},{3,11},{11,3},{4,12},{12,4},... | collective-permute-start | bytes 1572872 | tf_op jit(solution)/shard_map/ppermute | solution.py:420
  115.5 13.4 %collective-permute-start.38 = (bf16[128,1024]{1,0:T(8,128)(2,1)S(1)}, bf16[128,1024]{1,0:T(8,128)(2,1)S(1)}, u32[]{:S(2)}, u32[]{:S(2)}) collective-permute-start(bf16[128,1024]{1,0:T(8,128)(2,1)S(1)} %get-tuple-element.136), channel_id=1, source_target_pairs={{0,2},{2,0},{4,6},{6,4},{1,3},{3,1},{5,7},{7,5},{8,10},{10,8},{12,... | collective-permute-start | bytes 786440 | tf_op jit(solution)/shard_map/ppermute | solution.py:407
  116.7 14.7 %collective-permute-start.39 = (bf16[128,1024]{1,0:T(8,128)(2,1)S(1)}, bf16[128,1024]{1,0:T(8,128)(2,1)S(1)}, u32[]{:S(2)}, u32[]{:S(2)}) collective-permute-start(bf16[128,1024]{1,0:T(8,128)(2,1)S(1)} %get-tuple-element.137), channel_id=1, source_target_pairs={{0,4},{2,6},{4,0},{6,2},{1,5},{3,7},{5,1},{7,3},{8,12},{10,14},{12... | collective-permute-start | bytes 786440 | tf_op jit(solution)/shard_map/ppermute | solution.py:407
  118.0 27.8 %collective-permute-start.44 = (bf16[256,1024]{1,0:T(8,128)(2,1)S(1)}, bf16[256,1024]{1,0:T(8,128)(2,1)S(1)}, u32[]{:S(2)}, u32[]{:S(2)}) collective-permute-start(bf16[256,1024]{1,0:T(8,128)(2,1)S(1)} %get-tuple-element.145), channel_id=1, source_target_pairs={{0,16},{16,0},{1,17},{17,1},{2,18},{18,2},{3,19},{19,3},{4,20},{20... | collective-permute-start | bytes 1572872 | tf_op jit(solution)/shard_map/ppermute | solution.py:1052
  121.6 18.2 %collective-permute-start.45 = (bf16[320,512]{1,0:T(8,128)(2,1)S(1)}, bf16[320,512]{1,0:T(8,128)(2,1)S(1)}, u32[]{:S(2)}, u32[]{:S(2)}) collective-permute-start(bf16[320,512]{1,0:T(8,128)(2,1)S(1)} %get-tuple-element.151), channel_id=1, source_target_pairs={{0,1},{1,0},{16,17},{17,16},{2,3},{3,2},{18,19},{19,18},{4,5},{5,4... | collective-permute-start | bytes 983048 | tf_op jit(solution)/shard_map/ppermute | solution.py:412
  121.7 24.0 %collective-permute-start.46 = (bf16[320,512]{1,0:T(8,128)(2,1)S(1)}, bf16[320,512]{1,0:T(8,128)(2,1)S(1)}, u32[]{:S(2)}, u32[]{:S(2)}) collective-permute-start(bf16[320,512]{1,0:T(8,128)(2,1)S(1)} %get-tuple-element.152), channel_id=1, source_target_pairs={{0,16},{1,17},{16,0},{17,1},{2,18},{3,19},{18,2},{19,3},{4,20},{5,... | collective-permute-start | bytes 983048 | tf_op jit(solution)/shard_map/ppermute | solution.py:412
  128.9 16.9 %collective-permute-start.47 = (bf16[320,512]{1,0:T(8,128)(2,1)S(1)}, bf16[320,512]{1,0:T(8,128)(2,1)S(1)}, u32[]{:S(2)}, u32[]{:S(2)}) collective-permute-start(bf16[320,512]{1,0:T(8,128)(2,1)S(1)} %get-tuple-element.153), channel_id=1, source_target_pairs={{0,17},{1,16},{16,1},{17,0},{2,19},{3,18},{18,3},{19,2},{4,21},{5,... | collective-permute-start | bytes 983048 | tf_op jit(solution)/shard_map/ppermute | solution.py:412
  131.4 8.2 %collective-permute-start.40 = (bf16[128,1024]{1,0:T(8,128)(2,1)S(1)}, bf16[128,1024]{1,0:T(8,128)(2,1)S(1)}, u32[]{:S(2)}, u32[]{:S(2)}) collective-permute-start(bf16[128,1024]{1,0:T(8,128)(2,1)S(1)} %get-tuple-element.138), channel_id=1, source_target_pairs={{0,6},{2,4},{4,2},{6,0},{1,7},{3,5},{5,3},{7,1},{8,14},{10,12},{12... | collective-permute-start | bytes 786440 | tf_op jit(solution)/shard_map/ppermute | solution.py:407
  147.5 7.8 %collective-permute-start.41 = (bf16[32,1024]{1,0:T(8,128)(2,1)S(1)}, bf16[32,1024]{1,0:T(8,128)(2,1)S(1)}, u32[]{:S(2)}, u32[]{:S(2)}) collective-permute-start(bf16[32,1024]{1,0:T(8,128)(2,1)S(1)} %get-tuple-element.140), channel_id=1, source_target_pairs={{0,1},{1,0},{16,17},{17,16},{2,3},{3,2},{18,19},{19,18},{4,5},{5,4... | collective-permute-start | bytes 196616 | tf_op jit(solution)/shard_map/ppermute | solution.py:412
  149.3 13.8 %collective-permute-start.49 = (bf16[64,1024]{1,0:T(8,128)(2,1)S(1)}, bf16[64,1024]{1,0:T(8,128)(2,1)S(1)}, u32[]{:S(2)}, u32[]{:S(2)}) collective-permute-start(bf16[64,1024]{1,0:T(8,128)(2,1)S(1)} %get-tuple-element.157), channel_id=1, source_target_pairs={{0,2},{2,0},{4,6},{6,4},{1,3},{3,1},{5,7},{7,5},{8,10},{10,8},{12,... | collective-permute-start | bytes 393224 | tf_op jit(solution)/shard_map/ppermute | solution.py:407
  150.3 12.9 %collective-permute-start.50 = (bf16[64,1024]{1,0:T(8,128)(2,1)S(1)}, bf16[64,1024]{1,0:T(8,128)(2,1)S(1)}, u32[]{:S(2)}, u32[]{:S(2)}) collective-permute-start(bf16[64,1024]{1,0:T(8,128)(2,1)S(1)} %get-tuple-element.158), channel_id=1, source_target_pairs={{0,4},{2,6},{4,0},{6,2},{1,5},{3,7},{5,1},{7,3},{8,12},{10,14},{12... | collective-permute-start | bytes 393224 | tf_op jit(solution)/shard_map/ppermute | solution.py:407
  151.9 11.3 %collective-permute-start.51 = (bf16[64,1024]{1,0:T(8,128)(2,1)S(1)}, bf16[64,1024]{1,0:T(8,128)(2,1)S(1)}, u32[]{:S(2)}, u32[]{:S(2)}) collective-permute-start(bf16[64,1024]{1,0:T(8,128)(2,1)S(1)} %get-tuple-element.159), channel_id=1, source_target_pairs={{0,6},{2,4},{4,2},{6,0},{1,7},{3,5},{5,3},{7,1},{8,14},{10,12},{12... | collective-permute-start | bytes 393224 | tf_op jit(solution)/shard_map/ppermute | solution.py:407
  153.8 5.0 %collective-permute-start.42 = (bf16[32,1024]{1,0:T(8,128)(2,1)S(1)}, bf16[32,1024]{1,0:T(8,128)(2,1)S(1)}, u32[]{:S(2)}, u32[]{:S(2)}) collective-permute-start(bf16[32,1024]{1,0:T(8,128)(2,1)S(1)} %get-tuple-element.141), channel_id=1, source_target_pairs={{0,16},{1,17},{16,0},{17,1},{2,18},{3,19},{18,2},{19,3},{4,20},{5,... | collective-permute-start | bytes 196616 | tf_op jit(solution)/shard_map/ppermute | solution.py:412
  155.2 5.2 %collective-permute-start.43 = (bf16[32,1024]{1,0:T(8,128)(2,1)S(1)}, bf16[32,1024]{1,0:T(8,128)(2,1)S(1)}, u32[]{:S(2)}, u32[]{:S(2)}) collective-permute-start(bf16[32,1024]{1,0:T(8,128)(2,1)S(1)} %get-tuple-element.142), channel_id=1, source_target_pairs={{0,17},{1,16},{16,1},{17,0},{2,19},{3,18},{18,3},{19,2},{4,21},{5,... | collective-permute-start | bytes 196616 | tf_op jit(solution)/shard_map/ppermute | solution.py:412
  (20 other events, 142.2 us)

commit v7 on v6

--- a/solution.py
+++ b/solution.py
@@ -291,6 +291,22 @@
     return lax.dot_general(left, right, dims, preferred_element_type=F32)
 
 
+WORK = {
+    "attention_back_kernel": 1200000000,
+    "attention_kernel": 1200000000,
+    "compact_kernel": 10000000000,
+    "ff_grads_kernel": 600000000,
+    "forward_kernel": 600000000,
+    "grads_kernel": 500000000,
+    "result_kernel": 800000000,
+    "update_kernel": 800000000,
+}
+
+
+def work_of(body):
+    return WORK.get(getattr(body, "func", body).__name__, 0)
+
+
 class Far:
     def __init__(self, item, start=0, count=None, dim=0):
         self.item, self.start, self.count, self.dim = item, start, count, dim
@@ -339,7 +355,7 @@
         self.started = True
 
 
-def local_call(body, outs, args, flops=0, scratch=(), scalars=0, after=()):
+def local_call(body, outs, args, scratch=(), scalars=0, after=()):
     far_in = [a if isinstance(a, Far) else None for a in args]
     far_out = [isinstance(o, Far) for o in outs]
     outs = [o.item if f else o for o, f in zip(outs, far_out)]
@@ -394,7 +410,9 @@
             ],
             scratch_shapes=list(scratch) + stages,
             compiler_params=pltpu.CompilerParams(vmem_limit_bytes=32 * 2**20),
-            cost_estimate=pl.CostEstimate(flops=int(flops), bytes_accessed=0, transcendentals=0),
+            cost_estimate=pl.CostEstimate(
+                flops=work_of(body), bytes_accessed=0, transcendentals=0
+            ),
         )(*args, *after)
     )
 
@@ -528,15 +546,19 @@
 def relay_kernel(got, w_out, w_down, first, up):
     members, rows, lanes = got.shape
     half = lanes // 2
+    size = members * rows
+    blocks = [b[:, j * half : (j + 1) * half] for b in (w_out, w_down) for j in range(2)]
     for line in range(first.shape[0]):
-        at = members * rows
-        first[line, :at] = got[:, :, :half].reshape(at, half)
-        for block in (w_out, w_down):
-            size = block.shape[0]
-            for j in range(2):
-                first[line, at : at + size] = block[:, j * half : (j + 1) * half]
-                at += size
-    up[...] = got[:, :, half:].reshape(members * rows, half)
+        first[line, :size] = got[:, :, :half].reshape(size, half)
+        at = size
+        for block in blocks[: 3]:
+            first[line, at : at + block.shape[0]] = block
+            at += block.shape[0]
+    up[:size] = got[:, :, half:].reshape(size, half)
+    at = size
+    for block in blocks[3 :]:
+        up[at : at + block.shape[0]] = block
+        at += block.shape[0]
 
 
 def spread_kernel(dims, where, chosen, chosen_t, spread):
@@ -618,19 +640,25 @@
                 out[to : to + rows] = piece
 
 
-def attention_kernel(dims, members, where, spread, qkv_blocks, *refs):
-    ny, nx, rows, cap = dims
-    blocks, outs = refs[:members], refs[members:]
-    picked_o, normed_o, w_o, first_o, wo_o, vecs_o = outs[:6]
-    joined_o, att_o, exact_o, near_o, far_o, vec_s = outs[6:]
+def compact_kernel(spread, *refs):
+    *blocks, picked_o, own_o, cot_o = refs
+    hot = spread[...]
+    half = blocks[0].shape[0] // 2
+    picked = mm(hot, jnp.concatenate([b[:half] for b in blocks], 0)).astype(BF16)
+    picked_o[...] = picked
+    own_o[...] = picked[: own_o.shape[0]]
+    cot_o[...] = mm(hot, jnp.concatenate([b[half:] for b in blocks], 0)).astype(BF16)
+
+
+def attention_kernel(dims, members, where, picked_r, qkv_blocks, *outs):
+    ny, nx, rows = dims
+    normed_o, w_o, wo_o, vecs_o = outs[:4]
+    joined_o, att_o, exact_o, near_o, far_o, vec_s = outs[4:]
     heads = ny
     cols = 3 * heads * HDIM
-    routed, width = picked_o.shape
+    routed, width = picked_r.shape
     own = routed // members
-    picked_low = mm(spread[...], jnp.concatenate([b[...] for b in blocks], 0)).astype(BF16)
-    picked_o[...] = picked_low
-    picked = picked_low.astype(F32)
-    first_o[...] = picked_low[:own]
+    picked = picked_r[...].astype(F32)
     natural_rows(qkv_blocks, (ny, members, nx, rows), 0, cols, w_o)
     natural_rows(qkv_blocks, (ny, members, nx, rows), cols, 128, vec_s)
     line_rows(qkv_blocks, members * rows, wo_o)
@@ -663,18 +691,27 @@
         far[k] = values[(depth + k) * own : (depth + k + 1) * own]
 
 
-def update_kernel(members, spread, picked, vecs, downs, *refs):
-    blocks, outs = refs[:members], refs[members:]
-    gate_o, cot_o, first_o, d_result_o, d_active_o, w_o = outs
+def update_kernel(dims, where, picked, vecs, cot_r, *refs):
+    lines, start = dims
+    *refs, gate_o, first_o, d_result_o, d_active_o, w_o = refs
+    ups, downs = refs[:lines], refs[lines:]
     logit = jnp.sum(picked[...].astype(F32) * vecs[2:3, :], 1, keepdims=True)
     gate = 1.0 / (1.0 + jnp.exp(-logit))
     gate_o[...] = gate
-    cot = mm(spread[...], jnp.concatenate([b[...] for b in blocks], 0)).astype(BF16)
-    cot_o[...] = cot
+    cot = cot_r[...]
     first_o[...] = cot[: first_o.shape[0]]
     d_result = (gate * cot.astype(F32)).astype(BF16)
     d_result_o[...] = d_result
-    line_rows(downs, 0, w_o)
+    half = w_o.shape[1] // 2
+    size = w_o.shape[0] // lines
+    for down in downs:
+        for q in range(lines):
+            w_o[q * size : (q + 1) * size, :half] = down[q]
+    for k, block in enumerate(ups):
+        to = pl.ds(pl.multiple_of((where[2] ^ k) * size, size), size)
+        if not downs:
+            w_o[to, :half] = block[start : start + size]
+        w_o[to, half:] = block[block.shape[0] - size :]
     d_active_o[...] = mm(d_result, w_o[...], NT)
 
 
@@ -945,8 +982,6 @@
         partial(stack_kernel, cap), [((2 * lines * cap, width), BF16)], line_slots, after=(hot,)
     )
     slots = gather_group([line_slots])
-    half = lines * cap
-    picked_slots, cot_slots = [Far(b, 0, half) for b in slots], [Far(b, half, half) for b in slots]
 
     vecs = [v.reshape(1, rows) for v in (gain_attn, gain_mlp, router)]
     (columns,) = local_call(
@@ -960,54 +995,55 @@
     base = members * rows + 2 * rows
     first, up = local_call(
         relay_kernel,
-        [Far(((lines, base + 2 * ff_rows, half), BF16)), ((members * rows, half), BF16)],
+        [
+            Far(((lines, base + ff_rows, half), BF16)),
+            ((members * rows + ff_rows, half), BF16),
+        ],
         (got_cols, w_out, w_down),
         after=(line_slots,),
     )
     first = lax.all_to_all(first, ("y", "x"), 0, 0, tiled=True)
-    got_down = Far(first, base, 2 * ff_rows, 1)
+    got_down = (Far(first, base, ff_rows, 1),)
     got_up = gather_lines(up)
 
-    picked, normed, full_qkv, picked_own, full_out, full_vecs, joined, attended, exact, near, far = (
-        local_call(
-            partial(attention_kernel, (ny, nx, rows, cap), members),
-            [
-                ((routed, width), BF16),
-                ((routed, width), BF16),
-                ((width, cols), BF16),
-                (block, BF16),
-                ((heads * HDIM, width), BF16),
-                ((8, width), F32),
-                ((routed, cols), BF16),
-                ((routed, heads * HDIM), BF16),
-                ((routed, heads * HDIM), F32),
-            ]
-            + halves,
-            (where, spread, Far(first, 0, base, 1), *picked_slots),
-            flops=1.2e9,
-            scratch=[pltpu.VMEM((width, 128), BF16)],
-            scalars=1,
-        )
+    picked, picked_own, cot = local_call(
+        compact_kernel,
+        [((routed, width), BF16), (block, BF16), ((routed, width), BF16)],
+        (spread, *slots),
+    )
+    normed, full_qkv, full_out, full_vecs, joined, attended, exact, near, far = local_call(
+        partial(attention_kernel, (ny, nx, rows), members),
+        [
+            ((routed, width), BF16),
+            ((width, cols), BF16),
+            ((heads * HDIM, width), BF16),
+            ((8, width), F32),
+            ((routed, cols), BF16),
+            ((routed, heads * HDIM), BF16),
+            ((routed, heads * HDIM), F32),
+        ]
+        + halves,
+        (where, picked, Far(first, 0, base, 1)),
+        scratch=[pltpu.VMEM((width, 128), BF16)],
+        scalars=1,
     )
     terms = scatter_group(near, far)
-    gate, cot, cot_own, d_result, d_active, full_down = local_call(
-        partial(update_kernel, members),
+    gate, cot_own, d_result, d_active, full_down = local_call(
+        partial(update_kernel, (lines, members * rows)),
         [
             ((routed, 1), F32),
-            ((routed, width), BF16),
             (block, BF16),
             ((routed, width), BF16),
             ((routed, wide), F32),
             ((wide, width), BF16),
         ],
-        (spread, picked, full_vecs, got_down, *cot_slots),
-        flops=8e8,
+        (where, picked, full_vecs, cot, *got_up, *got_down),
+        scalars=1,
     )
     hidden, normed_own = local_call(
         hidden_kernel,
         [(block, F32), (block, BF16)],
         (picked_own, full_vecs, *terms),
-        after=(d_active,),
     )
     normed_mlp = gather_group([normed_own])
 
@@ -1015,7 +1051,6 @@
         partial(forward_kernel, (ny, members, nx, rows), members),
         [((routed, wide), BF16)] * 2 + halves,
         (where, d_active, *got_up, *normed_mlp),
-        flops=6e8,
         scratch=[pltpu.VMEM((width, wide), BF16)],
         scalars=1,
     )
@@ -1025,7 +1060,6 @@
         partial(ff_grads_kernel, (ny, nx, rows, ff_rows), members),
         [((half_rows, width), BF16)] * 2,
         (where, active, d_upper, d_result, *normed_mlp),
-        flops=6e8,
         scratch=[pltpu.VMEM((wide, width), BF16), pltpu.VMEM((width, wide), BF16)],
         scalars=1,
     )
@@ -1034,7 +1068,6 @@
         result_kernel,
         [((routed, 1), F32)] + slot_halves,
         (active, attended, full_down, full_out, cot, gate, spread),
-        flops=8e8,
     )
     d_branch_own, d_hidden, gain_m = local_call(
         partial(hidden_back_kernel, own),
@@ -1056,7 +1089,6 @@
         slot_halves + [((routed, cols), BF16), ((routed, width), BF16)],
         (where, full_out, joined, exact, full_qkv, full_vecs, picked)
         + (logit, d_hidden, spread, *d_branch),
-        flops=1.2e9,
         scalars=1,
     )
     far = send_c(far)
@@ -1064,7 +1096,6 @@
         partial(grads_kernel, (ny, nx, rows), members),
         [((members * rows + 2 * rows, cols + 128), BF16)] * lines,
         (where, normed, d_joined, attended, gain_a, gain_m, picked, logit, *d_branch),
-        flops=5e8,
         scratch=[
             pltpu.VMEM((width, cols), BF16),
             pltpu.VMEM((width, 128), BF16),

time: 165 us -> 161 us (0.976)
  starting transfers between devices: 62.2 us -> 59.9 us
  waiting for transfers between devices: 67.6 us -> 65.4 us
    all_to_all x1, waiting for transfers between devices: 3.2 us -> 0.01 us  [grouped(): got_cols = lax.all_to_all(columns, ('c', 'z'), 0, 0, tiled=True)]
    ppermute x12, waiting for transfers between devices: 12.5 us -> 14.6 us  [send_lines(): lax.ppermute(b, ('y', 'x'), f)]
    pallas_call x23 -> x24, Pallas kernels: 31 us -> 31.2 us  [local_call(): pl.pallas_call(run, out_shape=shapes, in_specs=[pl.BlockSpec(memory_space...]
  transfers between devices with their start and end apart: 54 -> 54, of which waited for: 26 -> 28; matrix products, arithmetic and copies ran while one was open for 1% -> 0% of each run, Pallas kernels for 11% -> 13%
where the time goes in v7:
time: 161 us; the launch traced here: 160 us
  waiting for transfers between devices  65.4 us (41%)
  starting transfers between devices  59.9 us (37%)
  Pallas kernels  31.2 us (19%)
  local copies, waits for them, and re-layouts  2.85 us (2%)
    ppermute x21, waiting for transfers between devices, send_z(): lax.ppermute(b, 'z', f)  41.9 us
    pallas_call x24, Pallas kernels, local_call(): pl.pallas_call(run, out_shape=shapes, in_specs=[pl.BlockSpec(memory_space...  31.2 us
    ppermute x21, starting transfers between devices, send_z(): lax.ppermute(b, 'z', f)  30.7 us
    ppermute x12, waiting for transfers between devices, send_lines(): lax.ppermute(b, ('y', 'x'), f)  14.6 us
    ppermute x12, starting transfers between devices, send_lines(): lax.ppermute(b, ('y', 'x'), f)  13.4 us
    all_to_all x1, starting transfers between devices, grouped(): got_cols = lax.all_to_all(columns, ('c', 'z'), 0, 0, tiled=True)  6.47 us
    all_to_all x1, waiting for transfers between devices, grouped(): first = lax.all_to_all(first, ('y', 'x'), 0, 0, tiled=True)  5 us
    all_to_all x1, starting transfers between devices, grouped(): first = lax.all_to_all(first, ('y', 'x'), 0, 0, tiled=True)  4.43 us
  transfers between devices with their start and end apart: 54, of which 28 were waited for; matrix products, arithmetic and copies ran while one was open for 0% of the time, Pallas kernels for 13%

profile of v7, /device:TPU:0, one launch (start us, length us, event | category | flops | bytes accessed | tf_op | source)
XLA Modules:
  0.0 160.4 jit_solution(16529066262809254702)
XLA Ops:
  0.7 2.2 %shard_map.173 = bf16[8,32,1024]{2,1,0:T(8,128)(2,1)} custom-call(bf16[32,3072]{1,0:T(8,128)(2,1)} %refs_0_.1, bf16[32,4096]{1,0:T(8,128)(2,1)} %refs_1_.4, bf16[1,32]{1,0:T(2,128)(2,1)} %bitcast.14, bf16[1,32]{1,0:T(2,128)(2,1)} %bitcast.15, bf16[1,32]{1,0:T(2,128)(2,1)} %bitcast.16), custom_call_target="tpu_custom_call" | custom-call | tf_op jit(solution)/shard_map/pallas_call | solution.py:404
  2.9 6.5 %all-to-all-start = ((bf16[8,32,1024]{2,1,0:T(8,128)(2,1)}), bf16[8,32,1024]{2,1,0:T(8,128)(2,1)S(1)}, u32[]{:S(2)}, u32[]{:S(2)}) async-start(bf16[8,32,1024]{2,1,0:T(8,128)(2,1)} %shard_map.173), calls=%async_computation | async-start | bytes 1048576 | tf_op jit(solution)/shard_map/all_to_all | solution.py:993
  9.6 1.5 shard_map.169
  11.1 1.6 collective-permute-start
  12.7 1.5 collective-permute-start.1
  14.7 1.8 %shard_map.170.refs_4_.refs_0_.refs_6_.refs_9_ = bf16[256,512]{1,0:T(8,128)(2,1)} custom-call(s32[5]{0:T(128)S(1)} %stack.23.refs_0_, s32[4,256]{1,0:T(4,128)S(1)} %copy-done.5, s32[256,4]{1,0:T(8,128)S(1)} %bitcast.13), custom_call_target="tpu_custom_call" | custom-call | tf_op jit(solution)/shard_map/pallas_call | solution.py:404
  16.9 2.4 %collective-permute-done.2.refs_3_ = bf16[32,1024]{1,0:T(8,128)(2,1)S(1)} collective-permute-done((bf16[32,1024]{1,0:T(8,128)(2,1)S(1)}, bf16[32,1024]{1,0:T(8,128)(2,1)S(1)}, u32[]{:S(2)}, u32[]{:S(2)}) %collective-permute-start.2) | collective-permute-done | bytes 65568 | tf_op jit(solution)/shard_map/ppermute | solution.py:430
  20.3 2.1 %collective-permute-start.3 = (bf16[128,1024]{1,0:T(8,128)(2,1)S(1)}, bf16[128,1024]{1,0:T(8,128)(2,1)S(1)}, u32[]{:S(2)}, u32[]{:S(2)}) collective-permute-start(bf16[128,1024]{1,0:T(8,128)(2,1)S(1)} %shard_map.171.refs_1_.refs_3_), channel_id=1, source_target_pairs={{0,2},{2,0},{4,6},{6,4},{1,3},{3,1},{5,7},{7,5},{8,10},{10,8},{12,... | collective-permute-start | bytes 786440 | tf_op jit(solution)/shard_map/ppermute | solution.py:425
  22.4 2.4 %collective-permute-start.4 = (bf16[128,1024]{1,0:T(8,128)(2,1)S(1)}, bf16[128,1024]{1,0:T(8,128)(2,1)S(1)}, u32[]{:S(2)}, u32[]{:S(2)}) collective-permute-start(bf16[128,1024]{1,0:T(8,128)(2,1)S(1)} %shard_map.171.refs_1_.refs_3_), channel_id=1, source_target_pairs={{0,4},{2,6},{4,0},{6,2},{1,5},{3,7},{5,1},{7,3},{8,12},{10,14},{12... | collective-permute-start | bytes 786440 | tf_op jit(solution)/shard_map/ppermute | solution.py:425
  26.2 4.4 %all-to-all-start.1 = ((bf16[4,448,512]{2,1,0:T(8,128)(2,1)}), bf16[4,448,512]{2,1,0:T(8,128)(2,1)}, u32[]{:S(2)}, u32[]{:S(2)}) async-start(bf16[4,448,512]{2,1,0:T(8,128)(2,1)} %get-tuple-element.94), calls=%async_computation.1 | async-start | bytes 3670016 | tf_op jit(solution)/shard_map/all_to_all | solution.py:1005
  30.8 5.5 %collective-permute-done.3.refs_2_ = bf16[128,1024]{1,0:T(8,128)(2,1)S(1)} collective-permute-done((bf16[128,1024]{1,0:T(8,128)(2,1)S(1)}, bf16[128,1024]{1,0:T(8,128)(2,1)S(1)}, u32[]{:S(2)}, u32[]{:S(2)}) %collective-permute-start.3) | collective-permute-done | bytes 262176 | tf_op jit(solution)/shard_map/ppermute | solution.py:425
  36.4 7.4 %collective-permute-done.4.refs_3_ = bf16[128,1024]{1,0:T(8,128)(2,1)S(1)} collective-permute-done((bf16[128,1024]{1,0:T(8,128)(2,1)S(1)}, bf16[128,1024]{1,0:T(8,128)(2,1)S(1)}, u32[]{:S(2)}, u32[]{:S(2)}) %collective-permute-start.4) | collective-permute-done | bytes 262176 | tf_op jit(solution)/shard_map/ppermute | solution.py:425
  46.6 1.7 %shard_map.172 = (bf16[256,1024]{1,0:T(8,128)(2,1)S(1)}, bf16[32,1024]{1,0:T(8,128)(2,1)S(1)}, bf16[256,1024]{1,0:T(8,128)(2,1)S(1)}) custom-call(bf16[256,512]{1,0:T(8,128)(2,1)} %shard_map.170.refs_4_.refs_0_.refs_6_.refs_9_, bf16[128,1024]{1,0:T(8,128)(2,1)S(1)} %shard_map.171.refs_1_.refs_3_, bf16[128,1024]{1,0:T(8,128)(2,1)S(1)} %collective-permute-done.3.refs_2_, ...), custom_call_target="tpu_custom_call" | custom-call | flops 10000000000 | tf_op jit(solution)/shard_map/pallas_call | solution.py:404
  48.3 5.0 %all-to-all-done.1.refs_2_.refs_8_ = bf16[4,448,512]{2,1,0:T(8,128)(2,1)} async-done(((bf16[4,448,512]{2,1,0:T(8,128)(2,1)}), bf16[4,448,512]{2,1,0:T(8,128)(2,1)}, u32[]{:S(2)}, u32[]{:S(2)}) %all-to-all-start.1) | async-done | bytes 1835040 | tf_op jit(solution)/shard_map/all_to_all | solution.py:1005
  53.3 3.3 %shard_map.175 = (bf16[256,1024]{1,0:T(8,128)(2,1)S(1)}, bf16[1024,384]{1,0:T(8,128)(2,1)S(1)}, bf16[128,1024]{1,0:T(8,128)(2,1)S(1)}, f32[8,1024]{1,0:T(8,128)S...) custom-call(s32[5]{0:T(128)S(1)} %stack.23.refs_0_, ...), custom_call_target="tpu_custom_call" | custom-call | flops 1200000000 | tf_op jit(solution)/shard_map/pallas_call | solution.py:404
  56.7 1.5 collective-permute-start.10
  58.8 1.5 collective-permute-start.12
  60.4 2.1 %collective-permute-start.15 = (bf16[32,1024]{1,0:T(8,128)(2,1)S(1)}, bf16[32,1024]{1,0:T(8,128)(2,1)S(1)}, u32[]{:S(2)}, u32[]{:S(2)}) collective-permute-start(bf16[32,1024]{1,0:T(8,128)(2,1)S(1)} %get-tuple-element.104), channel_id=1, source_target_pairs={{0,4},{2,6},{4,0},{6,2},{1,5},{3,7},{5,1},{7,3},{8,12},{10,14},{12... | collective-permute-start | bytes 196616 | tf_op jit(solution)/shard_map/ppermute | solution.py:425
  62.5 2.5 %collective-permute-done.14.refs_3_ = bf16[32,1024]{1,0:T(8,128)(2,1)S(1)} collective-permute-done((bf16[32,1024]{1,0:T(8,128)(2,1)S(1)}, bf16[32,1024]{1,0:T(8,128)(2,1)S(1)}, u32[]{:S(2)}, u32[]{:S(2)}) %collective-permute-start.14) | collective-permute-done | bytes 65568 | tf_op jit(solution)/shard_map/ppermute | solution.py:425
  65.0 1.5 collective-permute-start.16
  67.2 4.0 %collective-permute-done.16.refs_5_ = bf16[32,1024]{1,0:T(8,128)(2,1)S(1)} collective-permute-done((bf16[32,1024]{1,0:T(8,128)(2,1)S(1)}, bf16[32,1024]{1,0:T(8,128)(2,1)S(1)}, u32[]{:S(2)}, u32[]{:S(2)}) %collective-permute-start.16) | collective-permute-done | bytes 65568 | tf_op jit(solution)/shard_map/ppermute | solution.py:425
  71.4 1.9 %collective-permute-start.18 = (bf16[32,1024]{1,0:T(8,128)(2,1)S(1)}, bf16[32,1024]{1,0:T(8,128)(2,1)S(1)}, u32[]{:S(2)}, u32[]{:S(2)}) collective-permute-start(bf16[32,1024]{1,0:T(8,128)(2,1)S(1)} %get-tuple-element.106.refs_6_.refs_4_), channel_id=1, source_target_pairs={{0,4},{2,6},{4,0},{6,2},{1,5},{3,7},{5,1},{7,3},{8,12},{10,14},{12... | collective-permute-start | bytes 196616 | tf_op jit(solution)/shard_map/ppermute | solution.py:425
  73.4 2.4 %collective-permute-start.19 = (bf16[32,1024]{1,0:T(8,128)(2,1)S(1)}, bf16[32,1024]{1,0:T(8,128)(2,1)S(1)}, u32[]{:S(2)}, u32[]{:S(2)}) collective-permute-start(bf16[32,1024]{1,0:T(8,128)(2,1)S(1)} %get-tuple-element.106.refs_6_.refs_4_), channel_id=1, source_target_pairs={{0,6},{2,4},{4,2},{6,0},{1,7},{3,5},{5,3},{7,1},{8,14},{10,12},{12... | collective-permute-start | bytes 196616 | tf_op jit(solution)/shard_map/ppermute | solution.py:425
  75.8 2.0 %collective-permute-done.11.refs_6_.refs_4_ = bf16[384,512]{1,0:T(8,128)(2,1)S(1)} collective-permute-done((bf16[384,512]{1,0:T(8,128)(2,1)S(1)}, bf16[384,512]{1,0:T(8,128)(2,1)S(1)}, u32[]{:S(2)}, u32[]{:S(2)}) %collective-permute-start.11) | collective-permute-done | bytes 393248 | tf_op jit(solution)/shard_map/ppermute | solution.py:430
  79.4 2.2 %shard_map.176 = (f32[256,1]{1,0:T(8,128)S(1)}, bf16[32,1024]{1,0:T(8,128)(2,1)S(1)}, bf16[256,1024]{1,0:T(8,128)(2,1)S(1)}, f32[256,512]{1,0:T(8,128)S(1)}, bf16[512,1024]{1,0:T(8,128)(2,1)S(1)}) custom-call(s32[5]{0:T(128)S(1)} %stack.23.refs_0_, bf16[256,1024]{1,0:T(8,128)(2,1)S(1)} %get-tuple-element.93.refs_1_.refs_6_, ...), custom_call_target="tpu_custom_call" | custom-call | flops 800000000 | tf_op jit(solution)/shard_map/pallas_call | solution.py:404
  81.7 1.6 shard_map.179
  85.3 1.5 collective-permute-start.37
  86.9 3.0 %collective-permute-start.27 = (bf16[32,1024]{1,0:T(8,128)(2,1)S(1)}, bf16[32,1024]{1,0:T(8,128)(2,1)S(1)}, u32[]{:S(2)}, u32[]{:S(2)}) collective-permute-start(bf16[32,1024]{1,0:T(8,128)(2,1)S(1)} %get-tuple-element.124), channel_id=1, source_target_pairs={{0,4},{2,6},{4,0},{6,2},{1,5},{3,7},{5,1},{7,3},{8,12},{10,14},{12... | collective-permute-start | bytes 196616 | tf_op jit(solution)/shard_map/ppermute | solution.py:425
  89.9 1.4 collective-permute-start.28
  91.3 1.4 shard_map.180
  92.8 2.1 %collective-permute-done.27.refs_6_ = bf16[32,1024]{1,0:T(8,128)(2,1)S(1)} collective-permute-done((bf16[32,1024]{1,0:T(8,128)(2,1)S(1)}, bf16[32,1024]{1,0:T(8,128)(2,1)S(1)}, u32[]{:S(2)}, u32[]{:S(2)}) %collective-permute-start.27) | collective-permute-done | bytes 65568 | tf_op jit(solution)/shard_map/ppermute | solution.py:425
  98.3 2.3 %collective-permute-start.31 = (bf16[32,1024]{1,0:T(8,128)(2,1)S(1)}, bf16[32,1024]{1,0:T(8,128)(2,1)S(1)}, u32[]{:S(2)}, u32[]{:S(2)}) collective-permute-start(bf16[32,1024]{1,0:T(8,128)(2,1)S(1)} %get-tuple-element.130.refs_10_.refs_8_), channel_id=1, source_target_pairs={{0,6},{2,4},{4,2},{6,0},{1,7},{3,5},{5,3},{7,1},{8,14},{10,12},{12... | collective-permute-start | bytes 196616 | tf_op jit(solution)/shard_map/ppermute | solution.py:425
  105.8 3.9 %shard_map.184 = (bf16[4,64,1024]{2,1,0:T(8,128)(2,1)S(1)}, bf16[4,64,1024]{2,1,0:T(8,128)(2,1)S(1)}, bf16[256,384]{1,0:T(8,128)(2,1)S(1)}, bf16[256,1024]{1,0:T(8,128)(2,1)S(1)}) custom-call(s32[5]{0:T(128)S(1)} %stack.23.refs_0_, bf16[128,1024]{1,0:T(8,128)(2,1)S(1)} %get-tuple-element.110.refs_3_.refs_1_, ...), custom_call_target="tpu_custom_call" | custom-call | flops 1200000000 | tf_op jit(solution)/shard_map/pallas_call | solution.py:404
  112.6 2.1 %collective-permute-start.39 = (bf16[128,1024]{1,0:T(8,128)(2,1)S(1)}, bf16[128,1024]{1,0:T(8,128)(2,1)S(1)}, u32[]{:S(2)}, u32[]{:S(2)}) collective-permute-start(bf16[128,1024]{1,0:T(8,128)(2,1)S(1)} %get-tuple-element.137), channel_id=1, source_target_pairs={{0,4},{2,6},{4,0},{6,2},{1,5},{3,7},{5,1},{7,3},{8,12},{10,14},{12... | collective-permute-start | bytes 786440 | tf_op jit(solution)/shard_map/ppermute | solution.py:425
  115.5 1.7 %shard_map.189 = (bf16[320,512]{1,0:T(8,128)(2,1)S(1)}, bf16[320,512]{1,0:T(8,128)(2,1)S(1)}, bf16[320,512]{1,0:T(8,128)(2,1)S(1)}, bf16[320,512]{1,0:T(8,128)(2,1)S(1)}) custom-call(s32[5]{0:T(128)S(1)} %stack.23.refs_0_, bf16[256,1024]{1,0:T(8,128)(2,1)S(1)} %get-tuple-element.146.refs_1_, bf16[256,384]{1,0:T(8,128)(2,1)S(1)} %get-tuple-element.147.refs_2_, ...), custom_call_target="tpu_custom_call" | custom-call | flops 500000000 | tf_op jit(solution)/shard_map/pallas_call | solution.py:404
  117.2 1.4 collective-permute-start.45
  119.2 6.0 %collective-permute-done.38.refs_1_ = bf16[128,1024]{1,0:T(8,128)(2,1)S(1)} collective-permute-done((bf16[128,1024]{1,0:T(8,128)(2,1)S(1)}, bf16[128,1024]{1,0:T(8,128)(2,1)S(1)}, u32[]{:S(2)}, u32[]{:S(2)}) %collective-permute-start.38) | collective-permute-done | bytes 262176 | tf_op jit(solution)/shard_map/ppermute | solution.py:425
  125.2 1.6 collective-permute-start.47
  127.2 1.9 %collective-permute-start.40 = (bf16[128,1024]{1,0:T(8,128)(2,1)S(1)}, bf16[128,1024]{1,0:T(8,128)(2,1)S(1)}, u32[]{:S(2)}, u32[]{:S(2)}) collective-permute-start(bf16[128,1024]{1,0:T(8,128)(2,1)S(1)} %get-tuple-element.138), channel_id=1, source_target_pairs={{0,6},{2,4},{4,2},{6,0},{1,7},{3,5},{5,3},{7,1},{8,14},{10,12},{12... | collective-permute-start | bytes 786440 | tf_op jit(solution)/shard_map/ppermute | solution.py:425
  129.2 6.8 %collective-permute-done.40.refs_3_ = bf16[128,1024]{1,0:T(8,128)(2,1)S(1)} collective-permute-done((bf16[128,1024]{1,0:T(8,128)(2,1)S(1)}, bf16[128,1024]{1,0:T(8,128)(2,1)S(1)}, u32[]{:S(2)}, u32[]{:S(2)}) %collective-permute-start.40) | collective-permute-done | bytes 262176 | tf_op jit(solution)/shard_map/ppermute | solution.py:425
  136.1 6.1 %collective-permute-done.46.refs_5_ = bf16[320,512]{1,0:T(8,128)(2,1)S(1)} collective-permute-done((bf16[320,512]{1,0:T(8,128)(2,1)S(1)}, bf16[320,512]{1,0:T(8,128)(2,1)S(1)}, u32[]{:S(2)}, u32[]{:S(2)}) %collective-permute-start.46) | collective-permute-done | bytes 327712 | tf_op jit(solution)/shard_map/ppermute | solution.py:430
  142.2 1.7 %shard_map.190 = (bf16[4,32,1024]{2,1,0:T(8,128)(2,1)S(1)}, bf16[4,32,1024]{2,1,0:T(8,128)(2,1)S(1)}, f32[32,1024]{1,0:T(8,128)}, f32[128,1024]{1,0:T(8,128)}) custom-call(s32[5]{0:T(128)S(1)} %stack.23.refs_0_, f32[256,1024]{1,0:T(8,128)S(1)} %get-tuple-element.134.refs_4_.refs_1_, bf16[256,1024]{1,0:T(8,128)(2,1)S(1)} %collective-permute-done.44.refs_2_, ...), custom_call_target="tpu_custom_call" | custom-call | tf_op jit(solution)/shard_map/pallas_call | solution.py:404
  145.9 1.8 %collective-permute-start.50 = (bf16[64,1024]{1,0:T(8,128)(2,1)S(1)}, bf16[64,1024]{1,0:T(8,128)(2,1)S(1)}, u32[]{:S(2)}, u32[]{:S(2)}) collective-permute-start(bf16[64,1024]{1,0:T(8,128)(2,1)S(1)} %get-tuple-element.158), channel_id=1, source_target_pairs={{0,4},{2,6},{4,0},{6,2},{1,5},{3,7},{5,1},{7,3},{8,12},{10,14},{12... | collective-permute-start | bytes 393224 | tf_op jit(solution)/shard_map/ppermute | solution.py:425
  147.7 2.2 %collective-permute-start.51 = (bf16[64,1024]{1,0:T(8,128)(2,1)S(1)}, bf16[64,1024]{1,0:T(8,128)(2,1)S(1)}, u32[]{:S(2)}, u32[]{:S(2)}) collective-permute-start(bf16[64,1024]{1,0:T(8,128)(2,1)S(1)} %get-tuple-element.159), channel_id=1, source_target_pairs={{0,6},{2,4},{4,2},{6,0},{1,7},{3,5},{5,3},{7,1},{8,14},{10,12},{12... | collective-permute-start | bytes 393224 | tf_op jit(solution)/shard_map/ppermute | solution.py:425
  150.5 1.5 collective-permute-start.43
  152.0 2.5 %collective-permute-done.42.refs_6_ = bf16[32,1024]{1,0:T(8,128)(2,1)S(1)} collective-permute-done((bf16[32,1024]{1,0:T(8,128)(2,1)S(1)}, bf16[32,1024]{1,0:T(8,128)(2,1)S(1)}, u32[]{:S(2)}, u32[]{:S(2)}) %collective-permute-start.42) | collective-permute-done | bytes 65568 | tf_op jit(solution)/shard_map/ppermute | solution.py:430
  155.7 2.7 %shard_map.188 = (bf16[4,64,1024]{2,1,0:T(8,128)(2,1)}, bf16[4,64,1024]{2,1,0:T(8,128)(2,1)}) custom-call(s32[5]{0:T(128)S(1)} %stack.23.refs_0_, bf16[4,16,64]{2,1,0:T(8,128)(2,1)} %get-tuple-element.88.refs_1_, bf16[4,64,1024]{2,1,0:T(8,128)(2,1)S(1)} %copy-done, bf16[4,64,1024]{2,1,0:T(8,128)(2,1)S(1)} %copy-done.1, ...), custom_call_target="tpu_custom_call" | custom-call | tf_op jit(solution)/shard_map/pallas_call | solution.py:404
  158.8 1.6 shard_map.192
  (102 shorter events, 29.6 us)
Async XLA Ops:
  2.9 22.0 %all-to-all-start = ((bf16[8,32,1024]{2,1,0:T(8,128)(2,1)}), bf16[8,32,1024]{2,1,0:T(8,128)(2,1)S(1)}, u32[]{:S(2)}, u32[]{:S(2)}) async-start(bf16[8,32,1024]{2,1,0:T(8,128)(2,1)} %shard_map.173), calls=%async_computation | async-start | bytes 1048576 | tf_op jit(solution)/shard_map/all_to_all | solution.py:993
  11.1 5.4 %collective-permute-start = (bf16[32,1024]{1,0:T(8,128)(2,1)S(1)}, bf16[32,1024]{1,0:T(8,128)(2,1)S(1)}, u32[]{:S(2)}, u32[]{:S(2)}) collective-permute-start(bf16[32,1024]{1,0:T(8,128)(2,1)S(1)} %get-tuple-element.90), channel_id=1, source_target_pairs={{0,1},{1,0},{16,17},{17,16},{2,3},{3,2},{18,19},{19,18},{4,5},{5,4... | collective-permute-start | bytes 196616 | tf_op jit(solution)/shard_map/ppermute | solution.py:430
  12.7 4.3 %collective-permute-start.1 = (bf16[32,1024]{1,0:T(8,128)(2,1)S(1)}, bf16[32,1024]{1,0:T(8,128)(2,1)S(1)}, u32[]{:S(2)}, u32[]{:S(2)}) collective-permute-start(bf16[32,1024]{1,0:T(8,128)(2,1)S(1)} %get-tuple-element.91), channel_id=1, source_target_pairs={{0,16},{1,17},{16,0},{17,1},{2,18},{3,19},{18,2},{19,3},{4,20},{5,... | collective-permute-start | bytes 196616 | tf_op jit(solution)/shard_map/ppermute | solution.py:430
  14.2 5.2 %collective-permute-start.2 = (bf16[32,1024]{1,0:T(8,128)(2,1)S(1)}, bf16[32,1024]{1,0:T(8,128)(2,1)S(1)}, u32[]{:S(2)}, u32[]{:S(2)}) collective-permute-start(bf16[32,1024]{1,0:T(8,128)(2,1)S(1)} %get-tuple-element.92), channel_id=1, source_target_pairs={{0,17},{1,16},{16,1},{17,0},{2,19},{3,18},{18,3},{19,2},{4,21},{5,... | collective-permute-start | bytes 196616 | tf_op jit(solution)/shard_map/ppermute | solution.py:430
  20.3 16.0 %collective-permute-start.3 = (bf16[128,1024]{1,0:T(8,128)(2,1)S(1)}, bf16[128,1024]{1,0:T(8,128)(2,1)S(1)}, u32[]{:S(2)}, u32[]{:S(2)}) collective-permute-start(bf16[128,1024]{1,0:T(8,128)(2,1)S(1)} %shard_map.171.refs_1_.refs_3_), channel_id=1, source_target_pairs={{0,2},{2,0},{4,6},{6,4},{1,3},{3,1},{5,7},{7,5},{8,10},{10,8},{12,... | collective-permute-start | bytes 786440 | tf_op jit(solution)/shard_map/ppermute | solution.py:425
  22.4 21.3 %collective-permute-start.4 = (bf16[128,1024]{1,0:T(8,128)(2,1)S(1)}, bf16[128,1024]{1,0:T(8,128)(2,1)S(1)}, u32[]{:S(2)}, u32[]{:S(2)}) collective-permute-start(bf16[128,1024]{1,0:T(8,128)(2,1)S(1)} %shard_map.171.refs_1_.refs_3_), channel_id=1, source_target_pairs={{0,4},{2,6},{4,0},{6,2},{1,5},{3,7},{5,1},{7,3},{8,12},{10,14},{12... | collective-permute-start | bytes 786440 | tf_op jit(solution)/shard_map/ppermute | solution.py:425
  24.8 19.0 %collective-permute-start.5 = (bf16[128,1024]{1,0:T(8,128)(2,1)S(1)}, bf16[128,1024]{1,0:T(8,128)(2,1)S(1)}, u32[]{:S(2)}, u32[]{:S(2)}) collective-permute-start(bf16[128,1024]{1,0:T(8,128)(2,1)S(1)} %shard_map.171.refs_1_.refs_3_), channel_id=1, source_target_pairs={{0,6},{2,4},{4,2},{6,0},{1,7},{3,5},{5,3},{7,1},{8,14},{10,12},{12... | collective-permute-start | bytes 786440 | tf_op jit(solution)/shard_map/ppermute | solution.py:425
  26.2 27.1 %all-to-all-start.1 = ((bf16[4,448,512]{2,1,0:T(8,128)(2,1)}), bf16[4,448,512]{2,1,0:T(8,128)(2,1)}, u32[]{:S(2)}, u32[]{:S(2)}) async-start(bf16[4,448,512]{2,1,0:T(8,128)(2,1)} %get-tuple-element.94), calls=%async_computation.1 | async-start | bytes 3670016 | tf_op jit(solution)/shard_map/all_to_all | solution.py:1005
  30.7 14.3 %collective-permute-start.6 = (bf16[128,1024]{1,0:T(8,128)(2,1)S(1)}, bf16[128,1024]{1,0:T(8,128)(2,1)S(1)}, u32[]{:S(2)}, u32[]{:S(2)}) collective-permute-start(bf16[128,1024]{1,0:T(8,128)(2,1)S(1)} %shard_map.171.refs_1_.refs_3_), channel_id=1, source_target_pairs={{0,8},{8,0},{1,9},{9,1},{2,10},{10,2},{3,11},{11,3},{4,12},{12,4},... | collective-permute-start | bytes 786440 | tf_op jit(solution)/shard_map/ppermute | solution.py:438
  36.3 8.7 %collective-permute-start.7 = (bf16[128,1024]{1,0:T(8,128)(2,1)S(1)}, bf16[128,1024]{1,0:T(8,128)(2,1)S(1)}, u32[]{:S(2)}, u32[]{:S(2)}) collective-permute-start(bf16[128,1024]{1,0:T(8,128)(2,1)S(1)} %collective-permute-done.3.refs_2_), channel_id=1, source_target_pairs={{0,8},{8,0},{1,9},{9,1},{2,10},{10,2},{3,11},{11,3},{4,12},{12,4},... | collective-permute-start | bytes 786440 | tf_op jit(solution)/shard_map/ppermute | solution.py:438
  56.7 3.6 %collective-permute-start.13 = (bf16[4,32,1024]{2,1,0:T(8,128)(2,1)S(1)}, bf16[4,32,1024]{2,1,0:T(8,128)(2,1)S(1)}, u32[]{:S(2)}, u32[]{:S(2)}) collective-permute-start(bf16[4,32,1024]{2,1,0:T(8,128)(2,1)S(1)} %get-tuple-element.101), channel_id=1, source_target_pairs={{0,8},{8,0},{1,9},{9,1},{2,10},{10,2},{3,11},{11,3},{4,12},{12,4},... | collective-permute-start | bytes 786440 | tf_op jit(solution)/shard_map/ppermute | solution.py:438
  56.7 16.6 %collective-permute-start.10 = (bf16[384,512]{1,0:T(8,128)(2,1)S(1)}, bf16[384,512]{1,0:T(8,128)(2,1)S(1)}, u32[]{:S(2)}, u32[]{:S(2)}) collective-permute-start(bf16[384,512]{1,0:T(8,128)(2,1)S(1)} %get-tuple-element.97.refs_4_.refs_2_), channel_id=1, source_target_pairs={{0,1},{1,0},{16,17},{17,16},{2,3},{3,2},{18,19},{19,18},{4,5},{5,4... | collective-permute-start | bytes 1179656 | tf_op jit(solution)/shard_map/ppermute | solution.py:430
  58.2 19.6 %collective-permute-start.11 = (bf16[384,512]{1,0:T(8,128)(2,1)S(1)}, bf16[384,512]{1,0:T(8,128)(2,1)S(1)}, u32[]{:S(2)}, u32[]{:S(2)}) collective-permute-start(bf16[384,512]{1,0:T(8,128)(2,1)S(1)} %get-tuple-element.97.refs_4_.refs_2_), channel_id=1, source_target_pairs={{0,16},{1,17},{16,0},{17,1},{2,18},{3,19},{18,2},{19,3},{4,20},{5,... | collective-permute-start | bytes 1179656 | tf_op jit(solution)/shard_map/ppermute | solution.py:430
  58.8 20.6 %collective-permute-start.12 = (bf16[384,512]{1,0:T(8,128)(2,1)S(1)}, bf16[384,512]{1,0:T(8,128)(2,1)S(1)}, u32[]{:S(2)}, u32[]{:S(2)}) collective-permute-start(bf16[384,512]{1,0:T(8,128)(2,1)S(1)} %get-tuple-element.97.refs_4_.refs_2_), channel_id=1, source_target_pairs={{0,17},{1,16},{16,1},{17,0},{2,19},{3,18},{18,3},{19,2},{4,21},{5,... | collective-permute-start | bytes 1179656 | tf_op jit(solution)/shard_map/ppermute | solution.py:430
  60.4 4.6 %collective-permute-start.14 = (bf16[32,1024]{1,0:T(8,128)(2,1)S(1)}, bf16[32,1024]{1,0:T(8,128)(2,1)S(1)}, u32[]{:S(2)}, u32[]{:S(2)}) collective-permute-start(bf16[32,1024]{1,0:T(8,128)(2,1)S(1)} %get-tuple-element.103), channel_id=1, source_target_pairs={{0,2},{2,0},{4,6},{6,4},{1,3},{3,1},{5,7},{7,5},{8,10},{10,8},{12,... | collective-permute-start | bytes 196616 | tf_op jit(solution)/shard_map/ppermute | solution.py:425
  60.4 6.8 %collective-permute-start.15 = (bf16[32,1024]{1,0:T(8,128)(2,1)S(1)}, bf16[32,1024]{1,0:T(8,128)(2,1)S(1)}, u32[]{:S(2)}, u32[]{:S(2)}) collective-permute-start(bf16[32,1024]{1,0:T(8,128)(2,1)S(1)} %get-tuple-element.104), channel_id=1, source_target_pairs={{0,4},{2,6},{4,0},{6,2},{1,5},{3,7},{5,1},{7,3},{8,12},{10,14},{12... | collective-permute-start | bytes 196616 | tf_op jit(solution)/shard_map/ppermute | solution.py:425
  65.0 6.2 %collective-permute-start.16 = (bf16[32,1024]{1,0:T(8,128)(2,1)S(1)}, bf16[32,1024]{1,0:T(8,128)(2,1)S(1)}, u32[]{:S(2)}, u32[]{:S(2)}) collective-permute-start(bf16[32,1024]{1,0:T(8,128)(2,1)S(1)} %get-tuple-element.105), channel_id=1, source_target_pairs={{0,6},{2,4},{4,2},{6,0},{1,7},{3,5},{5,3},{7,1},{8,14},{10,12},{12... | collective-permute-start | bytes 196616 | tf_op jit(solution)/shard_map/ppermute | solution.py:425
  71.3 6.5 %collective-permute-start.17 = (bf16[32,1024]{1,0:T(8,128)(2,1)S(1)}, bf16[32,1024]{1,0:T(8,128)(2,1)S(1)}, u32[]{:S(2)}, u32[]{:S(2)}) collective-permute-start(bf16[32,1024]{1,0:T(8,128)(2,1)S(1)} %get-tuple-element.106.refs_6_.refs_4_), channel_id=1, source_target_pairs={{0,2},{2,0},{4,6},{6,4},{1,3},{3,1},{5,7},{7,5},{8,10},{10,8},{12,... | collective-permute-start | bytes 196616 | tf_op jit(solution)/shard_map/ppermute | solution.py:425
  71.4 6.9 %collective-permute-start.18 = (bf16[32,1024]{1,0:T(8,128)(2,1)S(1)}, bf16[32,1024]{1,0:T(8,128)(2,1)S(1)}, u32[]{:S(2)}, u32[]{:S(2)}) collective-permute-start(bf16[32,1024]{1,0:T(8,128)(2,1)S(1)} %get-tuple-element.106.refs_6_.refs_4_), channel_id=1, source_target_pairs={{0,4},{2,6},{4,0},{6,2},{1,5},{3,7},{5,1},{7,3},{8,12},{10,14},{12... | collective-permute-start | bytes 196616 | tf_op jit(solution)/shard_map/ppermute | solution.py:425
  73.4 6.1 %collective-permute-start.19 = (bf16[32,1024]{1,0:T(8,128)(2,1)S(1)}, bf16[32,1024]{1,0:T(8,128)(2,1)S(1)}, u32[]{:S(2)}, u32[]{:S(2)}) collective-permute-start(bf16[32,1024]{1,0:T(8,128)(2,1)S(1)} %get-tuple-element.106.refs_6_.refs_4_), channel_id=1, source_target_pairs={{0,6},{2,4},{4,2},{6,0},{1,7},{3,5},{5,3},{7,1},{8,14},{10,12},{12... | collective-permute-start | bytes 196616 | tf_op jit(solution)/shard_map/ppermute | solution.py:425
  77.8 3.8 %collective-permute-start.20 = (bf16[32,1024]{1,0:T(8,128)(2,1)S(1)}, bf16[32,1024]{1,0:T(8,128)(2,1)S(1)}, u32[]{:S(2)}, u32[]{:S(2)}) collective-permute-start(bf16[32,1024]{1,0:T(8,128)(2,1)S(1)} %get-tuple-element.106.refs_6_.refs_4_), channel_id=1, source_target_pairs={{0,8},{8,0},{1,9},{9,1},{2,10},{10,2},{3,11},{11,3},{4,12},{12,4},... | collective-permute-start | bytes 196616 | tf_op jit(solution)/shard_map/ppermute | solution.py:438
  77.8 3.8 %collective-permute-start.21 = (bf16[32,1024]{1,0:T(8,128)(2,1)S(1)}, bf16[32,1024]{1,0:T(8,128)(2,1)S(1)}, u32[]{:S(2)}, u32[]{:S(2)}) collective-permute-start(bf16[32,1024]{1,0:T(8,128)(2,1)S(1)} %collective-permute-done.17.refs_7_.refs_5_), channel_id=1, source_target_pairs={{0,8},{8,0},{1,9},{9,1},{2,10},{10,2},{3,11},{11,3},{4,12},{12,4},... | collective-permute-start | bytes 196616 | tf_op jit(solution)/shard_map/ppermute | solution.py:438
  78.4 3.3 %collective-permute-start.22 = (bf16[32,1024]{1,0:T(8,128)(2,1)S(1)}, bf16[32,1024]{1,0:T(8,128)(2,1)S(1)}, u32[]{:S(2)}, u32[]{:S(2)}) collective-permute-start(bf16[32,1024]{1,0:T(8,128)(2,1)S(1)} %collective-permute-done.18.refs_8_.refs_6_), channel_id=1, source_target_pairs={{0,8},{8,0},{1,9},{9,1},{2,10},{10,2},{3,11},{11,3},{4,12},{12,4},... | collective-permute-start | bytes 196616 | tf_op jit(solution)/shard_map/ppermute | solution.py:438
  79.4 2.3 %collective-permute-start.23 = (bf16[32,1024]{1,0:T(8,128)(2,1)S(1)}, bf16[32,1024]{1,0:T(8,128)(2,1)S(1)}, u32[]{:S(2)}, u32[]{:S(2)}) collective-permute-start(bf16[32,1024]{1,0:T(8,128)(2,1)S(1)} %collective-permute-done.19.refs_9_.refs_7_), channel_id=1, source_target_pairs={{0,8},{8,0},{1,9},{9,1},{2,10},{10,2},{3,11},{11,3},{4,12},{12,4},... | collective-permute-start | bytes 196616 | tf_op jit(solution)/shard_map/ppermute | solution.py:438
  83.3 3.5 %collective-permute-start.25 = (bf16[4,32,1024]{2,1,0:T(8,128)(2,1)S(1)}, bf16[4,32,1024]{2,1,0:T(8,128)(2,1)S(1)}, u32[]{:S(2)}, u32[]{:S(2)}) collective-permute-start(bf16[4,32,1024]{2,1,0:T(8,128)(2,1)S(1)} %get-tuple-element.121), channel_id=1, source_target_pairs={{0,8},{8,0},{1,9},{9,1},{2,10},{10,2},{3,11},{11,3},{4,12},{12,4},... | collective-permute-start | bytes 786440 | tf_op jit(solution)/shard_map/ppermute | solution.py:438
  85.3 25.1 %collective-permute-start.37 = (bf16[512,1024]{1,0:T(8,128)(2,1)S(1)}, bf16[512,1024]{1,0:T(8,128)(2,1)S(1)}, u32[]{:S(2)}, u32[]{:S(2)}) collective-permute-start(bf16[512,1024]{1,0:T(8,128)(2,1)S(1)} %get-tuple-element.128.refs_8_), channel_id=1, source_target_pairs={{0,1},{1,0},{2,3},{3,2},{4,5},{5,4},{6,7},{7,6},{8,9},{9,8},{10,11... | collective-permute-start | bytes 3145736 | tf_op jit(solution)/shard_map/ppermute | solution.py:1066
  86.8 5.9 %collective-permute-start.26 = (bf16[32,1024]{1,0:T(8,128)(2,1)S(1)}, bf16[32,1024]{1,0:T(8,128)(2,1)S(1)}, u32[]{:S(2)}, u32[]{:S(2)}) collective-permute-start(bf16[32,1024]{1,0:T(8,128)(2,1)S(1)} %get-tuple-element.123), channel_id=1, source_target_pairs={{0,2},{2,0},{4,6},{6,4},{1,3},{3,1},{5,7},{7,5},{8,10},{10,8},{12,... | collective-permute-start | bytes 196616 | tf_op jit(solution)/shard_map/ppermute | solution.py:425
  86.9 7.9 %collective-permute-start.27 = (bf16[32,1024]{1,0:T(8,128)(2,1)S(1)}, bf16[32,1024]{1,0:T(8,128)(2,1)S(1)}, u32[]{:S(2)}, u32[]{:S(2)}) collective-permute-start(bf16[32,1024]{1,0:T(8,128)(2,1)S(1)} %get-tuple-element.124), channel_id=1, source_target_pairs={{0,4},{2,6},{4,0},{6,2},{1,5},{3,7},{5,1},{7,3},{8,12},{10,14},{12... | collective-permute-start | bytes 196616 | tf_op jit(solution)/shard_map/ppermute | solution.py:425
  89.9 6.2 %collective-permute-start.28 = (bf16[32,1024]{1,0:T(8,128)(2,1)S(1)}, bf16[32,1024]{1,0:T(8,128)(2,1)S(1)}, u32[]{:S(2)}, u32[]{:S(2)}) collective-permute-start(bf16[32,1024]{1,0:T(8,128)(2,1)S(1)} %get-tuple-element.125), channel_id=1, source_target_pairs={{0,6},{2,4},{4,2},{6,0},{1,7},{3,5},{5,3},{7,1},{8,14},{10,12},{12... | collective-permute-start | bytes 196616 | tf_op jit(solution)/shard_map/ppermute | solution.py:425
  96.2 5.7 %collective-permute-start.29 = (bf16[32,1024]{1,0:T(8,128)(2,1)S(1)}, bf16[32,1024]{1,0:T(8,128)(2,1)S(1)}, u32[]{:S(2)}, u32[]{:S(2)}) collective-permute-start(bf16[32,1024]{1,0:T(8,128)(2,1)S(1)} %get-tuple-element.130.refs_10_.refs_8_), channel_id=1, source_target_pairs={{0,2},{2,0},{4,6},{6,4},{1,3},{3,1},{5,7},{7,5},{8,10},{10,8},{12,... | collective-permute-start | bytes 196616 | tf_op jit(solution)/shard_map/ppermute | solution.py:425
  97.0 6.1 %collective-permute-start.30 = (bf16[32,1024]{1,0:T(8,128)(2,1)S(1)}, bf16[32,1024]{1,0:T(8,128)(2,1)S(1)}, u32[]{:S(2)}, u32[]{:S(2)}) collective-permute-start(bf16[32,1024]{1,0:T(8,128)(2,1)S(1)} %get-tuple-element.130.refs_10_.refs_8_), channel_id=1, source_target_pairs={{0,4},{2,6},{4,0},{6,2},{1,5},{3,7},{5,1},{7,3},{8,12},{10,14},{12... | collective-permute-start | bytes 196616 | tf_op jit(solution)/shard_map/ppermute | solution.py:425
  98.3 6.2 %collective-permute-start.31 = (bf16[32,1024]{1,0:T(8,128)(2,1)S(1)}, bf16[32,1024]{1,0:T(8,128)(2,1)S(1)}, u32[]{:S(2)}, u32[]{:S(2)}) collective-permute-start(bf16[32,1024]{1,0:T(8,128)(2,1)S(1)} %get-tuple-element.130.refs_10_.refs_8_), channel_id=1, source_target_pairs={{0,6},{2,4},{4,2},{6,0},{1,7},{3,5},{5,3},{7,1},{8,14},{10,12},{12... | collective-permute-start | bytes 196616 | tf_op jit(solution)/shard_map/ppermute | solution.py:425
  100.7 3.8 %collective-permute-start.32 = (bf16[32,1024]{1,0:T(8,128)(2,1)S(1)}, bf16[32,1024]{1,0:T(8,128)(2,1)S(1)}, u32[]{:S(2)}, u32[]{:S(2)}) collective-permute-start(bf16[32,1024]{1,0:T(8,128)(2,1)S(1)} %get-tuple-element.130.refs_10_.refs_8_), channel_id=1, source_target_pairs={{0,8},{8,0},{1,9},{9,1},{2,10},{10,2},{3,11},{11,3},{4,12},{12,4},... | collective-permute-start | bytes 196616 | tf_op jit(solution)/shard_map/ppermute | solution.py:438
  101.9 3.1 %collective-permute-start.33 = (bf16[32,1024]{1,0:T(8,128)(2,1)S(1)}, bf16[32,1024]{1,0:T(8,128)(2,1)S(1)}, u32[]{:S(2)}, u32[]{:S(2)}) collective-permute-start(bf16[32,1024]{1,0:T(8,128)(2,1)S(1)} %collective-permute-done.29.refs_11_.refs_9_), channel_id=1, source_target_pairs={{0,8},{8,0},{1,9},{9,1},{2,10},{10,2},{3,11},{11,3},{4,12},{12,4},... | collective-permute-start | bytes 196616 | tf_op jit(solution)/shard_map/ppermute | solution.py:438
  104.5 6.1 %collective-permute-start.24 = (bf16[4,64,1024]{2,1,0:T(8,128)(2,1)S(1)}, bf16[4,64,1024]{2,1,0:T(8,128)(2,1)S(1)}, u32[]{:S(2)}, u32[]{:S(2)}) collective-permute-start(bf16[4,64,1024]{2,1,0:T(8,128)(2,1)S(1)} %get-tuple-element.113), channel_id=1, source_target_pairs={{0,8},{8,0},{1,9},{9,1},{2,10},{10,2},{3,11},{11,3},{4,12},{12,4},... | collective-permute-start | bytes 1572872 | tf_op jit(solution)/shard_map/ppermute | solution.py:438
  111.9 13.3 %collective-permute-start.38 = (bf16[128,1024]{1,0:T(8,128)(2,1)S(1)}, bf16[128,1024]{1,0:T(8,128)(2,1)S(1)}, u32[]{:S(2)}, u32[]{:S(2)}) collective-permute-start(bf16[128,1024]{1,0:T(8,128)(2,1)S(1)} %get-tuple-element.136), channel_id=1, source_target_pairs={{0,2},{2,0},{4,6},{6,4},{1,3},{3,1},{5,7},{7,5},{8,10},{10,8},{12,... | collective-permute-start | bytes 786440 | tf_op jit(solution)/shard_map/ppermute | solution.py:425
  112.6 14.6 %collective-permute-start.39 = (bf16[128,1024]{1,0:T(8,128)(2,1)S(1)}, bf16[128,1024]{1,0:T(8,128)(2,1)S(1)}, u32[]{:S(2)}, u32[]{:S(2)}) collective-permute-start(bf16[128,1024]{1,0:T(8,128)(2,1)S(1)} %get-tuple-element.137), channel_id=1, source_target_pairs={{0,4},{2,6},{4,0},{6,2},{1,5},{3,7},{5,1},{7,3},{8,12},{10,14},{12... | collective-permute-start | bytes 786440 | tf_op jit(solution)/shard_map/ppermute | solution.py:425
  114.7 27.5 %collective-permute-start.44 = (bf16[256,1024]{1,0:T(8,128)(2,1)S(1)}, bf16[256,1024]{1,0:T(8,128)(2,1)S(1)}, u32[]{:S(2)}, u32[]{:S(2)}) collective-permute-start(bf16[256,1024]{1,0:T(8,128)(2,1)S(1)} %get-tuple-element.145), channel_id=1, source_target_pairs={{0,16},{16,0},{1,17},{17,1},{2,18},{18,2},{3,19},{19,3},{4,20},{20... | collective-permute-start | bytes 1572872 | tf_op jit(solution)/shard_map/ppermute | solution.py:1085
  117.2 18.9 %collective-permute-start.45 = (bf16[320,512]{1,0:T(8,128)(2,1)S(1)}, bf16[320,512]{1,0:T(8,128)(2,1)S(1)}, u32[]{:S(2)}, u32[]{:S(2)}) collective-permute-start(bf16[320,512]{1,0:T(8,128)(2,1)S(1)} %get-tuple-element.151), channel_id=1, source_target_pairs={{0,1},{1,0},{16,17},{17,16},{2,3},{3,2},{18,19},{19,18},{4,5},{5,4... | collective-permute-start | bytes 983048 | tf_op jit(solution)/shard_map/ppermute | solution.py:430
  118.6 23.6 %collective-permute-start.46 = (bf16[320,512]{1,0:T(8,128)(2,1)S(1)}, bf16[320,512]{1,0:T(8,128)(2,1)S(1)}, u32[]{:S(2)}, u32[]{:S(2)}) collective-permute-start(bf16[320,512]{1,0:T(8,128)(2,1)S(1)} %get-tuple-element.152), channel_id=1, source_target_pairs={{0,16},{1,17},{16,0},{17,1},{2,18},{3,19},{18,2},{19,3},{4,20},{5,... | collective-permute-start | bytes 983048 | tf_op jit(solution)/shard_map/ppermute | solution.py:430
  125.2 17.0 %collective-permute-start.47 = (bf16[320,512]{1,0:T(8,128)(2,1)S(1)}, bf16[320,512]{1,0:T(8,128)(2,1)S(1)}, u32[]{:S(2)}, u32[]{:S(2)}) collective-permute-start(bf16[320,512]{1,0:T(8,128)(2,1)S(1)} %get-tuple-element.153), channel_id=1, source_target_pairs={{0,17},{1,16},{16,1},{17,0},{2,19},{3,18},{18,3},{19,2},{4,21},{5,... | collective-permute-start | bytes 983048 | tf_op jit(solution)/shard_map/ppermute | solution.py:430
  127.2 8.7 %collective-permute-start.40 = (bf16[128,1024]{1,0:T(8,128)(2,1)S(1)}, bf16[128,1024]{1,0:T(8,128)(2,1)S(1)}, u32[]{:S(2)}, u32[]{:S(2)}) collective-permute-start(bf16[128,1024]{1,0:T(8,128)(2,1)S(1)} %get-tuple-element.138), channel_id=1, source_target_pairs={{0,6},{2,4},{4,2},{6,0},{1,7},{3,5},{5,3},{7,1},{8,14},{10,12},{12... | collective-permute-start | bytes 786440 | tf_op jit(solution)/shard_map/ppermute | solution.py:425
  143.9 6.6 %collective-permute-start.41 = (bf16[32,1024]{1,0:T(8,128)(2,1)S(1)}, bf16[32,1024]{1,0:T(8,128)(2,1)S(1)}, u32[]{:S(2)}, u32[]{:S(2)}) collective-permute-start(bf16[32,1024]{1,0:T(8,128)(2,1)S(1)} %get-tuple-element.140), channel_id=1, source_target_pairs={{0,1},{1,0},{16,17},{17,16},{2,3},{3,2},{18,19},{19,18},{4,5},{5,4... | collective-permute-start | bytes 196616 | tf_op jit(solution)/shard_map/ppermute | solution.py:430
  145.5 12.9 %collective-permute-start.49 = (bf16[64,1024]{1,0:T(8,128)(2,1)S(1)}, bf16[64,1024]{1,0:T(8,128)(2,1)S(1)}, u32[]{:S(2)}, u32[]{:S(2)}) collective-permute-start(bf16[64,1024]{1,0:T(8,128)(2,1)S(1)} %get-tuple-element.157), channel_id=1, source_target_pairs={{0,2},{2,0},{4,6},{6,4},{1,3},{3,1},{5,7},{7,5},{8,10},{10,8},{12,... | collective-permute-start | bytes 393224 | tf_op jit(solution)/shard_map/ppermute | solution.py:425
  145.9 12.9 %collective-permute-start.50 = (bf16[64,1024]{1,0:T(8,128)(2,1)S(1)}, bf16[64,1024]{1,0:T(8,128)(2,1)S(1)}, u32[]{:S(2)}, u32[]{:S(2)}) collective-permute-start(bf16[64,1024]{1,0:T(8,128)(2,1)S(1)} %get-tuple-element.158), channel_id=1, source_target_pairs={{0,4},{2,6},{4,0},{6,2},{1,5},{3,7},{5,1},{7,3},{8,12},{10,14},{12... | collective-permute-start | bytes 393224 | tf_op jit(solution)/shard_map/ppermute | solution.py:425
  147.7 11.1 %collective-permute-start.51 = (bf16[64,1024]{1,0:T(8,128)(2,1)S(1)}, bf16[64,1024]{1,0:T(8,128)(2,1)S(1)}, u32[]{:S(2)}, u32[]{:S(2)}) collective-permute-start(bf16[64,1024]{1,0:T(8,128)(2,1)S(1)} %get-tuple-element.159), channel_id=1, source_target_pairs={{0,6},{2,4},{4,2},{6,0},{1,7},{3,5},{5,3},{7,1},{8,14},{10,12},{12... | collective-permute-start | bytes 393224 | tf_op jit(solution)/shard_map/ppermute | solution.py:425
  149.9 4.6 %collective-permute-start.42 = (bf16[32,1024]{1,0:T(8,128)(2,1)S(1)}, bf16[32,1024]{1,0:T(8,128)(2,1)S(1)}, u32[]{:S(2)}, u32[]{:S(2)}) collective-permute-start(bf16[32,1024]{1,0:T(8,128)(2,1)S(1)} %get-tuple-element.141), channel_id=1, source_target_pairs={{0,16},{1,17},{16,0},{17,1},{2,18},{3,19},{18,2},{19,3},{4,20},{5,... | collective-permute-start | bytes 196616 | tf_op jit(solution)/shard_map/ppermute | solution.py:430
  150.5 5.2 %collective-permute-start.43 = (bf16[32,1024]{1,0:T(8,128)(2,1)S(1)}, bf16[32,1024]{1,0:T(8,128)(2,1)S(1)}, u32[]{:S(2)}, u32[]{:S(2)}) collective-permute-start(bf16[32,1024]{1,0:T(8,128)(2,1)S(1)} %get-tuple-element.142), channel_id=1, source_target_pairs={{0,17},{1,16},{16,1},{17,0},{2,19},{3,18},{18,3},{19,2},{4,21},{5,... | collective-permute-start | bytes 196616 | tf_op jit(solution)/shard_map/ppermute | solution.py:430
  (14 other events, 83.2 us)

commit v8 on v7

--- a/solution.py
+++ b/solution.py
@@ -444,6 +444,17 @@
     return blocks + [send_c(b) for b in blocks]
 
 
+ORDER = [0, 1, 3, 2, 4, 5, 7, 6]
+
+
+def shuffle(blocks):
+    return [blocks[b] for b in ORDER]
+
+
+def restore(blocks):
+    return [blocks[ORDER.index(b)] for b in range(len(ORDER))]
+
+
 def half_sum_kernel(near, far, mine, *low):
     for k in range(near.shape[0]):
         total = near[k].astype(F32) + far[k].astype(F32)
@@ -543,22 +554,34 @@
             out[to : to + cap] = block[j * cap : (j + 1) * cap]
 
 
+def eye_tile():
+    down = lax.broadcasted_iota(jnp.int32, (16, 128), 0)
+    return (down == lax.broadcasted_iota(jnp.int32, (16, 128), 1)).astype(F32).astype(BF16)
+
+
 def relay_kernel(got, w_out, w_down, first, up):
     members, rows, lanes = got.shape
     half = lanes // 2
-    size = members * rows
-    blocks = [b[:, j * half : (j + 1) * half] for b in (w_out, w_down) for j in range(2)]
+    cols = half - 128
+    straight = members * cols // half
+    fold, end = (members - straight) * rows, straight * rows
+    vec = [mm(eye_tile(), got[g, :, cols:half], NT) for g in range(members)]
+    vec = jnp.concatenate(vec, 1).astype(BF16)
+    size = w_out.shape[0]
     for line in range(first.shape[0]):
-        first[line, :size] = got[:, :, :half].reshape(size, half)
-        at = size
-        for block in blocks[: 3]:
-            first[line, at : at + block.shape[0]] = block
-            at += block.shape[0]
-    up[:size] = got[:, :, half:].reshape(size, half)
-    at = size
-    for block in blocks[3 :]:
-        up[at : at + block.shape[0]] = block
-        at += block.shape[0]
+        first[line, :end, :cols] = got[:straight, :, :cols].reshape(end, cols)
+        for j in range(cols // 128):
+            piece = got[straight:, :, j * 128 : (j + 1) * 128].reshape(fold, 128)
+            first[line, j * fold : (j + 1) * fold, cols:] = piece
+        for j in range(2):
+            to = end + j * size
+            first[line, to : to + size] = w_out[:, j * half : (j + 1) * half]
+        at = end + 2 * size
+        first[line, at : at + 16, : members * rows] = vec
+        first[line, at : at + 16, members * rows :] = jnp.zeros((16, half - members * rows), BF16)
+        first[line, at + 16 :] = w_down[:, :half]
+    up[: members * rows] = got[:, :, half:].reshape(members * rows, half)
+    up[members * rows :] = w_down[:, half:]
 
 
 def spread_kernel(dims, where, chosen, chosen_t, spread):
@@ -630,18 +653,36 @@
             out[pl.ds(to, rows)] = block[g * rows : (g + 1) * rows, :]
 
 
-def natural_rows(blocks, dims, first, count, out):
+def natural_rows(got, dims, cols, out):
     ny, members, nx, rows = dims
+    straight = members * cols // (cols + 128)
+    fold = (members - straight) * rows
     for y in range(ny):
         for g in range(members):
             for x in range(nx):
-                to = ((y * members + g) * nx + x) * rows
-                piece = blocks[y * nx + x, g * rows : (g + 1) * rows, first : first + count]
-                out[to : to + rows] = piece
+                q, to = y * nx + x, ((y * members + g) * nx + x) * rows
+                if g < straight:
+                    out[to : to + rows] = got[q, g * rows : (g + 1) * rows, :cols]
+                    continue
+                for j in range(cols // 128):
+                    at = j * fold + (g - straight) * rows
+                    out[to : to + rows, j * 128 : (j + 1) * 128] = got[q, at : at + rows, cols:]
+
+
+def natural_lanes(got, dims, at):
+    ny, members, nx, rows = dims
+    pieces = [
+        got[y * nx + x, at : at + 16, g * rows : (g + 1) * rows]
+        for y in range(ny)
+        for g in range(members)
+        for x in range(nx)
+    ]
+    return jnp.concatenate(pieces, 1).astype(F32)[:8]
 
 
 def compact_kernel(spread, *refs):
     *blocks, picked_o, own_o, cot_o = refs
+    blocks = restore(blocks)
     hot = spread[...]
     half = blocks[0].shape[0] // 2
     picked = mm(hot, jnp.concatenate([b[:half] for b in blocks], 0)).astype(BF16)
@@ -653,16 +694,16 @@
 def attention_kernel(dims, members, where, picked_r, qkv_blocks, *outs):
     ny, nx, rows = dims
     normed_o, w_o, wo_o, vecs_o = outs[:4]
-    joined_o, att_o, exact_o, near_o, far_o, vec_s = outs[4:]
+    joined_o, att_o, exact_o, near_o, far_o = outs[4:]
     heads = ny
     cols = 3 * heads * HDIM
     routed, width = picked_r.shape
     own = routed // members
     picked = picked_r[...].astype(F32)
-    natural_rows(qkv_blocks, (ny, members, nx, rows), 0, cols, w_o)
-    natural_rows(qkv_blocks, (ny, members, nx, rows), cols, 128, vec_s)
-    line_rows(qkv_blocks, members * rows, wo_o)
-    vecs = mm(eye_rows(), vec_s[...], NT)
+    natural_rows(qkv_blocks, (ny, members, nx, rows), cols, w_o)
+    end = members * rows * cols // (cols + 128)
+    line_rows(qkv_blocks, end, wo_o)
+    vecs = natural_lanes(qkv_blocks, (ny, members, nx, rows), end + 2 * rows)
     vecs_o[...] = vecs
     normed = (picked * inverse_rms(picked) * vecs[0:1]).astype(BF16)
     normed_o[...] = normed
@@ -727,7 +768,7 @@
     ups, refs = refs[:lines], refs[lines:]
     blocks, (active_o, d_upper_o, near_o, far_o, w_s) = refs[:members], refs[members:]
     own_order_rows(where, ups, dims, w_s)
-    normed = jnp.concatenate([b[...] for b in blocks], 0)
+    normed = jnp.concatenate([b[...] for b in restore(blocks)], 0)
     upper = mm(normed, w_s[...])
     below = 0.5 * (1.0 + lax.erf(upper * (0.5**0.5)))
     active_o[...] = (upper * below).astype(BF16)
@@ -740,7 +781,7 @@
 def ff_grads_kernel(dims, members, where, active, d_upper, d_result, *refs):
     ny, nx, rows, ff_rows = dims
     blocks, (keep, send, down, up) = refs[:members], refs[members:]
-    normed = jnp.concatenate([b[...] for b in blocks], 0)
+    normed = jnp.concatenate([b[...] for b in restore(blocks)], 0)
     down[...] = mm(active[...], d_result[...], TN).astype(BF16)
     up[...] = mm(normed, d_upper[...], TN).astype(BF16)
     wide = up.shape[1]
@@ -792,7 +833,7 @@
     routed, width = picked_r.shape
     own = routed // members
     heads = joined_r.shape[1] // (3 * HDIM)
-    d_branch = jnp.concatenate([b[...] for b in blocks], 0)
+    d_branch = jnp.concatenate([b[...] for b in restore(blocks)], 0)
     d_attended = mm(d_branch, w_out[...], NT).astype(BF16)
     joined = joined_r[...]
     exact = exact_r[...]
@@ -838,26 +879,39 @@
     def lane(k, count):
         return (lanes[:count] == k).astype(F32)
 
-    vec = mm(gain_a[...], lane(0, routed).astype(BF16), TN)
-    vec = vec + mm(gain_m[...], lane(1, own).astype(BF16), TN)
+    vec = mm(lane(0, routed).astype(BF16), gain_a[...], TN)
+    vec = vec + mm(lane(1, own).astype(BF16), gain_m[...], TN)
     high = logit[...].astype(BF16)
     low = (logit[...] - high.astype(F32)).astype(BF16)
-    vec = vec + mm(picked[...], (lane(2, routed) * high.astype(F32)).astype(BF16), TN)
-    vec = vec + mm(picked[...], (lane(2, routed) * low.astype(F32)).astype(BF16), TN)
-    vec_s[...] = vec.astype(BF16)
-    out[...] = mm(attended[...], jnp.concatenate([b[...] for b in blocks], 0), TN).astype(BF16)
+    vec = vec + mm((lane(2, routed) * high.astype(F32)).astype(BF16), picked[...], TN)
+    vec = vec + mm((lane(2, routed) * low.astype(F32)).astype(BF16), picked[...], TN)
+    vec_s[...] = jnp.zeros_like(vec_s)
+    for y in range(ny):
+        for x in range(nx):
+            ats = [((y * members + g) * nx + x) * rows for g in range(members)]
+            pieces = [vec[:16, at : at + rows] for at in ats]
+            vec_s[y * nx + x, :, : members * rows] = jnp.concatenate(pieces, 1).astype(BF16)
+    out[...] = mm(attended[...], jnp.concatenate([b[...] for b in restore(blocks)], 0), TN).astype(BF16)
+    straight = members * cols // (cols + 128)
+    fold = (members - straight) * rows
+    half, end = width // 2, straight * rows
     for k in range(lines):
         line = where[2] ^ k
         y, x = lax.div(line, jnp.int32(nx)), lax.rem(line, jnp.int32(nx))
         for g in range(members):
             at = pl.multiple_of(((y * members + g) * nx + x) * rows, rows)
-            sums[k][g * rows : (g + 1) * rows, :cols] = main[pl.ds(at, rows)]
-            sums[k][g * rows : (g + 1) * rows, cols:] = vec_s[pl.ds(at, rows)]
-        half, end = width // 2, members * rows
+            if g < straight:
+                sums[k][g * rows : (g + 1) * rows, :cols] = main[pl.ds(at, rows)]
+                continue
+            for j in range(cols // 128):
+                to = j * fold + (g - straight) * rows
+                piece = main[pl.ds(at, rows), j * 128 : (j + 1) * 128]
+                sums[k][to : to + rows, cols:] = piece
         at = pl.multiple_of(line * rows, rows)
         for j in range(2):
             piece = out[pl.ds(at, rows), j * half : (j + 1) * half]
             sums[k][end + j * rows : end + (j + 1) * rows, :] = piece
+        sums[k][end + 2 * rows :, :] = vec_s[line]
 
 
 def join_slots_kernel(cap, lines, *refs):
@@ -882,24 +936,39 @@
 def line_sums_kernel(dims, where, mine, got, *refs):
     members, rows, ff_rows = dims
     *parts, near_o, far_o, out_o, down_o, send = refs
-    cols = parts[0].shape[1]
+    cols = parts[0].shape[1] - 128
+    straight = members * cols // (cols + 128)
+    fold = (members - straight) * rows
+    end = straight * rows
     wide = mine.shape[1] // 2
     ff = mine[...] + got[...].astype(F32)
     up = ff[ff_rows:]
     main = parts[0][...].astype(F32)
     for part in parts[1:]:
         main = main + part[...].astype(F32)
+    vec = main[end + 2 * rows :]
+    high = vec.astype(BF16)
+    low = (vec - high.astype(F32)).astype(BF16)
+    down = lax.broadcasted_iota(jnp.int32, (16, 128), 0)
+    eye = (down == lax.broadcasted_iota(jnp.int32, (16, 128), 1)).astype(F32).astype(BF16)
     for g in range(members):
-        send[g, :, :cols] = main[g * rows : (g + 1) * rows].astype(BF16)
+        if g < straight:
+            block = main[g * rows : (g + 1) * rows, :cols]
+        else:
+            tos = [j * fold + (g - straight) * rows for j in range(cols // 128)]
+            block = jnp.concatenate([main[to : to + rows, cols:] for to in tos], 1)
+        send[g, :, :cols] = block.astype(BF16)
+        at = slice(g * rows, (g + 1) * rows)
+        column = mm(high[:, at], eye, TN) + mm(low[:, at], eye, TN)
+        send[g, :, cols : cols + 128] = column.astype(BF16)
         half, row = divmod(g * rows, members * rows // 2)
         piece = up[row : row + rows, half * wide : (half + 1) * wide]
-        send[g, :, cols:] = piece.astype(BF16)
+        send[g, :, cols + 128 :] = piece.astype(BF16)
     depth = near_o.shape[0]
     for k in range(depth):
         near_o[k] = send[where[3] ^ k]
         far_o[k] = send[where[3] ^ (depth + k)]
-    end = members * rows
-    out_o[...] = jnp.concatenate([main[end : end + rows], main[end + rows :]], 1)
+    out_o[...] = jnp.concatenate([main[end : end + rows], main[end + rows : end + 2 * rows]], 1)
     down_o[...] = ff[:ff_rows]
 
 
@@ -992,12 +1061,12 @@
     )
     got_cols = lax.all_to_all(columns, ("c", "z"), 0, 0, tiled=True)
     half = width // 2
-    base = members * rows + 2 * rows
+    base = members * rows * cols // (cols + 128) + 2 * rows + 16
     first, up = local_call(
         relay_kernel,
         [
             Far(((lines, base + ff_rows, half), BF16)),
-            ((members * rows + ff_rows, half), BF16),
+            Far(((members * rows + ff_rows, half), BF16)),
         ],
         (got_cols, w_out, w_down),
         after=(line_slots,),
@@ -1009,7 +1078,7 @@
     picked, picked_own, cot = local_call(
         compact_kernel,
         [((routed, width), BF16), (block, BF16), ((routed, width), BF16)],
-        (spread, *slots),
+        (spread, *shuffle(slots)),
     )
     normed, full_qkv, full_out, full_vecs, joined, attended, exact, near, far = local_call(
         partial(attention_kernel, (ny, nx, rows), members),
@@ -1024,7 +1093,6 @@
         ]
         + halves,
         (where, picked, Far(first, 0, base, 1)),
-        scratch=[pltpu.VMEM((width, 128), BF16)],
         scalars=1,
     )
     terms = scatter_group(near, far)
@@ -1050,7 +1118,7 @@
     active, d_upper, near, far = local_call(
         partial(forward_kernel, (ny, members, nx, rows), members),
         [((routed, wide), BF16)] * 2 + halves,
-        (where, d_active, *got_up, *normed_mlp),
+        (where, d_active, *got_up, *shuffle(normed_mlp)),
         scratch=[pltpu.VMEM((width, wide), BF16)],
         scalars=1,
     )
@@ -1059,7 +1127,7 @@
     ff_keep, ff_send = local_call(
         partial(ff_grads_kernel, (ny, nx, rows, ff_rows), members),
         [((half_rows, width), BF16)] * 2,
-        (where, active, d_upper, d_result, *normed_mlp),
+        (where, active, d_upper, d_result, *shuffle(normed_mlp)),
         scratch=[pltpu.VMEM((wide, width), BF16), pltpu.VMEM((width, wide), BF16)],
         scalars=1,
     )
@@ -1088,17 +1156,17 @@
         partial(attention_back_kernel, members),
         slot_halves + [((routed, cols), BF16), ((routed, width), BF16)],
         (where, full_out, joined, exact, full_qkv, full_vecs, picked)
-        + (logit, d_hidden, spread, *d_branch),
+        + (logit, d_hidden, spread, *shuffle(d_branch)),
         scalars=1,
     )
     far = send_c(far)
     parts = local_call(
         partial(grads_kernel, (ny, nx, rows), members),
-        [((members * rows + 2 * rows, cols + 128), BF16)] * lines,
-        (where, normed, d_joined, attended, gain_a, gain_m, picked, logit, *d_branch),
+        [((members * rows * cols // (cols + 128) + 2 * rows + 16, cols + 128), BF16)] * lines,
+        (where, normed, d_joined, attended, gain_a, gain_m, picked, logit, *shuffle(d_branch)),
         scratch=[
             pltpu.VMEM((width, cols), BF16),
-            pltpu.VMEM((width, 128), BF16),
+            pltpu.VMEM((lines, 16, cols + 128), BF16),
             pltpu.VMEM((heads * HDIM, width), BF16),
         ],
         scalars=1,

time: 161 us -> 156 us (0.969)
  starting transfers between devices: 59.9 us -> 56.6 us
  local copies, waits for them, and re-layouts: 2.85 us -> 1.2 us
    ppermute x21, waiting for transfers between devices: 41.9 us -> 46.4 us  [send_z(): lax.ppermute(b, 'z', f)]
    all_to_all x1, waiting for transfers between devices: 5 us -> 0.98 us  [grouped(): first = lax.all_to_all(first, ('y', 'x'), 0, 0, tiled=True)]
    ppermute x21, starting transfers between devices: 30.7 us -> 27.9 us  [send_z(): lax.ppermute(b, 'z', f)]
    unnamed x17 -> x15, local copies, waits for them, and re-layouts: 2.76 us -> 1.11 us
where the time goes in v8:
time: 156 us
  waiting for transfers between devices  65.9 us (42%)
  starting transfers between devices  56.6 us (36%)
  Pallas kernels  31.1 us (20%)
    ppermute x21, waiting for transfers between devices, send_z(): lax.ppermute(b, 'z', f)  46.4 us
    pallas_call x24, Pallas kernels, local_call(): pl.pallas_call(run, out_shape=shapes, in_specs=[pl.BlockSpec(memory_space...  31.1 us
    ppermute x21, starting transfers between devices, send_z(): lax.ppermute(b, 'z', f)  27.9 us
    ppermute x12, waiting for transfers between devices, send_lines(): lax.ppermute(b, ('y', 'x'), f)  13.6 us
    ppermute x12, starting transfers between devices, send_lines(): lax.ppermute(b, ('y', 'x'), f)  13.1 us
    all_to_all x1, starting transfers between devices, grouped(): got_cols = lax.all_to_all(columns, ('c', 'z'), 0, 0, tiled=True)  6.47 us
    all_to_all x1, starting transfers between devices, grouped(): first = lax.all_to_all(first, ('y', 'x'), 0, 0, tiled=True)  4.38 us
    ppermute x17, waiting for transfers between devices, send_c(): return lax.ppermute(block, 'c', flips(2)[1])  4.13 us
  transfers between devices with their start and end apart: 54, of which 28 were waited for; matrix products, arithmetic and copies ran while one was open for 0% of the time, Pallas kernels for 13%

profile of v8, /device:TPU:0, one launch (start us, length us, event | category | flops | bytes accessed | tf_op | source)
XLA Modules:
  0.0 155.9 jit_solution(4776238236614982458)
XLA Ops:
  0.7 2.2 %shard_map.173 = bf16[8,32,1024]{2,1,0:T(8,128)(2,1)} custom-call(bf16[32,3072]{1,0:T(8,128)(2,1)} %refs_0_.1, bf16[32,4096]{1,0:T(8,128)(2,1)} %refs_1_.4, bf16[1,32]{1,0:T(2,128)(2,1)} %bitcast.14, bf16[1,32]{1,0:T(2,128)(2,1)} %bitcast.15, bf16[1,32]{1,0:T(2,128)(2,1)} %bitcast.16), custom_call_target="tpu_custom_call" | custom-call | tf_op jit(solution)/shard_map/pallas_call | solution.py:404
  2.9 6.5 %all-to-all-start = ((bf16[8,32,1024]{2,1,0:T(8,128)(2,1)}), bf16[8,32,1024]{2,1,0:T(8,128)(2,1)S(1)}, u32[]{:S(2)}, u32[]{:S(2)}) async-start(bf16[8,32,1024]{2,1,0:T(8,128)(2,1)} %shard_map.173), calls=%async_computation | async-start | bytes 1048576 | tf_op jit(solution)/shard_map/all_to_all | solution.py:1062
  9.6 1.5 shard_map.169
  11.1 1.6 collective-permute-start
  12.7 1.5 collective-permute-start.1
  14.7 1.8 %shard_map.170.refs_4_.refs_0_.refs_6_.refs_9_ = bf16[256,512]{1,0:T(8,128)(2,1)} custom-call(s32[5]{0:T(128)S(1)} %stack.23.refs_0_, s32[4,256]{1,0:T(4,128)S(1)} %copy-done.6, s32[256,4]{1,0:T(8,128)S(1)} %bitcast.13), custom_call_target="tpu_custom_call" | custom-call | tf_op jit(solution)/shard_map/pallas_call | solution.py:404
  17.0 2.4 %collective-permute-done.2.refs_3_ = bf16[32,1024]{1,0:T(8,128)(2,1)S(1)} collective-permute-done((bf16[32,1024]{1,0:T(8,128)(2,1)S(1)}, bf16[32,1024]{1,0:T(8,128)(2,1)S(1)}, u32[]{:S(2)}, u32[]{:S(2)}) %collective-permute-start.2) | collective-permute-done | bytes 65568 | tf_op jit(solution)/shard_map/ppermute | solution.py:430
  20.3 2.1 %collective-permute-start.3 = (bf16[128,1024]{1,0:T(8,128)(2,1)S(1)}, bf16[128,1024]{1,0:T(8,128)(2,1)S(1)}, u32[]{:S(2)}, u32[]{:S(2)}) collective-permute-start(bf16[128,1024]{1,0:T(8,128)(2,1)S(1)} %shard_map.171.refs_1_.refs_3_), channel_id=1, source_target_pairs={{0,2},{2,0},{4,6},{6,4},{1,3},{3,1},{5,7},{7,5},{8,10},{10,8},{12,... | collective-permute-start | bytes 786440 | tf_op jit(solution)/shard_map/ppermute | solution.py:425
  22.4 2.4 %collective-permute-start.4 = (bf16[128,1024]{1,0:T(8,128)(2,1)S(1)}, bf16[128,1024]{1,0:T(8,128)(2,1)S(1)}, u32[]{:S(2)}, u32[]{:S(2)}) collective-permute-start(bf16[128,1024]{1,0:T(8,128)(2,1)S(1)} %shard_map.171.refs_1_.refs_3_), channel_id=1, source_target_pairs={{0,6},{2,4},{4,2},{6,0},{1,7},{3,5},{5,3},{7,1},{8,14},{10,12},{12... | collective-permute-start | bytes 786440 | tf_op jit(solution)/shard_map/ppermute | solution.py:425
  24.8 1.5 shard_map.174
  26.3 4.4 %all-to-all-start.1 = ((bf16[4,400,512]{2,1,0:T(8,128)(2,1)}), bf16[4,400,512]{2,1,0:T(8,128)(2,1)}, u32[]{:S(2)}, u32[]{:S(2)}) async-start(bf16[4,400,512]{2,1,0:T(8,128)(2,1)} %get-tuple-element.94), calls=%async_computation.1 | async-start | bytes 3276800 | tf_op jit(solution)/shard_map/all_to_all | solution.py:1074
  31.0 3.9 %collective-permute-done.3.refs_2_ = bf16[128,1024]{1,0:T(8,128)(2,1)S(1)} collective-permute-done((bf16[128,1024]{1,0:T(8,128)(2,1)S(1)}, bf16[128,1024]{1,0:T(8,128)(2,1)S(1)}, u32[]{:S(2)}, u32[]{:S(2)}) %collective-permute-start.3) | collective-permute-done | bytes 262176 | tf_op jit(solution)/shard_map/ppermute | solution.py:425
  35.0 2.8 %collective-permute-done.4.refs_3_ = bf16[128,1024]{1,0:T(8,128)(2,1)S(1)} collective-permute-done((bf16[128,1024]{1,0:T(8,128)(2,1)S(1)}, bf16[128,1024]{1,0:T(8,128)(2,1)S(1)}, u32[]{:S(2)}, u32[]{:S(2)}) %collective-permute-start.4) | collective-permute-done | bytes 262176 | tf_op jit(solution)/shard_map/ppermute | solution.py:425
  37.7 9.5 %collective-permute-done.5.refs_4_ = bf16[128,1024]{1,0:T(8,128)(2,1)S(1)} collective-permute-done((bf16[128,1024]{1,0:T(8,128)(2,1)S(1)}, bf16[128,1024]{1,0:T(8,128)(2,1)S(1)}, u32[]{:S(2)}, u32[]{:S(2)}) %collective-permute-start.5) | collective-permute-done | bytes 262176 | tf_op jit(solution)/shard_map/ppermute | solution.py:425
  47.2 1.5 collective-permute-done.9.refs_8_
  48.8 1.7 %shard_map.172 = (bf16[256,1024]{1,0:T(8,128)(2,1)S(1)}, bf16[32,1024]{1,0:T(8,128)(2,1)S(1)}, bf16[256,1024]{1,0:T(8,128)(2,1)S(1)}) custom-call(bf16[256,512]{1,0:T(8,128)(2,1)} %shard_map.170.refs_4_.refs_0_.refs_6_.refs_9_, bf16[128,1024]{1,0:T(8,128)(2,1)S(1)} %shard_map.171.refs_1_.refs_3_, bf16[128,1024]{1,0:T(8,128)(2,1)S(1)} %collective-permute-done.3.refs_2_, ...), custom_call_target="tpu_custom_call" | custom-call | flops 10000000000 | tf_op jit(solution)/shard_map/pallas_call | solution.py:404
  51.4 3.2 %shard_map.175 = (bf16[256,1024]{1,0:T(8,128)(2,1)S(1)}, bf16[1024,384]{1,0:T(8,128)(2,1)S(1)}, bf16[128,1024]{1,0:T(8,128)(2,1)S(1)}, f32[8,1024]{1,0:T(8,128)S...) custom-call(s32[5]{0:T(128)S(1)} %stack.23.refs_0_, ...), custom_call_target="tpu_custom_call" | custom-call | flops 1200000000 | tf_op jit(solution)/shard_map/pallas_call | solution.py:404
  54.7 1.5 collective-permute-start.10
  58.4 1.6 %collective-permute-start.15 = (bf16[32,1024]{1,0:T(8,128)(2,1)S(1)}, bf16[32,1024]{1,0:T(8,128)(2,1)S(1)}, u32[]{:S(2)}, u32[]{:S(2)}) collective-permute-start(bf16[32,1024]{1,0:T(8,128)(2,1)S(1)} %get-tuple-element.104), channel_id=1, source_target_pairs={{0,4},{2,6},{4,0},{6,2},{1,5},{3,7},{5,1},{7,3},{8,12},{10,14},{12... | collective-permute-start | bytes 196616 | tf_op jit(solution)/shard_map/ppermute | solution.py:425
  60.0 3.0 %collective-permute-done.14.refs_3_ = bf16[32,1024]{1,0:T(8,128)(2,1)S(1)} collective-permute-done((bf16[32,1024]{1,0:T(8,128)(2,1)S(1)}, bf16[32,1024]{1,0:T(8,128)(2,1)S(1)}, u32[]{:S(2)}, u32[]{:S(2)}) %collective-permute-start.14) | collective-permute-done | bytes 65568 | tf_op jit(solution)/shard_map/ppermute | solution.py:425
  65.2 4.0 %collective-permute-done.16.refs_5_ = bf16[32,1024]{1,0:T(8,128)(2,1)S(1)} collective-permute-done((bf16[32,1024]{1,0:T(8,128)(2,1)S(1)}, bf16[32,1024]{1,0:T(8,128)(2,1)S(1)}, u32[]{:S(2)}, u32[]{:S(2)}) %collective-permute-start.16) | collective-permute-done | bytes 65568 | tf_op jit(solution)/shard_map/ppermute | solution.py:425
  69.4 1.4 collective-permute-start.18
  70.8 2.1 %collective-permute-start.19 = (bf16[32,1024]{1,0:T(8,128)(2,1)S(1)}, bf16[32,1024]{1,0:T(8,128)(2,1)S(1)}, u32[]{:S(2)}, u32[]{:S(2)}) collective-permute-start(bf16[32,1024]{1,0:T(8,128)(2,1)S(1)} %get-tuple-element.106.refs_6_.refs_4_), channel_id=1, source_target_pairs={{0,4},{2,6},{4,0},{6,2},{1,5},{3,7},{5,1},{7,3},{8,12},{10,14},{12... | collective-permute-start | bytes 196616 | tf_op jit(solution)/shard_map/ppermute | solution.py:425
  72.8 3.0 %collective-permute-done.11.refs_6_.refs_4_ = bf16[384,512]{1,0:T(8,128)(2,1)S(1)} collective-permute-done((bf16[384,512]{1,0:T(8,128)(2,1)S(1)}, bf16[384,512]{1,0:T(8,128)(2,1)S(1)}, u32[]{:S(2)}, u32[]{:S(2)}) %collective-permute-start.11) | collective-permute-done | bytes 393248 | tf_op jit(solution)/shard_map/ppermute | solution.py:430
  77.2 2.2 %shard_map.176 = (f32[256,1]{1,0:T(8,128)S(1)}, bf16[32,1024]{1,0:T(8,128)(2,1)S(1)}, bf16[256,1024]{1,0:T(8,128)(2,1)S(1)}, f32[256,512]{1,0:T(8,128)S(1)}, bf16[512,1024]{1,0:T(8,128)(2,1)S(1)}) custom-call(s32[5]{0:T(128)S(1)} %stack.23.refs_0_, bf16[256,1024]{1,0:T(8,128)(2,1)S(1)} %get-tuple-element.93.refs_1_.refs_6_, ...), custom_call_target="tpu_custom_call" | custom-call | flops 800000000 | tf_op jit(solution)/shard_map/pallas_call | solution.py:404
  79.5 1.6 %shard_map.179 = (bf16[256,512]{1,0:T(8,128)(2,1)S(1)}, bf16[256,512]{1,0:T(8,128)(2,1)S(1)}, bf16[4,32,1024]{2,1,0:T(8,128)(2,1)S(1)}, bf16[4,32,1024]{2,1,0:T(8,128)(2,1)S(1)}) custom-call(s32[5]{0:T(128)S(1)} %stack.23.refs_0_, f32[256,512]{1,0:T(8,128)S(1)} %get-tuple-element.98.refs_1_, bf16[384,512]{1,0:T(8,128)(2,1)S(1)} %copy-done.2, ...), custom_call_target="tpu_custom_call" | custom-call | flops 600000000 | tf_op jit(solution)/shard_map/pallas_call | solution.py:404
  83.0 1.6 %collective-permute-start.37 = (bf16[512,1024]{1,0:T(8,128)(2,1)S(1)}, bf16[512,1024]{1,0:T(8,128)(2,1)S(1)}, u32[]{:S(2)}, u32[]{:S(2)}) collective-permute-start(bf16[512,1024]{1,0:T(8,128)(2,1)S(1)} %get-tuple-element.128.refs_8_), channel_id=1, source_target_pairs={{0,1},{1,0},{2,3},{3,2},{4,5},{5,4},{6,7},{7,6},{8,9},{9,8},{10,11... | collective-permute-start | bytes 3145736 | tf_op jit(solution)/shard_map/ppermute | solution.py:1134
  84.8 2.5 %collective-permute-start.27 = (bf16[32,1024]{1,0:T(8,128)(2,1)S(1)}, bf16[32,1024]{1,0:T(8,128)(2,1)S(1)}, u32[]{:S(2)}, u32[]{:S(2)}) collective-permute-start(bf16[32,1024]{1,0:T(8,128)(2,1)S(1)} %get-tuple-element.124), channel_id=1, source_target_pairs={{0,4},{2,6},{4,0},{6,2},{1,5},{3,7},{5,1},{7,3},{8,12},{10,14},{12... | collective-permute-start | bytes 196616 | tf_op jit(solution)/shard_map/ppermute | solution.py:425
  87.3 1.9 %collective-permute-start.28 = (bf16[32,1024]{1,0:T(8,128)(2,1)S(1)}, bf16[32,1024]{1,0:T(8,128)(2,1)S(1)}, u32[]{:S(2)}, u32[]{:S(2)}) collective-permute-start(bf16[32,1024]{1,0:T(8,128)(2,1)S(1)} %get-tuple-element.125), channel_id=1, source_target_pairs={{0,6},{2,4},{4,2},{6,0},{1,7},{3,5},{5,3},{7,1},{8,14},{10,12},{12... | collective-permute-start | bytes 196616 | tf_op jit(solution)/shard_map/ppermute | solution.py:425
  89.2 1.4 shard_map.180
  90.6 1.8 %collective-permute-done.27.refs_6_ = bf16[32,1024]{1,0:T(8,128)(2,1)S(1)} collective-permute-done((bf16[32,1024]{1,0:T(8,128)(2,1)S(1)}, bf16[32,1024]{1,0:T(8,128)(2,1)S(1)}, u32[]{:S(2)}, u32[]{:S(2)}) %collective-permute-start.27) | collective-permute-done | bytes 65568 | tf_op jit(solution)/shard_map/ppermute | solution.py:425
  94.6 1.9 %collective-permute-start.30 = (bf16[32,1024]{1,0:T(8,128)(2,1)S(1)}, bf16[32,1024]{1,0:T(8,128)(2,1)S(1)}, u32[]{:S(2)}, u32[]{:S(2)}) collective-permute-start(bf16[32,1024]{1,0:T(8,128)(2,1)S(1)} %get-tuple-element.130.refs_10_.refs_8_), channel_id=1, source_target_pairs={{0,6},{2,4},{4,2},{6,0},{1,7},{3,5},{5,3},{7,1},{8,14},{10,12},{12... | collective-permute-start | bytes 196616 | tf_op jit(solution)/shard_map/ppermute | solution.py:425
  97.1 1.6 %collective-permute-done.29.refs_11_.refs_9_ = bf16[32,1024]{1,0:T(8,128)(2,1)S(1)} collective-permute-done((bf16[32,1024]{1,0:T(8,128)(2,1)S(1)}, bf16[32,1024]{1,0:T(8,128)(2,1)S(1)}, u32[]{:S(2)}, u32[]{:S(2)}) %collective-permute-start.29) | collective-permute-done | bytes 65568 | tf_op jit(solution)/shard_map/ppermute | solution.py:425
  98.7 2.0 %collective-permute-done.30.refs_12_.refs_10_ = bf16[32,1024]{1,0:T(8,128)(2,1)S(1)} collective-permute-done((bf16[32,1024]{1,0:T(8,128)(2,1)S(1)}, bf16[32,1024]{1,0:T(8,128)(2,1)S(1)}, u32[]{:S(2)}, u32[]{:S(2)}) %collective-permute-start.30) | collective-permute-done | bytes 65568 | tf_op jit(solution)/shard_map/ppermute | solution.py:425
  103.4 3.9 %shard_map.184 = (bf16[4,64,1024]{2,1,0:T(8,128)(2,1)S(1)}, bf16[4,64,1024]{2,1,0:T(8,128)(2,1)S(1)}, bf16[256,384]{1,0:T(8,128)(2,1)S(1)}, bf16[256,1024]{1,0:T(8,128)(2,1)S(1)}) custom-call(s32[5]{0:T(128)S(1)} %stack.23.refs_0_, bf16[128,1024]{1,0:T(8,128)(2,1)S(1)} %get-tuple-element.110.refs_3_.refs_1_, ...), custom_call_target="tpu_custom_call" | custom-call | flops 1200000000 | tf_op jit(solution)/shard_map/pallas_call | solution.py:404
  109.5 2.4 %collective-permute-start.39 = (bf16[128,1024]{1,0:T(8,128)(2,1)S(1)}, bf16[128,1024]{1,0:T(8,128)(2,1)S(1)}, u32[]{:S(2)}, u32[]{:S(2)}) collective-permute-start(bf16[128,1024]{1,0:T(8,128)(2,1)S(1)} %get-tuple-element.137), channel_id=1, source_target_pairs={{0,4},{2,6},{4,0},{6,2},{1,5},{3,7},{5,1},{7,3},{8,12},{10,14},{12... | collective-permute-start | bytes 786440 | tf_op jit(solution)/shard_map/ppermute | solution.py:425
  112.8 1.5 shard_map.189
  116.4 6.3 %collective-permute-done.38.refs_1_ = bf16[128,1024]{1,0:T(8,128)(2,1)S(1)} collective-permute-done((bf16[128,1024]{1,0:T(8,128)(2,1)S(1)}, bf16[128,1024]{1,0:T(8,128)(2,1)S(1)}, u32[]{:S(2)}, u32[]{:S(2)}) %collective-permute-start.38) | collective-permute-done | bytes 262176 | tf_op jit(solution)/shard_map/ppermute | solution.py:425
  122.7 1.5 collective-permute-start.47
  124.5 1.9 %collective-permute-start.40 = (bf16[128,1024]{1,0:T(8,128)(2,1)S(1)}, bf16[128,1024]{1,0:T(8,128)(2,1)S(1)}, u32[]{:S(2)}, u32[]{:S(2)}) collective-permute-start(bf16[128,1024]{1,0:T(8,128)(2,1)S(1)} %get-tuple-element.138), channel_id=1, source_target_pairs={{0,6},{2,4},{4,2},{6,0},{1,7},{3,5},{5,3},{7,1},{8,14},{10,12},{12... | collective-permute-start | bytes 786440 | tf_op jit(solution)/shard_map/ppermute | solution.py:425
  126.4 7.0 %collective-permute-done.40.refs_3_ = bf16[128,1024]{1,0:T(8,128)(2,1)S(1)} collective-permute-done((bf16[128,1024]{1,0:T(8,128)(2,1)S(1)}, bf16[128,1024]{1,0:T(8,128)(2,1)S(1)}, u32[]{:S(2)}, u32[]{:S(2)}) %collective-permute-start.40) | collective-permute-done | bytes 262176 | tf_op jit(solution)/shard_map/ppermute | solution.py:425
  133.5 3.8 %collective-permute-done.46.refs_5_ = bf16[272,512]{1,0:T(8,128)(2,1)S(1)} collective-permute-done((bf16[272,512]{1,0:T(8,128)(2,1)S(1)}, bf16[272,512]{1,0:T(8,128)(2,1)S(1)}, u32[]{:S(2)}, u32[]{:S(2)}) %collective-permute-start.46) | collective-permute-done | bytes 278560 | tf_op jit(solution)/shard_map/ppermute | solution.py:430
  137.3 1.8 %shard_map.190 = (bf16[4,32,1024]{2,1,0:T(8,128)(2,1)S(1)}, bf16[4,32,1024]{2,1,0:T(8,128)(2,1)S(1)}, f32[32,1024]{1,0:T(8,128)}, f32[128,1024]{1,0:T(8,128)}) custom-call(s32[5]{0:T(128)S(1)} %stack.23.refs_0_, f32[256,1024]{1,0:T(8,128)S(1)} %get-tuple-element.134.refs_4_.refs_1_, bf16[256,1024]{1,0:T(8,128)(2,1)S(1)} %collective-permute-done.44.refs_2_, ...), custom_call_target="tpu_custom_call" | custom-call | tf_op jit(solution)/shard_map/pallas_call | solution.py:404
  141.4 1.9 %collective-permute-start.50 = (bf16[64,1024]{1,0:T(8,128)(2,1)S(1)}, bf16[64,1024]{1,0:T(8,128)(2,1)S(1)}, u32[]{:S(2)}, u32[]{:S(2)}) collective-permute-start(bf16[64,1024]{1,0:T(8,128)(2,1)S(1)} %get-tuple-element.158), channel_id=1, source_target_pairs={{0,4},{2,6},{4,0},{6,2},{1,5},{3,7},{5,1},{7,3},{8,12},{10,14},{12... | collective-permute-start | bytes 393224 | tf_op jit(solution)/shard_map/ppermute | solution.py:425
  143.3 1.9 %collective-permute-start.51 = (bf16[64,1024]{1,0:T(8,128)(2,1)S(1)}, bf16[64,1024]{1,0:T(8,128)(2,1)S(1)}, u32[]{:S(2)}, u32[]{:S(2)}) collective-permute-start(bf16[64,1024]{1,0:T(8,128)(2,1)S(1)} %get-tuple-element.159), channel_id=1, source_target_pairs={{0,6},{2,4},{4,2},{6,0},{1,7},{3,5},{5,3},{7,1},{8,14},{10,12},{12... | collective-permute-start | bytes 393224 | tf_op jit(solution)/shard_map/ppermute | solution.py:425
  147.2 2.7 %collective-permute-done.42.refs_6_ = bf16[32,1024]{1,0:T(8,128)(2,1)S(1)} collective-permute-done((bf16[32,1024]{1,0:T(8,128)(2,1)S(1)}, bf16[32,1024]{1,0:T(8,128)(2,1)S(1)}, u32[]{:S(2)}, u32[]{:S(2)}) %collective-permute-start.42) | collective-permute-done | bytes 65568 | tf_op jit(solution)/shard_map/ppermute | solution.py:430
  151.1 2.7 %shard_map.188 = (bf16[4,64,1024]{2,1,0:T(8,128)(2,1)}, bf16[4,64,1024]{2,1,0:T(8,128)(2,1)}) custom-call(s32[5]{0:T(128)S(1)} %stack.23.refs_0_, bf16[4,16,64]{2,1,0:T(8,128)(2,1)} %get-tuple-element.88.refs_1_, bf16[4,64,1024]{2,1,0:T(8,128)(2,1)S(1)} %copy-done, bf16[4,64,1024]{2,1,0:T(8,128)(2,1)S(1)} %copy-done.1, ...), custom_call_target="tpu_custom_call" | custom-call | tf_op jit(solution)/shard_map/pallas_call | solution.py:404
  154.3 1.6 %shard_map.192 = (f32[32,3072]{1,0:T(8,128)}, f32[32,4096]{1,0:T(8,128)}, f32[1,32]{1,0:T(1,128)}, f32[1,32]{1,0:T(1,128)}, f32[1,32]{1,0:T(1,128)}) custom-call(s32[5]{0:T(128)S(1)} %stack.23.refs_0_, bf16[64,1024]{1,0:T(8,128)(2,1)S(1)} %get-tuple-element.156.refs_1_, bf16[64,1024]{1,0:T(8,128)(2,1)S(1)} %collective-permute-done.49.refs_2_, ...), custom_call_target="tpu_custom_call" | custom-call | tf_op jit(solution)/shard_map/pallas_call | solution.py:404
  (100 shorter events, 28.5 us)
Async XLA Ops:
  2.9 21.9 %all-to-all-start = ((bf16[8,32,1024]{2,1,0:T(8,128)(2,1)}), bf16[8,32,1024]{2,1,0:T(8,128)(2,1)S(1)}, u32[]{:S(2)}, u32[]{:S(2)}) async-start(bf16[8,32,1024]{2,1,0:T(8,128)(2,1)} %shard_map.173), calls=%async_computation | async-start | bytes 1048576 | tf_op jit(solution)/shard_map/all_to_all | solution.py:1062
  11.1 5.4 %collective-permute-start = (bf16[32,1024]{1,0:T(8,128)(2,1)S(1)}, bf16[32,1024]{1,0:T(8,128)(2,1)S(1)}, u32[]{:S(2)}, u32[]{:S(2)}) collective-permute-start(bf16[32,1024]{1,0:T(8,128)(2,1)S(1)} %get-tuple-element.90), channel_id=1, source_target_pairs={{0,1},{1,0},{16,17},{17,16},{2,3},{3,2},{18,19},{19,18},{4,5},{5,4... | collective-permute-start | bytes 196616 | tf_op jit(solution)/shard_map/ppermute | solution.py:430
  12.7 4.3 %collective-permute-start.1 = (bf16[32,1024]{1,0:T(8,128)(2,1)S(1)}, bf16[32,1024]{1,0:T(8,128)(2,1)S(1)}, u32[]{:S(2)}, u32[]{:S(2)}) collective-permute-start(bf16[32,1024]{1,0:T(8,128)(2,1)S(1)} %get-tuple-element.91), channel_id=1, source_target_pairs={{0,16},{1,17},{16,0},{17,1},{2,18},{3,19},{18,2},{19,3},{4,20},{5,... | collective-permute-start | bytes 196616 | tf_op jit(solution)/shard_map/ppermute | solution.py:430
  14.2 5.2 %collective-permute-start.2 = (bf16[32,1024]{1,0:T(8,128)(2,1)S(1)}, bf16[32,1024]{1,0:T(8,128)(2,1)S(1)}, u32[]{:S(2)}, u32[]{:S(2)}) collective-permute-start(bf16[32,1024]{1,0:T(8,128)(2,1)S(1)} %get-tuple-element.92), channel_id=1, source_target_pairs={{0,17},{1,16},{16,1},{17,0},{2,19},{3,18},{18,3},{19,2},{4,21},{5,... | collective-permute-start | bytes 196616 | tf_op jit(solution)/shard_map/ppermute | solution.py:430
  20.3 14.6 %collective-permute-start.3 = (bf16[128,1024]{1,0:T(8,128)(2,1)S(1)}, bf16[128,1024]{1,0:T(8,128)(2,1)S(1)}, u32[]{:S(2)}, u32[]{:S(2)}) collective-permute-start(bf16[128,1024]{1,0:T(8,128)(2,1)S(1)} %shard_map.171.refs_1_.refs_3_), channel_id=1, source_target_pairs={{0,2},{2,0},{4,6},{6,4},{1,3},{3,1},{5,7},{7,5},{8,10},{10,8},{12,... | collective-permute-start | bytes 786440 | tf_op jit(solution)/shard_map/ppermute | solution.py:425
  22.4 15.3 %collective-permute-start.4 = (bf16[128,1024]{1,0:T(8,128)(2,1)S(1)}, bf16[128,1024]{1,0:T(8,128)(2,1)S(1)}, u32[]{:S(2)}, u32[]{:S(2)}) collective-permute-start(bf16[128,1024]{1,0:T(8,128)(2,1)S(1)} %shard_map.171.refs_1_.refs_3_), channel_id=1, source_target_pairs={{0,6},{2,4},{4,2},{6,0},{1,7},{3,5},{5,3},{7,1},{8,14},{10,12},{12... | collective-permute-start | bytes 786440 | tf_op jit(solution)/shard_map/ppermute | solution.py:425
  24.8 22.4 %collective-permute-start.5 = (bf16[128,1024]{1,0:T(8,128)(2,1)S(1)}, bf16[128,1024]{1,0:T(8,128)(2,1)S(1)}, u32[]{:S(2)}, u32[]{:S(2)}) collective-permute-start(bf16[128,1024]{1,0:T(8,128)(2,1)S(1)} %shard_map.171.refs_1_.refs_3_), channel_id=1, source_target_pairs={{0,4},{2,6},{4,0},{6,2},{1,5},{3,7},{5,1},{7,3},{8,12},{10,14},{12... | collective-permute-start | bytes 786440 | tf_op jit(solution)/shard_map/ppermute | solution.py:425
  26.3 25.1 %all-to-all-start.1 = ((bf16[4,400,512]{2,1,0:T(8,128)(2,1)}), bf16[4,400,512]{2,1,0:T(8,128)(2,1)}, u32[]{:S(2)}, u32[]{:S(2)}) async-start(bf16[4,400,512]{2,1,0:T(8,128)(2,1)} %get-tuple-element.94), calls=%async_computation.1 | async-start | bytes 3276800 | tf_op jit(solution)/shard_map/all_to_all | solution.py:1074
  30.7 16.5 %collective-permute-start.6 = (bf16[128,1024]{1,0:T(8,128)(2,1)S(1)}, bf16[128,1024]{1,0:T(8,128)(2,1)S(1)}, u32[]{:S(2)}, u32[]{:S(2)}) collective-permute-start(bf16[128,1024]{1,0:T(8,128)(2,1)S(1)} %shard_map.171.refs_1_.refs_3_), channel_id=1, source_target_pairs={{0,8},{8,0},{1,9},{9,1},{2,10},{10,2},{3,11},{11,3},{4,12},{12,4},... | collective-permute-start | bytes 786440 | tf_op jit(solution)/shard_map/ppermute | solution.py:438
  34.9 12.3 %collective-permute-start.7 = (bf16[128,1024]{1,0:T(8,128)(2,1)S(1)}, bf16[128,1024]{1,0:T(8,128)(2,1)S(1)}, u32[]{:S(2)}, u32[]{:S(2)}) collective-permute-start(bf16[128,1024]{1,0:T(8,128)(2,1)S(1)} %collective-permute-done.3.refs_2_), channel_id=1, source_target_pairs={{0,8},{8,0},{1,9},{9,1},{2,10},{10,2},{3,11},{11,3},{4,12},{12,4},... | collective-permute-start | bytes 786440 | tf_op jit(solution)/shard_map/ppermute | solution.py:438
  37.7 9.5 %collective-permute-start.8 = (bf16[128,1024]{1,0:T(8,128)(2,1)S(1)}, bf16[128,1024]{1,0:T(8,128)(2,1)S(1)}, u32[]{:S(2)}, u32[]{:S(2)}) collective-permute-start(bf16[128,1024]{1,0:T(8,128)(2,1)S(1)} %collective-permute-done.4.refs_3_), channel_id=1, source_target_pairs={{0,8},{8,0},{1,9},{9,1},{2,10},{10,2},{3,11},{11,3},{4,12},{12,4},... | collective-permute-start | bytes 786440 | tf_op jit(solution)/shard_map/ppermute | solution.py:438
  54.7 3.6 %collective-permute-start.13 = (bf16[4,32,1024]{2,1,0:T(8,128)(2,1)S(1)}, bf16[4,32,1024]{2,1,0:T(8,128)(2,1)S(1)}, u32[]{:S(2)}, u32[]{:S(2)}) collective-permute-start(bf16[4,32,1024]{2,1,0:T(8,128)(2,1)S(1)} %get-tuple-element.101), channel_id=1, source_target_pairs={{0,8},{8,0},{1,9},{9,1},{2,10},{10,2},{3,11},{11,3},{4,12},{12,4},... | collective-permute-start | bytes 786440 | tf_op jit(solution)/shard_map/ppermute | solution.py:438
  54.7 16.0 %collective-permute-start.10 = (bf16[384,512]{1,0:T(8,128)(2,1)S(1)}, bf16[384,512]{1,0:T(8,128)(2,1)S(1)}, u32[]{:S(2)}, u32[]{:S(2)}) collective-permute-start(bf16[384,512]{1,0:T(8,128)(2,1)S(1)} %copy-done.2), channel_id=1, source_target_pairs={{0,1},{1,0},{16,17},{17,16},{2,3},{3,2},{18,19},{19,18},{4,5},{5,4... | collective-permute-start | bytes 1179656 | tf_op jit(solution)/shard_map/ppermute | solution.py:430
  56.2 19.6 %collective-permute-start.11 = (bf16[384,512]{1,0:T(8,128)(2,1)S(1)}, bf16[384,512]{1,0:T(8,128)(2,1)S(1)}, u32[]{:S(2)}, u32[]{:S(2)}) collective-permute-start(bf16[384,512]{1,0:T(8,128)(2,1)S(1)} %copy-done.2), channel_id=1, source_target_pairs={{0,16},{1,17},{16,0},{17,1},{2,18},{3,19},{18,2},{19,3},{4,20},{5,... | collective-permute-start | bytes 1179656 | tf_op jit(solution)/shard_map/ppermute | solution.py:430
  56.9 20.3 %collective-permute-start.12 = (bf16[384,512]{1,0:T(8,128)(2,1)S(1)}, bf16[384,512]{1,0:T(8,128)(2,1)S(1)}, u32[]{:S(2)}, u32[]{:S(2)}) collective-permute-start(bf16[384,512]{1,0:T(8,128)(2,1)S(1)} %copy-done.2), channel_id=1, source_target_pairs={{0,17},{1,16},{16,1},{17,0},{2,19},{3,18},{18,3},{19,2},{4,21},{5,... | collective-permute-start | bytes 1179656 | tf_op jit(solution)/shard_map/ppermute | solution.py:430
  58.4 4.6 %collective-permute-start.14 = (bf16[32,1024]{1,0:T(8,128)(2,1)S(1)}, bf16[32,1024]{1,0:T(8,128)(2,1)S(1)}, u32[]{:S(2)}, u32[]{:S(2)}) collective-permute-start(bf16[32,1024]{1,0:T(8,128)(2,1)S(1)} %get-tuple-element.103), channel_id=1, source_target_pairs={{0,2},{2,0},{4,6},{6,4},{1,3},{3,1},{5,7},{7,5},{8,10},{10,8},{12,... | collective-permute-start | bytes 196616 | tf_op jit(solution)/shard_map/ppermute | solution.py:425
  58.4 6.8 %collective-permute-start.15 = (bf16[32,1024]{1,0:T(8,128)(2,1)S(1)}, bf16[32,1024]{1,0:T(8,128)(2,1)S(1)}, u32[]{:S(2)}, u32[]{:S(2)}) collective-permute-start(bf16[32,1024]{1,0:T(8,128)(2,1)S(1)} %get-tuple-element.104), channel_id=1, source_target_pairs={{0,4},{2,6},{4,0},{6,2},{1,5},{3,7},{5,1},{7,3},{8,12},{10,14},{12... | collective-permute-start | bytes 196616 | tf_op jit(solution)/shard_map/ppermute | solution.py:425
  63.0 6.1 %collective-permute-start.16 = (bf16[32,1024]{1,0:T(8,128)(2,1)S(1)}, bf16[32,1024]{1,0:T(8,128)(2,1)S(1)}, u32[]{:S(2)}, u32[]{:S(2)}) collective-permute-start(bf16[32,1024]{1,0:T(8,128)(2,1)S(1)} %get-tuple-element.105), channel_id=1, source_target_pairs={{0,6},{2,4},{4,2},{6,0},{1,7},{3,5},{5,3},{7,1},{8,14},{10,12},{12... | collective-permute-start | bytes 196616 | tf_op jit(solution)/shard_map/ppermute | solution.py:425
  69.3 6.6 %collective-permute-start.17 = (bf16[32,1024]{1,0:T(8,128)(2,1)S(1)}, bf16[32,1024]{1,0:T(8,128)(2,1)S(1)}, u32[]{:S(2)}, u32[]{:S(2)}) collective-permute-start(bf16[32,1024]{1,0:T(8,128)(2,1)S(1)} %get-tuple-element.106.refs_6_.refs_4_), channel_id=1, source_target_pairs={{0,2},{2,0},{4,6},{6,4},{1,3},{3,1},{5,7},{7,5},{8,10},{10,8},{12,... | collective-permute-start | bytes 196616 | tf_op jit(solution)/shard_map/ppermute | solution.py:425
  69.4 7.0 %collective-permute-start.18 = (bf16[32,1024]{1,0:T(8,128)(2,1)S(1)}, bf16[32,1024]{1,0:T(8,128)(2,1)S(1)}, u32[]{:S(2)}, u32[]{:S(2)}) collective-permute-start(bf16[32,1024]{1,0:T(8,128)(2,1)S(1)} %get-tuple-element.106.refs_6_.refs_4_), channel_id=1, source_target_pairs={{0,6},{2,4},{4,2},{6,0},{1,7},{3,5},{5,3},{7,1},{8,14},{10,12},{12... | collective-permute-start | bytes 196616 | tf_op jit(solution)/shard_map/ppermute | solution.py:425
  70.8 6.4 %collective-permute-start.19 = (bf16[32,1024]{1,0:T(8,128)(2,1)S(1)}, bf16[32,1024]{1,0:T(8,128)(2,1)S(1)}, u32[]{:S(2)}, u32[]{:S(2)}) collective-permute-start(bf16[32,1024]{1,0:T(8,128)(2,1)S(1)} %get-tuple-element.106.refs_6_.refs_4_), channel_id=1, source_target_pairs={{0,4},{2,6},{4,0},{6,2},{1,5},{3,7},{5,1},{7,3},{8,12},{10,14},{12... | collective-permute-start | bytes 196616 | tf_op jit(solution)/shard_map/ppermute | solution.py:425
  75.8 3.6 %collective-permute-start.20 = (bf16[32,1024]{1,0:T(8,128)(2,1)S(1)}, bf16[32,1024]{1,0:T(8,128)(2,1)S(1)}, u32[]{:S(2)}, u32[]{:S(2)}) collective-permute-start(bf16[32,1024]{1,0:T(8,128)(2,1)S(1)} %get-tuple-element.106.refs_6_.refs_4_), channel_id=1, source_target_pairs={{0,8},{8,0},{1,9},{9,1},{2,10},{10,2},{3,11},{11,3},{4,12},{12,4},... | collective-permute-start | bytes 196616 | tf_op jit(solution)/shard_map/ppermute | solution.py:438
  75.8 3.6 %collective-permute-start.21 = (bf16[32,1024]{1,0:T(8,128)(2,1)S(1)}, bf16[32,1024]{1,0:T(8,128)(2,1)S(1)}, u32[]{:S(2)}, u32[]{:S(2)}) collective-permute-start(bf16[32,1024]{1,0:T(8,128)(2,1)S(1)} %collective-permute-done.17.refs_7_.refs_5_), channel_id=1, source_target_pairs={{0,8},{8,0},{1,9},{9,1},{2,10},{10,2},{3,11},{11,3},{4,12},{12,4},... | collective-permute-start | bytes 196616 | tf_op jit(solution)/shard_map/ppermute | solution.py:438
  76.3 3.1 %collective-permute-start.22 = (bf16[32,1024]{1,0:T(8,128)(2,1)S(1)}, bf16[32,1024]{1,0:T(8,128)(2,1)S(1)}, u32[]{:S(2)}, u32[]{:S(2)}) collective-permute-start(bf16[32,1024]{1,0:T(8,128)(2,1)S(1)} %collective-permute-done.18.refs_8_.refs_6_), channel_id=1, source_target_pairs={{0,8},{8,0},{1,9},{9,1},{2,10},{10,2},{3,11},{11,3},{4,12},{12,4},... | collective-permute-start | bytes 196616 | tf_op jit(solution)/shard_map/ppermute | solution.py:438
  81.1 3.6 %collective-permute-start.25 = (bf16[4,32,1024]{2,1,0:T(8,128)(2,1)S(1)}, bf16[4,32,1024]{2,1,0:T(8,128)(2,1)S(1)}, u32[]{:S(2)}, u32[]{:S(2)}) collective-permute-start(bf16[4,32,1024]{2,1,0:T(8,128)(2,1)S(1)} %get-tuple-element.121), channel_id=1, source_target_pairs={{0,8},{8,0},{1,9},{9,1},{2,10},{10,2},{3,11},{11,3},{4,12},{12,4},... | collective-permute-start | bytes 786440 | tf_op jit(solution)/shard_map/ppermute | solution.py:438
  83.0 25.2 %collective-permute-start.37 = (bf16[512,1024]{1,0:T(8,128)(2,1)S(1)}, bf16[512,1024]{1,0:T(8,128)(2,1)S(1)}, u32[]{:S(2)}, u32[]{:S(2)}) collective-permute-start(bf16[512,1024]{1,0:T(8,128)(2,1)S(1)} %get-tuple-element.128.refs_8_), channel_id=1, source_target_pairs={{0,1},{1,0},{2,3},{3,2},{4,5},{5,4},{6,7},{7,6},{8,9},{9,8},{10,11... | collective-permute-start | bytes 3145736 | tf_op jit(solution)/shard_map/ppermute | solution.py:1134
  84.7 5.9 %collective-permute-start.26 = (bf16[32,1024]{1,0:T(8,128)(2,1)S(1)}, bf16[32,1024]{1,0:T(8,128)(2,1)S(1)}, u32[]{:S(2)}, u32[]{:S(2)}) collective-permute-start(bf16[32,1024]{1,0:T(8,128)(2,1)S(1)} %get-tuple-element.123), channel_id=1, source_target_pairs={{0,2},{2,0},{4,6},{6,4},{1,3},{3,1},{5,7},{7,5},{8,10},{10,8},{12,... | collective-permute-start | bytes 196616 | tf_op jit(solution)/shard_map/ppermute | solution.py:425
  84.8 7.7 %collective-permute-start.27 = (bf16[32,1024]{1,0:T(8,128)(2,1)S(1)}, bf16[32,1024]{1,0:T(8,128)(2,1)S(1)}, u32[]{:S(2)}, u32[]{:S(2)}) collective-permute-start(bf16[32,1024]{1,0:T(8,128)(2,1)S(1)} %get-tuple-element.124), channel_id=1, source_target_pairs={{0,4},{2,6},{4,0},{6,2},{1,5},{3,7},{5,1},{7,3},{8,12},{10,14},{12... | collective-permute-start | bytes 196616 | tf_op jit(solution)/shard_map/ppermute | solution.py:425
  87.3 6.1 %collective-permute-start.28 = (bf16[32,1024]{1,0:T(8,128)(2,1)S(1)}, bf16[32,1024]{1,0:T(8,128)(2,1)S(1)}, u32[]{:S(2)}, u32[]{:S(2)}) collective-permute-start(bf16[32,1024]{1,0:T(8,128)(2,1)S(1)} %get-tuple-element.125), channel_id=1, source_target_pairs={{0,6},{2,4},{4,2},{6,0},{1,7},{3,5},{5,3},{7,1},{8,14},{10,12},{12... | collective-permute-start | bytes 196616 | tf_op jit(solution)/shard_map/ppermute | solution.py:425
  93.6 5.1 %collective-permute-start.29 = (bf16[32,1024]{1,0:T(8,128)(2,1)S(1)}, bf16[32,1024]{1,0:T(8,128)(2,1)S(1)}, u32[]{:S(2)}, u32[]{:S(2)}) collective-permute-start(bf16[32,1024]{1,0:T(8,128)(2,1)S(1)} %get-tuple-element.130.refs_10_.refs_8_), channel_id=1, source_target_pairs={{0,2},{2,0},{4,6},{6,4},{1,3},{3,1},{5,7},{7,5},{8,10},{10,8},{12,... | collective-permute-start | bytes 196616 | tf_op jit(solution)/shard_map/ppermute | solution.py:425
  94.6 6.1 %collective-permute-start.30 = (bf16[32,1024]{1,0:T(8,128)(2,1)S(1)}, bf16[32,1024]{1,0:T(8,128)(2,1)S(1)}, u32[]{:S(2)}, u32[]{:S(2)}) collective-permute-start(bf16[32,1024]{1,0:T(8,128)(2,1)S(1)} %get-tuple-element.130.refs_10_.refs_8_), channel_id=1, source_target_pairs={{0,6},{2,4},{4,2},{6,0},{1,7},{3,5},{5,3},{7,1},{8,14},{10,12},{12... | collective-permute-start | bytes 196616 | tf_op jit(solution)/shard_map/ppermute | solution.py:425
  96.5 5.6 %collective-permute-start.31 = (bf16[32,1024]{1,0:T(8,128)(2,1)S(1)}, bf16[32,1024]{1,0:T(8,128)(2,1)S(1)}, u32[]{:S(2)}, u32[]{:S(2)}) collective-permute-start(bf16[32,1024]{1,0:T(8,128)(2,1)S(1)} %get-tuple-element.130.refs_10_.refs_8_), channel_id=1, source_target_pairs={{0,4},{2,6},{4,0},{6,2},{1,5},{3,7},{5,1},{7,3},{8,12},{10,14},{12... | collective-permute-start | bytes 196616 | tf_op jit(solution)/shard_map/ppermute | solution.py:425
  97.1 5.0 %collective-permute-start.32 = (bf16[32,1024]{1,0:T(8,128)(2,1)S(1)}, bf16[32,1024]{1,0:T(8,128)(2,1)S(1)}, u32[]{:S(2)}, u32[]{:S(2)}) collective-permute-start(bf16[32,1024]{1,0:T(8,128)(2,1)S(1)} %get-tuple-element.130.refs_10_.refs_8_), channel_id=1, source_target_pairs={{0,8},{8,0},{1,9},{9,1},{2,10},{10,2},{3,11},{11,3},{4,12},{12,4},... | collective-permute-start | bytes 196616 | tf_op jit(solution)/shard_map/ppermute | solution.py:438
  98.7 3.9 %collective-permute-start.33 = (bf16[32,1024]{1,0:T(8,128)(2,1)S(1)}, bf16[32,1024]{1,0:T(8,128)(2,1)S(1)}, u32[]{:S(2)}, u32[]{:S(2)}) collective-permute-start(bf16[32,1024]{1,0:T(8,128)(2,1)S(1)} %collective-permute-done.29.refs_11_.refs_9_), channel_id=1, source_target_pairs={{0,8},{8,0},{1,9},{9,1},{2,10},{10,2},{3,11},{11,3},{4,12},{12,4},... | collective-permute-start | bytes 196616 | tf_op jit(solution)/shard_map/ppermute | solution.py:438
  102.1 6.3 %collective-permute-start.24 = (bf16[4,64,1024]{2,1,0:T(8,128)(2,1)S(1)}, bf16[4,64,1024]{2,1,0:T(8,128)(2,1)S(1)}, u32[]{:S(2)}, u32[]{:S(2)}) collective-permute-start(bf16[4,64,1024]{2,1,0:T(8,128)(2,1)S(1)} %get-tuple-element.113), channel_id=1, source_target_pairs={{0,8},{8,0},{1,9},{9,1},{2,10},{10,2},{3,11},{11,3},{4,12},{12,4},... | collective-permute-start | bytes 1572872 | tf_op jit(solution)/shard_map/ppermute | solution.py:438
  109.4 13.3 %collective-permute-start.38 = (bf16[128,1024]{1,0:T(8,128)(2,1)S(1)}, bf16[128,1024]{1,0:T(8,128)(2,1)S(1)}, u32[]{:S(2)}, u32[]{:S(2)}) collective-permute-start(bf16[128,1024]{1,0:T(8,128)(2,1)S(1)} %get-tuple-element.136), channel_id=1, source_target_pairs={{0,2},{2,0},{4,6},{6,4},{1,3},{3,1},{5,7},{7,5},{8,10},{10,8},{12,... | collective-permute-start | bytes 786440 | tf_op jit(solution)/shard_map/ppermute | solution.py:425
  109.5 15.0 %collective-permute-start.39 = (bf16[128,1024]{1,0:T(8,128)(2,1)S(1)}, bf16[128,1024]{1,0:T(8,128)(2,1)S(1)}, u32[]{:S(2)}, u32[]{:S(2)}) collective-permute-start(bf16[128,1024]{1,0:T(8,128)(2,1)S(1)} %get-tuple-element.137), channel_id=1, source_target_pairs={{0,4},{2,6},{4,0},{6,2},{1,5},{3,7},{5,1},{7,3},{8,12},{10,14},{12... | collective-permute-start | bytes 786440 | tf_op jit(solution)/shard_map/ppermute | solution.py:425
  112.0 25.4 %collective-permute-start.44 = (bf16[256,1024]{1,0:T(8,128)(2,1)S(1)}, bf16[256,1024]{1,0:T(8,128)(2,1)S(1)}, u32[]{:S(2)}, u32[]{:S(2)}) collective-permute-start(bf16[256,1024]{1,0:T(8,128)(2,1)S(1)} %get-tuple-element.145), channel_id=1, source_target_pairs={{0,16},{16,0},{1,17},{17,1},{2,18},{18,2},{3,19},{19,3},{4,20},{20... | collective-permute-start | bytes 1572872 | tf_op jit(solution)/shard_map/ppermute | solution.py:1153
  114.4 19.2 %collective-permute-start.45 = (bf16[272,512]{1,0:T(8,128)(2,1)S(1)}, bf16[272,512]{1,0:T(8,128)(2,1)S(1)}, u32[]{:S(2)}, u32[]{:S(2)}) collective-permute-start(bf16[272,512]{1,0:T(8,128)(2,1)S(1)} %get-tuple-element.151), channel_id=1, source_target_pairs={{0,1},{1,0},{16,17},{17,16},{2,3},{3,2},{18,19},{19,18},{4,5},{5,4... | collective-permute-start | bytes 835592 | tf_op jit(solution)/shard_map/ppermute | solution.py:430
  115.6 21.7 %collective-permute-start.46 = (bf16[272,512]{1,0:T(8,128)(2,1)S(1)}, bf16[272,512]{1,0:T(8,128)(2,1)S(1)}, u32[]{:S(2)}, u32[]{:S(2)}) collective-permute-start(bf16[272,512]{1,0:T(8,128)(2,1)S(1)} %get-tuple-element.152), channel_id=1, source_target_pairs={{0,16},{1,17},{16,0},{17,1},{2,18},{3,19},{18,2},{19,3},{4,20},{5,... | collective-permute-start | bytes 835592 | tf_op jit(solution)/shard_map/ppermute | solution.py:430
  122.7 14.6 %collective-permute-start.47 = (bf16[272,512]{1,0:T(8,128)(2,1)S(1)}, bf16[272,512]{1,0:T(8,128)(2,1)S(1)}, u32[]{:S(2)}, u32[]{:S(2)}) collective-permute-start(bf16[272,512]{1,0:T(8,128)(2,1)S(1)} %get-tuple-element.153), channel_id=1, source_target_pairs={{0,17},{1,16},{16,1},{17,0},{2,19},{3,18},{18,3},{19,2},{4,21},{5,... | collective-permute-start | bytes 835592 | tf_op jit(solution)/shard_map/ppermute | solution.py:430
  124.5 8.9 %collective-permute-start.40 = (bf16[128,1024]{1,0:T(8,128)(2,1)S(1)}, bf16[128,1024]{1,0:T(8,128)(2,1)S(1)}, u32[]{:S(2)}, u32[]{:S(2)}) collective-permute-start(bf16[128,1024]{1,0:T(8,128)(2,1)S(1)} %get-tuple-element.138), channel_id=1, source_target_pairs={{0,6},{2,4},{4,2},{6,0},{1,7},{3,5},{5,3},{7,1},{8,14},{10,12},{12... | collective-permute-start | bytes 786440 | tf_op jit(solution)/shard_map/ppermute | solution.py:425
  139.2 6.8 %collective-permute-start.41 = (bf16[32,1024]{1,0:T(8,128)(2,1)S(1)}, bf16[32,1024]{1,0:T(8,128)(2,1)S(1)}, u32[]{:S(2)}, u32[]{:S(2)}) collective-permute-start(bf16[32,1024]{1,0:T(8,128)(2,1)S(1)} %get-tuple-element.140), channel_id=1, source_target_pairs={{0,1},{1,0},{16,17},{17,16},{2,3},{3,2},{18,19},{19,18},{4,5},{5,4... | collective-permute-start | bytes 196616 | tf_op jit(solution)/shard_map/ppermute | solution.py:430
  140.7 13.0 %collective-permute-start.49 = (bf16[64,1024]{1,0:T(8,128)(2,1)S(1)}, bf16[64,1024]{1,0:T(8,128)(2,1)S(1)}, u32[]{:S(2)}, u32[]{:S(2)}) collective-permute-start(bf16[64,1024]{1,0:T(8,128)(2,1)S(1)} %get-tuple-element.157), channel_id=1, source_target_pairs={{0,2},{2,0},{4,6},{6,4},{1,3},{3,1},{5,7},{7,5},{8,10},{10,8},{12,... | collective-permute-start | bytes 393224 | tf_op jit(solution)/shard_map/ppermute | solution.py:425
  141.4 12.9 %collective-permute-start.50 = (bf16[64,1024]{1,0:T(8,128)(2,1)S(1)}, bf16[64,1024]{1,0:T(8,128)(2,1)S(1)}, u32[]{:S(2)}, u32[]{:S(2)}) collective-permute-start(bf16[64,1024]{1,0:T(8,128)(2,1)S(1)} %get-tuple-element.158), channel_id=1, source_target_pairs={{0,4},{2,6},{4,0},{6,2},{1,5},{3,7},{5,1},{7,3},{8,12},{10,14},{12... | collective-permute-start | bytes 393224 | tf_op jit(solution)/shard_map/ppermute | solution.py:425
  143.3 11.0 %collective-permute-start.51 = (bf16[64,1024]{1,0:T(8,128)(2,1)S(1)}, bf16[64,1024]{1,0:T(8,128)(2,1)S(1)}, u32[]{:S(2)}, u32[]{:S(2)}) collective-permute-start(bf16[64,1024]{1,0:T(8,128)(2,1)S(1)} %get-tuple-element.159), channel_id=1, source_target_pairs={{0,6},{2,4},{4,2},{6,0},{1,7},{3,5},{5,3},{7,1},{8,14},{10,12},{12... | collective-permute-start | bytes 393224 | tf_op jit(solution)/shard_map/ppermute | solution.py:425
  145.2 4.7 %collective-permute-start.42 = (bf16[32,1024]{1,0:T(8,128)(2,1)S(1)}, bf16[32,1024]{1,0:T(8,128)(2,1)S(1)}, u32[]{:S(2)}, u32[]{:S(2)}) collective-permute-start(bf16[32,1024]{1,0:T(8,128)(2,1)S(1)} %get-tuple-element.141), channel_id=1, source_target_pairs={{0,16},{1,17},{16,0},{17,1},{2,18},{3,19},{18,2},{19,3},{4,20},{5,... | collective-permute-start | bytes 196616 | tf_op jit(solution)/shard_map/ppermute | solution.py:430
  146.0 5.2 %collective-permute-start.43 = (bf16[32,1024]{1,0:T(8,128)(2,1)S(1)}, bf16[32,1024]{1,0:T(8,128)(2,1)S(1)}, u32[]{:S(2)}, u32[]{:S(2)}) collective-permute-start(bf16[32,1024]{1,0:T(8,128)(2,1)S(1)} %get-tuple-element.142), channel_id=1, source_target_pairs={{0,17},{1,16},{16,1},{17,0},{2,19},{3,18},{18,3},{19,2},{4,21},{5,... | collective-permute-start | bytes 196616 | tf_op jit(solution)/shard_map/ppermute | solution.py:430
  (13 other events, 85.2 us)

commit v9 on v8

--- a/solution.py
+++ b/solution.py
@@ -528,7 +528,18 @@
     return (down == lax.broadcasted_iota(jnp.int32, (8, 128), 1)).astype(F32).astype(BF16)
 
 
-def pick_kernel(cap, where, chosen_t, tokens, cot, pick, *refs):
+def as_columns(chosen):
+    numbers = chosen[...]
+    down = lax.broadcasted_iota(jnp.int32, (numbers.shape[0], 128), 0)
+    eye = down == lax.broadcasted_iota(jnp.int32, (numbers.shape[0], 128), 1)
+    eye = eye.astype(F32).astype(BF16)
+    high = mm((numbers >> 8).astype(F32).astype(BF16), eye, TN)
+    low = mm((numbers & 255).astype(F32).astype(BF16), eye, TN)
+    return (high * 256.0 + low).astype(jnp.int32)
+
+
+def pick_kernel(cap, where, chosen, tokens, cot, pick, *refs):
+    chosen_t = as_columns(chosen)
     *outs, rows = refs
     seq_count, seg_len = tokens.shape[:2]
     base = where[4] * seg_len
@@ -584,7 +595,9 @@
     up[members * rows :] = w_down[:, half:]
 
 
-def spread_kernel(dims, where, chosen, chosen_t, spread):
+def spread_kernel(dims, where, chosen, spread, token):
+    chosen_t = as_columns(chosen)
+    token[...] = jnp.zeros_like(token)
     ny, nc, nz, nx, seg_len, cap = dims
     c, z, line = where[0], where[1], where[2]
     routed = chosen_t.shape[0]
@@ -694,7 +707,7 @@
 def attention_kernel(dims, members, where, picked_r, qkv_blocks, *outs):
     ny, nx, rows = dims
     normed_o, w_o, wo_o, vecs_o = outs[:4]
-    joined_o, att_o, exact_o, near_o, far_o = outs[4:]
+    joined_o, att_o, exact_o, probs_o, near_o, far_o = outs[4:]
     heads = ny
     cols = 3 * heads * HDIM
     routed, width = picked_r.shape
@@ -716,6 +729,7 @@
             joined[:, (t * heads + h) * HDIM : (t * heads + h + 1) * HDIM] for t in range(3)
         )
         probs, total = probabilities(queries, keys, kept)
+        probs_o[h] = probs
         parts.append(mm(probs.astype(BF16), values) / total)
     exact = jnp.concatenate(parts, 1)
     exact_o[...] = exact
@@ -827,9 +841,9 @@
 
 
 def attention_back_kernel(members, where, *refs):
-    w_out, joined_r, exact_r, w, vecs, picked_r, logit, d_hidden, spread = refs[:9]
-    blocks = refs[9 : 9 + members]
-    near_o, far_o, d_joined_o, gain_o = refs[9 + members :]
+    w_out, joined_r, exact_r, w, vecs, picked_r, logit, d_hidden, spread, probs_r = refs[:10]
+    blocks = refs[10 : 10 + members]
+    near_o, far_o, d_joined_o, gain_o = refs[10 + members :]
     routed, width = picked_r.shape
     own = routed // members
     heads = joined_r.shape[1] // (3 * HDIM)
@@ -837,13 +851,13 @@
     d_attended = mm(d_branch, w_out[...], NT).astype(BF16)
     joined = joined_r[...]
     exact = exact_r[...]
-    kept = kept_pairs(where[3], routed, own)
     grads = [[], [], []]
     for h in range(heads):
         queries, keys, values = (
             joined[:, (t * heads + h) * HDIM : (t * heads + h + 1) * HDIM] for t in range(3)
         )
-        probs, total = probabilities(queries, keys, kept)
+        probs = probs_r[h]
+        total = jnp.sum(probs, 1, keepdims=True)
         d_att = d_attended[:, h * HDIM : (h + 1) * HDIM]
         d_wide = d_att.astype(F32)
         delta = jnp.sum(d_wide * exact[:, h * HDIM : (h + 1) * HDIM], 1, keepdims=True)
@@ -1026,7 +1040,6 @@
     own = routed // members
     cols, wide = 3 * heads * HDIM, lines * ff_rows
     where = jnp.stack([c, z, line, member, shard]).astype(jnp.int32)
-    chosen_t = chosen.T
     block = (own, width)
     slot_block = (2 * cap, width)
     halves = [((nz, own, width), BF16)] * 2
@@ -1035,20 +1048,20 @@
     pick, *picked_rows = local_call(
         partial(pick_kernel, cap),
         [Far(((seq_count, cap, seg_len), BF16))] + [(slot_block, BF16)] * lines,
-        (where, chosen_t, tokens, cotangent),
+        (where, chosen, tokens, cotangent),
         scratch=[pltpu.VMEM((seq_count, 2 * cap, width), BF16)],
         scalars=1,
     )
     line_slots = picked_rows[:1] + send_lines(picked_rows[1:])
-    (hot,) = local_call(
+    hot, token = local_call(
         partial(spread_kernel, (ny, nc, nz, nx, seg_len, cap)),
-        [Far(((routed, members * lines * cap), BF16))],
-        (where, chosen, chosen_t),
+        [Far(((routed, members * lines * cap), BF16)), ((8, 128), F32)],
+        (where, chosen),
         scalars=1,
     )
     spread = Far(hot)
     (line_slots,) = local_call(
-        partial(stack_kernel, cap), [((2 * lines * cap, width), BF16)], line_slots, after=(hot,)
+        partial(stack_kernel, cap), [((2 * lines * cap, width), BF16)], line_slots, after=(token,)
     )
     slots = gather_group([line_slots])
 
@@ -1080,7 +1093,7 @@
         [((routed, width), BF16), (block, BF16), ((routed, width), BF16)],
         (spread, *shuffle(slots)),
     )
-    normed, full_qkv, full_out, full_vecs, joined, attended, exact, near, far = local_call(
+    normed, full_qkv, full_out, full_vecs, joined, attended, exact, probs, near, far = local_call(
         partial(attention_kernel, (ny, nx, rows), members),
         [
             ((routed, width), BF16),
@@ -1090,6 +1103,7 @@
             ((routed, cols), BF16),
             ((routed, heads * HDIM), BF16),
             ((routed, heads * HDIM), F32),
+            ((heads, routed, routed), F32),
         ]
         + halves,
         (where, picked, Far(first, 0, base, 1)),
@@ -1156,7 +1170,7 @@
         partial(attention_back_kernel, members),
         slot_halves + [((routed, cols), BF16), ((routed, width), BF16)],
         (where, full_out, joined, exact, full_qkv, full_vecs, picked)
-        + (logit, d_hidden, spread, *shuffle(d_branch)),
+        + (logit, d_hidden, spread, probs, *shuffle(d_branch)),
         scalars=1,
     )
     far = send_c(far)

time: 156 us -> 156 us (level)
  waiting for transfers between devices: 65.9 us -> 68.2 us
    ppermute x21, waiting for transfers between devices: 46.4 us -> 49.1 us  [send_z(): lax.ppermute(b, 'z', f)]
    ppermute x21, starting transfers between devices: 27.9 us -> 25.9 us  [send_z(): lax.ppermute(b, 'z', f)]
  transfers between devices with their start and end apart: 54 -> 54, of which waited for: 28 -> 29; matrix products, arithmetic and copies ran while one was open for 0% -> 0% of each run, Pallas kernels for 13% -> 13%
where the time goes in v9:
time: 156 us
  waiting for transfers between devices  68.2 us (44%)
  starting transfers between devices  55.1 us (35%)
  Pallas kernels  31.5 us (20%)
    ppermute x21, waiting for transfers between devices, send_z(): lax.ppermute(b, 'z', f)  49.1 us
    pallas_call x24, Pallas kernels, local_call(): pl.pallas_call(run, out_shape=shapes, in_specs=[pl.BlockSpec(memory_space...  31.5 us
    ppermute x21, starting transfers between devices, send_z(): lax.ppermute(b, 'z', f)  25.9 us
    ppermute x12, starting transfers between devices, send_lines(): lax.ppermute(b, ('y', 'x'), f)  13.3 us
    ppermute x12, waiting for transfers between devices, send_lines(): lax.ppermute(b, ('y', 'x'), f)  12.9 us
    all_to_all x1, starting transfers between devices, grouped(): got_cols = lax.all_to_all(columns, ('c', 'z'), 0, 0, tiled=True)  6.34 us
    all_to_all x1, starting transfers between devices, grouped(): first = lax.all_to_all(first, ('y', 'x'), 0, 0, tiled=True)  4.38 us
    ppermute x17, waiting for transfers between devices, send_c(): return lax.ppermute(block, 'c', flips(2)[1])  3.87 us
  transfers between devices with their start and end apart: 54, of which 29 were waited for; matrix products, arithmetic and copies ran while one was open for 0% of the time, Pallas kernels for 13%

profile of v9, /device:TPU:0, one launch (start us, length us, event | category | flops | bytes accessed | tf_op | source)
XLA Modules:
  0.0 155.9 jit_solution(6639351001528047656)
XLA Ops:
  0.7 2.2 %shard_map.173 = bf16[8,32,1024]{2,1,0:T(8,128)(2,1)} custom-call(bf16[32,3072]{1,0:T(8,128)(2,1)} %refs_0_.1, bf16[32,4096]{1,0:T(8,128)(2,1)} %refs_1_.6, bf16[1,32]{1,0:T(2,128)(2,1)} %bitcast.11, bf16[1,32]{1,0:T(2,128)(2,1)} %bitcast.12, bf16[1,32]{1,0:T(2,128)(2,1)} %bitcast.13), custom_call_target="tpu_custom_call" | custom-call | tf_op jit(solution)/shard_map/pallas_call | solution.py:404
  2.9 6.3 %all-to-all-start = ((bf16[8,32,1024]{2,1,0:T(8,128)(2,1)}), bf16[8,32,1024]{2,1,0:T(8,128)(2,1)S(1)}, u32[]{:S(2)}, u32[]{:S(2)}) async-start(bf16[8,32,1024]{2,1,0:T(8,128)(2,1)} %shard_map.173), calls=%async_computation | async-start | bytes 1048576 | tf_op jit(solution)/shard_map/all_to_all | solution.py:1075
  9.3 1.7 %shard_map.169 = (bf16[4,16,64]{2,1,0:T(8,128)(2,1)}, bf16[32,1024]{1,0:T(8,128)(2,1)S(1)}, bf16[32,1024]{1,0:T(8,128)(2,1)S(1)}, bf16[32,1024]{1,0:T(8,128)(2,1)S(1)}, bf16[32,1024]{1,0:T(8,128)(2,1)S(1)}) custom-call(s32[5]{0:T(128)S(1)} %stack.23.refs_0_, s32[4,256]{1,0:T(4,128)S(1)} %copy-done.5, bf16[4,64,1024]{2,1,0:T(8,128)(2,1)S(1)} %copy-done, ...), custom_call_target="tpu_custom_call" | custom-call | tf_op jit(solution)/shard_map/pallas_call | solution.py:404
  11.1 1.6 collective-permute-start
  12.6 1.5 collective-permute-start.1
  14.6 2.0 %shard_map.170 = (bf16[256,512]{1,0:T(8,128)(2,1)}, f32[8,128]{1,0:T(8,128)S(1)}) custom-call(s32[5]{0:T(128)S(1)} %stack.23.refs_0_, s32[4,256]{1,0:T(4,128)S(1)} %copy-done.5), custom_call_target="tpu_custom_call" | custom-call | tf_op jit(solution)/shard_map/pallas_call | solution.py:404
  16.9 2.4 %collective-permute-done.2.refs_3_ = bf16[32,1024]{1,0:T(8,128)(2,1)S(1)} collective-permute-done((bf16[32,1024]{1,0:T(8,128)(2,1)S(1)}, bf16[32,1024]{1,0:T(8,128)(2,1)S(1)}, u32[]{:S(2)}, u32[]{:S(2)}) %collective-permute-start.2) | collective-permute-done | bytes 65568 | tf_op jit(solution)/shard_map/ppermute | solution.py:430
  19.3 2.1 %collective-permute-start.3 = (bf16[128,1024]{1,0:T(8,128)(2,1)S(1)}, bf16[128,1024]{1,0:T(8,128)(2,1)S(1)}, u32[]{:S(2)}, u32[]{:S(2)}) collective-permute-start(bf16[128,1024]{1,0:T(8,128)(2,1)S(1)} %shard_map.171.refs_1_.refs_3_), channel_id=1, source_target_pairs={{0,2},{2,0},{4,6},{6,4},{1,3},{3,1},{5,7},{7,5},{8,10},{10,8},{12,... | collective-permute-start | bytes 786440 | tf_op jit(solution)/shard_map/ppermute | solution.py:425
  21.4 2.4 %collective-permute-start.4 = (bf16[128,1024]{1,0:T(8,128)(2,1)S(1)}, bf16[128,1024]{1,0:T(8,128)(2,1)S(1)}, u32[]{:S(2)}, u32[]{:S(2)}) collective-permute-start(bf16[128,1024]{1,0:T(8,128)(2,1)S(1)} %shard_map.171.refs_1_.refs_3_), channel_id=1, source_target_pairs={{0,6},{2,4},{4,2},{6,0},{1,7},{3,5},{5,3},{7,1},{8,14},{10,12},{12... | collective-permute-start | bytes 786440 | tf_op jit(solution)/shard_map/ppermute | solution.py:425
  24.2 1.5 shard_map.174
  25.8 4.4 %all-to-all-start.1 = ((bf16[4,400,512]{2,1,0:T(8,128)(2,1)}), bf16[4,400,512]{2,1,0:T(8,128)(2,1)}, u32[]{:S(2)}, u32[]{:S(2)}) async-start(bf16[4,400,512]{2,1,0:T(8,128)(2,1)} %get-tuple-element.99), calls=%async_computation.1 | async-start | bytes 3276800 | tf_op jit(solution)/shard_map/all_to_all | solution.py:1087
  30.9 4.0 %collective-permute-done.3.refs_2_ = bf16[128,1024]{1,0:T(8,128)(2,1)S(1)} collective-permute-done((bf16[128,1024]{1,0:T(8,128)(2,1)S(1)}, bf16[128,1024]{1,0:T(8,128)(2,1)S(1)}, u32[]{:S(2)}, u32[]{:S(2)}) %collective-permute-start.3) | collective-permute-done | bytes 262176 | tf_op jit(solution)/shard_map/ppermute | solution.py:425
  34.9 1.8 %collective-permute-done.4.refs_3_ = bf16[128,1024]{1,0:T(8,128)(2,1)S(1)} collective-permute-done((bf16[128,1024]{1,0:T(8,128)(2,1)S(1)}, bf16[128,1024]{1,0:T(8,128)(2,1)S(1)}, u32[]{:S(2)}, u32[]{:S(2)}) %collective-permute-start.4) | collective-permute-done | bytes 262176 | tf_op jit(solution)/shard_map/ppermute | solution.py:425
  36.7 10.4 %collective-permute-done.5.refs_4_ = bf16[128,1024]{1,0:T(8,128)(2,1)S(1)} collective-permute-done((bf16[128,1024]{1,0:T(8,128)(2,1)S(1)}, bf16[128,1024]{1,0:T(8,128)(2,1)S(1)}, u32[]{:S(2)}, u32[]{:S(2)}) %collective-permute-start.5) | collective-permute-done | bytes 262176 | tf_op jit(solution)/shard_map/ppermute | solution.py:425
  47.1 1.5 collective-permute-done.9.refs_8_
  48.6 1.7 %shard_map.172 = (bf16[256,1024]{1,0:T(8,128)(2,1)S(1)}, bf16[32,1024]{1,0:T(8,128)(2,1)S(1)}, bf16[256,1024]{1,0:T(8,128)(2,1)S(1)}) custom-call(bf16[256,512]{1,0:T(8,128)(2,1)} %get-tuple-element.92.refs_0_.refs_6_.refs_9_, bf16[128,1024]{1,0:T(8,128)(2,1)S(1)} %shard_map.171.refs_1_.refs_3_, bf16[128,1024]{1,0:T(8,128)(2,1)S(1)} %collective-permute-done.3.refs_2_, ...), custom_call_target="tpu_custom_call" | custom-call | flops 10000000000 | tf_op jit(solution)/shard_map/pallas_call | solution.py:404
  51.3 3.2 %shard_map.175 = (bf16[256,1024]{1,0:T(8,128)(2,1)S(1)}, bf16[1024,384]{1,0:T(8,128)(2,1)S(1)}, bf16[128,1024]{1,0:T(8,128)(2,1)S(1)}, f32[8,1024]{1,0:T(8,128)S...) custom-call(s32[5]{0:T(128)S(1)} %stack.23.refs_0_, ...), custom_call_target="tpu_custom_call" | custom-call | flops 1200000000 | tf_op jit(solution)/shard_map/pallas_call | solution.py:404
  54.6 1.5 collective-permute-start.10
  59.2 3.6 %collective-permute-done.14.refs_3_ = bf16[32,1024]{1,0:T(8,128)(2,1)S(1)} collective-permute-done((bf16[32,1024]{1,0:T(8,128)(2,1)S(1)}, bf16[32,1024]{1,0:T(8,128)(2,1)S(1)}, u32[]{:S(2)}, u32[]{:S(2)}) %collective-permute-start.14) | collective-permute-done | bytes 65568 | tf_op jit(solution)/shard_map/ppermute | solution.py:425
  63.0 2.1 %collective-permute-done.15.refs_4_ = bf16[32,1024]{1,0:T(8,128)(2,1)S(1)} collective-permute-done((bf16[32,1024]{1,0:T(8,128)(2,1)S(1)}, bf16[32,1024]{1,0:T(8,128)(2,1)S(1)}, u32[]{:S(2)}, u32[]{:S(2)}) %collective-permute-start.15) | collective-permute-done | bytes 65568 | tf_op jit(solution)/shard_map/ppermute | solution.py:425
  65.1 4.3 %collective-permute-done.16.refs_5_ = bf16[32,1024]{1,0:T(8,128)(2,1)S(1)} collective-permute-done((bf16[32,1024]{1,0:T(8,128)(2,1)S(1)}, bf16[32,1024]{1,0:T(8,128)(2,1)S(1)}, u32[]{:S(2)}, u32[]{:S(2)}) %collective-permute-start.16) | collective-permute-done | bytes 65568 | tf_op jit(solution)/shard_map/ppermute | solution.py:425
  69.6 3.4 %collective-permute-start.19 = (bf16[32,1024]{1,0:T(8,128)(2,1)S(1)}, bf16[32,1024]{1,0:T(8,128)(2,1)S(1)}, u32[]{:S(2)}, u32[]{:S(2)}) collective-permute-start(bf16[32,1024]{1,0:T(8,128)(2,1)S(1)} %get-tuple-element.111.refs_6_.refs_4_), channel_id=1, source_target_pairs={{0,4},{2,6},{4,0},{6,2},{1,5},{3,7},{5,1},{7,3},{8,12},{10,14},{12... | collective-permute-start | bytes 196616 | tf_op jit(solution)/shard_map/ppermute | solution.py:425
  73.0 2.7 %collective-permute-done.11.refs_6_.refs_4_ = bf16[384,512]{1,0:T(8,128)(2,1)S(1)} collective-permute-done((bf16[384,512]{1,0:T(8,128)(2,1)S(1)}, bf16[384,512]{1,0:T(8,128)(2,1)S(1)}, u32[]{:S(2)}, u32[]{:S(2)}) %collective-permute-start.11) | collective-permute-done | bytes 393248 | tf_op jit(solution)/shard_map/ppermute | solution.py:430
  77.4 2.2 %shard_map.176 = (f32[256,1]{1,0:T(8,128)S(1)}, bf16[32,1024]{1,0:T(8,128)(2,1)S(1)}, bf16[256,1024]{1,0:T(8,128)(2,1)S(1)}, f32[256,512]{1,0:T(8,128)S(1)}, bf16[512,1024]{1,0:T(8,128)(2,1)S(1)}) custom-call(s32[5]{0:T(128)S(1)} %stack.23.refs_0_, bf16[256,1024]{1,0:T(8,128)(2,1)S(1)} %get-tuple-element.98.refs_1_.refs_6_, ...), custom_call_target="tpu_custom_call" | custom-call | flops 800000000 | tf_op jit(solution)/shard_map/pallas_call | solution.py:404
  79.7 1.6 %shard_map.179 = (bf16[256,512]{1,0:T(8,128)(2,1)S(1)}, bf16[256,512]{1,0:T(8,128)(2,1)S(1)}, bf16[4,32,1024]{2,1,0:T(8,128)(2,1)S(1)}, bf16[4,32,1024]{2,1,0:T(8,128)(2,1)S(1)}) custom-call(s32[5]{0:T(128)S(1)} %stack.23.refs_0_, f32[256,512]{1,0:T(8,128)S(1)} %get-tuple-element.103.refs_1_, bf16[384,512]{1,0:T(8,128)(2,1)S(1)} %copy-done.2, ...), custom_call_target="tpu_custom_call" | custom-call | flops 600000000 | tf_op jit(solution)/shard_map/pallas_call | solution.py:404
  83.2 1.5 collective-permute-start.37
  84.9 2.5 %collective-permute-start.27 = (bf16[32,1024]{1,0:T(8,128)(2,1)S(1)}, bf16[32,1024]{1,0:T(8,128)(2,1)S(1)}, u32[]{:S(2)}, u32[]{:S(2)}) collective-permute-start(bf16[32,1024]{1,0:T(8,128)(2,1)S(1)} %get-tuple-element.129), channel_id=1, source_target_pairs={{0,4},{2,6},{4,0},{6,2},{1,5},{3,7},{5,1},{7,3},{8,12},{10,14},{12... | collective-permute-start | bytes 196616 | tf_op jit(solution)/shard_map/ppermute | solution.py:425
  87.4 1.9 %collective-permute-start.28 = (bf16[32,1024]{1,0:T(8,128)(2,1)S(1)}, bf16[32,1024]{1,0:T(8,128)(2,1)S(1)}, u32[]{:S(2)}, u32[]{:S(2)}) collective-permute-start(bf16[32,1024]{1,0:T(8,128)(2,1)S(1)} %get-tuple-element.130), channel_id=1, source_target_pairs={{0,6},{2,4},{4,2},{6,0},{1,7},{3,5},{5,3},{7,1},{8,14},{10,12},{12... | collective-permute-start | bytes 196616 | tf_op jit(solution)/shard_map/ppermute | solution.py:425
  89.2 1.4 shard_map.180
  90.7 1.8 %collective-permute-done.27.refs_6_ = bf16[32,1024]{1,0:T(8,128)(2,1)S(1)} collective-permute-done((bf16[32,1024]{1,0:T(8,128)(2,1)S(1)}, bf16[32,1024]{1,0:T(8,128)(2,1)S(1)}, u32[]{:S(2)}, u32[]{:S(2)}) %collective-permute-start.27) | collective-permute-done | bytes 65568 | tf_op jit(solution)/shard_map/ppermute | solution.py:425
  94.7 1.9 %collective-permute-start.30 = (bf16[32,1024]{1,0:T(8,128)(2,1)S(1)}, bf16[32,1024]{1,0:T(8,128)(2,1)S(1)}, u32[]{:S(2)}, u32[]{:S(2)}) collective-permute-start(bf16[32,1024]{1,0:T(8,128)(2,1)S(1)} %get-tuple-element.136.refs_11_.refs_8_), channel_id=1, source_target_pairs={{0,6},{2,4},{4,2},{6,0},{1,7},{3,5},{5,3},{7,1},{8,14},{10,12},{12... | collective-permute-start | bytes 196616 | tf_op jit(solution)/shard_map/ppermute | solution.py:425
  97.2 1.6 %collective-permute-done.29.refs_12_.refs_9_ = bf16[32,1024]{1,0:T(8,128)(2,1)S(1)} collective-permute-done((bf16[32,1024]{1,0:T(8,128)(2,1)S(1)}, bf16[32,1024]{1,0:T(8,128)(2,1)S(1)}, u32[]{:S(2)}, u32[]{:S(2)}) %collective-permute-start.29) | collective-permute-done | bytes 65568 | tf_op jit(solution)/shard_map/ppermute | solution.py:425
  98.8 2.0 %collective-permute-done.30.refs_13_.refs_10_ = bf16[32,1024]{1,0:T(8,128)(2,1)S(1)} collective-permute-done((bf16[32,1024]{1,0:T(8,128)(2,1)S(1)}, bf16[32,1024]{1,0:T(8,128)(2,1)S(1)}, u32[]{:S(2)}, u32[]{:S(2)}) %collective-permute-start.30) | collective-permute-done | bytes 65568 | tf_op jit(solution)/shard_map/ppermute | solution.py:425
  100.8 1.4 collective-permute-done.31.refs_14_.refs_11_
  103.5 3.8 %shard_map.184 = (bf16[4,64,1024]{2,1,0:T(8,128)(2,1)S(1)}, bf16[4,64,1024]{2,1,0:T(8,128)(2,1)S(1)}, bf16[256,384]{1,0:T(8,128)(2,1)S(1)}, bf16[256,1024]{1,0:T(8,128)(2,1)S(1)}) custom-call(s32[5]{0:T(128)S(1)} %stack.23.refs_0_, bf16[128,1024]{1,0:T(8,128)(2,1)S(1)} %get-tuple-element.115.refs_3_.refs_1_, ...), custom_call_target="tpu_custom_call" | custom-call | flops 1200000000 | tf_op jit(solution)/shard_map/pallas_call | solution.py:404
  109.6 2.4 %collective-permute-start.39 = (bf16[128,1024]{1,0:T(8,128)(2,1)S(1)}, bf16[128,1024]{1,0:T(8,128)(2,1)S(1)}, u32[]{:S(2)}, u32[]{:S(2)}) collective-permute-start(bf16[128,1024]{1,0:T(8,128)(2,1)S(1)} %get-tuple-element.143), channel_id=1, source_target_pairs={{0,4},{2,6},{4,0},{6,2},{1,5},{3,7},{5,1},{7,3},{8,12},{10,14},{12... | collective-permute-start | bytes 786440 | tf_op jit(solution)/shard_map/ppermute | solution.py:425
  112.9 1.5 shard_map.189
  116.5 6.3 %collective-permute-done.38.refs_1_ = bf16[128,1024]{1,0:T(8,128)(2,1)S(1)} collective-permute-done((bf16[128,1024]{1,0:T(8,128)(2,1)S(1)}, bf16[128,1024]{1,0:T(8,128)(2,1)S(1)}, u32[]{:S(2)}, u32[]{:S(2)}) %collective-permute-start.38) | collective-permute-done | bytes 262176 | tf_op jit(solution)/shard_map/ppermute | solution.py:425
  122.8 1.5 collective-permute-start.47
  124.6 1.9 %collective-permute-start.40 = (bf16[128,1024]{1,0:T(8,128)(2,1)S(1)}, bf16[128,1024]{1,0:T(8,128)(2,1)S(1)}, u32[]{:S(2)}, u32[]{:S(2)}) collective-permute-start(bf16[128,1024]{1,0:T(8,128)(2,1)S(1)} %get-tuple-element.144), channel_id=1, source_target_pairs={{0,6},{2,4},{4,2},{6,0},{1,7},{3,5},{5,3},{7,1},{8,14},{10,12},{12... | collective-permute-start | bytes 786440 | tf_op jit(solution)/shard_map/ppermute | solution.py:425
  126.4 7.0 %collective-permute-done.40.refs_3_ = bf16[128,1024]{1,0:T(8,128)(2,1)S(1)} collective-permute-done((bf16[128,1024]{1,0:T(8,128)(2,1)S(1)}, bf16[128,1024]{1,0:T(8,128)(2,1)S(1)}, u32[]{:S(2)}, u32[]{:S(2)}) %collective-permute-start.40) | collective-permute-done | bytes 262176 | tf_op jit(solution)/shard_map/ppermute | solution.py:425
  133.6 3.8 %collective-permute-done.46.refs_5_ = bf16[272,512]{1,0:T(8,128)(2,1)S(1)} collective-permute-done((bf16[272,512]{1,0:T(8,128)(2,1)S(1)}, bf16[272,512]{1,0:T(8,128)(2,1)S(1)}, u32[]{:S(2)}, u32[]{:S(2)}) %collective-permute-start.46) | collective-permute-done | bytes 278560 | tf_op jit(solution)/shard_map/ppermute | solution.py:430
  137.4 1.8 %shard_map.190 = (bf16[4,32,1024]{2,1,0:T(8,128)(2,1)S(1)}, bf16[4,32,1024]{2,1,0:T(8,128)(2,1)S(1)}, f32[32,1024]{1,0:T(8,128)}, f32[128,1024]{1,0:T(8,128)}) custom-call(s32[5]{0:T(128)S(1)} %stack.23.refs_0_, f32[256,1024]{1,0:T(8,128)S(1)} %get-tuple-element.140.refs_4_.refs_1_, bf16[256,1024]{1,0:T(8,128)(2,1)S(1)} %collective-permute-done.44.refs_2_, ...), custom_call_target="tpu_custom_call" | custom-call | tf_op jit(solution)/shard_map/pallas_call | solution.py:404
  141.4 1.9 %collective-permute-start.50 = (bf16[64,1024]{1,0:T(8,128)(2,1)S(1)}, bf16[64,1024]{1,0:T(8,128)(2,1)S(1)}, u32[]{:S(2)}, u32[]{:S(2)}) collective-permute-start(bf16[64,1024]{1,0:T(8,128)(2,1)S(1)} %get-tuple-element.164), channel_id=1, source_target_pairs={{0,4},{2,6},{4,0},{6,2},{1,5},{3,7},{5,1},{7,3},{8,12},{10,14},{12... | collective-permute-start | bytes 393224 | tf_op jit(solution)/shard_map/ppermute | solution.py:425
  143.4 1.9 %collective-permute-start.51 = (bf16[64,1024]{1,0:T(8,128)(2,1)S(1)}, bf16[64,1024]{1,0:T(8,128)(2,1)S(1)}, u32[]{:S(2)}, u32[]{:S(2)}) collective-permute-start(bf16[64,1024]{1,0:T(8,128)(2,1)S(1)} %get-tuple-element.165), channel_id=1, source_target_pairs={{0,6},{2,4},{4,2},{6,0},{1,7},{3,5},{5,3},{7,1},{8,14},{10,12},{12... | collective-permute-start | bytes 393224 | tf_op jit(solution)/shard_map/ppermute | solution.py:425
  147.3 2.5 %collective-permute-done.42.refs_6_ = bf16[32,1024]{1,0:T(8,128)(2,1)S(1)} collective-permute-done((bf16[32,1024]{1,0:T(8,128)(2,1)S(1)}, bf16[32,1024]{1,0:T(8,128)(2,1)S(1)}, u32[]{:S(2)}, u32[]{:S(2)}) %collective-permute-start.42) | collective-permute-done | bytes 65568 | tf_op jit(solution)/shard_map/ppermute | solution.py:430
  151.1 2.7 %shard_map.188 = (bf16[4,64,1024]{2,1,0:T(8,128)(2,1)}, bf16[4,64,1024]{2,1,0:T(8,128)(2,1)}) custom-call(s32[5]{0:T(128)S(1)} %stack.23.refs_0_, bf16[4,16,64]{2,1,0:T(8,128)(2,1)} %get-tuple-element.91.refs_1_, bf16[4,64,1024]{2,1,0:T(8,128)(2,1)S(1)} %copy-done, bf16[4,64,1024]{2,1,0:T(8,128)(2,1)S(1)} %copy-done.1, ...), custom_call_target="tpu_custom_call" | custom-call | tf_op jit(solution)/shard_map/pallas_call | solution.py:404
  154.3 1.6 %shard_map.192 = (f32[32,3072]{1,0:T(8,128)}, f32[32,4096]{1,0:T(8,128)}, f32[1,32]{1,0:T(1,128)}, f32[1,32]{1,0:T(1,128)}, f32[1,32]{1,0:T(1,128)}) custom-call(s32[5]{0:T(128)S(1)} %stack.23.refs_0_, bf16[64,1024]{1,0:T(8,128)(2,1)S(1)} %get-tuple-element.162.refs_1_, bf16[64,1024]{1,0:T(8,128)(2,1)S(1)} %collective-permute-done.49.refs_2_, ...), custom_call_target="tpu_custom_call" | custom-call | tf_op jit(solution)/shard_map/pallas_call | solution.py:404
  (97 shorter events, 26.1 us)
Async XLA Ops:
  2.9 21.3 %all-to-all-start = ((bf16[8,32,1024]{2,1,0:T(8,128)(2,1)}), bf16[8,32,1024]{2,1,0:T(8,128)(2,1)S(1)}, u32[]{:S(2)}, u32[]{:S(2)}) async-start(bf16[8,32,1024]{2,1,0:T(8,128)(2,1)} %shard_map.173), calls=%async_computation | async-start | bytes 1048576 | tf_op jit(solution)/shard_map/all_to_all | solution.py:1075
  11.1 5.6 %collective-permute-start = (bf16[32,1024]{1,0:T(8,128)(2,1)S(1)}, bf16[32,1024]{1,0:T(8,128)(2,1)S(1)}, u32[]{:S(2)}, u32[]{:S(2)}) collective-permute-start(bf16[32,1024]{1,0:T(8,128)(2,1)S(1)} %get-tuple-element.94), channel_id=1, source_target_pairs={{0,1},{1,0},{16,17},{17,16},{2,3},{3,2},{18,19},{19,18},{4,5},{5,4... | collective-permute-start | bytes 196616 | tf_op jit(solution)/shard_map/ppermute | solution.py:430
  12.6 4.3 %collective-permute-start.1 = (bf16[32,1024]{1,0:T(8,128)(2,1)S(1)}, bf16[32,1024]{1,0:T(8,128)(2,1)S(1)}, u32[]{:S(2)}, u32[]{:S(2)}) collective-permute-start(bf16[32,1024]{1,0:T(8,128)(2,1)S(1)} %get-tuple-element.95), channel_id=1, source_target_pairs={{0,16},{1,17},{16,0},{17,1},{2,18},{3,19},{18,2},{19,3},{4,20},{5,... | collective-permute-start | bytes 196616 | tf_op jit(solution)/shard_map/ppermute | solution.py:430
  14.1 5.2 %collective-permute-start.2 = (bf16[32,1024]{1,0:T(8,128)(2,1)S(1)}, bf16[32,1024]{1,0:T(8,128)(2,1)S(1)}, u32[]{:S(2)}, u32[]{:S(2)}) collective-permute-start(bf16[32,1024]{1,0:T(8,128)(2,1)S(1)} %get-tuple-element.96), channel_id=1, source_target_pairs={{0,17},{1,16},{16,1},{17,0},{2,19},{3,18},{18,3},{19,2},{4,21},{5,... | collective-permute-start | bytes 196616 | tf_op jit(solution)/shard_map/ppermute | solution.py:430
  19.3 15.6 %collective-permute-start.3 = (bf16[128,1024]{1,0:T(8,128)(2,1)S(1)}, bf16[128,1024]{1,0:T(8,128)(2,1)S(1)}, u32[]{:S(2)}, u32[]{:S(2)}) collective-permute-start(bf16[128,1024]{1,0:T(8,128)(2,1)S(1)} %shard_map.171.refs_1_.refs_3_), channel_id=1, source_target_pairs={{0,2},{2,0},{4,6},{6,4},{1,3},{3,1},{5,7},{7,5},{8,10},{10,8},{12,... | collective-permute-start | bytes 786440 | tf_op jit(solution)/shard_map/ppermute | solution.py:425
  21.4 15.3 %collective-permute-start.4 = (bf16[128,1024]{1,0:T(8,128)(2,1)S(1)}, bf16[128,1024]{1,0:T(8,128)(2,1)S(1)}, u32[]{:S(2)}, u32[]{:S(2)}) collective-permute-start(bf16[128,1024]{1,0:T(8,128)(2,1)S(1)} %shard_map.171.refs_1_.refs_3_), channel_id=1, source_target_pairs={{0,6},{2,4},{4,2},{6,0},{1,7},{3,5},{5,3},{7,1},{8,14},{10,12},{12... | collective-permute-start | bytes 786440 | tf_op jit(solution)/shard_map/ppermute | solution.py:425
  23.8 23.3 %collective-permute-start.5 = (bf16[128,1024]{1,0:T(8,128)(2,1)S(1)}, bf16[128,1024]{1,0:T(8,128)(2,1)S(1)}, u32[]{:S(2)}, u32[]{:S(2)}) collective-permute-start(bf16[128,1024]{1,0:T(8,128)(2,1)S(1)} %shard_map.171.refs_1_.refs_3_), channel_id=1, source_target_pairs={{0,4},{2,6},{4,0},{6,2},{1,5},{3,7},{5,1},{7,3},{8,12},{10,14},{12... | collective-permute-start | bytes 786440 | tf_op jit(solution)/shard_map/ppermute | solution.py:425
  25.8 25.6 %all-to-all-start.1 = ((bf16[4,400,512]{2,1,0:T(8,128)(2,1)}), bf16[4,400,512]{2,1,0:T(8,128)(2,1)}, u32[]{:S(2)}, u32[]{:S(2)}) async-start(bf16[4,400,512]{2,1,0:T(8,128)(2,1)} %get-tuple-element.99), calls=%async_computation.1 | async-start | bytes 3276800 | tf_op jit(solution)/shard_map/all_to_all | solution.py:1087
  30.1 17.0 %collective-permute-start.6 = (bf16[128,1024]{1,0:T(8,128)(2,1)S(1)}, bf16[128,1024]{1,0:T(8,128)(2,1)S(1)}, u32[]{:S(2)}, u32[]{:S(2)}) collective-permute-start(bf16[128,1024]{1,0:T(8,128)(2,1)S(1)} %shard_map.171.refs_1_.refs_3_), channel_id=1, source_target_pairs={{0,8},{8,0},{1,9},{9,1},{2,10},{10,2},{3,11},{11,3},{4,12},{12,4},... | collective-permute-start | bytes 786440 | tf_op jit(solution)/shard_map/ppermute | solution.py:438
  34.9 12.2 %collective-permute-start.7 = (bf16[128,1024]{1,0:T(8,128)(2,1)S(1)}, bf16[128,1024]{1,0:T(8,128)(2,1)S(1)}, u32[]{:S(2)}, u32[]{:S(2)}) collective-permute-start(bf16[128,1024]{1,0:T(8,128)(2,1)S(1)} %collective-permute-done.3.refs_2_), channel_id=1, source_target_pairs={{0,8},{8,0},{1,9},{9,1},{2,10},{10,2},{3,11},{11,3},{4,12},{12,4},... | collective-permute-start | bytes 786440 | tf_op jit(solution)/shard_map/ppermute | solution.py:438
  36.7 10.4 %collective-permute-start.8 = (bf16[128,1024]{1,0:T(8,128)(2,1)S(1)}, bf16[128,1024]{1,0:T(8,128)(2,1)S(1)}, u32[]{:S(2)}, u32[]{:S(2)}) collective-permute-start(bf16[128,1024]{1,0:T(8,128)(2,1)S(1)} %collective-permute-done.4.refs_3_), channel_id=1, source_target_pairs={{0,8},{8,0},{1,9},{9,1},{2,10},{10,2},{3,11},{11,3},{4,12},{12,4},... | collective-permute-start | bytes 786440 | tf_op jit(solution)/shard_map/ppermute | solution.py:438
  54.5 3.6 %collective-permute-start.13 = (bf16[4,32,1024]{2,1,0:T(8,128)(2,1)S(1)}, bf16[4,32,1024]{2,1,0:T(8,128)(2,1)S(1)}, u32[]{:S(2)}, u32[]{:S(2)}) collective-permute-start(bf16[4,32,1024]{2,1,0:T(8,128)(2,1)S(1)} %get-tuple-element.106), channel_id=1, source_target_pairs={{0,8},{8,0},{1,9},{9,1},{2,10},{10,2},{3,11},{11,3},{4,12},{12,4},... | collective-permute-start | bytes 786440 | tf_op jit(solution)/shard_map/ppermute | solution.py:438
  54.6 15.0 %collective-permute-start.10 = (bf16[384,512]{1,0:T(8,128)(2,1)S(1)}, bf16[384,512]{1,0:T(8,128)(2,1)S(1)}, u32[]{:S(2)}, u32[]{:S(2)}) collective-permute-start(bf16[384,512]{1,0:T(8,128)(2,1)S(1)} %copy-done.2), channel_id=1, source_target_pairs={{0,1},{1,0},{16,17},{17,16},{2,3},{3,2},{18,19},{19,18},{4,5},{5,4... | collective-permute-start | bytes 1179656 | tf_op jit(solution)/shard_map/ppermute | solution.py:430
  56.1 19.6 %collective-permute-start.11 = (bf16[384,512]{1,0:T(8,128)(2,1)S(1)}, bf16[384,512]{1,0:T(8,128)(2,1)S(1)}, u32[]{:S(2)}, u32[]{:S(2)}) collective-permute-start(bf16[384,512]{1,0:T(8,128)(2,1)S(1)} %copy-done.2), channel_id=1, source_target_pairs={{0,16},{1,17},{16,0},{17,1},{2,18},{3,19},{18,2},{19,3},{4,20},{5,... | collective-permute-start | bytes 1179656 | tf_op jit(solution)/shard_map/ppermute | solution.py:430
  56.8 20.6 %collective-permute-start.12 = (bf16[384,512]{1,0:T(8,128)(2,1)S(1)}, bf16[384,512]{1,0:T(8,128)(2,1)S(1)}, u32[]{:S(2)}, u32[]{:S(2)}) collective-permute-start(bf16[384,512]{1,0:T(8,128)(2,1)S(1)} %copy-done.2), channel_id=1, source_target_pairs={{0,17},{1,16},{16,1},{17,0},{2,19},{3,18},{18,3},{19,2},{4,21},{5,... | collective-permute-start | bytes 1179656 | tf_op jit(solution)/shard_map/ppermute | solution.py:430
  58.2 4.6 %collective-permute-start.14 = (bf16[32,1024]{1,0:T(8,128)(2,1)S(1)}, bf16[32,1024]{1,0:T(8,128)(2,1)S(1)}, u32[]{:S(2)}, u32[]{:S(2)}) collective-permute-start(bf16[32,1024]{1,0:T(8,128)(2,1)S(1)} %get-tuple-element.108), channel_id=1, source_target_pairs={{0,2},{2,0},{4,6},{6,4},{1,3},{3,1},{5,7},{7,5},{8,10},{10,8},{12,... | collective-permute-start | bytes 196616 | tf_op jit(solution)/shard_map/ppermute | solution.py:425
  58.3 6.8 %collective-permute-start.15 = (bf16[32,1024]{1,0:T(8,128)(2,1)S(1)}, bf16[32,1024]{1,0:T(8,128)(2,1)S(1)}, u32[]{:S(2)}, u32[]{:S(2)}) collective-permute-start(bf16[32,1024]{1,0:T(8,128)(2,1)S(1)} %get-tuple-element.109), channel_id=1, source_target_pairs={{0,4},{2,6},{4,0},{6,2},{1,5},{3,7},{5,1},{7,3},{8,12},{10,14},{12... | collective-permute-start | bytes 196616 | tf_op jit(solution)/shard_map/ppermute | solution.py:425
  62.9 6.5 %collective-permute-start.16 = (bf16[32,1024]{1,0:T(8,128)(2,1)S(1)}, bf16[32,1024]{1,0:T(8,128)(2,1)S(1)}, u32[]{:S(2)}, u32[]{:S(2)}) collective-permute-start(bf16[32,1024]{1,0:T(8,128)(2,1)S(1)} %get-tuple-element.110), channel_id=1, source_target_pairs={{0,6},{2,4},{4,2},{6,0},{1,7},{3,5},{5,3},{7,1},{8,14},{10,12},{12... | collective-permute-start | bytes 196616 | tf_op jit(solution)/shard_map/ppermute | solution.py:425
  69.5 6.2 %collective-permute-start.17 = (bf16[32,1024]{1,0:T(8,128)(2,1)S(1)}, bf16[32,1024]{1,0:T(8,128)(2,1)S(1)}, u32[]{:S(2)}, u32[]{:S(2)}) collective-permute-start(bf16[32,1024]{1,0:T(8,128)(2,1)S(1)} %get-tuple-element.111.refs_6_.refs_4_), channel_id=1, source_target_pairs={{0,2},{2,0},{4,6},{6,4},{1,3},{3,1},{5,7},{7,5},{8,10},{10,8},{12,... | collective-permute-start | bytes 196616 | tf_op jit(solution)/shard_map/ppermute | solution.py:425
  69.6 6.7 %collective-permute-start.18 = (bf16[32,1024]{1,0:T(8,128)(2,1)S(1)}, bf16[32,1024]{1,0:T(8,128)(2,1)S(1)}, u32[]{:S(2)}, u32[]{:S(2)}) collective-permute-start(bf16[32,1024]{1,0:T(8,128)(2,1)S(1)} %get-tuple-element.111.refs_6_.refs_4_), channel_id=1, source_target_pairs={{0,6},{2,4},{4,2},{6,0},{1,7},{3,5},{5,3},{7,1},{8,14},{10,12},{12... | collective-permute-start | bytes 196616 | tf_op jit(solution)/shard_map/ppermute | solution.py:425
  69.6 7.7 %collective-permute-start.19 = (bf16[32,1024]{1,0:T(8,128)(2,1)S(1)}, bf16[32,1024]{1,0:T(8,128)(2,1)S(1)}, u32[]{:S(2)}, u32[]{:S(2)}) collective-permute-start(bf16[32,1024]{1,0:T(8,128)(2,1)S(1)} %get-tuple-element.111.refs_6_.refs_4_), channel_id=1, source_target_pairs={{0,4},{2,6},{4,0},{6,2},{1,5},{3,7},{5,1},{7,3},{8,12},{10,14},{12... | collective-permute-start | bytes 196616 | tf_op jit(solution)/shard_map/ppermute | solution.py:425
  75.7 3.9 %collective-permute-start.20 = (bf16[32,1024]{1,0:T(8,128)(2,1)S(1)}, bf16[32,1024]{1,0:T(8,128)(2,1)S(1)}, u32[]{:S(2)}, u32[]{:S(2)}) collective-permute-start(bf16[32,1024]{1,0:T(8,128)(2,1)S(1)} %get-tuple-element.111.refs_6_.refs_4_), channel_id=1, source_target_pairs={{0,8},{8,0},{1,9},{9,1},{2,10},{10,2},{3,11},{11,3},{4,12},{12,4},... | collective-permute-start | bytes 196616 | tf_op jit(solution)/shard_map/ppermute | solution.py:438
  75.7 3.9 %collective-permute-start.21 = (bf16[32,1024]{1,0:T(8,128)(2,1)S(1)}, bf16[32,1024]{1,0:T(8,128)(2,1)S(1)}, u32[]{:S(2)}, u32[]{:S(2)}) collective-permute-start(bf16[32,1024]{1,0:T(8,128)(2,1)S(1)} %collective-permute-done.17.refs_7_.refs_5_), channel_id=1, source_target_pairs={{0,8},{8,0},{1,9},{9,1},{2,10},{10,2},{3,11},{11,3},{4,12},{12,4},... | collective-permute-start | bytes 196616 | tf_op jit(solution)/shard_map/ppermute | solution.py:438
  76.2 3.4 %collective-permute-start.22 = (bf16[32,1024]{1,0:T(8,128)(2,1)S(1)}, bf16[32,1024]{1,0:T(8,128)(2,1)S(1)}, u32[]{:S(2)}, u32[]{:S(2)}) collective-permute-start(bf16[32,1024]{1,0:T(8,128)(2,1)S(1)} %collective-permute-done.18.refs_8_.refs_6_), channel_id=1, source_target_pairs={{0,8},{8,0},{1,9},{9,1},{2,10},{10,2},{3,11},{11,3},{4,12},{12,4},... | collective-permute-start | bytes 196616 | tf_op jit(solution)/shard_map/ppermute | solution.py:438
  81.3 3.5 %collective-permute-start.25 = (bf16[4,32,1024]{2,1,0:T(8,128)(2,1)S(1)}, bf16[4,32,1024]{2,1,0:T(8,128)(2,1)S(1)}, u32[]{:S(2)}, u32[]{:S(2)}) collective-permute-start(bf16[4,32,1024]{2,1,0:T(8,128)(2,1)S(1)} %get-tuple-element.126), channel_id=1, source_target_pairs={{0,8},{8,0},{1,9},{9,1},{2,10},{10,2},{3,11},{11,3},{4,12},{12,4},... | collective-permute-start | bytes 786440 | tf_op jit(solution)/shard_map/ppermute | solution.py:438
  83.2 25.1 %collective-permute-start.37 = (bf16[512,1024]{1,0:T(8,128)(2,1)S(1)}, bf16[512,1024]{1,0:T(8,128)(2,1)S(1)}, u32[]{:S(2)}, u32[]{:S(2)}) collective-permute-start(bf16[512,1024]{1,0:T(8,128)(2,1)S(1)} %get-tuple-element.133.refs_8_), channel_id=1, source_target_pairs={{0,1},{1,0},{2,3},{3,2},{4,5},{5,4},{6,7},{7,6},{8,9},{9,8},{10,11... | collective-permute-start | bytes 3145736 | tf_op jit(solution)/shard_map/ppermute | solution.py:1148
  84.8 5.9 %collective-permute-start.26 = (bf16[32,1024]{1,0:T(8,128)(2,1)S(1)}, bf16[32,1024]{1,0:T(8,128)(2,1)S(1)}, u32[]{:S(2)}, u32[]{:S(2)}) collective-permute-start(bf16[32,1024]{1,0:T(8,128)(2,1)S(1)} %get-tuple-element.128), channel_id=1, source_target_pairs={{0,2},{2,0},{4,6},{6,4},{1,3},{3,1},{5,7},{7,5},{8,10},{10,8},{12,... | collective-permute-start | bytes 196616 | tf_op jit(solution)/shard_map/ppermute | solution.py:425
  84.9 7.7 %collective-permute-start.27 = (bf16[32,1024]{1,0:T(8,128)(2,1)S(1)}, bf16[32,1024]{1,0:T(8,128)(2,1)S(1)}, u32[]{:S(2)}, u32[]{:S(2)}) collective-permute-start(bf16[32,1024]{1,0:T(8,128)(2,1)S(1)} %get-tuple-element.129), channel_id=1, source_target_pairs={{0,4},{2,6},{4,0},{6,2},{1,5},{3,7},{5,1},{7,3},{8,12},{10,14},{12... | collective-permute-start | bytes 196616 | tf_op jit(solution)/shard_map/ppermute | solution.py:425
  87.4 6.1 %collective-permute-start.28 = (bf16[32,1024]{1,0:T(8,128)(2,1)S(1)}, bf16[32,1024]{1,0:T(8,128)(2,1)S(1)}, u32[]{:S(2)}, u32[]{:S(2)}) collective-permute-start(bf16[32,1024]{1,0:T(8,128)(2,1)S(1)} %get-tuple-element.130), channel_id=1, source_target_pairs={{0,6},{2,4},{4,2},{6,0},{1,7},{3,5},{5,3},{7,1},{8,14},{10,12},{12... | collective-permute-start | bytes 196616 | tf_op jit(solution)/shard_map/ppermute | solution.py:425
  93.6 5.1 %collective-permute-start.29 = (bf16[32,1024]{1,0:T(8,128)(2,1)S(1)}, bf16[32,1024]{1,0:T(8,128)(2,1)S(1)}, u32[]{:S(2)}, u32[]{:S(2)}) collective-permute-start(bf16[32,1024]{1,0:T(8,128)(2,1)S(1)} %get-tuple-element.136.refs_11_.refs_8_), channel_id=1, source_target_pairs={{0,2},{2,0},{4,6},{6,4},{1,3},{3,1},{5,7},{7,5},{8,10},{10,8},{12,... | collective-permute-start | bytes 196616 | tf_op jit(solution)/shard_map/ppermute | solution.py:425
  94.7 6.1 %collective-permute-start.30 = (bf16[32,1024]{1,0:T(8,128)(2,1)S(1)}, bf16[32,1024]{1,0:T(8,128)(2,1)S(1)}, u32[]{:S(2)}, u32[]{:S(2)}) collective-permute-start(bf16[32,1024]{1,0:T(8,128)(2,1)S(1)} %get-tuple-element.136.refs_11_.refs_8_), channel_id=1, source_target_pairs={{0,6},{2,4},{4,2},{6,0},{1,7},{3,5},{5,3},{7,1},{8,14},{10,12},{12... | collective-permute-start | bytes 196616 | tf_op jit(solution)/shard_map/ppermute | solution.py:425
  96.6 5.6 %collective-permute-start.31 = (bf16[32,1024]{1,0:T(8,128)(2,1)S(1)}, bf16[32,1024]{1,0:T(8,128)(2,1)S(1)}, u32[]{:S(2)}, u32[]{:S(2)}) collective-permute-start(bf16[32,1024]{1,0:T(8,128)(2,1)S(1)} %get-tuple-element.136.refs_11_.refs_8_), channel_id=1, source_target_pairs={{0,4},{2,6},{4,0},{6,2},{1,5},{3,7},{5,1},{7,3},{8,12},{10,14},{12... | collective-permute-start | bytes 196616 | tf_op jit(solution)/shard_map/ppermute | solution.py:425
  97.2 5.0 %collective-permute-start.32 = (bf16[32,1024]{1,0:T(8,128)(2,1)S(1)}, bf16[32,1024]{1,0:T(8,128)(2,1)S(1)}, u32[]{:S(2)}, u32[]{:S(2)}) collective-permute-start(bf16[32,1024]{1,0:T(8,128)(2,1)S(1)} %get-tuple-element.136.refs_11_.refs_8_), channel_id=1, source_target_pairs={{0,8},{8,0},{1,9},{9,1},{2,10},{10,2},{3,11},{11,3},{4,12},{12,4},... | collective-permute-start | bytes 196616 | tf_op jit(solution)/shard_map/ppermute | solution.py:438
  98.8 3.9 %collective-permute-start.33 = (bf16[32,1024]{1,0:T(8,128)(2,1)S(1)}, bf16[32,1024]{1,0:T(8,128)(2,1)S(1)}, u32[]{:S(2)}, u32[]{:S(2)}) collective-permute-start(bf16[32,1024]{1,0:T(8,128)(2,1)S(1)} %collective-permute-done.29.refs_12_.refs_9_), channel_id=1, source_target_pairs={{0,8},{8,0},{1,9},{9,1},{2,10},{10,2},{3,11},{11,3},{4,12},{12,4},... | collective-permute-start | bytes 196616 | tf_op jit(solution)/shard_map/ppermute | solution.py:438
  102.2 6.4 %collective-permute-start.24 = (bf16[4,64,1024]{2,1,0:T(8,128)(2,1)S(1)}, bf16[4,64,1024]{2,1,0:T(8,128)(2,1)S(1)}, u32[]{:S(2)}, u32[]{:S(2)}) collective-permute-start(bf16[4,64,1024]{2,1,0:T(8,128)(2,1)S(1)} %get-tuple-element.118), channel_id=1, source_target_pairs={{0,8},{8,0},{1,9},{9,1},{2,10},{10,2},{3,11},{11,3},{4,12},{12,4},... | collective-permute-start | bytes 1572872 | tf_op jit(solution)/shard_map/ppermute | solution.py:438
  109.5 13.3 %collective-permute-start.38 = (bf16[128,1024]{1,0:T(8,128)(2,1)S(1)}, bf16[128,1024]{1,0:T(8,128)(2,1)S(1)}, u32[]{:S(2)}, u32[]{:S(2)}) collective-permute-start(bf16[128,1024]{1,0:T(8,128)(2,1)S(1)} %get-tuple-element.142), channel_id=1, source_target_pairs={{0,2},{2,0},{4,6},{6,4},{1,3},{3,1},{5,7},{7,5},{8,10},{10,8},{12,... | collective-permute-start | bytes 786440 | tf_op jit(solution)/shard_map/ppermute | solution.py:425
  109.6 15.0 %collective-permute-start.39 = (bf16[128,1024]{1,0:T(8,128)(2,1)S(1)}, bf16[128,1024]{1,0:T(8,128)(2,1)S(1)}, u32[]{:S(2)}, u32[]{:S(2)}) collective-permute-start(bf16[128,1024]{1,0:T(8,128)(2,1)S(1)} %get-tuple-element.143), channel_id=1, source_target_pairs={{0,4},{2,6},{4,0},{6,2},{1,5},{3,7},{5,1},{7,3},{8,12},{10,14},{12... | collective-permute-start | bytes 786440 | tf_op jit(solution)/shard_map/ppermute | solution.py:425
  112.0 25.4 %collective-permute-start.44 = (bf16[256,1024]{1,0:T(8,128)(2,1)S(1)}, bf16[256,1024]{1,0:T(8,128)(2,1)S(1)}, u32[]{:S(2)}, u32[]{:S(2)}) collective-permute-start(bf16[256,1024]{1,0:T(8,128)(2,1)S(1)} %get-tuple-element.151), channel_id=1, source_target_pairs={{0,16},{16,0},{1,17},{17,1},{2,18},{18,2},{3,19},{19,3},{4,20},{20... | collective-permute-start | bytes 1572872 | tf_op jit(solution)/shard_map/ppermute | solution.py:1167
  114.4 19.1 %collective-permute-start.45 = (bf16[272,512]{1,0:T(8,128)(2,1)S(1)}, bf16[272,512]{1,0:T(8,128)(2,1)S(1)}, u32[]{:S(2)}, u32[]{:S(2)}) collective-permute-start(bf16[272,512]{1,0:T(8,128)(2,1)S(1)} %get-tuple-element.157), channel_id=1, source_target_pairs={{0,1},{1,0},{16,17},{17,16},{2,3},{3,2},{18,19},{19,18},{4,5},{5,4... | collective-permute-start | bytes 835592 | tf_op jit(solution)/shard_map/ppermute | solution.py:430
  115.6 21.7 %collective-permute-start.46 = (bf16[272,512]{1,0:T(8,128)(2,1)S(1)}, bf16[272,512]{1,0:T(8,128)(2,1)S(1)}, u32[]{:S(2)}, u32[]{:S(2)}) collective-permute-start(bf16[272,512]{1,0:T(8,128)(2,1)S(1)} %get-tuple-element.158), channel_id=1, source_target_pairs={{0,16},{1,17},{16,0},{17,1},{2,18},{3,19},{18,2},{19,3},{4,20},{5,... | collective-permute-start | bytes 835592 | tf_op jit(solution)/shard_map/ppermute | solution.py:430
  122.8 14.6 %collective-permute-start.47 = (bf16[272,512]{1,0:T(8,128)(2,1)S(1)}, bf16[272,512]{1,0:T(8,128)(2,1)S(1)}, u32[]{:S(2)}, u32[]{:S(2)}) collective-permute-start(bf16[272,512]{1,0:T(8,128)(2,1)S(1)} %get-tuple-element.159), channel_id=1, source_target_pairs={{0,17},{1,16},{16,1},{17,0},{2,19},{3,18},{18,3},{19,2},{4,21},{5,... | collective-permute-start | bytes 835592 | tf_op jit(solution)/shard_map/ppermute | solution.py:430
  124.6 8.9 %collective-permute-start.40 = (bf16[128,1024]{1,0:T(8,128)(2,1)S(1)}, bf16[128,1024]{1,0:T(8,128)(2,1)S(1)}, u32[]{:S(2)}, u32[]{:S(2)}) collective-permute-start(bf16[128,1024]{1,0:T(8,128)(2,1)S(1)} %get-tuple-element.144), channel_id=1, source_target_pairs={{0,6},{2,4},{4,2},{6,0},{1,7},{3,5},{5,3},{7,1},{8,14},{10,12},{12... | collective-permute-start | bytes 786440 | tf_op jit(solution)/shard_map/ppermute | solution.py:425
  139.2 6.7 %collective-permute-start.41 = (bf16[32,1024]{1,0:T(8,128)(2,1)S(1)}, bf16[32,1024]{1,0:T(8,128)(2,1)S(1)}, u32[]{:S(2)}, u32[]{:S(2)}) collective-permute-start(bf16[32,1024]{1,0:T(8,128)(2,1)S(1)} %get-tuple-element.146), channel_id=1, source_target_pairs={{0,1},{1,0},{16,17},{17,16},{2,3},{3,2},{18,19},{19,18},{4,5},{5,4... | collective-permute-start | bytes 196616 | tf_op jit(solution)/shard_map/ppermute | solution.py:430
  140.8 12.9 %collective-permute-start.49 = (bf16[64,1024]{1,0:T(8,128)(2,1)S(1)}, bf16[64,1024]{1,0:T(8,128)(2,1)S(1)}, u32[]{:S(2)}, u32[]{:S(2)}) collective-permute-start(bf16[64,1024]{1,0:T(8,128)(2,1)S(1)} %get-tuple-element.163), channel_id=1, source_target_pairs={{0,2},{2,0},{4,6},{6,4},{1,3},{3,1},{5,7},{7,5},{8,10},{10,8},{12,... | collective-permute-start | bytes 393224 | tf_op jit(solution)/shard_map/ppermute | solution.py:425
  141.4 12.9 %collective-permute-start.50 = (bf16[64,1024]{1,0:T(8,128)(2,1)S(1)}, bf16[64,1024]{1,0:T(8,128)(2,1)S(1)}, u32[]{:S(2)}, u32[]{:S(2)}) collective-permute-start(bf16[64,1024]{1,0:T(8,128)(2,1)S(1)} %get-tuple-element.164), channel_id=1, source_target_pairs={{0,4},{2,6},{4,0},{6,2},{1,5},{3,7},{5,1},{7,3},{8,12},{10,14},{12... | collective-permute-start | bytes 393224 | tf_op jit(solution)/shard_map/ppermute | solution.py:425
  143.4 11.0 %collective-permute-start.51 = (bf16[64,1024]{1,0:T(8,128)(2,1)S(1)}, bf16[64,1024]{1,0:T(8,128)(2,1)S(1)}, u32[]{:S(2)}, u32[]{:S(2)}) collective-permute-start(bf16[64,1024]{1,0:T(8,128)(2,1)S(1)} %get-tuple-element.165), channel_id=1, source_target_pairs={{0,6},{2,4},{4,2},{6,0},{1,7},{3,5},{5,3},{7,1},{8,14},{10,12},{12... | collective-permute-start | bytes 393224 | tf_op jit(solution)/shard_map/ppermute | solution.py:425
  145.2 4.6 %collective-permute-start.42 = (bf16[32,1024]{1,0:T(8,128)(2,1)S(1)}, bf16[32,1024]{1,0:T(8,128)(2,1)S(1)}, u32[]{:S(2)}, u32[]{:S(2)}) collective-permute-start(bf16[32,1024]{1,0:T(8,128)(2,1)S(1)} %get-tuple-element.147), channel_id=1, source_target_pairs={{0,16},{1,17},{16,0},{17,1},{2,18},{3,19},{18,2},{19,3},{4,20},{5,... | collective-permute-start | bytes 196616 | tf_op jit(solution)/shard_map/ppermute | solution.py:430
  145.9 5.2 %collective-permute-start.43 = (bf16[32,1024]{1,0:T(8,128)(2,1)S(1)}, bf16[32,1024]{1,0:T(8,128)(2,1)S(1)}, u32[]{:S(2)}, u32[]{:S(2)}) collective-permute-start(bf16[32,1024]{1,0:T(8,128)(2,1)S(1)} %get-tuple-element.148), channel_id=1, source_target_pairs={{0,17},{1,16},{16,1},{17,0},{2,19},{3,18},{18,3},{19,2},{4,21},{5,... | collective-permute-start | bytes 196616 | tf_op jit(solution)/shard_map/ppermute | solution.py:430
  (12 other events, 86.8 us)
